TPU v7x, 32 devices: a whole 2x2x4 slice. The times are simulated.
32 devices in a mesh: blk: 8 (over z, y), grp: 4 (over x, core).
Axes of the slice: x: 2, y: 2, z: 4, core: 2. Of those that a mesh axis runs over, the one named last changes fastest.
Arguments:
- acts: bfloat16 [1, 128, 256, 4096], P(None, 'blk', 'grp'), may hold values from -6 to 6
- out_grads: bfloat16 [1, 128, 256, 4096], P(None, 'blk', 'grp'), may hold values from -6 to 6
- proj_in: bfloat16 [1, 4096, 64], replicated, may hold values from -0.09375 to 0.09375
- proj_out: bfloat16 [1, 4096, 64], replicated, may hold values from -0.09375 to 0.09375
- lengths: int32 [128], P('blk'), may hold values from 1 to 256
- queries: bfloat16 [512, 4096], P('blk'), may hold values from -0.09375 to 0.09375
Outputs:
- scores: float32 [128, 512], P(('blk', 'grp'))
All inputs are finite; a program needn't handle non-finite values.
Results may differ from a plain program's by a relative error of at most 0.0049.
Values may be sent and summed in bfloat16 or wider, within the bound.
No kernel may reach another device: no remote copies, remote signals or barrier semaphores. Data moves between devices by JAX's collectives and lax.ppermute only.
A program may use at most 128 MiB of HBM per device.

v0:
```python
import jax
import jax.numpy as jnp
from jax import lax
from jax.sharding import PartitionSpec as P


def project(rows, matrix):
    return jnp.einsum("lctd,ldr->lctr", rows, matrix, preferred_element_type=jnp.float32).astype(
        jnp.bfloat16
    )


def outer_sums(grad_side, input_side, lens):
    positions = jnp.arange(grad_side.shape[2], dtype=jnp.int32)
    masked = (positions[None, :] < lens[:, None]).astype(jnp.bfloat16)
    grad_masked = grad_side * masked[None, :, :, None]
    block = jnp.einsum(
        "lcta,lctb->clab", grad_masked, input_side, preferred_element_type=jnp.float32
    )
    return block.reshape(block.shape[0], -1)


def on_device(acts, out_grads, proj_in, proj_out, lengths, queries):
    group = lax.axis_index("grp")
    groups = lax.axis_size("grp")
    cand_blk = acts.shape[1]
    owned = cand_blk // groups
    stacked = jnp.concatenate([project(out_grads, proj_out), project(acts, proj_in)], axis=3)
    stacked = lax.all_to_all(stacked, "grp", split_axis=1, concat_axis=2, tiled=True)
    width = proj_in.shape[2]
    own_lens = lax.dynamic_slice_in_dim(lengths, group * owned, owned)
    grads = outer_sums(stacked[..., :width], stacked[..., width:], own_lens)
    scale = lax.rsqrt(jnp.mean(grads * grads, axis=1, keepdims=True) + 1e-06)
    unit = (grads * scale).astype(jnp.bfloat16)
    return lax.dot_general(
        unit,
        lax.all_gather(queries, "blk", axis=0, tiled=True),
        (((1,), (1,)), ((), ())),
        preferred_element_type=jnp.float32,
    )


def solution(mesh):
    in_specs = (
        P(None, "blk", "grp", None),
        P(None, "blk", "grp", None),
        P(),
        P(),
        P("blk"),
        P("blk", None),
    )
    out_specs = P(("blk", "grp"), None)
    return jax.shard_map(
        on_device, mesh=mesh, in_specs=in_specs, out_specs=out_specs, check_vma=False
    )
```

profile of v0, /device:TPU:0, one launch (start us, length us, event | category | flops | bytes accessed | tf_op | source)
XLA Modules:
  0.0 96.4 jit_solution(11072109660876124498)
XLA Ops:
  6.5 0.0 copy-start
  6.5 0.0 copy-start.2
  6.5 0.0 all-gather.2.cloned.1.call-start
  6.5 0.7 all-gather.2.cloned.1.call-update
  7.3 0.3 copy-done
  7.6 0.0 copy-start.1
  7.6 5.8 %fusion.10 = bf16[1,16,64,64]{3,2,1,0:T(8,128)(2,1)S(1)} fusion(bf16[1,16,64,4096]{3,2,1,0:T(8,128)(2,1)} %param.6, bf16[1,4096,64]{1,2,0:T(8,128)(2,1)S(1)} %copy-done), kind=kOutput, calls=%fused_computation.6 | convolution fusion | flops 536936448 | bytes 9043968 | tf_op jit(solution)/shard_map/lctd,ldr->lctr/dot_general | solution.py:8
  13.4 0.0 copy-done.2
  13.4 0.0 copy-done.1
  13.4 0.0 copy-start.3
  13.5 2.4 %fusion.13 = bf16[1,16,64,64]{3,2,1,0:T(8,128)(2,1)S(1)} fusion(bf16[1,16,64,4096]{3,2,1,0:T(8,128)(2,1)S(1)} %copy-done.1, bf16[1,4096,64]{1,2,0:T(8,128)(2,1)S(1)} %copy-done.2), kind=kOutput, calls=%fused_computation.7 | convolution fusion | flops 536936448 | bytes 9043968 | tf_op jit(solution)/shard_map/lctd,ldr->lctr/dot_general | solution.py:8
  15.8 0.9 maximum_bitcast_fusion
  16.7 4.2 %all-to-all-start = ((bf16[1,16,64,128]{3,2,0,1:T(8,128)(2,1)}), bf16[1,16,64,128]{3,2,0,1:T(8,128)(2,1)S(1)}, u32[]{:S(2)}, u32[]{:S(2)}) async-start(bf16[1,16,64,128]{3,2,0,1:T(8,128)(2,1)} %maximum_bitcast_fusion), calls=%async_computation | async-start | bytes 524288 | tf_op jit(solution)/shard_map/all_to_all | solution.py:29
  20.9 0.0 copy-done.3
  20.9 0.1 dynamic_slice.3
  21.0 0.1 fusion.24
  21.0 5.9 %all-to-all-done = bf16[1,16,64,128]{3,2,0,1:T(8,128)(2,1)S(1)} async-done(((bf16[1,16,64,128]{3,2,0,1:T(8,128)(2,1)}), bf16[1,16,64,128]{3,2,0,1:T(8,128)(2,1)S(1)}, u32[]{:S(2)}, u32[]{:S(2)}) %all-to-all-start) | async-done | bytes 262176 | tf_op jit(solution)/shard_map/all_to_all | solution.py:29
  26.9 0.6 multiply_reduce_fusion
  27.5 0.1 reshape.65
  27.6 58.0 %all-gather.2.cloned.1.call-done = bf16[512,4096]{1,0:T(8,128)(2,1)} async-done(((bf16[64,4096]{1,0:T(8,128)(2,1)}), bf16[512,4096]{1,0:T(8,128)(2,1)}) %all-gather.2.cloned.1.call-update) | async-done | bytes 4194320 | tf_op jit(solution)/shard_map/all_gather | solution.py:37
  85.6 4.0 %fusion.22 = f32[4,512]{1,0:T(4,128)} fusion(bf16[512,4096]{1,0:T(8,128)(2,1)} %all-gather.2.cloned.1.call-done, f32[4,4096]{1,0:T(4,128)S(1)} %reshape.65, f32[4]{0:T(128)S(1)} %add_rsqrt_fusion), kind=kOutput, calls=%fused_computation.18 | convolution fusion | flops 16809984 | bytes 4268048 | tf_op jit(solution)/shard_map/dot_general | solution.py:35
  (2 shorter events, 0.0 us)
Async XLA Ops:
  6.5 1.0 %copy-start = (bf16[1,4096,64]{1,2,0:T(8,128)(2,1)S(1)}, bf16[1,4096,64]{1,2,0:T(8,128)(2,1)}, u32[]{:S(2)}) copy-start(bf16[1,4096,64]{1,2,0:T(8,128)(2,1)} %param.8) | copy-start | bytes 1572868
  6.5 6.9 %copy-start.2 = (bf16[1,4096,64]{1,2,0:T(8,128)(2,1)S(1)}, bf16[1,4096,64]{1,2,0:T(8,128)(2,1)}, u32[]{:S(2)}) copy-start(bf16[1,4096,64]{1,2,0:T(8,128)(2,1)} %param.9) | copy-start | bytes 1572868
  6.5 79.1 %all-gather.2.cloned.1.call-start = ((), (), s32[]{:S(2)}) async-start(), calls=%async_computation.1 | async-start | bytes 4718592 | tf_op jit(solution)/shard_map/all_gather | solution.py:37
  7.6 5.9 %copy-start.1 = (bf16[1,16,64,4096]{3,2,1,0:T(8,128)(2,1)S(1)}, bf16[1,16,64,4096]{3,2,1,0:T(8,128)(2,1)}, u32[]{:S(2)}) copy-start(bf16[1,16,64,4096]{3,2,1,0:T(8,128)(2,1)} %param.7) | copy-start | bytes 25165828
  13.4 7.4 %copy-start.3 = (s32[16]{0:T(128)S(1)}, s32[16]{0:T(128)}, u32[]{:S(2)}) copy-start(s32[16]{0:T(128)} %param.10) | copy-start | bytes 196
  16.7 10.2 %all-to-all-start = ((bf16[1,16,64,128]{3,2,0,1:T(8,128)(2,1)}), bf16[1,16,64,128]{3,2,0,1:T(8,128)(2,1)S(1)}, u32[]{:S(2)}, u32[]{:S(2)}) async-start(bf16[1,16,64,128]{3,2,0,1:T(8,128)(2,1)} %maximum_bitcast_fusion), calls=%async_computation | async-start | bytes 524288 | tf_op jit(solution)/shard_map/all_to_all | solution.py:29
Sparse Core Ops, SparseCore 0:
  9.5 76.0 all-gather.1
where the time goes:
time: 96.7 us; the launch traced here: 96.4 us
  waiting for transfers between devices  64.6 us (67%)
  between operations  13.4 us (14%)
  matrix products  12.7 us (13%)
  starting transfers between devices  4.21 us (4%)
    all_gather x1, waiting for transfers between devices, on_device(): lax.all_gather(queries, 'blk', axis=0, tiled=True)  58 us
    dot_general x2, matrix products, project(): jnp.einsum('lctd,ldr->lctr', rows, matrix, preferred_element_type=jnp.flo...  8.19 us
    all_to_all x1, waiting for transfers between devices, on_device(): lax.all_to_all(stacked, 'grp', split_axis=1, concat_axis=2, tiled=True)  5.89 us
    all_to_all x1, starting transfers between devices, on_device(): lax.all_to_all(stacked, 'grp', split_axis=1, concat_axis=2, tiled=True)  4.21 us
    dot_general x1, matrix products, on_device(): lax.dot_general(unit, lax.all_gather(queries, 'blk', axis=0, tiled=True),...  3.98 us
  transfers between devices with their start and end apart: 2, of which 2 were waited for; matrix products, arithmetic and copies ran while one was open for 10% of the time, Pallas kernels for 0%

commit v1 on v0

v1 whole, which is shorter than its diff:
```python
import functools

import jax
import jax.numpy as jnp
from jax import lax
from jax.experimental import pallas as pl
from jax.experimental.pallas import tpu as pltpu
from jax.sharding import PartitionSpec as P

EPS = 1e-06
NEAR = 2
F32 = jnp.float32
BF16 = jnp.bfloat16
VMEM = pl.BlockSpec(memory_space=pltpu.VMEM)
SMEM = pl.BlockSpec(memory_space=pltpu.SMEM)
ANY = pl.BlockSpec(memory_space=pl.ANY)


def team_rank(groups):
    near = lax.rem(lax.axis_index("blk"), NEAR)
    return near * groups + lax.axis_index("grp")


def grads_kernel(dims, lens, acts, out_grads, w_in, w_out, *rest):
    cands, tokens, width, team, groups, per = dims
    outs = rest[:team]
    act_buf, grad_buf, win_buf, wout_buf, square, store, sems, wsems = rest[team:]
    chunks = cands // per
    rows = per * tokens
    load_w = [
        pltpu.make_async_copy(w_out, wout_buf, wsems.at[0]),
        pltpu.make_async_copy(w_in, win_buf, wsems.at[1]),
    ]
    loads = []
    for i in range(chunks):
        part = pl.ds(i * rows, rows)
        loads.append(
            (
                pltpu.make_async_copy(out_grads.at[part], grad_buf.at[part], sems.at[0, i]),
                pltpu.make_async_copy(acts.at[part], act_buf.at[part], sems.at[1, i]),
            )
        )
    load_w[0].start()
    loads[0][0].start()
    load_w[1].start()
    loads[0][1].start()
    for pair in loads[1:]:
        for load in pair:
            load.start()
    first = lax.axis_index("grp") * tokens
    fold = 128 // width
    lines = width * width // 128
    each = lines // team
    position = lax.broadcasted_iota(jnp.int32, (tokens, width), 0) + first
    for i in range(chunks):
        part = pl.ds(i * rows, rows)
        if i == 0:
            load_w[0].wait()
        loads[i][0].wait()
        gp = jnp.dot(grad_buf[part, :], wout_buf[...], preferred_element_type=F32).astype(BF16)
        if i == 0:
            load_w[1].wait()
        loads[i][1].wait()
        xp = jnp.dot(act_buf[part, :], win_buf[...], preferred_element_type=F32).astype(BF16)
        for j in range(per):
            cand = i * per + j
            here = slice(j * tokens, (j + 1) * tokens)
            masked = jnp.where(position < lens[cand], gp[here].astype(F32), 0.0)
            block = jnp.dot(masked.T.astype(BF16), xp[here], preferred_element_type=F32)
            square[cand % 2, :, :width] = block
            line = jnp.concatenate(
                [square[cand % 2, pl.ds(h, lines, stride=fold), :width] for h in range(fold)], axis=1
            )
            for s in range(team):
                store[s, cand * each : (cand + 1) * each, :] = line[s * each : (s + 1) * each]
    rank = team_rank(groups)
    for k in range(team):
        outs[k][...] = store[jnp.bitwise_xor(rank, k)].astype(BF16)


def scores_kernel(dims, *refs):
    cands, team, groups, blks, each = dims
    parts = refs[:team]
    queries = refs[team : team + blks]
    outs = refs[team + blks : 2 * team + blks]
    grads, table, result, sems = refs[2 * team + blks :]
    nq = queries[0].shape[0]
    blk = lax.axis_index("blk")
    loads = []
    for k in range(blks):
        row = pl.multiple_of(jnp.bitwise_xor(blk, k) * nq, nq)
        loads.append(pltpu.make_async_copy(queries[k], table.at[pl.ds(row, nq)], sems.at[k]))
    for load in loads:
        load.start()
    rows = cands * each
    for half in range(NEAR):
        total = parts[half * groups][...].astype(F32)
        for g in range(1, groups):
            total = total + parts[half * groups + g][...].astype(F32)
        grads[half * rows : (half + 1) * rows, :] = total
    lines = [grads[pl.ds(e, NEAR * cands, stride=each), :] for e in range(each)]
    squares = lines[0] * lines[0]
    for line in lines[1:]:
        squares = squares + line * line
    left = jnp.concatenate([line.astype(BF16) for line in lines], axis=1)
    for load in loads:
        load.wait()
    scores = lax.dot_general(left, table[...], (((1,), (1,)), ((), ())), preferred_element_type=F32)
    owned = cands // groups
    total_q = blks * nq
    for j in range(team):
        result[j, :, :total_q] = scores[j * owned : (j + 1) * owned]
        result[j, :, total_q:] = squares[j * owned : (j + 1) * owned]
    grp = lax.axis_index("grp")
    for k in range(team):
        half, other = k // groups, k % groups
        outs[k][...] = result[half * groups + jnp.bitwise_xor(grp, other)]


def finish_kernel(pdim, *refs):
    out = refs[-1]
    total = refs[0][...]
    for ref in refs[1:-1]:
        total = total + ref[...]
    nq = out.shape[1]
    mean = jnp.sum(total[:, nq:], axis=1, keepdims=True) / pdim
    out[...] = total[:, :nq] * lax.rsqrt(mean + EPS)


def on_device(blks, groups, acts, out_grads, proj_in, proj_out, lengths, queries):
    _, cands, tokens, depth = acts.shape
    width = proj_in.shape[2]
    team = NEAR * groups
    per = 4
    pdim = width * width
    each = pdim // 128 // team
    nq = queries.shape[0]
    both = ("blk", "grp")

    def team_swap(x, k):
        near, other = k // groups, k % groups
        perm = [
            (b * groups + g, (b ^ near) * groups + (g ^ other)) for b in range(blks) for g in range(groups)
        ]
        return lax.ppermute(x, both, perm)

    slice_width = pdim // team
    rank = team_rank(groups)
    cut = [
        lax.dynamic_slice(queries, (0, jnp.bitwise_xor(rank, near * groups) * slice_width), (nq, slice_width))
        for near in range(NEAR)
    ]
    gathered = [cut[0]] + [
        lax.ppermute(cut[k % NEAR], "blk", [(b, b ^ k) for b in range(blks)]) for k in range(1, blks)
    ]

    rows = cands * tokens
    parts = pl.pallas_call(
        functools.partial(grads_kernel, (cands, tokens, width, team, groups, per)),
        out_shape=[jax.ShapeDtypeStruct((cands * each, 128), BF16)] * team,
        in_specs=[SMEM, ANY, ANY, ANY, ANY],
        out_specs=[VMEM] * team,
        scratch_shapes=[
            pltpu.VMEM((rows, depth), BF16),
            pltpu.VMEM((rows, depth), BF16),
            pltpu.VMEM((depth, width), BF16),
            pltpu.VMEM((depth, width), BF16),
            pltpu.VMEM((2, width, 128), F32),
            pltpu.VMEM((team, cands * each, 128), F32),
            pltpu.SemaphoreType.DMA((2, cands // per)),
            pltpu.SemaphoreType.DMA((2,)),
        ],
        compiler_params=pltpu.CompilerParams(vmem_limit_bytes=40 * 2**20),
        cost_estimate=pl.CostEstimate(
            flops=4 * rows * depth * width, bytes_accessed=4 * rows * depth, transcendentals=0
        ),
        name="grads",
    )(
        lengths,
        acts.reshape(rows, depth),
        out_grads.reshape(rows, depth),
        proj_in.reshape(depth, width),
        proj_out.reshape(depth, width),
    )
    parts = [parts[0]] + [team_swap(parts[k], k) for k in range(1, team)]

    owned = cands // groups
    total_q = nq * blks
    packed = jax.ShapeDtypeStruct((owned, total_q + 128), F32)
    sums = pl.pallas_call(
        functools.partial(scores_kernel, (cands, team, groups, blks, each)),
        out_shape=[packed] * team,
        in_specs=[VMEM] * team + [ANY] * blks,
        out_specs=[VMEM] * team,
        scratch_shapes=[
            pltpu.VMEM((NEAR * cands * each, 128), F32),
            pltpu.VMEM((total_q, slice_width), BF16),
            pltpu.VMEM((team, owned, total_q + 128), F32),
            pltpu.SemaphoreType.DMA((blks,)),
        ],
        compiler_params=pltpu.CompilerParams(vmem_limit_bytes=24 * 2**20),
        cost_estimate=pl.CostEstimate(
            flops=2 * NEAR * cands * total_q * slice_width,
            bytes_accessed=2 * total_q * slice_width,
            transcendentals=0,
        ),
        name="scores",
    )(*parts, *gathered)
    sums = [sums[0]] + [team_swap(sums[k], k) for k in range(1, team)]

    return pl.pallas_call(
        functools.partial(finish_kernel, pdim),
        out_shape=jax.ShapeDtypeStruct((owned, total_q), F32),
        in_specs=[VMEM] * team,
        out_specs=VMEM,
        name="finish",
    )(*sums)


def solution(mesh):
    in_specs = (
        P(None, "blk", "grp", None),
        P(None, "blk", "grp", None),
        P(),
        P(),
        P("blk"),
        P("blk", None),
    )
    return jax.shard_map(
        functools.partial(on_device, mesh.shape["blk"], mesh.shape["grp"]),
        mesh=mesh,
        in_specs=in_specs,
        out_specs=P(("blk", "grp"), None),
        check_vma=False,
    )
```

time: 96.7 us -> 57.2 us (0.59)
  waiting for transfers between devices: 64.6 us -> 12 us
  starting transfers between devices: 4.21 us -> 24.3 us
  between operations: 13.4 us -> 0.14 us
  matrix products: 12.7 us -> 0 us
  Pallas kernels: 0 us -> 11.2 us
  local copies, waits for them, and re-layouts: 0.53 us -> 9.12 us
    all_gather x1 -> x0, waiting for transfers between devices: 58 us -> none  [on_device(): lax.all_gather(queries, 'blk', axis=0, tiled=True)]
    ppermute x0 -> x21, starting transfers between devices: none -> 24.3 us  [the longest x7 13.2 us: on_device(): lax.ppermute(cut[k % NEAR], 'blk', [(b, b ^ k) for b in range(blks)])]
    dot_general x4 -> x0, matrix products: 12.7 us -> none  [the longest x2 8.19 us: project(): jnp.einsum('lctd,ldr->lctr', rows, matrix, preferred_element_type=jnp.flo...]
    ppermute x0 -> x21, waiting for transfers between devices: none -> 12 us  [the longest x14 6.85 us: team_swap(): return lax.ppermute(x, both, perm)]
    pallas_call x0 -> x3, Pallas kernels: none -> 11.2 us  [the longest x1 8.67 us: on_device(): pl.pallas_call(functools.partial(grads_kernel, (cands, tokens, width, tea...]
    unnamed x8 -> x22, local copies, waits for them, and re-layouts: 0.33 us -> 8.24 us
    all_to_all x1 -> x0, waiting for transfers between devices: 5.89 us -> none  [on_device(): lax.all_to_all(stacked, 'grp', split_axis=1, concat_axis=2, tiled=True)]
    all_to_all x1 -> x0, starting transfers between devices: 4.21 us -> none  [on_device(): lax.all_to_all(stacked, 'grp', split_axis=1, concat_axis=2, tiled=True)]
  transfers between devices with their start and end apart: 2 -> 21, of which waited for: 2 -> 7; matrix products, arithmetic and copies ran while one was open for 10% -> 5% of each run, Pallas kernels for 0% -> 15%
where the time goes in v1:
time: 57.2 us; the launch traced here: 56.8 us
  starting transfers between devices  24.3 us (42%)
  waiting for transfers between devices  12 us (21%)
  Pallas kernels  11.2 us (20%)
  local copies, waits for them, and re-layouts  9.12 us (16%)
    ppermute x7, starting transfers between devices, on_device(): lax.ppermute(cut[k % NEAR], 'blk', [(b, b ^ k) for b in range(blks)])  13.2 us
    ppermute x14, starting transfers between devices, team_swap(): return lax.ppermute(x, both, perm)  11.1 us
    pallas_call x1, Pallas kernels, on_device(): pl.pallas_call(functools.partial(grads_kernel, (cands, tokens, width, tea...  8.67 us
    unnamed x22, local copies, waits for them, and re-layouts  8.24 us
    ppermute x14, waiting for transfers between devices, team_swap(): return lax.ppermute(x, both, perm)  6.85 us
    ppermute x7, waiting for transfers between devices, on_device(): lax.ppermute(cut[k % NEAR], 'blk', [(b, b ^ k) for b in range(blks)])  5.14 us
    pallas_call x1, Pallas kernels, on_device(): pl.pallas_call(functools.partial(finish_kernel, pdim), out_shape=jax.Shap...  1.51 us
  transfers between devices with their start and end apart: 21, of which 7 were waited for; matrix products, arithmetic and copies ran while one was open for 5% of the time, Pallas kernels for 15%

profile of v1, /device:TPU:0, one launch (start us, length us, event | category | flops | bytes accessed | tf_op | source)
XLA Modules:
  0.0 56.8 jit_solution(15726315523269161152)
XLA Ops:
  0.0 0.9 %constant_dynamic-slice_fusion = (bf16[64,512]{1,0:T(8,128)(2,1)S(1)}, bf16[64,512]{1,0:T(8,128)(2,1)S(1)}) fusion(bf16[64,4096]{1,0:T(8,128)(2,1)} %param.11, s32[]{:T(128)S(6)} %select_n.7, s32[]{:T(128)S(6)} %select_n.6), kind=kLoop, calls=%fused_computation | loop fusion | bytes 262152 | tf_op jit(solution)/shard_map/dynamic_slice | solution.py:150
  0.9 3.0 %collective-permute-start.7 = (bf16[64,512]{1,0:T(8,128)(2,1)S(1)}, bf16[64,512]{1,0:T(8,128)(2,1)S(1)}, u32[]{:S(2)}, u32[]{:S(2)}) collective-permute-start(bf16[64,512]{1,0:T(8,128)(2,1)S(1)} %get-tuple-element.37), channel_id=1, source_target_pairs={{0,4},{4,0},{8,12},{12,8},{16,20},{20,16},{24,28},{28,24},{1,5},{5... | collective-permute-start | bytes 196616 | tf_op jit(solution)/shard_map/ppermute | solution.py:154
  3.9 1.6 %collective-permute-start.8 = (bf16[64,512]{1,0:T(8,128)(2,1)S(1)}, bf16[64,512]{1,0:T(8,128)(2,1)S(1)}, u32[]{:S(2)}, u32[]{:S(2)}) collective-permute-start(bf16[64,512]{1,0:T(8,128)(2,1)S(1)} %get-tuple-element.38.refs_8_), channel_id=1, source_target_pairs={{0,8},{4,12},{8,0},{12,4},{16,24},{20,28},{24,16},{28,20},{1,9},{5... | collective-permute-start | bytes 196616 | tf_op jit(solution)/shard_map/ppermute | solution.py:154
  5.5 1.5 %copy.7 = bf16[1,4096,64]{2,1,0:T(8,128)(2,1)S(1)} copy(bf16[1,4096,64]{1,2,0:T(8,128)(2,1)} %param.8) | data formatting | bytes 1048576 | tf_op args[2]
  7.0 1.5 %copy.8 = bf16[1,4096,64]{2,1,0:T(8,128)(2,1)S(1)} copy(bf16[1,4096,64]{1,2,0:T(8,128)(2,1)} %param.9) | data formatting | bytes 1048576 | tf_op args[3]
  8.6 3.4 %copy-done = bf16[1,16,64,4096]{3,2,1,0:T(8,128)(2,1)S(1)} copy-done((bf16[1,16,64,4096]{3,2,1,0:T(8,128)(2,1)S(1)}, bf16[1,16,64,4096]{3,2,1,0:T(8,128)(2,1)}, u32[]{:S(2)}) %copy-start) | copy-done | bytes 8388632
  11.9 0.7 %copy-done.2 = s32[16]{0:T(128)S(1)} copy-done((s32[16]{0:T(128)S(1)}, s32[16]{0:T(128)}, u32[]{:S(2)}) %copy-start.2) | copy-done | bytes 88
  12.6 8.7 %grads.1 = (bf16[64,128]{1,0:T(8,128)(2,1)S(1)}, bf16[64,128]{1,0:T(8,128)(2,1)S(1)}, bf16[64,128]{1,0:T(8,128)(2,1)S(1)}, bf16[64,128]{1,0:T(8,128)(2,1)S(1)}, ...) custom-call(s32[16]{0:T(128)S(1)} %copy-done.2, ...), custom_call_target="tpu_custom_call" | custom-call | flops 1073741824 | bytes 16777216 | tf_op jit(solution)/shard_map/grads/pallas_call | solution.py:158
  21.3 1.6 %collective-permute-start.1 = (bf16[64,128]{1,0:T(8,128)(2,1)S(1)}, bf16[64,128]{1,0:T(8,128)(2,1)S(1)}, u32[]{:S(2)}, u32[]{:S(2)}) collective-permute-start(bf16[64,128]{1,0:T(8,128)(2,1)S(1)} %get-tuple-element.23), channel_id=1, source_target_pairs={{0,2},{1,3},{2,0},{3,1},{4,6},{5,7},{6,4},{7,5},{8,10},{9,11},{10,... | collective-permute-start | bytes 49160 | tf_op jit(solution)/shard_map/ppermute | solution.py:145
  23.7 1.4 %collective-permute-done.1.refs_2_ = bf16[64,128]{1,0:T(8,128)(2,1)S(1)} collective-permute-done((bf16[64,128]{1,0:T(8,128)(2,1)S(1)}, bf16[64,128]{1,0:T(8,128)(2,1)S(1)}, u32[]{:S(2)}, u32[]{:S(2)}) %collective-permute-start.1) | collective-permute-done | bytes 16416 | tf_op jit(solution)/shard_map/ppermute | solution.py:145
  25.1 0.9 %collective-permute-done.2.refs_3_ = bf16[64,128]{1,0:T(8,128)(2,1)S(1)} collective-permute-done((bf16[64,128]{1,0:T(8,128)(2,1)S(1)}, bf16[64,128]{1,0:T(8,128)(2,1)S(1)}, u32[]{:S(2)}, u32[]{:S(2)}) %collective-permute-start.2) | collective-permute-done | bytes 16416 | tf_op jit(solution)/shard_map/ppermute | solution.py:145
  26.1 0.9 %collective-permute-start.5 = (bf16[64,128]{1,0:T(8,128)(2,1)S(1)}, bf16[64,128]{1,0:T(8,128)(2,1)S(1)}, u32[]{:S(2)}, u32[]{:S(2)}) collective-permute-start(bf16[64,128]{1,0:T(8,128)(2,1)S(1)} %get-tuple-element.27), channel_id=1, source_target_pairs={{0,6},{1,7},{2,4},{3,5},{4,2},{5,3},{6,0},{7,1},{8,14},{9,15},{10,... | collective-permute-start | bytes 49160 | tf_op jit(solution)/shard_map/ppermute | solution.py:145
  27.0 1.5 %collective-permute-start.6 = (bf16[64,128]{1,0:T(8,128)(2,1)S(1)}, bf16[64,128]{1,0:T(8,128)(2,1)S(1)}, u32[]{:S(2)}, u32[]{:S(2)}) collective-permute-start(bf16[64,128]{1,0:T(8,128)(2,1)S(1)} %get-tuple-element.28), channel_id=1, source_target_pairs={{0,7},{1,6},{2,5},{3,4},{4,3},{5,2},{6,1},{7,0},{8,15},{9,14},{10,... | collective-permute-start | bytes 49160 | tf_op jit(solution)/shard_map/ppermute | solution.py:145
  28.5 1.0 %collective-permute-start.9 = (bf16[64,512]{1,0:T(8,128)(2,1)S(1)}, bf16[64,512]{1,0:T(8,128)(2,1)S(1)}, u32[]{:S(2)}, u32[]{:S(2)}) collective-permute-start(bf16[64,512]{1,0:T(8,128)(2,1)S(1)} %get-tuple-element.37), channel_id=1, source_target_pairs={{0,12},{4,8},{8,4},{12,0},{16,28},{20,24},{24,20},{28,16},{1,13},{... | collective-permute-start | bytes 196616 | tf_op jit(solution)/shard_map/ppermute | solution.py:154
  29.4 1.3 %collective-permute-done.5.refs_6_ = bf16[64,128]{1,0:T(8,128)(2,1)S(1)} collective-permute-done((bf16[64,128]{1,0:T(8,128)(2,1)S(1)}, bf16[64,128]{1,0:T(8,128)(2,1)S(1)}, u32[]{:S(2)}, u32[]{:S(2)}) %collective-permute-start.5) | collective-permute-done | bytes 16416 | tf_op jit(solution)/shard_map/ppermute | solution.py:145
  30.7 2.6 %collective-permute-start.10 = (bf16[64,512]{1,0:T(8,128)(2,1)S(1)}, bf16[64,512]{1,0:T(8,128)(2,1)S(1)}, u32[]{:S(2)}, u32[]{:S(2)}) collective-permute-start(bf16[64,512]{1,0:T(8,128)(2,1)S(1)} %get-tuple-element.38.refs_8_), channel_id=1, source_target_pairs={{0,16},{4,20},{8,24},{12,28},{16,0},{20,4},{24,8},{28,12},{1,17},{... | collective-permute-start | bytes 196616 | tf_op jit(solution)/shard_map/ppermute | solution.py:154
  33.3 1.0 %collective-permute-start.11 = (bf16[64,512]{1,0:T(8,128)(2,1)S(1)}, bf16[64,512]{1,0:T(8,128)(2,1)S(1)}, u32[]{:S(2)}, u32[]{:S(2)}) collective-permute-start(bf16[64,512]{1,0:T(8,128)(2,1)S(1)} %get-tuple-element.37), channel_id=1, source_target_pairs={{0,20},{4,16},{8,28},{12,24},{16,4},{20,0},{24,12},{28,8},{1,21},{... | collective-permute-start | bytes 196616 | tf_op jit(solution)/shard_map/ppermute | solution.py:154
  34.3 2.0 %collective-permute-start.12 = (bf16[64,512]{1,0:T(8,128)(2,1)S(1)}, bf16[64,512]{1,0:T(8,128)(2,1)S(1)}, u32[]{:S(2)}, u32[]{:S(2)}) collective-permute-start(bf16[64,512]{1,0:T(8,128)(2,1)S(1)} %get-tuple-element.38.refs_8_), channel_id=1, source_target_pairs={{0,24},{4,28},{8,16},{12,20},{16,8},{20,12},{24,0},{28,4},{1,25},{... | collective-permute-start | bytes 196616 | tf_op jit(solution)/shard_map/ppermute | solution.py:154
  36.4 2.0 %collective-permute-start.13 = (bf16[64,512]{1,0:T(8,128)(2,1)S(1)}, bf16[64,512]{1,0:T(8,128)(2,1)S(1)}, u32[]{:S(2)}, u32[]{:S(2)}) collective-permute-start(bf16[64,512]{1,0:T(8,128)(2,1)S(1)} %get-tuple-element.37), channel_id=1, source_target_pairs={{0,28},{4,24},{8,20},{12,16},{16,12},{20,8},{24,4},{28,0},{1,29},{... | collective-permute-start | bytes 196616 | tf_op jit(solution)/shard_map/ppermute | solution.py:154
  38.4 1.2 %collective-permute-done.10.refs_12_ = bf16[64,512]{1,0:T(8,128)(2,1)S(1)} collective-permute-done((bf16[64,512]{1,0:T(8,128)(2,1)S(1)}, bf16[64,512]{1,0:T(8,128)(2,1)S(1)}, u32[]{:S(2)}, u32[]{:S(2)}) %collective-permute-start.10) | collective-permute-done | bytes 65568 | tf_op jit(solution)/shard_map/ppermute | solution.py:154
  39.6 4.0 %collective-permute-done.11.refs_13_ = bf16[64,512]{1,0:T(8,128)(2,1)S(1)} collective-permute-done((bf16[64,512]{1,0:T(8,128)(2,1)S(1)}, bf16[64,512]{1,0:T(8,128)(2,1)S(1)}, u32[]{:S(2)}, u32[]{:S(2)}) %collective-permute-start.11) | collective-permute-done | bytes 65568 | tf_op jit(solution)/shard_map/ppermute | solution.py:154
  43.5 1.1 %scores.1 = (f32[4,640]{1,0:T(4,128)S(1)}, f32[4,640]{1,0:T(4,128)S(1)}, f32[4,640]{1,0:T(4,128)S(1)}, f32[4,640]{1,0:T(4,128)S(1)}, f32[4,640]{1,0:T(4,128)S(1)...) custom-call(bf16[64,128]{1,0:T(8,128)(2,1)S(1)} %get-tuple-element.21.refs_0_, ...), custom_call_target="tpu_custom_call" | custom-call | flops 16777216 | bytes 524288 | tf_op jit(solution)/shard_map/scores/pallas_call | solution.py:190
  44.6 0.6 %copy-done.1 = f32[4,640]{1,0:T(4,128)} copy-done((f32[4,640]{1,0:T(4,128)}, f32[4,640]{1,0:T(4,128)S(1)}, u32[]{:S(2)}) %copy-start.1) | copy-done | bytes 10264
  45.2 1.3 %collective-permute-start.15 = (f32[4,640]{1,0:T(4,128)S(1)}, f32[4,640]{1,0:T(4,128)S(1)}, u32[]{:S(2)}, u32[]{:S(2)}) collective-permute-start(f32[4,640]{1,0:T(4,128)S(1)} %get-tuple-element.31), channel_id=1, source_target_pairs={{0,2},{1,3},{2,0},{3,1},{4,6},{5,7},{6,4},{7,5},{8,10},{9,11},{10,... | collective-permute-start | bytes 30728 | tf_op jit(solution)/shard_map/ppermute | solution.py:145
  47.1 1.1 %collective-permute-start.17 = (f32[4,640]{1,0:T(4,128)S(1)}, f32[4,640]{1,0:T(4,128)S(1)}, u32[]{:S(2)}, u32[]{:S(2)}) collective-permute-start(f32[4,640]{1,0:T(4,128)S(1)} %get-tuple-element.33), channel_id=1, source_target_pairs={{0,4},{1,5},{2,6},{3,7},{4,0},{5,1},{6,2},{7,3},{8,12},{9,13},{10,... | collective-permute-start | bytes 30728 | tf_op jit(solution)/shard_map/ppermute | solution.py:145
  48.2 0.5 collective-permute-start.18
  48.7 2.0 %collective-permute-start.19 = (f32[4,640]{1,0:T(4,128)S(1)}, f32[4,640]{1,0:T(4,128)S(1)}, u32[]{:S(2)}, u32[]{:S(2)}) collective-permute-start(f32[4,640]{1,0:T(4,128)S(1)} %get-tuple-element.35), channel_id=1, source_target_pairs={{0,6},{1,7},{2,4},{3,5},{4,2},{5,3},{6,0},{7,1},{8,14},{9,15},{10,... | collective-permute-start | bytes 30728 | tf_op jit(solution)/shard_map/ppermute | solution.py:145
  50.7 0.7 %collective-permute-start.20 = (f32[4,640]{1,0:T(4,128)S(1)}, f32[4,640]{1,0:T(4,128)S(1)}, u32[]{:S(2)}, u32[]{:S(2)}) collective-permute-start(f32[4,640]{1,0:T(4,128)S(1)} %get-tuple-element.36), channel_id=1, source_target_pairs={{0,7},{1,6},{2,5},{3,4},{4,3},{5,2},{6,1},{7,0},{8,15},{9,14},{10,... | collective-permute-start | bytes 30728 | tf_op jit(solution)/shard_map/ppermute | solution.py:145
  51.5 1.8 %collective-permute-done.19.refs_6_ = f32[4,640]{1,0:T(4,128)S(1)} collective-permute-done((f32[4,640]{1,0:T(4,128)S(1)}, f32[4,640]{1,0:T(4,128)S(1)}, u32[]{:S(2)}, u32[]{:S(2)}) %collective-permute-start.19) | collective-permute-done | bytes 10272 | tf_op jit(solution)/shard_map/ppermute | solution.py:145
  53.3 1.4 %collective-permute-done.20.refs_7_ = f32[4,640]{1,0:T(4,128)S(1)} collective-permute-done((f32[4,640]{1,0:T(4,128)S(1)}, f32[4,640]{1,0:T(4,128)S(1)}, u32[]{:S(2)}, u32[]{:S(2)}) %collective-permute-start.20) | collective-permute-done | bytes 10272 | tf_op jit(solution)/shard_map/ppermute | solution.py:145
  54.8 0.6 copy-done.9
  55.3 1.5 %finish.1 = f32[4,512]{1,0:T(4,128)} custom-call(f32[4,640]{1,0:T(4,128)} %copy-done.1, f32[4,640]{1,0:T(4,128)} %copy-done.3, f32[4,640]{1,0:T(4,128)} %copy-done.4, f32[4,640]{1,0:T(4,128)} %copy-done.5, f32[4,640]{1,0:T(4,128)} %copy-done.6, f32[4,640]{1,0:T(4,128)} %copy-done.7, f32[4,640]{1,0:T(4,128)} %copy-done.8, f32[4,640]{1,0:T(4,128)} %copy-done.9), custom_call_target="tpu_custom_call" | custom-call | tf_op jit(solution)/shard_map/finish/pallas_call | solution.py:211
  (36 shorter events, 1.5 us)
Async XLA Ops:
  0.9 33.5 %collective-permute-start.7 = (bf16[64,512]{1,0:T(8,128)(2,1)S(1)}, bf16[64,512]{1,0:T(8,128)(2,1)S(1)}, u32[]{:S(2)}, u32[]{:S(2)}) collective-permute-start(bf16[64,512]{1,0:T(8,128)(2,1)S(1)} %get-tuple-element.37), channel_id=1, source_target_pairs={{0,4},{4,0},{8,12},{12,8},{16,20},{20,16},{24,28},{28,24},{1,5},{5... | collective-permute-start | bytes 196616 | tf_op jit(solution)/shard_map/ppermute | solution.py:154
  3.9 32.5 %collective-permute-start.8 = (bf16[64,512]{1,0:T(8,128)(2,1)S(1)}, bf16[64,512]{1,0:T(8,128)(2,1)S(1)}, u32[]{:S(2)}, u32[]{:S(2)}) collective-permute-start(bf16[64,512]{1,0:T(8,128)(2,1)S(1)} %get-tuple-element.38.refs_8_), channel_id=1, source_target_pairs={{0,8},{4,12},{8,0},{12,4},{16,24},{20,28},{24,16},{28,20},{1,9},{5... | collective-permute-start | bytes 196616 | tf_op jit(solution)/shard_map/ppermute | solution.py:154
  8.5 3.4 %copy-start = (bf16[1,16,64,4096]{3,2,1,0:T(8,128)(2,1)S(1)}, bf16[1,16,64,4096]{3,2,1,0:T(8,128)(2,1)}, u32[]{:S(2)}) copy-start(bf16[1,16,64,4096]{3,2,1,0:T(8,128)(2,1)} %param.6) | copy-start | bytes 25165828
  11.9 0.7 %copy-start.2 = (s32[16]{0:T(128)S(1)}, s32[16]{0:T(128)}, u32[]{:S(2)}) copy-start(s32[16]{0:T(128)} %lens.1) | copy-start | bytes 196
  21.3 1.9 %collective-permute-start = (bf16[64,128]{1,0:T(8,128)(2,1)S(1)}, bf16[64,128]{1,0:T(8,128)(2,1)S(1)}, u32[]{:S(2)}, u32[]{:S(2)}) collective-permute-start(bf16[64,128]{1,0:T(8,128)(2,1)S(1)} %get-tuple-element.22), channel_id=1, source_target_pairs={{0,1},{1,0},{2,3},{3,2},{4,5},{5,4},{6,7},{7,6},{8,9},{9,8},{10,11... | collective-permute-start | bytes 49160 | tf_op jit(solution)/shard_map/ppermute | solution.py:145
  21.3 3.8 %collective-permute-start.1 = (bf16[64,128]{1,0:T(8,128)(2,1)S(1)}, bf16[64,128]{1,0:T(8,128)(2,1)S(1)}, u32[]{:S(2)}, u32[]{:S(2)}) collective-permute-start(bf16[64,128]{1,0:T(8,128)(2,1)S(1)} %get-tuple-element.23), channel_id=1, source_target_pairs={{0,2},{1,3},{2,0},{3,1},{4,6},{5,7},{6,4},{7,5},{8,10},{9,11},{10,... | collective-permute-start | bytes 49160 | tf_op jit(solution)/shard_map/ppermute | solution.py:145
  22.9 3.2 %collective-permute-start.2 = (bf16[64,128]{1,0:T(8,128)(2,1)S(1)}, bf16[64,128]{1,0:T(8,128)(2,1)S(1)}, u32[]{:S(2)}, u32[]{:S(2)}) collective-permute-start(bf16[64,128]{1,0:T(8,128)(2,1)S(1)} %get-tuple-element.24), channel_id=1, source_target_pairs={{0,3},{1,2},{2,1},{3,0},{4,7},{5,6},{6,5},{7,4},{8,11},{9,10},{10,... | collective-permute-start | bytes 49160 | tf_op jit(solution)/shard_map/ppermute | solution.py:145
  23.2 3.8 %collective-permute-start.3 = (bf16[64,128]{1,0:T(8,128)(2,1)S(1)}, bf16[64,128]{1,0:T(8,128)(2,1)S(1)}, u32[]{:S(2)}, u32[]{:S(2)}) collective-permute-start(bf16[64,128]{1,0:T(8,128)(2,1)S(1)} %get-tuple-element.25), channel_id=1, source_target_pairs={{0,4},{1,5},{2,6},{3,7},{4,0},{5,1},{6,2},{7,3},{8,12},{9,13},{10,... | collective-permute-start | bytes 49160 | tf_op jit(solution)/shard_map/ppermute | solution.py:145
  25.1 3.3 %collective-permute-start.4 = (bf16[64,128]{1,0:T(8,128)(2,1)S(1)}, bf16[64,128]{1,0:T(8,128)(2,1)S(1)}, u32[]{:S(2)}, u32[]{:S(2)}) collective-permute-start(bf16[64,128]{1,0:T(8,128)(2,1)S(1)} %get-tuple-element.26), channel_id=1, source_target_pairs={{0,5},{1,4},{2,7},{3,6},{4,1},{5,0},{6,3},{7,2},{8,13},{9,12},{10,... | collective-permute-start | bytes 49160 | tf_op jit(solution)/shard_map/ppermute | solution.py:145
  26.1 4.6 %collective-permute-start.5 = (bf16[64,128]{1,0:T(8,128)(2,1)S(1)}, bf16[64,128]{1,0:T(8,128)(2,1)S(1)}, u32[]{:S(2)}, u32[]{:S(2)}) collective-permute-start(bf16[64,128]{1,0:T(8,128)(2,1)S(1)} %get-tuple-element.27), channel_id=1, source_target_pairs={{0,6},{1,7},{2,4},{3,5},{4,2},{5,3},{6,0},{7,1},{8,14},{9,15},{10,... | collective-permute-start | bytes 49160 | tf_op jit(solution)/shard_map/ppermute | solution.py:145
  27.0 6.3 %collective-permute-start.6 = (bf16[64,128]{1,0:T(8,128)(2,1)S(1)}, bf16[64,128]{1,0:T(8,128)(2,1)S(1)}, u32[]{:S(2)}, u32[]{:S(2)}) collective-permute-start(bf16[64,128]{1,0:T(8,128)(2,1)S(1)} %get-tuple-element.28), channel_id=1, source_target_pairs={{0,7},{1,6},{2,5},{3,4},{4,3},{5,2},{6,1},{7,0},{8,15},{9,14},{10,... | collective-permute-start | bytes 49160 | tf_op jit(solution)/shard_map/ppermute | solution.py:145
  28.5 9.9 %collective-permute-start.9 = (bf16[64,512]{1,0:T(8,128)(2,1)S(1)}, bf16[64,512]{1,0:T(8,128)(2,1)S(1)}, u32[]{:S(2)}, u32[]{:S(2)}) collective-permute-start(bf16[64,512]{1,0:T(8,128)(2,1)S(1)} %get-tuple-element.37), channel_id=1, source_target_pairs={{0,12},{4,8},{8,4},{12,0},{16,28},{20,24},{24,20},{28,16},{1,13},{... | collective-permute-start | bytes 196616 | tf_op jit(solution)/shard_map/ppermute | solution.py:154
  30.7 8.9 %collective-permute-start.10 = (bf16[64,512]{1,0:T(8,128)(2,1)S(1)}, bf16[64,512]{1,0:T(8,128)(2,1)S(1)}, u32[]{:S(2)}, u32[]{:S(2)}) collective-permute-start(bf16[64,512]{1,0:T(8,128)(2,1)S(1)} %get-tuple-element.38.refs_8_), channel_id=1, source_target_pairs={{0,16},{4,20},{8,24},{12,28},{16,0},{20,4},{24,8},{28,12},{1,17},{... | collective-permute-start | bytes 196616 | tf_op jit(solution)/shard_map/ppermute | solution.py:154
  33.3 10.2 %collective-permute-start.11 = (bf16[64,512]{1,0:T(8,128)(2,1)S(1)}, bf16[64,512]{1,0:T(8,128)(2,1)S(1)}, u32[]{:S(2)}, u32[]{:S(2)}) collective-permute-start(bf16[64,512]{1,0:T(8,128)(2,1)S(1)} %get-tuple-element.37), channel_id=1, source_target_pairs={{0,20},{4,16},{8,28},{12,24},{16,4},{20,0},{24,12},{28,8},{1,21},{... | collective-permute-start | bytes 196616 | tf_op jit(solution)/shard_map/ppermute | solution.py:154
  34.3 9.2 %collective-permute-start.12 = (bf16[64,512]{1,0:T(8,128)(2,1)S(1)}, bf16[64,512]{1,0:T(8,128)(2,1)S(1)}, u32[]{:S(2)}, u32[]{:S(2)}) collective-permute-start(bf16[64,512]{1,0:T(8,128)(2,1)S(1)} %get-tuple-element.38.refs_8_), channel_id=1, source_target_pairs={{0,24},{4,28},{8,16},{12,20},{16,8},{20,12},{24,0},{28,4},{1,25},{... | collective-permute-start | bytes 196616 | tf_op jit(solution)/shard_map/ppermute | solution.py:154
  36.4 7.2 %collective-permute-start.13 = (bf16[64,512]{1,0:T(8,128)(2,1)S(1)}, bf16[64,512]{1,0:T(8,128)(2,1)S(1)}, u32[]{:S(2)}, u32[]{:S(2)}) collective-permute-start(bf16[64,512]{1,0:T(8,128)(2,1)S(1)} %get-tuple-element.37), channel_id=1, source_target_pairs={{0,28},{4,24},{8,20},{12,16},{16,12},{20,8},{24,4},{28,0},{1,29},{... | collective-permute-start | bytes 196616 | tf_op jit(solution)/shard_map/ppermute | solution.py:154
  44.6 0.6 %copy-start.1 = (f32[4,640]{1,0:T(4,128)}, f32[4,640]{1,0:T(4,128)S(1)}, u32[]{:S(2)}) copy-start(f32[4,640]{1,0:T(4,128)S(1)} %get-tuple-element.29.refs_0_) | copy-start | bytes 30724
  45.2 3.5 %collective-permute-start.14 = (f32[4,640]{1,0:T(4,128)S(1)}, f32[4,640]{1,0:T(4,128)S(1)}, u32[]{:S(2)}, u32[]{:S(2)}) collective-permute-start(f32[4,640]{1,0:T(4,128)S(1)} %get-tuple-element.30), channel_id=1, source_target_pairs={{0,1},{1,0},{2,3},{3,2},{4,5},{5,4},{6,7},{7,6},{8,9},{9,8},{10,11... | collective-permute-start | bytes 30728 | tf_op jit(solution)/shard_map/ppermute | solution.py:145
  45.2 5.5 %collective-permute-start.15 = (f32[4,640]{1,0:T(4,128)S(1)}, f32[4,640]{1,0:T(4,128)S(1)}, u32[]{:S(2)}, u32[]{:S(2)}) collective-permute-start(f32[4,640]{1,0:T(4,128)S(1)} %get-tuple-element.31), channel_id=1, source_target_pairs={{0,2},{1,3},{2,0},{3,1},{4,6},{5,7},{6,4},{7,5},{8,10},{9,11},{10,... | collective-permute-start | bytes 30728 | tf_op jit(solution)/shard_map/ppermute | solution.py:145
  46.5 4.9 %collective-permute-start.16 = (f32[4,640]{1,0:T(4,128)S(1)}, f32[4,640]{1,0:T(4,128)S(1)}, u32[]{:S(2)}, u32[]{:S(2)}) collective-permute-start(f32[4,640]{1,0:T(4,128)S(1)} %get-tuple-element.32), channel_id=1, source_target_pairs={{0,3},{1,2},{2,1},{3,0},{4,7},{5,6},{6,5},{7,4},{8,11},{9,10},{10,... | collective-permute-start | bytes 30728 | tf_op jit(solution)/shard_map/ppermute | solution.py:145
  47.1 4.4 %collective-permute-start.17 = (f32[4,640]{1,0:T(4,128)S(1)}, f32[4,640]{1,0:T(4,128)S(1)}, u32[]{:S(2)}, u32[]{:S(2)}) collective-permute-start(f32[4,640]{1,0:T(4,128)S(1)} %get-tuple-element.33), channel_id=1, source_target_pairs={{0,4},{1,5},{2,6},{3,7},{4,0},{5,1},{6,2},{7,3},{8,12},{9,13},{10,... | collective-permute-start | bytes 30728 | tf_op jit(solution)/shard_map/ppermute | solution.py:145
  48.2 3.3 %collective-permute-start.18 = (f32[4,640]{1,0:T(4,128)S(1)}, f32[4,640]{1,0:T(4,128)S(1)}, u32[]{:S(2)}, u32[]{:S(2)}) collective-permute-start(f32[4,640]{1,0:T(4,128)S(1)} %get-tuple-element.34), channel_id=1, source_target_pairs={{0,5},{1,4},{2,7},{3,6},{4,1},{5,0},{6,3},{7,2},{8,13},{9,12},{10,... | collective-permute-start | bytes 30728 | tf_op jit(solution)/shard_map/ppermute | solution.py:145
  48.7 6.0 %copy-start.3 = (f32[4,640]{1,0:T(4,128)}, f32[4,640]{1,0:T(4,128)S(1)}, u32[]{:S(2)}) copy-start(f32[4,640]{1,0:T(4,128)S(1)} %collective-permute-done.14.refs_1_) | copy-start | bytes 30724
  48.7 4.6 %collective-permute-start.19 = (f32[4,640]{1,0:T(4,128)S(1)}, f32[4,640]{1,0:T(4,128)S(1)}, u32[]{:S(2)}, u32[]{:S(2)}) collective-permute-start(f32[4,640]{1,0:T(4,128)S(1)} %get-tuple-element.35), channel_id=1, source_target_pairs={{0,6},{1,7},{2,4},{3,5},{4,2},{5,3},{6,0},{7,1},{8,14},{9,15},{10,... | collective-permute-start | bytes 30728 | tf_op jit(solution)/shard_map/ppermute | solution.py:145
  50.7 4.0 %copy-start.4 = (f32[4,640]{1,0:T(4,128)}, f32[4,640]{1,0:T(4,128)S(1)}, u32[]{:S(2)}) copy-start(f32[4,640]{1,0:T(4,128)S(1)} %collective-permute-done.15.refs_2_) | copy-start | bytes 30724
  50.7 4.0 %collective-permute-start.20 = (f32[4,640]{1,0:T(4,128)S(1)}, f32[4,640]{1,0:T(4,128)S(1)}, u32[]{:S(2)}, u32[]{:S(2)}) collective-permute-start(f32[4,640]{1,0:T(4,128)S(1)} %get-tuple-element.36), channel_id=1, source_target_pairs={{0,7},{1,6},{2,5},{3,4},{4,3},{5,2},{6,1},{7,0},{8,15},{9,14},{10,... | collective-permute-start | bytes 30728 | tf_op jit(solution)/shard_map/ppermute | solution.py:145
  51.5 3.3 %copy-start.5 = (f32[4,640]{1,0:T(4,128)}, f32[4,640]{1,0:T(4,128)S(1)}, u32[]{:S(2)}) copy-start(f32[4,640]{1,0:T(4,128)S(1)} %collective-permute-done.16.refs_3_) | copy-start | bytes 30724
  51.5 3.3 %copy-start.6 = (f32[4,640]{1,0:T(4,128)}, f32[4,640]{1,0:T(4,128)S(1)}, u32[]{:S(2)}) copy-start(f32[4,640]{1,0:T(4,128)S(1)} %collective-permute-done.17.refs_4_) | copy-start | bytes 30724
  51.5 3.3 %copy-start.7 = (f32[4,640]{1,0:T(4,128)}, f32[4,640]{1,0:T(4,128)S(1)}, u32[]{:S(2)}) copy-start(f32[4,640]{1,0:T(4,128)S(1)} %collective-permute-done.18.refs_5_) | copy-start | bytes 30724
  53.3 1.5 %copy-start.8 = (f32[4,640]{1,0:T(4,128)}, f32[4,640]{1,0:T(4,128)S(1)}, u32[]{:S(2)}) copy-start(f32[4,640]{1,0:T(4,128)S(1)} %collective-permute-done.19.refs_6_) | copy-start | bytes 30724
  54.7 0.6 %copy-start.9 = (f32[4,640]{1,0:T(4,128)}, f32[4,640]{1,0:T(4,128)S(1)}, u32[]{:S(2)}) copy-start(f32[4,640]{1,0:T(4,128)S(1)} %collective-permute-done.20.refs_7_) | copy-start | bytes 30724

commit v2 on v1

v2 whole, which is shorter than its diff:
```python
import functools

import jax
import jax.numpy as jnp
from jax import lax
from jax.experimental import pallas as pl
from jax.experimental.pallas import tpu as pltpu
from jax.sharding import Mesh
from jax.sharding import PartitionSpec as P

EPS = 1e-06
NEAR = 2
F32 = jnp.float32
BF16 = jnp.bfloat16
VMEM = pl.BlockSpec(memory_space=pltpu.VMEM)
ANY = pl.BlockSpec(memory_space=pl.ANY)


def grads_kernel(dims, lens_in, acts, out_grads, w_in, w_out, out, *rest):
    cands, tokens, width, team, per = dims
    act_buf, grad_buf, win_buf, wout_buf, lens, square, store, sems, wsems = rest
    chunks = cands // per
    rows = per * tokens
    load_lens = pltpu.make_async_copy(lens_in, lens, wsems.at[2])
    load_w = [
        pltpu.make_async_copy(w_out, wout_buf, wsems.at[0]),
        pltpu.make_async_copy(w_in, win_buf, wsems.at[1]),
    ]
    loads = []
    for i in range(chunks):
        part = pl.ds(i * rows, rows)
        loads.append(
            (
                pltpu.make_async_copy(out_grads.at[part], grad_buf.at[part], sems.at[0, i]),
                pltpu.make_async_copy(acts.at[part], act_buf.at[part], sems.at[1, i]),
            )
        )
    load_w[0].start()
    loads[0][0].start()
    load_w[1].start()
    loads[0][1].start()
    load_lens.start()
    for pair in loads[1:]:
        for load in pair:
            load.start()
    first = lax.axis_index("grp") * tokens
    fold = 128 // width
    lines = width * width // 128
    each = lines // team
    position = lax.broadcasted_iota(jnp.int32, (tokens, width), 0) + first
    transposed = (((1,), (1,)), ((), ()))
    for i in range(chunks):
        part = pl.ds(i * rows, rows)
        if i == 0:
            load_w[0].wait()
        loads[i][0].wait()
        gp = lax.dot_general(grad_buf[part, :], wout_buf[...], transposed, preferred_element_type=F32)
        gp = gp.astype(BF16)
        if i == 0:
            load_w[1].wait()
            load_lens.wait()
        loads[i][1].wait()
        xp = lax.dot_general(act_buf[part, :], win_buf[...], transposed, preferred_element_type=F32)
        xp = xp.astype(BF16)
        for j in range(per):
            cand = i * per + j
            here = slice(j * tokens, (j + 1) * tokens)
            masked = jnp.where(position < lens[cand], gp[here].astype(F32), 0.0)
            block = jnp.dot(masked.T.astype(BF16), xp[here], preferred_element_type=F32)
            square[cand % 2, :, :width] = block
            line = jnp.concatenate(
                [square[cand % 2, pl.ds(h, lines, stride=fold), :width] for h in range(fold)], axis=1
            )
            for s in range(team):
                store[s, cand * each : (cand + 1) * each, :] = line[s * each : (s + 1) * each]
    out[...] = store[...].astype(BF16)


def scores_kernel(dims, parts, queries, out, grads):
    cands, team, groups, each = dims
    rows = cands * each
    for half in range(NEAR):
        total = parts[half * groups].astype(F32)
        for g in range(1, groups):
            total = total + parts[half * groups + g].astype(F32)
        grads[half * rows : (half + 1) * rows, :] = total
    lines = [grads[pl.ds(e, NEAR * cands, stride=each), :] for e in range(each)]
    squares = lines[0] * lines[0]
    for line in lines[1:]:
        squares = squares + line * line
    left = jnp.concatenate([line.astype(BF16) for line in lines], axis=1)
    scores = lax.dot_general(left, queries[...], (((1,), (1,)), ((), ())), preferred_element_type=F32)
    owned = cands // groups
    nq = queries.shape[0]
    for j in range(team):
        out[j, :, :nq] = scores[j * owned : (j + 1) * owned]
        out[j, :, nq:] = squares[j * owned : (j + 1) * owned]


def finish_kernel(pdim, parts, out):
    total = parts[0]
    for k in range(1, parts.shape[0]):
        total = total + parts[k]
    nq = out.shape[1]
    mean = jnp.sum(total[:, nq:], axis=1, keepdims=True) / pdim
    out[...] = total[:, :nq] * lax.rsqrt(mean + EPS)


def on_device(acts, out_grads, proj_in, proj_out, lengths, queries):
    _, cands, tokens, depth = acts.shape
    far, groups = lax.axis_size("far"), lax.axis_size("grp")
    width = proj_in.shape[2]
    team = NEAR * groups
    per = 4
    pdim = width * width
    each = pdim // 128 // team
    nq = queries.shape[0]
    total_q = nq * far * NEAR
    slice_width = pdim // team
    grp = lax.axis_index("grp")
    cut = jnp.stack(
        [
            lax.dynamic_slice(queries, (0, (near * groups + grp) * slice_width), (nq, slice_width))
            for near in range(NEAR)
        ]
    )
    cut = jnp.broadcast_to(cut[None], (far, NEAR, nq, slice_width)).reshape(far * NEAR, nq, slice_width)
    gathered = lax.all_to_all(cut, ("far", "near"), 0, 0, tiled=True).reshape(total_q, slice_width)

    rows = cands * tokens
    parts = pl.pallas_call(
        functools.partial(grads_kernel, (cands, tokens, width, team, per)),
        out_shape=jax.ShapeDtypeStruct((team, cands * each, 128), BF16),
        in_specs=[ANY] * 5,
        out_specs=VMEM,
        scratch_shapes=[
            pltpu.VMEM((rows, depth), BF16),
            pltpu.VMEM((rows, depth), BF16),
            pltpu.VMEM((width, depth), BF16),
            pltpu.VMEM((width, depth), BF16),
            pltpu.SMEM((cands,), jnp.int32),
            pltpu.VMEM((2, width, 128), F32),
            pltpu.VMEM((team, cands * each, 128), F32),
            pltpu.SemaphoreType.DMA((2, cands // per)),
            pltpu.SemaphoreType.DMA((3,)),
        ],
        compiler_params=pltpu.CompilerParams(vmem_limit_bytes=58 * 2**20),
        cost_estimate=pl.CostEstimate(
            flops=4 * rows * depth * width, bytes_accessed=4 * rows * depth, transcendentals=0
        ),
        name="grads",
    )(
        lengths,
        acts.reshape(rows, depth),
        out_grads.reshape(rows, depth),
        proj_in.reshape(depth, width).T,
        proj_out.reshape(depth, width).T,
    )
    parts = lax.all_to_all(parts, ("near", "grp"), 0, 0, tiled=True)

    owned = cands // groups
    sums = pl.pallas_call(
        functools.partial(scores_kernel, (cands, team, groups, each)),
        out_shape=jax.ShapeDtypeStruct((team, owned, total_q + 128), F32),
        in_specs=[VMEM] * 2,
        out_specs=VMEM,
        scratch_shapes=[pltpu.VMEM((NEAR * cands * each, 128), F32)],
        compiler_params=pltpu.CompilerParams(vmem_limit_bytes=24 * 2**20),
        cost_estimate=pl.CostEstimate(
            flops=2 * NEAR * cands * total_q * slice_width,
            bytes_accessed=2 * total_q * slice_width,
            transcendentals=0,
        ),
        name="scores",
    )(parts, gathered)
    sums = lax.all_to_all(sums, ("near", "grp"), 0, 0, tiled=True)

    return pl.pallas_call(
        functools.partial(finish_kernel, pdim),
        out_shape=jax.ShapeDtypeStruct((owned, total_q), F32),
        in_specs=[VMEM],
        out_specs=VMEM,
        name="finish",
    )(sums)


def solution(mesh):
    blks, groups = mesh.shape["blk"], mesh.shape["grp"]
    fine = Mesh(mesh.devices.reshape(blks // NEAR, NEAR, groups), ("far", "near", "grp"))
    blk = ("far", "near")
    in_specs = (
        P(None, blk, "grp", None),
        P(None, blk, "grp", None),
        P(),
        P(),
        P(blk),
        P(blk, None),
    )
    return jax.shard_map(
        on_device, mesh=fine, in_specs=in_specs, out_specs=P(blk + ("grp",), None), check_vma=False
    )
```

time: 57.2 us -> 55.4 us (0.969)
  blocking collectives: 0 us -> 27.1 us
  starting transfers between devices: 24.3 us -> 5.18 us
  local copies, waits for them, and re-layouts: 9.12 us -> 0.92 us
  waiting for transfers between devices: 12 us -> 4.62 us
  Pallas kernels: 11.2 us -> 17.2 us
    all_to_all x0 -> x2, blocking collectives: none -> 27.1 us  [the longest x1 19 us: on_device(): lax.all_to_all(cut, ('far', 'near'), 0, 0, tiled=True)]
    ppermute x21 -> x0, starting transfers between devices: 24.3 us -> none  [the longest x7 13.2 us: on_device(): lax.ppermute(cut[k % NEAR], 'blk', [(b, b ^ k) for b in range(blks)])]
    ppermute x21 -> x0, waiting for transfers between devices: 12 us -> none  [the longest x14 6.85 us: team_swap(): return lax.ppermute(x, both, perm)]
    unnamed x22 -> x0, local copies, waits for them, and re-layouts: 8.24 us -> none
    pallas_call x1, Pallas kernels: 8.67 us -> 15.3 us  [on_device(): pl.pallas_call(functools.partial(grads_kernel, (cands, tokens, width, tea...]
    all_to_all x0 -> x1, starting transfers between devices: none -> 5.18 us  [on_device(): parts = lax.all_to_all(parts, ('near', 'grp'), 0, 0, tiled=True)]
    all_to_all x0 -> x1, waiting for transfers between devices: none -> 4.62 us  [on_device(): parts = lax.all_to_all(parts, ('near', 'grp'), 0, 0, tiled=True)]
    another operation x0 -> x1, local copies, waits for them, and re-layouts: none -> 0.88 us  [on_device(): jnp.stack([lax.dynamic_slice(queries, (0, (near * groups + grp) * slice_w...]
  transfers between devices with their start and end apart: 21 -> 1, of which waited for: 7 -> 1; matrix products, arithmetic and copies ran while one was open for 5% -> 2% of each run, Pallas kernels for 15% -> 0%
where the time goes in v2:
time: 55.4 us; the launch traced here: 55.1 us
  blocking collectives  27.1 us (49%)
  Pallas kernels  17.2 us (31%)
  starting transfers between devices  5.18 us (9%)
  waiting for transfers between devices  4.62 us (8%)
  local copies, waits for them, and re-layouts  0.92 us (2%)
    all_to_all x1, blocking collectives, on_device(): lax.all_to_all(cut, ('far', 'near'), 0, 0, tiled=True)  19 us
    pallas_call x1, Pallas kernels, on_device(): pl.pallas_call(functools.partial(grads_kernel, (cands, tokens, width, tea...  15.3 us
    all_to_all x1, blocking collectives, on_device(): sums = lax.all_to_all(sums, ('near', 'grp'), 0, 0, tiled=True)  8.18 us
    all_to_all x1, starting transfers between devices, on_device(): parts = lax.all_to_all(parts, ('near', 'grp'), 0, 0, tiled=True)  5.18 us
    all_to_all x1, waiting for transfers between devices, on_device(): parts = lax.all_to_all(parts, ('near', 'grp'), 0, 0, tiled=True)  4.62 us
    pallas_call x1, Pallas kernels, on_device(): pl.pallas_call(functools.partial(finish_kernel, pdim), out_shape=jax.Shap...  1.58 us
  transfers between devices with their start and end apart: 1, of which 1 were waited for; matrix products, arithmetic and copies ran while one was open for 2% of the time, Pallas kernels for 0%

profile of v2, /device:TPU:0, one launch (start us, length us, event | category | flops | bytes accessed | tf_op | source)
XLA Modules:
  0.0 55.1 jit_solution(11502915650214877508)
XLA Ops:
  0.0 15.3 %grads.1 = bf16[8,64,128]{2,1,0:T(8,128)(2,1)} custom-call(s32[16]{0:T(128)} %lens_in.1, bf16[1024,4096]{1,0:T(8,128)(2,1)} %bitcast.15, bf16[1024,4096]{1,0:T(8,128)(2,1)} %bitcast.16, bf16[64,4096]{1,0:T(8,128)(2,1)} %bitcast.18, bf16[64,4096]{1,0:T(8,128)(2,1)} %bitcast.19), custom_call_target="tpu_custom_call" | custom-call | flops 1073741824 | bytes 16777216 | tf_op jit(solution)/shard_map/grads/pallas_call | solution.py:131
  15.3 5.2 %all-to-all-start = ((bf16[8,64,128]{2,1,0:T(8,128)(2,1)}), bf16[8,64,128]{2,1,0:T(8,128)(2,1)S(1)}, u32[]{:S(2)}, u32[]{:S(2)}) async-start(bf16[8,64,128]{2,1,0:T(8,128)(2,1)} %grads.1), calls=%async_computation | async-start | bytes 262144 | tf_op jit(solution)/shard_map/all_to_all | solution.py:159
  20.5 0.9 %dynamic-slice_bitcast_fusion.1 = (bf16[1,64,512]{2,1,0:T(8,128)(2,1)S(1)}, bf16[1,64,512]{2,1,0:T(8,128)(2,1)S(1)}) fusion(bf16[64,4096]{1,0:T(8,128)(2,1)} %param.11, s32[]{:T(128)S(6)} %select_n.6, s32[]{:T(128)S(6)} %select_n.7), kind=kLoop, calls=%fused_computation.2 | loop fusion | bytes 262152 | tf_op jit(solution)/shard_map/stack | solution.py:121
  21.4 4.6 %all-to-all-done.parts = bf16[8,64,128]{2,1,0:T(8,128)(2,1)S(1)} async-done(((bf16[8,64,128]{2,1,0:T(8,128)(2,1)}), bf16[8,64,128]{2,1,0:T(8,128)(2,1)S(1)}, u32[]{:S(2)}, u32[]{:S(2)}) %all-to-all-start) | async-done | bytes 131104 | tf_op jit(solution)/shard_map/all_to_all | solution.py:159
  26.1 19.0 %all_to_all.15 = bf16[8,64,512]{2,1,0:T(8,128)(2,1)S(1)} all-to-all(bf16[8,64,512]{2,1,0:T(8,128)(2,1)S(1)} %bitcast.17), channel_id=1, replica_groups=mesh['far'=4,'near'=2,'grp'=4] {'far','near'}, dimensions={0} | all-to-all | bytes 1048576 | tf_op jit(solution)/shard_map/all_to_all | solution.py:128
  45.1 0.2 scores.1
  45.3 8.2 %all_to_all.16.parts = f32[8,4,640]{2,1,0:T(4,128)} all-to-all(f32[8,4,640]{2,1,0:T(4,128)S(1)} %scores.1), channel_id=1, replica_groups=mesh['far'=4,'near'=2,'grp'=4] {'near','grp'}, dimensions={0} | all-to-all | bytes 163840 | tf_op jit(solution)/shard_map/all_to_all | solution.py:176
  53.5 1.6 %finish.1 = f32[4,512]{1,0:T(4,128)} custom-call(f32[8,4,640]{2,1,0:T(4,128)} %all_to_all.16.parts), custom_call_target="tpu_custom_call" | custom-call | tf_op jit(solution)/shard_map/finish/pallas_call | solution.py:178
  (2 shorter events, 0.1 us)
Async XLA Ops:
  15.3 10.7 %all-to-all-start = ((bf16[8,64,128]{2,1,0:T(8,128)(2,1)}), bf16[8,64,128]{2,1,0:T(8,128)(2,1)S(1)}, u32[]{:S(2)}, u32[]{:S(2)}) async-start(bf16[8,64,128]{2,1,0:T(8,128)(2,1)} %grads.1), calls=%async_computation | async-start | bytes 262144 | tf_op jit(solution)/shard_map/all_to_all | solution.py:159

commit v3 on v2

v3 whole, which is shorter than its diff:
```python
import functools

import jax
import jax.numpy as jnp
from jax import lax
from jax.experimental import pallas as pl
from jax.experimental.pallas import tpu as pltpu
from jax.sharding import PartitionSpec as P

EPS = 1e-06
F32 = jnp.float32
BF16 = jnp.bfloat16
VMEM = pl.BlockSpec(memory_space=pltpu.VMEM)
ANY = pl.BlockSpec(memory_space=pl.ANY)
BY_ROWS = (((1,), (1,)), ((), ()))


def grads_kernel(dims, lens_in, acts, out_grads, w_in, w_out, *rest):
    cands, tokens, width, groups, per = dims
    outs = rest[:groups]
    act_buf, grad_buf, win_raw, wout_raw, win_buf, wout_buf, lens, square, store, sems, wsems = rest[groups:]
    chunks = cands // per
    rows = per * tokens
    load_lens = pltpu.make_async_copy(lens_in, lens, wsems.at[2])
    load_w = [
        pltpu.make_async_copy(w_out, wout_raw, wsems.at[0]),
        pltpu.make_async_copy(w_in, win_raw, wsems.at[1]),
    ]
    loads = []
    for i in range(chunks):
        part = pl.ds(i * rows, rows)
        loads.append(
            (
                pltpu.make_async_copy(out_grads.at[part], grad_buf.at[part], sems.at[0, i]),
                pltpu.make_async_copy(acts.at[part], act_buf.at[part], sems.at[1, i]),
            )
        )
    for load in load_w:
        load.start()
    load_lens.start()
    for pair in loads:
        for load in pair:
            load.start()
    grp = lax.axis_index("grp")
    fold = 128 // width
    lines = width * width // 128
    each = lines // groups
    position = lax.broadcasted_iota(jnp.int32, (tokens, width), 0) + grp * tokens
    load_w[0].wait()
    wout_buf[...] = wout_raw[...].T
    load_w[1].wait()
    win_buf[...] = win_raw[...].T
    load_lens.wait()
    for i in range(chunks):
        part = pl.ds(i * rows, rows)
        loads[i][0].wait()
        gp = jnp.dot(grad_buf[part, :], wout_buf[...], preferred_element_type=F32).astype(BF16)
        loads[i][1].wait()
        xp = jnp.dot(act_buf[part, :], win_buf[...], preferred_element_type=F32).astype(BF16)
        for j in range(per):
            cand = i * per + j
            here = slice(j * tokens, (j + 1) * tokens)
            masked = jnp.where(position < lens[cand], gp[here].astype(F32), 0.0)
            block = jnp.dot(masked.T.astype(BF16), xp[here], preferred_element_type=F32)
            square[cand % 2, :, :width] = block
            line = jnp.concatenate(
                [square[cand % 2, pl.ds(h, lines, stride=fold), :width] for h in range(fold)], axis=1
            )
            for s in range(groups):
                store[s, cand * each : (cand + 1) * each, :] = line[s * each : (s + 1) * each]
    for k in range(groups):
        outs[k][...] = store[jnp.bitwise_xor(grp, k)].astype(BF16)


def combine_kernel(dims, *refs):
    cands, groups, each = dims
    parts = refs[:groups]
    out, squares, grads = refs[groups:]
    total = parts[0][...].astype(F32)
    for part in parts[1:]:
        total = total + part[...].astype(F32)
    grads[...] = total
    lines = [grads[pl.ds(e, cands, stride=each), :] for e in range(each)]
    sums = lines[0] * lines[0]
    for line in lines[1:]:
        sums = sums + line * line
    squares[...] = sums
    out[...] = jnp.concatenate([line.astype(BF16) for line in lines], axis=1)


def near_scores(left, queries, place):
    far = len(queries)
    z = lax.axis_index("blk") // 2
    for k in range(far):
        place[jnp.bitwise_xor(z, k)] = lax.dot_general(
            left, queries[k][...], BY_ROWS, preferred_element_type=F32
        )
    return jnp.concatenate([place[k] for k in range(far)], axis=1)


def other_kernel(far, left, *refs):
    refs[far][...] = near_scores(left[...], refs[:far], refs[far + 1])


def own_kernel(dims, left, squares, *refs):
    far, groups = dims
    queries = refs[:far]
    other = refs[far]
    outs = refs[far + 1 : far + 1 + groups]
    place, result = refs[far + 1 + groups :]
    own = near_scores(left[...], queries, place)
    is_even = lax.rem(lax.axis_index("blk"), 2) == 0
    back = other[...]
    even = jnp.where(is_even, own, back)
    odd = jnp.where(is_even, back, own)
    half = own.shape[1]
    owned = own.shape[0] // groups
    for g in range(groups):
        here = slice(g * owned, (g + 1) * owned)
        result[g, :, :half] = even[here]
        result[g, :, half : 2 * half] = odd[here]
        result[g, :, 2 * half :] = squares[here, :]
    grp = lax.axis_index("grp")
    for k in range(groups):
        outs[k][...] = result[jnp.bitwise_xor(grp, k)]


def finish_kernel(dims, *refs):
    pdim, nq = dims
    out = refs[-1]
    total = refs[0][...]
    for ref in refs[1:-1]:
        total = total + ref[...]
    width = out.shape[1]
    mean = jnp.sum(total[:, width:], axis=1, keepdims=True) / pdim
    scaled = total[:, :width] * lax.rsqrt(mean + EPS)
    columns = []
    for start in range(0, width // 2, nq):
        columns.append(scaled[:, start : start + nq])
        columns.append(scaled[:, width // 2 + start : width // 2 + start + nq])
    out[...] = jnp.concatenate(columns, axis=1)


def on_device(blks, groups, acts, out_grads, proj_in, proj_out, lengths, queries):
    _, cands, tokens, depth = acts.shape
    width = proj_in.shape[2]
    per = 4
    far = blks // 2
    pdim = width * width
    each = pdim // 128 // groups
    nq = queries.shape[0]
    total_q = nq * blks
    owned = cands // groups
    slice_width = pdim // groups

    def grp_swap(x, k):
        return lax.ppermute(x, "grp", [(g, g ^ k) for g in range(groups)])

    def blk_swap(x, k):
        return lax.ppermute(x, "blk", [(b, b ^ k) for b in range(blks)])

    cut = lax.dynamic_slice(queries, (0, lax.axis_index("grp") * slice_width), (nq, slice_width))
    gathered = [cut] + [blk_swap(cut, 2 * k) for k in range(1, far)]

    rows = cands * tokens
    parts = pl.pallas_call(
        functools.partial(grads_kernel, (cands, tokens, width, groups, per)),
        out_shape=[jax.ShapeDtypeStruct((cands * each, 128), BF16)] * groups,
        in_specs=[ANY] * 5,
        out_specs=[VMEM] * groups,
        scratch_shapes=[
            pltpu.VMEM((rows, depth), BF16),
            pltpu.VMEM((rows, depth), BF16),
            pltpu.VMEM((width, depth), BF16),
            pltpu.VMEM((width, depth), BF16),
            pltpu.VMEM((depth, width), BF16),
            pltpu.VMEM((depth, width), BF16),
            pltpu.SMEM((cands,), jnp.int32),
            pltpu.VMEM((2, width, 128), F32),
            pltpu.VMEM((groups, cands * each, 128), F32),
            pltpu.SemaphoreType.DMA((2, cands // per)),
            pltpu.SemaphoreType.DMA((3,)),
        ],
        compiler_params=pltpu.CompilerParams(vmem_limit_bytes=58 * 2**20),
        cost_estimate=pl.CostEstimate(
            flops=16 * rows * depth * width, bytes_accessed=8 * rows * depth, transcendentals=0
        ),
        name="grads",
    )(
        lengths,
        acts.reshape(rows, depth),
        out_grads.reshape(rows, depth),
        proj_in.reshape(depth, width).T,
        proj_out.reshape(depth, width).T,
    )
    parts = [parts[0]] + [grp_swap(parts[k], k) for k in range(1, groups)]

    own, squares = pl.pallas_call(
        functools.partial(combine_kernel, (cands, groups, each)),
        out_shape=[
            jax.ShapeDtypeStruct((cands, slice_width), BF16),
            jax.ShapeDtypeStruct((cands, 128), F32),
        ],
        in_specs=[VMEM] * groups,
        out_specs=[VMEM] * 2,
        scratch_shapes=[pltpu.VMEM((cands * each, 128), F32)],
        name="combine",
    )(*parts)
    neighbour = blk_swap(own, 1)

    half = total_q // 2
    place = pltpu.VMEM((far, cands, nq), F32)
    back = pl.pallas_call(
        functools.partial(other_kernel, far),
        out_shape=jax.ShapeDtypeStruct((cands, half), F32),
        in_specs=[VMEM] * (1 + far),
        out_specs=VMEM,
        scratch_shapes=[place],
        compiler_params=pltpu.CompilerParams(vmem_limit_bytes=24 * 2**20),
        name="other_scores",
    )(neighbour, *gathered)
    back = blk_swap(back, 1)

    packed = jax.ShapeDtypeStruct((owned, total_q + 128), F32)
    sums = pl.pallas_call(
        functools.partial(own_kernel, (far, groups)),
        out_shape=[packed] * groups,
        in_specs=[VMEM] * (3 + far),
        out_specs=[VMEM] * groups,
        scratch_shapes=[place, pltpu.VMEM((groups, owned, total_q + 128), F32)],
        compiler_params=pltpu.CompilerParams(vmem_limit_bytes=24 * 2**20),
        name="own_scores",
    )(own, squares, *gathered, back)
    sums = [sums[0]] + [grp_swap(sums[k], k) for k in range(1, groups)]

    return pl.pallas_call(
        functools.partial(finish_kernel, (pdim, nq)),
        out_shape=jax.ShapeDtypeStruct((owned, total_q), F32),
        in_specs=[VMEM] * groups,
        out_specs=VMEM,
        name="finish",
    )(*sums)


def solution(mesh):
    in_specs = (
        P(None, "blk", "grp", None),
        P(None, "blk", "grp", None),
        P(),
        P(),
        P("blk"),
        P("blk", None),
    )
    return jax.shard_map(
        functools.partial(on_device, mesh.shape["blk"], mesh.shape["grp"]),
        mesh=mesh,
        in_specs=in_specs,
        out_specs=P(("blk", "grp"), None),
        check_vma=False,
    )
```

time: 55.4 us -> 44.1 us (0.80)
  blocking collectives: 27.1 us -> 0 us
  starting transfers between devices: 5.18 us -> 13.5 us
  waiting for transfers between devices: 4.62 us -> 9.86 us
  local copies, waits for them, and re-layouts: 0.92 us -> 4.3 us
  Pallas kernels: 17.2 us -> 15.9 us
    all_to_all x2 -> x0, blocking collectives: 27.1 us -> none  [the longest x1 19 us: on_device(): lax.all_to_all(cut, ('far', 'near'), 0, 0, tiled=True)]
    ppermute x0 -> x11, starting transfers between devices: none -> 13.5 us  [the longest x5 8.81 us: blk_swap(): return lax.ppermute(x, 'blk', [(b, b ^ k) for b in range(blks)])]
    ppermute x0 -> x11, waiting for transfers between devices: none -> 9.86 us  [the longest x6 5.02 us: grp_swap(): return lax.ppermute(x, 'grp', [(g, g ^ k) for g in range(groups)])]
    all_to_all x1 -> x0, starting transfers between devices: 5.18 us -> none  [on_device(): parts = lax.all_to_all(parts, ('near', 'grp'), 0, 0, tiled=True)]
    all_to_all x1 -> x0, waiting for transfers between devices: 4.62 us -> none  [on_device(): parts = lax.all_to_all(parts, ('near', 'grp'), 0, 0, tiled=True)]
    unnamed x0 -> x20, local copies, waits for them, and re-layouts: none -> 4.29 us
    pallas_call x3 -> x5, Pallas kernels: 17.2 us -> 15.9 us  [the longest x1 12.3 us: on_device(): pl.pallas_call(functools.partial(grads_kernel, (cands, tokens, width, gro...]
    another operation x1 -> x0, local copies, waits for them, and re-layouts: 0.88 us -> none  [on_device(): jnp.stack([lax.dynamic_slice(queries, (0, (near * groups + grp) * slice_w...]
  transfers between devices with their start and end apart: 1 -> 11, of which waited for: 1 -> 6; matrix products, arithmetic and copies ran while one was open for 2% -> 0% of each run, Pallas kernels for 0% -> 32%
where the time goes in v3:
time: 44.1 us; the launch traced here: 43.7 us
  Pallas kernels  15.9 us (36%)
  starting transfers between devices  13.5 us (31%)
  waiting for transfers between devices  9.86 us (22%)
  local copies, waits for them, and re-layouts  4.3 us (10%)
    pallas_call x1, Pallas kernels, on_device(): pl.pallas_call(functools.partial(grads_kernel, (cands, tokens, width, gro...  12.3 us
    ppermute x5, starting transfers between devices, blk_swap(): return lax.ppermute(x, 'blk', [(b, b ^ k) for b in range(blks)])  8.81 us
    ppermute x6, waiting for transfers between devices, grp_swap(): return lax.ppermute(x, 'grp', [(g, g ^ k) for g in range(groups)])  5.02 us
    ppermute x5, waiting for transfers between devices, blk_swap(): return lax.ppermute(x, 'blk', [(b, b ^ k) for b in range(blks)])  4.83 us
    ppermute x6, starting transfers between devices, grp_swap(): return lax.ppermute(x, 'grp', [(g, g ^ k) for g in range(groups)])  4.73 us
    unnamed x20, local copies, waits for them, and re-layouts  4.29 us
    pallas_call x1, Pallas kernels, on_device(): pl.pallas_call(functools.partial(finish_kernel, (pdim, nq)), out_shape=ja...  1.51 us
    pallas_call x1, Pallas kernels, on_device(): pl.pallas_call(functools.partial(combine_kernel, (cands, groups, each)),...  1.45 us
  transfers between devices with their start and end apart: 11, of which 6 were waited for; matrix products, arithmetic and copies ran while one was open for 0% of the time, Pallas kernels for 32%

profile of v3, /device:TPU:0, one launch (start us, length us, event | category | flops | bytes accessed | tf_op | source)
XLA Modules:
  0.0 43.7 jit_solution(14845055720477927674)
XLA Ops:
  0.0 1.0 %copy-done = bf16[64,4096]{1,0:T(8,128)(2,1)S(1)} copy-done((bf16[64,4096]{1,0:T(8,128)(2,1)S(1)}, bf16[64,4096]{1,0:T(8,128)(2,1)}, u32[]{:S(2)}) %copy-start) | copy-done | bytes 524312
  1.1 5.1 %collective-permute-start.5 = (bf16[64,1024]{1,0:T(8,128)(2,1)S(1)}, bf16[64,1024]{1,0:T(8,128)(2,1)S(1)}, u32[]{:S(2)}, u32[]{:S(2)}) collective-permute-start(bf16[64,1024]{1,0:T(8,128)(2,1)S(1)} %constant_dynamic-slice_fusion.refs_0_), channel_id=1, source_target_pairs={{0,24},{4,28},{8,16},{12,20},{16,8},{20,12},{24,0},{28,4},{1,25},{... | collective-permute-start | bytes 393224 | tf_op jit(solution)/shard_map/ppermute | solution.py:160
  6.2 0.0 collective-permute-start.4
  6.2 0.6 %collective-permute-start.3 = (bf16[64,1024]{1,0:T(8,128)(2,1)S(1)}, bf16[64,1024]{1,0:T(8,128)(2,1)S(1)}, u32[]{:S(2)}, u32[]{:S(2)}) collective-permute-start(bf16[64,1024]{1,0:T(8,128)(2,1)S(1)} %constant_dynamic-slice_fusion.refs_0_), channel_id=1, source_target_pairs={{0,8},{4,12},{8,0},{12,4},{16,24},{20,28},{24,16},{28,20},{1,9},{5... | collective-permute-start | bytes 393224 | tf_op jit(solution)/shard_map/ppermute | solution.py:160
  6.8 12.3 %grads.1 = (bf16[128,128]{1,0:T(8,128)(2,1)}, bf16[128,128]{1,0:T(8,128)(2,1)}, bf16[128,128]{1,0:T(8,128)(2,1)}, bf16[128,128]{1,0:T(8,128)(2,1)}) custom-call(s32[16]{0:T(128)} %lens_in.1, bf16[1024,4096]{1,0:T(8,128)(2,1)} %bitcast.8, bf16[1024,4096]{1,0:T(8,128)(2,1)} %bitcast.9, bf16[64,4096]{1,0:T(8,128)(2,1)} %bitcast.10, bf16[64,4096]{1,0:T(8,128)(2,1)} %bitcast.11), custom_call_target="tpu_custom_call" | custom-call | flops 4294967296 | bytes 33554432 | tf_op jit(solution)/shard_map/grads/pallas_call | solution.py:166
  19.1 0.1 collective-permute-start
  19.2 1.7 %collective-permute-start.1 = (bf16[128,128]{1,0:T(8,128)(2,1)}, bf16[128,128]{1,0:T(8,128)(2,1)S(1)}, u32[]{:S(2)}, u32[]{:S(2)}) collective-permute-start(bf16[128,128]{1,0:T(8,128)(2,1)} %get-tuple-element.17), channel_id=1, source_target_pairs={{0,2},{1,3},{2,0},{3,1},{4,6},{5,7},{6,4},{7,5},{8,10},{9,11},{10,... | collective-permute-start | bytes 98312 | tf_op jit(solution)/shard_map/ppermute | solution.py:157
  20.9 0.0 collective-permute-done.refs_1_
  20.9 1.1 %collective-permute-start.2 = (bf16[128,128]{1,0:T(8,128)(2,1)}, bf16[128,128]{1,0:T(8,128)(2,1)S(1)}, u32[]{:S(2)}, u32[]{:S(2)}) collective-permute-start(bf16[128,128]{1,0:T(8,128)(2,1)} %get-tuple-element.18), channel_id=1, source_target_pairs={{0,3},{1,2},{2,1},{3,0},{4,7},{5,6},{6,5},{7,4},{8,11},{9,10},{10,... | collective-permute-start | bytes 98312 | tf_op jit(solution)/shard_map/ppermute | solution.py:157
  22.0 1.4 %collective-permute-done.1.refs_2_ = bf16[128,128]{1,0:T(8,128)(2,1)S(1)} collective-permute-done((bf16[128,128]{1,0:T(8,128)(2,1)}, bf16[128,128]{1,0:T(8,128)(2,1)S(1)}, u32[]{:S(2)}, u32[]{:S(2)}) %collective-permute-start.1) | collective-permute-done | bytes 32800 | tf_op jit(solution)/shard_map/ppermute | solution.py:157
  23.4 1.1 %collective-permute-done.2.refs_3_ = bf16[128,128]{1,0:T(8,128)(2,1)S(1)} collective-permute-done((bf16[128,128]{1,0:T(8,128)(2,1)}, bf16[128,128]{1,0:T(8,128)(2,1)S(1)}, u32[]{:S(2)}, u32[]{:S(2)}) %collective-permute-start.2) | collective-permute-done | bytes 32800 | tf_op jit(solution)/shard_map/ppermute | solution.py:157
  24.5 0.6 %copy-done.6 = bf16[128,128]{1,0:T(8,128)(2,1)} copy-done((bf16[128,128]{1,0:T(8,128)(2,1)}, bf16[128,128]{1,0:T(8,128)(2,1)S(1)}, u32[]{:S(2)}) %copy-start.6) | copy-done | bytes 32792
  25.1 1.4 %combine.1 = (bf16[16,1024]{1,0:T(8,128)(2,1)}, f32[16,128]{1,0:T(8,128)}) custom-call(bf16[128,128]{1,0:T(8,128)(2,1)} %get-tuple-element.15.refs_0_, bf16[128,128]{1,0:T(8,128)(2,1)} %copy-done.4, bf16[128,128]{1,0:T(8,128)(2,1)} %copy-done.5, bf16[128,128]{1,0:T(8,128)(2,1)} %copy-done.6), custom_call_target="tpu_custom_call" | custom-call | tf_op jit(solution)/shard_map/combine/pallas_call | solution.py:198
  26.5 1.5 %collective-permute-start.6 = (bf16[16,1024]{1,0:T(8,128)(2,1)}, bf16[16,1024]{1,0:T(8,128)(2,1)S(1)}, u32[]{:S(2)}, u32[]{:S(2)}) collective-permute-start(bf16[16,1024]{1,0:T(8,128)(2,1)} %get-tuple-element.19.left), channel_id=1, source_target_pairs={{0,4},{4,0},{8,12},{12,8},{16,20},{20,16},{24,28},{28,24},{1,5},{5... | collective-permute-start | bytes 98312 | tf_op jit(solution)/shard_map/ppermute | solution.py:160
  28.1 2.6 %collective-permute-done.6.left = bf16[16,1024]{1,0:T(8,128)(2,1)S(1)} collective-permute-done((bf16[16,1024]{1,0:T(8,128)(2,1)}, bf16[16,1024]{1,0:T(8,128)(2,1)S(1)}, u32[]{:S(2)}, u32[]{:S(2)}) %collective-permute-start.6) | collective-permute-done | bytes 32800 | tf_op jit(solution)/shard_map/ppermute | solution.py:160
  30.7 0.0 collective-permute-done.5.refs_3_
  30.7 0.0 collective-permute-done.4.refs_2_
  30.7 0.0 collective-permute-done.3.refs_1_
  30.7 0.3 other_scores.1
  31.0 1.5 %collective-permute-start.7 = (f32[16,256]{1,0:T(8,128)S(1)}, f32[16,256]{1,0:T(8,128)S(1)}, u32[]{:S(2)}, u32[]{:S(2)}) collective-permute-start(f32[16,256]{1,0:T(8,128)S(1)} %other_scores.1), channel_id=1, source_target_pairs={{0,4},{4,0},{8,12},{12,8},{16,20},{20,16},{24,28},{28,24},{1,5},{5... | collective-permute-start | bytes 49160 | tf_op jit(solution)/shard_map/ppermute | solution.py:160
  32.5 2.2 %collective-permute-done.7.refs_4_ = f32[16,256]{1,0:T(8,128)S(1)} collective-permute-done((f32[16,256]{1,0:T(8,128)S(1)}, f32[16,256]{1,0:T(8,128)S(1)}, u32[]{:S(2)}, u32[]{:S(2)}) %collective-permute-start.7) | collective-permute-done | bytes 16416 | tf_op jit(solution)/shard_map/ppermute | solution.py:160
  34.7 0.8 %copy-done.1 = bf16[16,1024]{1,0:T(8,128)(2,1)S(1)} copy-done((bf16[16,1024]{1,0:T(8,128)(2,1)S(1)}, bf16[16,1024]{1,0:T(8,128)(2,1)}, u32[]{:S(2)}) %copy-start.1) | copy-done | bytes 32792
  35.5 0.7 %copy-done.3 = f32[16,128]{1,0:T(8,128)S(1)} copy-done((f32[16,128]{1,0:T(8,128)S(1)}, f32[16,128]{1,0:T(8,128)}, u32[]{:S(2)}) %copy-start.3) | copy-done | bytes 8216
  36.2 0.3 own_scores.1
  36.5 0.6 %copy-done.2 = f32[4,640]{1,0:T(4,128)} copy-done((f32[4,640]{1,0:T(4,128)}, f32[4,640]{1,0:T(4,128)S(1)}, u32[]{:S(2)}) %copy-start.2) | copy-done | bytes 10264
  37.1 1.3 %collective-permute-start.9 = (f32[4,640]{1,0:T(4,128)S(1)}, f32[4,640]{1,0:T(4,128)S(1)}, u32[]{:S(2)}, u32[]{:S(2)}) collective-permute-start(f32[4,640]{1,0:T(4,128)S(1)} %get-tuple-element.23), channel_id=1, source_target_pairs={{0,2},{1,3},{2,0},{3,1},{4,6},{5,7},{6,4},{7,5},{8,10},{9,11},{10,... | collective-permute-start | bytes 30728 | tf_op jit(solution)/shard_map/ppermute | solution.py:157
  38.5 0.5 %collective-permute-start.10 = (f32[4,640]{1,0:T(4,128)S(1)}, f32[4,640]{1,0:T(4,128)S(1)}, u32[]{:S(2)}, u32[]{:S(2)}) collective-permute-start(f32[4,640]{1,0:T(4,128)S(1)} %get-tuple-element.24), channel_id=1, source_target_pairs={{0,3},{1,2},{2,1},{3,0},{4,7},{5,6},{6,5},{7,4},{8,11},{9,10},{10,... | collective-permute-start | bytes 30728 | tf_op jit(solution)/shard_map/ppermute | solution.py:157
  39.0 0.0 collective-permute-done.8.refs_1_
  39.0 1.8 %collective-permute-done.9.refs_2_ = f32[4,640]{1,0:T(4,128)S(1)} collective-permute-done((f32[4,640]{1,0:T(4,128)S(1)}, f32[4,640]{1,0:T(4,128)S(1)}, u32[]{:S(2)}, u32[]{:S(2)}) %collective-permute-start.9) | collective-permute-done | bytes 10272 | tf_op jit(solution)/shard_map/ppermute | solution.py:157
  40.8 0.8 %collective-permute-done.10.refs_3_ = f32[4,640]{1,0:T(4,128)S(1)} collective-permute-done((f32[4,640]{1,0:T(4,128)S(1)}, f32[4,640]{1,0:T(4,128)S(1)}, u32[]{:S(2)}, u32[]{:S(2)}) %collective-permute-start.10) | collective-permute-done | bytes 10272 | tf_op jit(solution)/shard_map/ppermute | solution.py:157
  41.6 0.6 %copy-done.9 = f32[4,640]{1,0:T(4,128)} copy-done((f32[4,640]{1,0:T(4,128)}, f32[4,640]{1,0:T(4,128)S(1)}, u32[]{:S(2)}) %copy-start.9) | copy-done | bytes 10264
  42.2 1.5 %finish.1 = f32[4,512]{1,0:T(4,128)} custom-call(f32[4,640]{1,0:T(4,128)} %copy-done.2, f32[4,640]{1,0:T(4,128)} %copy-done.7, f32[4,640]{1,0:T(4,128)} %copy-done.8, f32[4,640]{1,0:T(4,128)} %copy-done.9), custom_call_target="tpu_custom_call" | custom-call | tf_op jit(solution)/shard_map/finish/pallas_call | solution.py:236
  (16 shorter events, 0.0 us)
Async XLA Ops:
  0.0 1.0 %copy-start = (bf16[64,4096]{1,0:T(8,128)(2,1)S(1)}, bf16[64,4096]{1,0:T(8,128)(2,1)}, u32[]{:S(2)}) copy-start(bf16[64,4096]{1,0:T(8,128)(2,1)} %param.11) | copy-start | bytes 1572868
  1.1 29.6 %collective-permute-start.5 = (bf16[64,1024]{1,0:T(8,128)(2,1)S(1)}, bf16[64,1024]{1,0:T(8,128)(2,1)S(1)}, u32[]{:S(2)}, u32[]{:S(2)}) collective-permute-start(bf16[64,1024]{1,0:T(8,128)(2,1)S(1)} %constant_dynamic-slice_fusion.refs_0_), channel_id=1, source_target_pairs={{0,24},{4,28},{8,16},{12,20},{16,8},{20,12},{24,0},{28,4},{1,25},{... | collective-permute-start | bytes 393224 | tf_op jit(solution)/shard_map/ppermute | solution.py:160
  6.2 24.5 %collective-permute-start.4 = (bf16[64,1024]{1,0:T(8,128)(2,1)S(1)}, bf16[64,1024]{1,0:T(8,128)(2,1)S(1)}, u32[]{:S(2)}, u32[]{:S(2)}) collective-permute-start(bf16[64,1024]{1,0:T(8,128)(2,1)S(1)} %constant_dynamic-slice_fusion.refs_0_), channel_id=1, source_target_pairs={{0,16},{4,20},{8,24},{12,28},{16,0},{20,4},{24,8},{28,12},{1,17},{... | collective-permute-start | bytes 393224 | tf_op jit(solution)/shard_map/ppermute | solution.py:160
  6.2 24.5 %collective-permute-start.3 = (bf16[64,1024]{1,0:T(8,128)(2,1)S(1)}, bf16[64,1024]{1,0:T(8,128)(2,1)S(1)}, u32[]{:S(2)}, u32[]{:S(2)}) collective-permute-start(bf16[64,1024]{1,0:T(8,128)(2,1)S(1)} %constant_dynamic-slice_fusion.refs_0_), channel_id=1, source_target_pairs={{0,8},{4,12},{8,0},{12,4},{16,24},{20,28},{24,16},{28,20},{1,9},{5... | collective-permute-start | bytes 393224 | tf_op jit(solution)/shard_map/ppermute | solution.py:160
  19.1 1.8 %collective-permute-start = (bf16[128,128]{1,0:T(8,128)(2,1)}, bf16[128,128]{1,0:T(8,128)(2,1)S(1)}, u32[]{:S(2)}, u32[]{:S(2)}) collective-permute-start(bf16[128,128]{1,0:T(8,128)(2,1)} %get-tuple-element.16), channel_id=1, source_target_pairs={{0,1},{1,0},{2,3},{3,2},{4,5},{5,4},{6,7},{7,6},{8,9},{9,8},{10,11... | collective-permute-start | bytes 98312 | tf_op jit(solution)/shard_map/ppermute | solution.py:157
  19.2 4.2 %collective-permute-start.1 = (bf16[128,128]{1,0:T(8,128)(2,1)}, bf16[128,128]{1,0:T(8,128)(2,1)S(1)}, u32[]{:S(2)}, u32[]{:S(2)}) collective-permute-start(bf16[128,128]{1,0:T(8,128)(2,1)} %get-tuple-element.17), channel_id=1, source_target_pairs={{0,2},{1,3},{2,0},{3,1},{4,6},{5,7},{6,4},{7,5},{8,10},{9,11},{10,... | collective-permute-start | bytes 98312 | tf_op jit(solution)/shard_map/ppermute | solution.py:157
  20.9 3.6 %copy-start.4 = (bf16[128,128]{1,0:T(8,128)(2,1)}, bf16[128,128]{1,0:T(8,128)(2,1)S(1)}, u32[]{:S(2)}) copy-start(bf16[128,128]{1,0:T(8,128)(2,1)S(1)} %collective-permute-done.refs_1_) | copy-start | bytes 98308
  20.9 3.6 %collective-permute-start.2 = (bf16[128,128]{1,0:T(8,128)(2,1)}, bf16[128,128]{1,0:T(8,128)(2,1)S(1)}, u32[]{:S(2)}, u32[]{:S(2)}) collective-permute-start(bf16[128,128]{1,0:T(8,128)(2,1)} %get-tuple-element.18), channel_id=1, source_target_pairs={{0,3},{1,2},{2,1},{3,0},{4,7},{5,6},{6,5},{7,4},{8,11},{9,10},{10,... | collective-permute-start | bytes 98312 | tf_op jit(solution)/shard_map/ppermute | solution.py:157
  23.4 1.1 %copy-start.5 = (bf16[128,128]{1,0:T(8,128)(2,1)}, bf16[128,128]{1,0:T(8,128)(2,1)S(1)}, u32[]{:S(2)}) copy-start(bf16[128,128]{1,0:T(8,128)(2,1)S(1)} %collective-permute-done.1.refs_2_) | copy-start | bytes 98308
  24.5 0.6 %copy-start.6 = (bf16[128,128]{1,0:T(8,128)(2,1)}, bf16[128,128]{1,0:T(8,128)(2,1)S(1)}, u32[]{:S(2)}) copy-start(bf16[128,128]{1,0:T(8,128)(2,1)S(1)} %collective-permute-done.2.refs_3_) | copy-start | bytes 98308
  26.5 4.1 %collective-permute-start.6 = (bf16[16,1024]{1,0:T(8,128)(2,1)}, bf16[16,1024]{1,0:T(8,128)(2,1)S(1)}, u32[]{:S(2)}, u32[]{:S(2)}) collective-permute-start(bf16[16,1024]{1,0:T(8,128)(2,1)} %get-tuple-element.19.left), channel_id=1, source_target_pairs={{0,4},{4,0},{8,12},{12,8},{16,20},{20,16},{24,28},{28,24},{1,5},{5... | collective-permute-start | bytes 98312 | tf_op jit(solution)/shard_map/ppermute | solution.py:160
  31.0 3.8 %collective-permute-start.7 = (f32[16,256]{1,0:T(8,128)S(1)}, f32[16,256]{1,0:T(8,128)S(1)}, u32[]{:S(2)}, u32[]{:S(2)}) collective-permute-start(f32[16,256]{1,0:T(8,128)S(1)} %other_scores.1), channel_id=1, source_target_pairs={{0,4},{4,0},{8,12},{12,8},{16,20},{20,16},{24,28},{28,24},{1,5},{5... | collective-permute-start | bytes 49160 | tf_op jit(solution)/shard_map/ppermute | solution.py:160
  34.7 0.8 %copy-start.1 = (bf16[16,1024]{1,0:T(8,128)(2,1)S(1)}, bf16[16,1024]{1,0:T(8,128)(2,1)}, u32[]{:S(2)}) copy-start(bf16[16,1024]{1,0:T(8,128)(2,1)} %get-tuple-element.19.left) | copy-start | bytes 98308
  35.5 0.7 %copy-start.3 = (f32[16,128]{1,0:T(8,128)S(1)}, f32[16,128]{1,0:T(8,128)}, u32[]{:S(2)}) copy-start(f32[16,128]{1,0:T(8,128)} %get-tuple-element.20.squares) | copy-start | bytes 24580
  36.5 0.6 %copy-start.2 = (f32[4,640]{1,0:T(4,128)}, f32[4,640]{1,0:T(4,128)S(1)}, u32[]{:S(2)}) copy-start(f32[4,640]{1,0:T(4,128)S(1)} %get-tuple-element.21.refs_0_) | copy-start | bytes 30724
  37.1 1.9 %collective-permute-start.8 = (f32[4,640]{1,0:T(4,128)S(1)}, f32[4,640]{1,0:T(4,128)S(1)}, u32[]{:S(2)}, u32[]{:S(2)}) collective-permute-start(f32[4,640]{1,0:T(4,128)S(1)} %get-tuple-element.22), channel_id=1, source_target_pairs={{0,1},{1,0},{2,3},{3,2},{4,5},{5,4},{6,7},{7,6},{8,9},{9,8},{10,11... | collective-permute-start | bytes 30728 | tf_op jit(solution)/shard_map/ppermute | solution.py:157
  37.1 3.7 %collective-permute-start.9 = (f32[4,640]{1,0:T(4,128)S(1)}, f32[4,640]{1,0:T(4,128)S(1)}, u32[]{:S(2)}, u32[]{:S(2)}) collective-permute-start(f32[4,640]{1,0:T(4,128)S(1)} %get-tuple-element.23), channel_id=1, source_target_pairs={{0,2},{1,3},{2,0},{3,1},{4,6},{5,7},{6,4},{7,5},{8,10},{9,11},{10,... | collective-permute-start | bytes 30728 | tf_op jit(solution)/shard_map/ppermute | solution.py:157
  38.5 3.1 %collective-permute-start.10 = (f32[4,640]{1,0:T(4,128)S(1)}, f32[4,640]{1,0:T(4,128)S(1)}, u32[]{:S(2)}, u32[]{:S(2)}) collective-permute-start(f32[4,640]{1,0:T(4,128)S(1)} %get-tuple-element.24), channel_id=1, source_target_pairs={{0,3},{1,2},{2,1},{3,0},{4,7},{5,6},{6,5},{7,4},{8,11},{9,10},{10,... | collective-permute-start | bytes 30728 | tf_op jit(solution)/shard_map/ppermute | solution.py:157
  39.0 2.6 %copy-start.7 = (f32[4,640]{1,0:T(4,128)}, f32[4,640]{1,0:T(4,128)S(1)}, u32[]{:S(2)}) copy-start(f32[4,640]{1,0:T(4,128)S(1)} %collective-permute-done.8.refs_1_) | copy-start | bytes 30724
  40.8 0.8 %copy-start.8 = (f32[4,640]{1,0:T(4,128)}, f32[4,640]{1,0:T(4,128)S(1)}, u32[]{:S(2)}) copy-start(f32[4,640]{1,0:T(4,128)S(1)} %collective-permute-done.9.refs_2_) | copy-start | bytes 30724
  41.6 0.6 %copy-start.9 = (f32[4,640]{1,0:T(4,128)}, f32[4,640]{1,0:T(4,128)S(1)}, u32[]{:S(2)}) copy-start(f32[4,640]{1,0:T(4,128)S(1)} %collective-permute-done.10.refs_3_) | copy-start | bytes 30724

commit v4 on v3

v4 whole, which is shorter than its diff:
```python
import functools

import jax
import jax.numpy as jnp
from jax import lax
from jax.experimental import pallas as pl
from jax.experimental.pallas import tpu as pltpu
from jax.sharding import PartitionSpec as P

EPS = 1e-06
F32 = jnp.float32
BF16 = jnp.bfloat16
VMEM = pl.BlockSpec(memory_space=pltpu.VMEM)
HBM = pl.BlockSpec(memory_space=pltpu.HBM)
BY_ROWS = (((1,), (1,)), ((), ()))


def grads_kernel(dims, lens_in, acts, out_grads, w_in, w_out, send, keep, *rest):
    cands, tokens, width, groups = dims
    act_buf, grad_buf, win_raw, wout_raw, win_buf, wout_buf, lens, store, sems, wsems = rest
    half = cands // 2
    chunks = half // 2
    rows = 4 * tokens
    load_lens = pltpu.make_async_copy(lens_in, lens, wsems.at[2])
    load_w = [
        pltpu.make_async_copy(w_out, wout_raw, wsems.at[0]),
        pltpu.make_async_copy(w_in, win_raw, wsems.at[1]),
    ]
    loads = []
    for i in range(chunks):
        for side, (source, buf) in enumerate(((out_grads, grad_buf), (acts, act_buf))):
            loads.append(
                [
                    pltpu.make_async_copy(
                        source.at[pl.ds((2 * i + h * half) * tokens, rows // 2)],
                        buf.at[pl.ds(i * rows + h * (rows // 2), rows // 2)],
                        sems.at[side, 2 * i + h],
                    )
                    for h in range(2)
                ]
            )
    load_w[0].start()
    load_w[1].start()
    load_lens.start()
    for pair in loads:
        for load in pair:
            load.start()
    grp = lax.axis_index("grp")
    lines = width // groups
    position = lax.broadcasted_iota(jnp.int32, (tokens, width), 0) + grp * tokens
    row_blk = lax.broadcasted_iota(jnp.int32, (rows, rows), 0) // tokens
    col_blk = lax.broadcasted_iota(jnp.int32, (rows, 4 * width), 1) // width
    diagonal = row_blk == col_blk // 2 + 2 * (col_blk % 2)
    load_w[0].wait()
    wout_buf[...] = wout_raw[...].T
    load_w[1].wait()
    load_lens.wait()
    for i in range(chunks):
        part = pl.ds(i * rows, rows)
        for load in loads[2 * i]:
            load.wait()
        gp = jnp.dot(grad_buf[part, :], wout_buf[...], preferred_element_type=F32)
        if i == 0:
            win_buf[...] = win_raw[...].T
        left = gp.T.astype(BF16)
        for load in loads[2 * i + 1]:
            load.wait()
        xp = jnp.dot(act_buf[part, :], win_buf[...], preferred_element_type=F32)
        used = []
        for j in range(4):
            cand = 2 * i + j % 2 + (j // 2) * half
            used.append(jnp.where(position < lens[cand], xp[j * tokens : (j + 1) * tokens], 0.0))
        wide = jnp.concatenate([jnp.concatenate(used, axis=0)] * 4, axis=1)
        right = jnp.where(diagonal, wide, 0.0).astype(BF16)
        blocks = jnp.dot(left, right, preferred_element_type=F32)
        for t in range(2):
            pair = 2 * i + t
            for s in range(groups):
                store[s, pair * lines : (pair + 1) * lines, :] = blocks[
                    s * lines : (s + 1) * lines, t * 128 : (t + 1) * 128
                ]
    core = lax.rem(grp, 2)
    for x in range(groups // 2):
        send[x] = store[2 * x + 1 - core].astype(BF16)
        keep[x] = store[2 * x + core]


def fold_kernel(keep, came, send, kept):
    x = lax.axis_index("grp") // 2
    send[...] = (keep[1 - x] + came[1 - x].astype(F32)).astype(BF16)
    kept[...] = keep[x] + came[x].astype(F32)


def combine_kernel(dims, kept, came, out, squares, grads):
    half, lines, width = dims
    grads[...] = kept[...] + came[...].astype(F32)
    low = lax.broadcasted_iota(jnp.int32, (half, 128), 1) < width
    sums, columns = None, []
    for e in range(0, lines, 2):
        first = grads[pl.ds(e, half, stride=lines), :]
        second = grads[pl.ds(e + 1, half, stride=lines), :]
        line = jnp.concatenate(
            [
                jnp.where(low, first, pltpu.roll(second, width, 1)),
                jnp.where(low, pltpu.roll(first, width, 1), second),
            ],
            axis=0,
        )
        columns.append(line.astype(BF16))
        sums = line * line if sums is None else sums + line * line
    squares[...] = sums
    out[...] = jnp.concatenate(columns, axis=1)


def near_scores(left, queries, place):
    far = len(queries)
    z = lax.axis_index("blk") // 2
    for k in range(far):
        place[jnp.bitwise_xor(z, k)] = lax.dot_general(
            left, queries[k][...], BY_ROWS, preferred_element_type=F32
        )
    return jnp.concatenate([place[k] for k in range(far)], axis=1)


def other_kernel(far, left, *refs):
    refs[far][...] = near_scores(left[...], refs[:far], refs[far + 1])


def own_kernel(dims, left, squares, *refs):
    far, groups = dims
    queries = refs[:far]
    other, send, keep, place, result = refs[far:]
    own = near_scores(left[...], queries, place)
    is_even = lax.rem(lax.axis_index("blk"), 2) == 0
    back = other[...]
    even = jnp.where(is_even, own, back)
    odd = jnp.where(is_even, back, own)
    half = own.shape[1]
    owned = own.shape[0] // groups
    for g in range(groups):
        here = slice(g * owned, (g + 1) * owned)
        result[g, :, :half] = even[here]
        result[g, :, half : 2 * half] = odd[here]
        result[g, :, 2 * half :] = squares[here, :]
    x = lax.axis_index("grp") // 2
    for core in range(2):
        send[core] = result[2 * (1 - x) + core]
        keep[core] = result[2 * x + core]


def pass_kernel(keep, came, send, kept):
    core = lax.rem(lax.axis_index("grp"), 2)
    send[...] = keep[1 - core] + came[1 - core]
    kept[...] = keep[core] + came[core]


def finish_kernel(dims, kept, came, out):
    pdim, nq = dims
    total = kept[...] + came[...]
    width = out.shape[1]
    mean = jnp.sum(total[:, width:], axis=1, keepdims=True) / pdim
    scaled = total[:, :width] * lax.rsqrt(mean + EPS)
    columns = []
    for start in range(0, width // 2, nq):
        columns.append(scaled[:, start : start + nq])
        columns.append(scaled[:, width // 2 + start : width // 2 + start + nq])
    out[...] = jnp.concatenate(columns, axis=1)


def small(kernel, out_shape, operands, scratch_shapes=(), name=None):
    one = not isinstance(out_shape, list)
    return pl.pallas_call(
        kernel,
        out_shape=out_shape,
        in_specs=[VMEM] * len(operands),
        out_specs=VMEM if one else [VMEM] * len(out_shape),
        scratch_shapes=list(scratch_shapes),
        compiler_params=pltpu.CompilerParams(vmem_limit_bytes=16 * 2**20),
        name=name,
    )(*operands)


def on_device(blks, groups, acts, out_grads, proj_in, proj_out, lengths, queries):
    _, cands, tokens, depth = acts.shape
    width = proj_in.shape[2]
    far = blks // 2
    pdim = width * width
    lines = width // groups
    nq = queries.shape[0]
    total_q = nq * blks
    owned = cands // groups
    slice_width = pdim // groups
    shape = jax.ShapeDtypeStruct

    def grp_swap(x, k):
        return lax.ppermute(x, "grp", [(g, g ^ k) for g in range(groups)])

    def blk_swap(x, k):
        return lax.ppermute(x, "blk", [(b, b ^ k) for b in range(blks)])

    cut = lax.dynamic_slice(queries, (0, lax.axis_index("grp") * slice_width), (nq, slice_width))
    gathered = [cut] + [blk_swap(cut, 2 * k) for k in range(1, far)]

    rows = cands * tokens
    piece = (cands // 2 * lines, 128)
    send, keep = pl.pallas_call(
        functools.partial(grads_kernel, (cands, tokens, width, groups)),
        out_shape=[shape((groups // 2,) + piece, BF16), shape((groups // 2,) + piece, F32)],
        in_specs=[HBM] * 5,
        out_specs=[VMEM] * 2,
        scratch_shapes=[
            pltpu.VMEM((rows, depth), BF16),
            pltpu.VMEM((rows, depth), BF16),
            pltpu.VMEM((width, depth), BF16),
            pltpu.VMEM((width, depth), BF16),
            pltpu.VMEM((depth, width), BF16),
            pltpu.VMEM((depth, width), BF16),
            pltpu.SMEM((cands,), jnp.int32),
            pltpu.VMEM((groups,) + piece, F32),
            pltpu.SemaphoreType.DMA((2, cands // 2)),
            pltpu.SemaphoreType.DMA((3,)),
        ],
        compiler_params=pltpu.CompilerParams(vmem_limit_bytes=54784 * 2**10),
        cost_estimate=pl.CostEstimate(
            flops=16 * rows * depth * width, bytes_accessed=8 * rows * depth, transcendentals=0
        ),
        name="grads",
    )(
        lengths,
        acts.reshape(rows, depth),
        out_grads.reshape(rows, depth),
        proj_in.reshape(depth, width).T,
        proj_out.reshape(depth, width).T,
    )
    send, kept = small(
        fold_kernel, [shape(piece, BF16), shape(piece, F32)], (keep, grp_swap(send, 1)), name="fold"
    )
    own, squares = small(
        functools.partial(combine_kernel, (cands // 2, lines, width)),
        [shape((cands, slice_width), BF16), shape((cands, 128), F32)],
        (kept, grp_swap(send, 2)),
        [pltpu.VMEM(piece, F32)],
        name="combine",
    )
    place = pltpu.VMEM((far, cands, nq), F32)
    back = small(
        functools.partial(other_kernel, far),
        shape((cands, total_q // 2), F32),
        (blk_swap(own, 1), *gathered),
        [place],
        name="other_scores",
    )
    line = (owned, total_q + 128)
    send, keep = small(
        functools.partial(own_kernel, (far, groups)),
        [shape((groups // 2,) + line, F32)] * 2,
        (own, squares, *gathered, blk_swap(back, 1)),
        [place, pltpu.VMEM((groups,) + line, F32)],
        name="own_scores",
    )
    send, kept = small(pass_kernel, [shape(line, F32)] * 2, (keep, grp_swap(send, 2)), name="pass")
    return small(
        functools.partial(finish_kernel, (pdim, nq)),
        shape((owned, total_q), F32),
        (kept, grp_swap(send, 1)),
        name="finish",
    )


def solution(mesh):
    in_specs = (
        P(None, "blk", "grp", None),
        P(None, "blk", "grp", None),
        P(),
        P(),
        P("blk"),
        P("blk", None),
    )
    return jax.shard_map(
        functools.partial(on_device, mesh.shape["blk"], mesh.shape["grp"]),
        mesh=mesh,
        in_specs=in_specs,
        out_specs=P(("blk", "grp"), None),
        check_vma=False,
    )
```

time: 44.1 us -> 39.4 us (0.89)
  local copies, waits for them, and re-layouts: 4.3 us -> 0.73 us
  waiting for transfers between devices: 9.86 us -> 12.3 us
  Pallas kernels: 15.9 us -> 13.8 us
  starting transfers between devices: 13.5 us -> 12.5 us
    unnamed x20 -> x4, local copies, waits for them, and re-layouts: 4.29 us -> 0.72 us
    pallas_call x4 -> x6, Pallas kernels: 3.61 us -> 1.52 us  [small(): pl.pallas_call(kernel, out_shape=out_shape, in_specs=[VMEM] * len(operand...]
    ppermute x5, waiting for transfers between devices: 4.83 us -> 6.61 us  [blk_swap(): return lax.ppermute(x, 'blk', [(b, b ^ k) for b in range(blks)])]
    ppermute x6 -> x4, starting transfers between devices: 4.73 us -> 3.86 us  [grp_swap(): return lax.ppermute(x, 'grp', [(g, g ^ k) for g in range(groups)])]
    ppermute x6 -> x4, waiting for transfers between devices: 5.02 us -> 5.66 us  [grp_swap(): return lax.ppermute(x, 'grp', [(g, g ^ k) for g in range(groups)])]
  transfers between devices with their start and end apart: 11 -> 9, of which waited for: 6 -> 5; matrix products, arithmetic and copies ran while one was open for 0% -> 0% of each run, Pallas kernels for 32% -> 0%
where the time goes in v4:
time: 39.4 us; the launch traced here: 39.3 us
  Pallas kernels  13.8 us (35%)
  starting transfers between devices  12.5 us (32%)
  waiting for transfers between devices  12.3 us (31%)
  local copies, waits for them, and re-layouts  0.73 us (2%)
    pallas_call x1, Pallas kernels, on_device(): pl.pallas_call(functools.partial(grads_kernel, (cands, tokens, width, gro...  12.3 us
    ppermute x5, starting transfers between devices, blk_swap(): return lax.ppermute(x, 'blk', [(b, b ^ k) for b in range(blks)])  8.61 us
    ppermute x5, waiting for transfers between devices, blk_swap(): return lax.ppermute(x, 'blk', [(b, b ^ k) for b in range(blks)])  6.61 us
    ppermute x4, waiting for transfers between devices, grp_swap(): return lax.ppermute(x, 'grp', [(g, g ^ k) for g in range(groups)])  5.66 us
    ppermute x4, starting transfers between devices, grp_swap(): return lax.ppermute(x, 'grp', [(g, g ^ k) for g in range(groups)])  3.86 us
    pallas_call x6, Pallas kernels, small(): pl.pallas_call(kernel, out_shape=out_shape, in_specs=[VMEM] * len(operand...  1.52 us
  transfers between devices with their start and end apart: 9, of which 5 were waited for; matrix products, arithmetic and copies ran while one was open for 0% of the time, Pallas kernels for 0%

profile of v4, /device:TPU:0, one launch (start us, length us, event | category | flops | bytes accessed | tf_op | source)
XLA Modules:
  0.0 39.3 jit_solution(1150594718707643656)
XLA Ops:
  0.0 0.0 copy-start
  0.0 0.0 copy-start.1
  0.0 0.7 %copy-done.1 = s32[16]{0:T(128)S(1)} copy-done((s32[16]{0:T(128)S(1)}, s32[16]{0:T(128)}, u32[]{:S(2)}) %copy-start.1) | copy-done | bytes 88
  0.7 12.3 %grads.1 = (bf16[2,128,128]{2,1,0:T(8,128)(2,1)S(1)}, f32[2,128,128]{2,1,0:T(8,128)S(1)}) custom-call(s32[16]{0:T(128)S(1)} %copy-done.1, bf16[1024,4096]{1,0:T(8,128)(2,1)} %bitcast.8, bf16[1024,4096]{1,0:T(8,128)(2,1)} %bitcast.9, bf16[64,4096]{1,0:T(8,128)(2,1)} %bitcast.10, bf16[64,4096]{1,0:T(8,128)(2,1)} %bitcast.11), custom_call_target="tpu_custom_call" | custom-call | flops 4294967296 | bytes 33554432 | tf_op jit(solution)/shard_map/grads/pallas_call | solution.py:206
  13.0 0.5 %collective-permute-start = (bf16[2,128,128]{2,1,0:T(8,128)(2,1)S(1)}, bf16[2,128,128]{2,1,0:T(8,128)(2,1)S(1)}, u32[]{:S(2)}, u32[]{:S(2)}) collective-permute-start(bf16[2,128,128]{2,1,0:T(8,128)(2,1)S(1)} %get-tuple-element.16), channel_id=1, source_target_pairs={{0,1},{1,0},{2,3},{3,2},{4,5},{5,4},{6,7},{7,6},{8,9},{9,8},{10,11... | collective-permute-start | bytes 196616 | tf_op jit(solution)/shard_map/ppermute | solution.py:196
  13.5 0.0 copy-done
  13.5 2.7 %collective-permute-start.2 = (bf16[64,1024]{1,0:T(8,128)(2,1)S(1)}, bf16[64,1024]{1,0:T(8,128)(2,1)S(1)}, u32[]{:S(2)}, u32[]{:S(2)}) collective-permute-start(bf16[64,1024]{1,0:T(8,128)(2,1)S(1)} %constant_dynamic-slice_fusion.refs_0_), channel_id=1, source_target_pairs={{0,8},{4,12},{8,0},{12,4},{16,24},{20,28},{24,16},{28,20},{1,9},{5... | collective-permute-start | bytes 393224 | tf_op jit(solution)/shard_map/ppermute | solution.py:199
  16.2 2.6 %collective-permute-start.3 = (bf16[64,1024]{1,0:T(8,128)(2,1)S(1)}, bf16[64,1024]{1,0:T(8,128)(2,1)S(1)}, u32[]{:S(2)}, u32[]{:S(2)}) collective-permute-start(bf16[64,1024]{1,0:T(8,128)(2,1)S(1)} %constant_dynamic-slice_fusion.refs_0_), channel_id=1, source_target_pairs={{0,16},{4,20},{8,24},{12,28},{16,0},{20,4},{24,8},{28,12},{1,17},{... | collective-permute-start | bytes 393224 | tf_op jit(solution)/shard_map/ppermute | solution.py:199
  18.8 0.0 collective-permute-start.4
  18.8 0.0 collective-permute-done.came
  18.8 1.8 %collective-permute-start.1 = (bf16[128,128]{1,0:T(8,128)(2,1)S(1)}, bf16[128,128]{1,0:T(8,128)(2,1)S(1)}, u32[]{:S(2)}, u32[]{:S(2)}) collective-permute-start(bf16[128,128]{1,0:T(8,128)(2,1)S(1)} %get-tuple-element.18), channel_id=1, source_target_pairs={{0,2},{1,3},{2,0},{3,1},{4,6},{5,7},{6,4},{7,5},{8,10},{9,11},{10,... | collective-permute-start | bytes 98312 | tf_op jit(solution)/shard_map/ppermute | solution.py:196
  20.6 2.2 %collective-permute-done.1.came = bf16[128,128]{1,0:T(8,128)(2,1)S(1)} collective-permute-done((bf16[128,128]{1,0:T(8,128)(2,1)S(1)}, bf16[128,128]{1,0:T(8,128)(2,1)S(1)}, u32[]{:S(2)}, u32[]{:S(2)}) %collective-permute-start.1) | collective-permute-done | bytes 32800 | tf_op jit(solution)/shard_map/ppermute | solution.py:196
  22.8 0.1 combine.1
  22.9 1.8 %collective-permute-start.5 = (bf16[16,1024]{1,0:T(8,128)(2,1)S(1)}, bf16[16,1024]{1,0:T(8,128)(2,1)S(1)}, u32[]{:S(2)}, u32[]{:S(2)}) collective-permute-start(bf16[16,1024]{1,0:T(8,128)(2,1)S(1)} %get-tuple-element.19.left), channel_id=1, source_target_pairs={{0,4},{4,0},{8,12},{12,8},{16,20},{20,16},{24,28},{28,24},{1,5},{5... | collective-permute-start | bytes 98312 | tf_op jit(solution)/shard_map/ppermute | solution.py:199
  24.7 0.0 collective-permute-done.2.refs_1_
  24.7 4.4 %collective-permute-done.3.refs_2_ = bf16[64,1024]{1,0:T(8,128)(2,1)S(1)} collective-permute-done((bf16[64,1024]{1,0:T(8,128)(2,1)S(1)}, bf16[64,1024]{1,0:T(8,128)(2,1)S(1)}, u32[]{:S(2)}, u32[]{:S(2)}) %collective-permute-start.3) | collective-permute-done | bytes 131104 | tf_op jit(solution)/shard_map/ppermute | solution.py:199
  29.1 0.0 collective-permute-done.4.refs_3_
  29.1 0.0 collective-permute-done.5.left
  29.1 0.3 other_scores.1
  29.4 1.5 %collective-permute-start.6 = (f32[16,256]{1,0:T(8,128)S(1)}, f32[16,256]{1,0:T(8,128)S(1)}, u32[]{:S(2)}, u32[]{:S(2)}) collective-permute-start(f32[16,256]{1,0:T(8,128)S(1)} %other_scores.1), channel_id=1, source_target_pairs={{0,4},{4,0},{8,12},{12,8},{16,20},{20,16},{24,28},{28,24},{1,5},{5... | collective-permute-start | bytes 49160 | tf_op jit(solution)/shard_map/ppermute | solution.py:199
  31.0 2.2 %collective-permute-done.6.refs_4_ = f32[16,256]{1,0:T(8,128)S(1)} collective-permute-done((f32[16,256]{1,0:T(8,128)S(1)}, f32[16,256]{1,0:T(8,128)S(1)}, u32[]{:S(2)}, u32[]{:S(2)}) %collective-permute-start.6) | collective-permute-done | bytes 16416 | tf_op jit(solution)/shard_map/ppermute | solution.py:199
  33.2 0.3 own_scores.1
  33.5 1.6 %collective-permute-start.7 = (f32[2,4,640]{2,1,0:T(4,128)S(1)}, f32[2,4,640]{2,1,0:T(4,128)S(1)}, u32[]{:S(2)}, u32[]{:S(2)}) collective-permute-start(f32[2,4,640]{2,1,0:T(4,128)S(1)} %get-tuple-element.22), channel_id=1, source_target_pairs={{0,2},{1,3},{2,0},{3,1},{4,6},{5,7},{6,4},{7,5},{8,10},{9,11},{10,... | collective-permute-start | bytes 61448 | tf_op jit(solution)/shard_map/ppermute | solution.py:196
  35.1 2.3 %collective-permute-done.7.came = f32[2,4,640]{2,1,0:T(4,128)S(1)} collective-permute-done((f32[2,4,640]{2,1,0:T(4,128)S(1)}, f32[2,4,640]{2,1,0:T(4,128)S(1)}, u32[]{:S(2)}, u32[]{:S(2)}) %collective-permute-start.7) | collective-permute-done | bytes 20512 | tf_op jit(solution)/shard_map/ppermute | solution.py:196
  37.4 0.0 collective-permute-start.8
  37.4 1.2 %collective-permute-done.8.came = f32[4,640]{1,0:T(4,128)S(1)} collective-permute-done((f32[4,640]{1,0:T(4,128)S(1)}, f32[4,640]{1,0:T(4,128)S(1)}, u32[]{:S(2)}, u32[]{:S(2)}) %collective-permute-start.8) | collective-permute-done | bytes 10272 | tf_op jit(solution)/shard_map/ppermute | solution.py:196
  38.5 0.8 %finish.1 = f32[4,512]{1,0:T(4,128)} custom-call(f32[4,640]{1,0:T(4,128)S(1)} %get-tuple-element.23.kept, f32[4,640]{1,0:T(4,128)S(1)} %collective-permute-done.8.came), custom_call_target="tpu_custom_call" | custom-call | tf_op jit(solution)/shard_map/finish/pallas_call | solution.py:172
  (3 shorter events, 0.0 us)
Async XLA Ops:
  0.0 13.5 %copy-start = (bf16[64,4096]{1,0:T(8,128)(2,1)S(1)}, bf16[64,4096]{1,0:T(8,128)(2,1)}, u32[]{:S(2)}) copy-start(bf16[64,4096]{1,0:T(8,128)(2,1)} %param.11) | copy-start | bytes 1572868
  0.0 0.7 %copy-start.1 = (s32[16]{0:T(128)S(1)}, s32[16]{0:T(128)}, u32[]{:S(2)}) copy-start(s32[16]{0:T(128)} %lens_in.1) | copy-start | bytes 196
  13.0 5.8 %collective-permute-start = (bf16[2,128,128]{2,1,0:T(8,128)(2,1)S(1)}, bf16[2,128,128]{2,1,0:T(8,128)(2,1)S(1)}, u32[]{:S(2)}, u32[]{:S(2)}) collective-permute-start(bf16[2,128,128]{2,1,0:T(8,128)(2,1)S(1)} %get-tuple-element.16), channel_id=1, source_target_pairs={{0,1},{1,0},{2,3},{3,2},{4,5},{5,4},{6,7},{7,6},{8,9},{9,8},{10,11... | collective-permute-start | bytes 196616 | tf_op jit(solution)/shard_map/ppermute | solution.py:196
  13.5 11.2 %collective-permute-start.2 = (bf16[64,1024]{1,0:T(8,128)(2,1)S(1)}, bf16[64,1024]{1,0:T(8,128)(2,1)S(1)}, u32[]{:S(2)}, u32[]{:S(2)}) collective-permute-start(bf16[64,1024]{1,0:T(8,128)(2,1)S(1)} %constant_dynamic-slice_fusion.refs_0_), channel_id=1, source_target_pairs={{0,8},{4,12},{8,0},{12,4},{16,24},{20,28},{24,16},{28,20},{1,9},{5... | collective-permute-start | bytes 393224 | tf_op jit(solution)/shard_map/ppermute | solution.py:199
  16.2 12.9 %collective-permute-start.3 = (bf16[64,1024]{1,0:T(8,128)(2,1)S(1)}, bf16[64,1024]{1,0:T(8,128)(2,1)S(1)}, u32[]{:S(2)}, u32[]{:S(2)}) collective-permute-start(bf16[64,1024]{1,0:T(8,128)(2,1)S(1)} %constant_dynamic-slice_fusion.refs_0_), channel_id=1, source_target_pairs={{0,16},{4,20},{8,24},{12,28},{16,0},{20,4},{24,8},{28,12},{1,17},{... | collective-permute-start | bytes 393224 | tf_op jit(solution)/shard_map/ppermute | solution.py:199
  18.8 10.3 %collective-permute-start.4 = (bf16[64,1024]{1,0:T(8,128)(2,1)S(1)}, bf16[64,1024]{1,0:T(8,128)(2,1)S(1)}, u32[]{:S(2)}, u32[]{:S(2)}) collective-permute-start(bf16[64,1024]{1,0:T(8,128)(2,1)S(1)} %constant_dynamic-slice_fusion.refs_0_), channel_id=1, source_target_pairs={{0,24},{4,28},{8,16},{12,20},{16,8},{20,12},{24,0},{28,4},{1,25},{... | collective-permute-start | bytes 393224 | tf_op jit(solution)/shard_map/ppermute | solution.py:199
  18.8 4.0 %collective-permute-start.1 = (bf16[128,128]{1,0:T(8,128)(2,1)S(1)}, bf16[128,128]{1,0:T(8,128)(2,1)S(1)}, u32[]{:S(2)}, u32[]{:S(2)}) collective-permute-start(bf16[128,128]{1,0:T(8,128)(2,1)S(1)} %get-tuple-element.18), channel_id=1, source_target_pairs={{0,2},{1,3},{2,0},{3,1},{4,6},{5,7},{6,4},{7,5},{8,10},{9,11},{10,... | collective-permute-start | bytes 98312 | tf_op jit(solution)/shard_map/ppermute | solution.py:196
  22.9 6.2 %collective-permute-start.5 = (bf16[16,1024]{1,0:T(8,128)(2,1)S(1)}, bf16[16,1024]{1,0:T(8,128)(2,1)S(1)}, u32[]{:S(2)}, u32[]{:S(2)}) collective-permute-start(bf16[16,1024]{1,0:T(8,128)(2,1)S(1)} %get-tuple-element.19.left), channel_id=1, source_target_pairs={{0,4},{4,0},{8,12},{12,8},{16,20},{20,16},{24,28},{28,24},{1,5},{5... | collective-permute-start | bytes 98312 | tf_op jit(solution)/shard_map/ppermute | solution.py:199
  29.4 3.8 %collective-permute-start.6 = (f32[16,256]{1,0:T(8,128)S(1)}, f32[16,256]{1,0:T(8,128)S(1)}, u32[]{:S(2)}, u32[]{:S(2)}) collective-permute-start(f32[16,256]{1,0:T(8,128)S(1)} %other_scores.1), channel_id=1, source_target_pairs={{0,4},{4,0},{8,12},{12,8},{16,20},{20,16},{24,28},{28,24},{1,5},{5... | collective-permute-start | bytes 49160 | tf_op jit(solution)/shard_map/ppermute | solution.py:199
  33.5 3.8 %collective-permute-start.7 = (f32[2,4,640]{2,1,0:T(4,128)S(1)}, f32[2,4,640]{2,1,0:T(4,128)S(1)}, u32[]{:S(2)}, u32[]{:S(2)}) collective-permute-start(f32[2,4,640]{2,1,0:T(4,128)S(1)} %get-tuple-element.22), channel_id=1, source_target_pairs={{0,2},{1,3},{2,0},{3,1},{4,6},{5,7},{6,4},{7,5},{8,10},{9,11},{10,... | collective-permute-start | bytes 61448 | tf_op jit(solution)/shard_map/ppermute | solution.py:196
  37.4 1.2 %collective-permute-start.8 = (f32[4,640]{1,0:T(4,128)S(1)}, f32[4,640]{1,0:T(4,128)S(1)}, u32[]{:S(2)}, u32[]{:S(2)}) collective-permute-start(f32[4,640]{1,0:T(4,128)S(1)} %get-tuple-element.24), channel_id=1, source_target_pairs={{0,1},{1,0},{2,3},{3,2},{4,5},{5,4},{6,7},{7,6},{8,9},{9,8},{10,11... | collective-permute-start | bytes 30728 | tf_op jit(solution)/shard_map/ppermute | solution.py:196

commit v5 on v4

--- a/solution.py
+++ b/solution.py
@@ -11,65 +11,29 @@
 F32 = jnp.float32
 BF16 = jnp.bfloat16
 VMEM = pl.BlockSpec(memory_space=pltpu.VMEM)
-HBM = pl.BlockSpec(memory_space=pltpu.HBM)
+SMEM = pl.BlockSpec(memory_space=pltpu.SMEM)
 BY_ROWS = (((1,), (1,)), ((), ()))
 
 
-def grads_kernel(dims, lens_in, acts, out_grads, w_in, w_out, send, keep, *rest):
+def grads_kernel(dims, lens, xp_in, gp_in, send, keep, store):
     cands, tokens, width, groups = dims
-    act_buf, grad_buf, win_raw, wout_raw, win_buf, wout_buf, lens, store, sems, wsems = rest
     half = cands // 2
-    chunks = half // 2
     rows = 4 * tokens
-    load_lens = pltpu.make_async_copy(lens_in, lens, wsems.at[2])
-    load_w = [
-        pltpu.make_async_copy(w_out, wout_raw, wsems.at[0]),
-        pltpu.make_async_copy(w_in, win_raw, wsems.at[1]),
-    ]
-    loads = []
-    for i in range(chunks):
-        for side, (source, buf) in enumerate(((out_grads, grad_buf), (acts, act_buf))):
-            loads.append(
-                [
-                    pltpu.make_async_copy(
-                        source.at[pl.ds((2 * i + h * half) * tokens, rows // 2)],
-                        buf.at[pl.ds(i * rows + h * (rows // 2), rows // 2)],
-                        sems.at[side, 2 * i + h],
-                    )
-                    for h in range(2)
-                ]
-            )
-    load_w[0].start()
-    load_w[1].start()
-    load_lens.start()
-    for pair in loads:
-        for load in pair:
-            load.start()
     grp = lax.axis_index("grp")
     lines = width // groups
     position = lax.broadcasted_iota(jnp.int32, (tokens, width), 0) + grp * tokens
     row_blk = lax.broadcasted_iota(jnp.int32, (rows, rows), 0) // tokens
     col_blk = lax.broadcasted_iota(jnp.int32, (rows, 4 * width), 1) // width
     diagonal = row_blk == col_blk // 2 + 2 * (col_blk % 2)
-    load_w[0].wait()
-    wout_buf[...] = wout_raw[...].T
-    load_w[1].wait()
-    load_lens.wait()
-    for i in range(chunks):
-        part = pl.ds(i * rows, rows)
-        for load in loads[2 * i]:
-            load.wait()
-        gp = jnp.dot(grad_buf[part, :], wout_buf[...], preferred_element_type=F32)
-        if i == 0:
-            win_buf[...] = win_raw[...].T
-        left = gp.T.astype(BF16)
-        for load in loads[2 * i + 1]:
-            load.wait()
-        xp = jnp.dot(act_buf[part, :], win_buf[...], preferred_element_type=F32)
-        used = []
-        for j in range(4):
-            cand = 2 * i + j % 2 + (j // 2) * half
-            used.append(jnp.where(position < lens[cand], xp[j * tokens : (j + 1) * tokens], 0.0))
+    for i in range(half // 2):
+        members = [2 * i, 2 * i + 1, 2 * i + half, 2 * i + 1 + half]
+        parts = [slice(cand * tokens, (cand + 2) * tokens) for cand in members[::2]]
+        left = jnp.concatenate([gp_in[:, part] for part in parts], axis=1)
+        xp = jnp.concatenate([xp_in[:, part].astype(F32).T for part in parts], axis=0)
+        used = [
+            jnp.where(position < lens[cand], xp[j * tokens : (j + 1) * tokens], 0.0)
+            for j, cand in enumerate(members)
+        ]
         wide = jnp.concatenate([jnp.concatenate(used, axis=0)] * 4, axis=1)
         right = jnp.where(diagonal, wide, 0.0).astype(BF16)
         blocks = jnp.dot(left, right, preferred_element_type=F32)
@@ -85,7 +49,8 @@
         keep[x] = store[2 * x + core]
 
 
-def fold_kernel(keep, came, send, kept):
+def fold_kernel(keep, came, *rest):
+    send, kept = rest[-2:]
     x = lax.axis_index("grp") // 2
     send[...] = (keep[1 - x] + came[1 - x].astype(F32)).astype(BF16)
     kept[...] = keep[x] + came[x].astype(F32)
@@ -167,12 +132,12 @@
     out[...] = jnp.concatenate(columns, axis=1)
 
 
-def small(kernel, out_shape, operands, scratch_shapes=(), name=None):
+def small(kernel, out_shape, operands, scratch_shapes=(), name=None, first=VMEM):
     one = not isinstance(out_shape, list)
     return pl.pallas_call(
         kernel,
         out_shape=out_shape,
-        in_specs=[VMEM] * len(operands),
+        in_specs=[first] + [VMEM] * (len(operands) - 1),
         out_specs=VMEM if one else [VMEM] * len(out_shape),
         scratch_shapes=list(scratch_shapes),
         compiler_params=pltpu.CompilerParams(vmem_limit_bytes=16 * 2**20),
@@ -203,37 +168,21 @@
 
     rows = cands * tokens
     piece = (cands // 2 * lines, 128)
-    send, keep = pl.pallas_call(
+    gp = jnp.dot(out_grads.reshape(rows, depth), proj_out[0], preferred_element_type=F32).astype(BF16)
+    xp = jnp.dot(acts.reshape(rows, depth), proj_in[0], preferred_element_type=F32).astype(BF16)
+    send, keep = small(
         functools.partial(grads_kernel, (cands, tokens, width, groups)),
-        out_shape=[shape((groups // 2,) + piece, BF16), shape((groups // 2,) + piece, F32)],
-        in_specs=[HBM] * 5,
-        out_specs=[VMEM] * 2,
-        scratch_shapes=[
-            pltpu.VMEM((rows, depth), BF16),
-            pltpu.VMEM((rows, depth), BF16),
-            pltpu.VMEM((width, depth), BF16),
-            pltpu.VMEM((width, depth), BF16),
-            pltpu.VMEM((depth, width), BF16),
-            pltpu.VMEM((depth, width), BF16),
-            pltpu.SMEM((cands,), jnp.int32),
-            pltpu.VMEM((groups,) + piece, F32),
-            pltpu.SemaphoreType.DMA((2, cands // 2)),
-            pltpu.SemaphoreType.DMA((3,)),
-        ],
-        compiler_params=pltpu.CompilerParams(vmem_limit_bytes=54784 * 2**10),
-        cost_estimate=pl.CostEstimate(
-            flops=16 * rows * depth * width, bytes_accessed=8 * rows * depth, transcendentals=0
-        ),
+        [shape((groups // 2,) + piece, BF16), shape((groups // 2,) + piece, F32)],
+        (lengths, xp.T, gp.T),
+        [pltpu.VMEM((groups,) + piece, F32)],
         name="grads",
-    )(
-        lengths,
-        acts.reshape(rows, depth),
-        out_grads.reshape(rows, depth),
-        proj_in.reshape(depth, width).T,
-        proj_out.reshape(depth, width).T,
+        first=SMEM,
     )
     send, kept = small(
-        fold_kernel, [shape(piece, BF16), shape(piece, F32)], (keep, grp_swap(send, 1)), name="fold"
+        fold_kernel,
+        [shape(piece, BF16), shape(piece, F32)],
+        (keep, grp_swap(send, 1), *gathered),
+        name="fold",
     )
     own, squares = small(
         functools.partial(combine_kernel, (cands // 2, lines, width)),

time: 39.4 us -> 36.6 us (0.929)
  Pallas kernels: 13.8 us -> 2.58 us
  matrix products: 0 us -> 8.89 us
  waiting for transfers between devices: 12.3 us -> 11.2 us
    pallas_call x7, Pallas kernels: 13.8 us -> 2.58 us  [small(): pl.pallas_call(kernel, out_shape=out_shape, in_specs=[first] + [VMEM] * (...]
    dot_general x0 -> x2, matrix products: none -> 8.89 us  [the longest x1 6.23 us: on_device(): jnp.dot(acts.reshape(rows, depth), proj_in[0], preferred_element_type=F32)]
    ppermute x5, waiting for transfers between devices: 6.61 us -> 4.34 us  [blk_swap(): return lax.ppermute(x, 'blk', [(b, b ^ k) for b in range(blks)])]
    ppermute x4, waiting for transfers between devices: 5.66 us -> 6.84 us  [grp_swap(): return lax.ppermute(x, 'grp', [(g, g ^ k) for g in range(groups)])]
    ppermute x5, starting transfers between devices: 8.61 us -> 9.16 us  [blk_swap(): return lax.ppermute(x, 'blk', [(b, b ^ k) for b in range(blks)])]
    unnamed x4 -> x8, local copies, waits for them, and re-layouts: 0.72 us -> 1.05 us
  transfers between devices with their start and end apart: 9 -> 9, of which waited for: 5 -> 6; matrix products, arithmetic and copies ran while one was open for 0% -> 24% of each run, Pallas kernels for 0% -> 3%
where the time goes in v5:
time: 36.6 us; the launch traced here: 36.4 us
  starting transfers between devices  12.6 us (34%)
  waiting for transfers between devices  11.2 us (31%)
  matrix products  8.89 us (24%)
  Pallas kernels  2.58 us (7%)
  local copies, waits for them, and re-layouts  1.06 us (3%)
    ppermute x5, starting transfers between devices, blk_swap(): return lax.ppermute(x, 'blk', [(b, b ^ k) for b in range(blks)])  9.16 us
    ppermute x4, waiting for transfers between devices, grp_swap(): return lax.ppermute(x, 'grp', [(g, g ^ k) for g in range(groups)])  6.84 us
    dot_general x1, matrix products, on_device(): jnp.dot(acts.reshape(rows, depth), proj_in[0], preferred_element_type=F32)  6.23 us
    ppermute x5, waiting for transfers between devices, blk_swap(): return lax.ppermute(x, 'blk', [(b, b ^ k) for b in range(blks)])  4.34 us
    ppermute x4, starting transfers between devices, grp_swap(): return lax.ppermute(x, 'grp', [(g, g ^ k) for g in range(groups)])  3.47 us
    dot_general x1, matrix products, on_device(): jnp.dot(out_grads.reshape(rows, depth), proj_out[0], preferred_element_ty...  2.66 us
    pallas_call x7, Pallas kernels, small(): pl.pallas_call(kernel, out_shape=out_shape, in_specs=[first] + [VMEM] * (...  2.58 us
    unnamed x8, local copies, waits for them, and re-layouts  1.05 us
  transfers between devices with their start and end apart: 9, of which 6 were waited for; matrix products, arithmetic and copies ran while one was open for 24% of the time, Pallas kernels for 3%

profile of v5, /device:TPU:0, one launch (start us, length us, event | category | flops | bytes accessed | tf_op | source)
XLA Modules:
  0.0 36.4 jit_solution(6764422545057811739)
XLA Ops:
  0.0 0.0 copy-start
  0.0 0.0 copy-start.3
  0.0 1.0 %copy-done = bf16[64,4096]{1,0:T(8,128)(2,1)S(1)} copy-done((bf16[64,4096]{1,0:T(8,128)(2,1)S(1)}, bf16[64,4096]{1,0:T(8,128)(2,1)}, u32[]{:S(2)}) %copy-start) | copy-done | bytes 524312
  1.0 0.0 copy-start.2
  1.1 5.1 %collective-permute-start.3 = (bf16[64,1024]{1,0:T(8,128)(2,1)S(1)}, bf16[64,1024]{1,0:T(8,128)(2,1)S(1)}, u32[]{:S(2)}, u32[]{:S(2)}) collective-permute-start(bf16[64,1024]{1,0:T(8,128)(2,1)S(1)} %constant_dynamic-slice_fusion.rest_0_.refs_0_), channel_id=1, source_target_pairs={{0,24},{4,28},{8,16},{12,20},{16,8},{20,12},{24,0},{28,4},{1,25},{... | collective-permute-start | bytes 393224 | tf_op jit(solution)/shard_map/ppermute | solution.py:164
  6.2 0.0 collective-permute-start.2
  6.2 0.6 %collective-permute-start.1 = (bf16[64,1024]{1,0:T(8,128)(2,1)S(1)}, bf16[64,1024]{1,0:T(8,128)(2,1)S(1)}, u32[]{:S(2)}, u32[]{:S(2)}) collective-permute-start(bf16[64,1024]{1,0:T(8,128)(2,1)S(1)} %constant_dynamic-slice_fusion.rest_0_.refs_0_), channel_id=1, source_target_pairs={{0,8},{4,12},{8,0},{12,4},{16,24},{20,28},{24,16},{28,20},{1,9},{5... | collective-permute-start | bytes 393224 | tf_op jit(solution)/shard_map/ppermute | solution.py:164
  6.8 6.2 %convolution_convert_fusion.1.xp_in = bf16[64,1024]{1,0:T(8,128)(2,1)S(1)} fusion(bf16[1024,4096]{1,0:T(8,128)(2,1)} %bitcast.10, bf16[1,4096,64]{1,2,0:T(8,128)(2,1)} %param.8), kind=kOutput, calls=%fused_computation.1 | convolution fusion | flops 536936448 | bytes 9043968 | tf_op jit(solution)/shard_map/dot_general | solution.py:172
  13.0 0.0 copy-done.3
  13.1 0.0 copy-done.2
  13.1 2.7 %convolution_convert_fusion.gp_in = bf16[64,1024]{1,0:T(8,128)(2,1)S(1)} fusion(bf16[1024,4096]{1,0:T(8,128)(2,1)S(1)} %bitcast.11, bf16[1,4096,64]{1,2,0:T(8,128)(2,1)S(1)} %copy-done.3), kind=kOutput, calls=%fused_computation | convolution fusion | flops 536936448 | bytes 9043968 | tf_op jit(solution)/shard_map/dot_general | solution.py:171
  15.7 0.0 copy-done.1
  15.7 1.0 %grads.1 = (bf16[2,128,128]{2,1,0:T(8,128)(2,1)S(1)}, f32[2,128,128]{2,1,0:T(8,128)S(1)}) custom-call(s32[16]{0:T(128)S(1)} %copy-done.1, bf16[64,1024]{1,0:T(8,128)(2,1)S(1)} %convolution_convert_fusion.1.xp_in, bf16[64,1024]{1,0:T(8,128)(2,1)S(1)} %convolution_convert_fusion.gp_in), custom_call_target="tpu_custom_call" | custom-call | tf_op jit(solution)/shard_map/grads/pallas_call | solution.py:137
  16.8 0.1 collective-permute-start
  16.9 1.2 %collective-permute-done.came = bf16[2,128,128]{2,1,0:T(8,128)(2,1)S(1)} collective-permute-done((bf16[2,128,128]{2,1,0:T(8,128)(2,1)S(1)}, bf16[2,128,128]{2,1,0:T(8,128)(2,1)S(1)}, u32[]{:S(2)}, u32[]{:S(2)}) %collective-permute-start) | collective-permute-done | bytes 65568 | tf_op jit(solution)/shard_map/ppermute | solution.py:161
  18.1 0.0 collective-permute-done.3.rest_3_.refs_3_
  18.1 0.0 collective-permute-done.2.rest_2_.refs_2_
  18.1 0.0 collective-permute-done.1.rest_1_.refs_1_
  18.1 1.7 %collective-permute-start.4 = (bf16[128,128]{1,0:T(8,128)(2,1)S(1)}, bf16[128,128]{1,0:T(8,128)(2,1)S(1)}, u32[]{:S(2)}, u32[]{:S(2)}) collective-permute-start(bf16[128,128]{1,0:T(8,128)(2,1)S(1)} %get-tuple-element.18), channel_id=1, source_target_pairs={{0,2},{1,3},{2,0},{3,1},{4,6},{5,7},{6,4},{7,5},{8,10},{9,11},{10,... | collective-permute-start | bytes 98312 | tf_op jit(solution)/shard_map/ppermute | solution.py:161
  19.8 2.3 %collective-permute-done.4.came = bf16[128,128]{1,0:T(8,128)(2,1)S(1)} collective-permute-done((bf16[128,128]{1,0:T(8,128)(2,1)S(1)}, bf16[128,128]{1,0:T(8,128)(2,1)S(1)}, u32[]{:S(2)}, u32[]{:S(2)}) %collective-permute-start.4) | collective-permute-done | bytes 32800 | tf_op jit(solution)/shard_map/ppermute | solution.py:161
  22.1 0.1 combine.1
  22.2 1.7 %collective-permute-start.5 = (bf16[16,1024]{1,0:T(8,128)(2,1)S(1)}, bf16[16,1024]{1,0:T(8,128)(2,1)S(1)}, u32[]{:S(2)}, u32[]{:S(2)}) collective-permute-start(bf16[16,1024]{1,0:T(8,128)(2,1)S(1)} %get-tuple-element.19.left), channel_id=1, source_target_pairs={{0,4},{4,0},{8,12},{12,8},{16,20},{20,16},{24,28},{28,24},{1,5},{5... | collective-permute-start | bytes 98312 | tf_op jit(solution)/shard_map/ppermute | solution.py:164
  24.0 2.3 %collective-permute-done.5.left = bf16[16,1024]{1,0:T(8,128)(2,1)S(1)} collective-permute-done((bf16[16,1024]{1,0:T(8,128)(2,1)S(1)}, bf16[16,1024]{1,0:T(8,128)(2,1)S(1)}, u32[]{:S(2)}, u32[]{:S(2)}) %collective-permute-start.5) | collective-permute-done | bytes 32800 | tf_op jit(solution)/shard_map/ppermute | solution.py:164
  26.2 0.3 other_scores.1
  26.5 1.7 %collective-permute-start.6 = (f32[16,256]{1,0:T(8,128)S(1)}, f32[16,256]{1,0:T(8,128)S(1)}, u32[]{:S(2)}, u32[]{:S(2)}) collective-permute-start(f32[16,256]{1,0:T(8,128)S(1)} %other_scores.1), channel_id=1, source_target_pairs={{0,4},{4,0},{8,12},{12,8},{16,20},{20,16},{24,28},{28,24},{1,5},{5... | collective-permute-start | bytes 49160 | tf_op jit(solution)/shard_map/ppermute | solution.py:164
  28.2 2.1 %collective-permute-done.6.refs_4_ = f32[16,256]{1,0:T(8,128)S(1)} collective-permute-done((f32[16,256]{1,0:T(8,128)S(1)}, f32[16,256]{1,0:T(8,128)S(1)}, u32[]{:S(2)}, u32[]{:S(2)}) %collective-permute-start.6) | collective-permute-done | bytes 16416 | tf_op jit(solution)/shard_map/ppermute | solution.py:164
  30.3 0.3 own_scores.1
  30.6 1.7 %collective-permute-start.7 = (f32[2,4,640]{2,1,0:T(4,128)S(1)}, f32[2,4,640]{2,1,0:T(4,128)S(1)}, u32[]{:S(2)}, u32[]{:S(2)}) collective-permute-start(f32[2,4,640]{2,1,0:T(4,128)S(1)} %get-tuple-element.22), channel_id=1, source_target_pairs={{0,2},{1,3},{2,0},{3,1},{4,6},{5,7},{6,4},{7,5},{8,10},{9,11},{10,... | collective-permute-start | bytes 61448 | tf_op jit(solution)/shard_map/ppermute | solution.py:161
  32.3 2.1 %collective-permute-done.7.came = f32[2,4,640]{2,1,0:T(4,128)S(1)} collective-permute-done((f32[2,4,640]{2,1,0:T(4,128)S(1)}, f32[2,4,640]{2,1,0:T(4,128)S(1)}, u32[]{:S(2)}, u32[]{:S(2)}) %collective-permute-start.7) | collective-permute-done | bytes 20512 | tf_op jit(solution)/shard_map/ppermute | solution.py:161
  34.5 0.0 collective-permute-start.8
  34.5 1.2 %collective-permute-done.8.came = f32[4,640]{1,0:T(4,128)S(1)} collective-permute-done((f32[4,640]{1,0:T(4,128)S(1)}, f32[4,640]{1,0:T(4,128)S(1)}, u32[]{:S(2)}, u32[]{:S(2)}) %collective-permute-start.8) | collective-permute-done | bytes 10272 | tf_op jit(solution)/shard_map/ppermute | solution.py:161
  35.6 0.8 %finish.1 = f32[4,512]{1,0:T(4,128)} custom-call(f32[4,640]{1,0:T(4,128)S(1)} %get-tuple-element.23.kept, f32[4,640]{1,0:T(4,128)S(1)} %collective-permute-done.8.came), custom_call_target="tpu_custom_call" | custom-call | tf_op jit(solution)/shard_map/finish/pallas_call | solution.py:137
  (4 shorter events, 0.0 us)
Async XLA Ops:
  0.0 1.0 %copy-start = (bf16[64,4096]{1,0:T(8,128)(2,1)S(1)}, bf16[64,4096]{1,0:T(8,128)(2,1)}, u32[]{:S(2)}) copy-start(bf16[64,4096]{1,0:T(8,128)(2,1)} %param.11) | copy-start | bytes 1572868
  0.0 13.0 %copy-start.3 = (bf16[1,4096,64]{1,2,0:T(8,128)(2,1)S(1)}, bf16[1,4096,64]{1,2,0:T(8,128)(2,1)}, u32[]{:S(2)}) copy-start(bf16[1,4096,64]{1,2,0:T(8,128)(2,1)} %param.9) | copy-start | bytes 1572868
  1.0 12.0 %copy-start.2 = (bf16[1,16,64,4096]{3,2,1,0:T(8,128)(2,1)S(1)}, bf16[1,16,64,4096]{3,2,1,0:T(8,128)(2,1)}, u32[]{:S(2)}) copy-start(bf16[1,16,64,4096]{3,2,1,0:T(8,128)(2,1)} %param.7) | copy-start | bytes 25165828
  1.1 17.0 %collective-permute-start.3 = (bf16[64,1024]{1,0:T(8,128)(2,1)S(1)}, bf16[64,1024]{1,0:T(8,128)(2,1)S(1)}, u32[]{:S(2)}, u32[]{:S(2)}) collective-permute-start(bf16[64,1024]{1,0:T(8,128)(2,1)S(1)} %constant_dynamic-slice_fusion.rest_0_.refs_0_), channel_id=1, source_target_pairs={{0,24},{4,28},{8,16},{12,20},{16,8},{20,12},{24,0},{28,4},{1,25},{... | collective-permute-start | bytes 393224 | tf_op jit(solution)/shard_map/ppermute | solution.py:164
  6.2 11.9 %collective-permute-start.2 = (bf16[64,1024]{1,0:T(8,128)(2,1)S(1)}, bf16[64,1024]{1,0:T(8,128)(2,1)S(1)}, u32[]{:S(2)}, u32[]{:S(2)}) collective-permute-start(bf16[64,1024]{1,0:T(8,128)(2,1)S(1)} %constant_dynamic-slice_fusion.rest_0_.refs_0_), channel_id=1, source_target_pairs={{0,16},{4,20},{8,24},{12,28},{16,0},{20,4},{24,8},{28,12},{1,17},{... | collective-permute-start | bytes 393224 | tf_op jit(solution)/shard_map/ppermute | solution.py:164
  6.2 11.9 %collective-permute-start.1 = (bf16[64,1024]{1,0:T(8,128)(2,1)S(1)}, bf16[64,1024]{1,0:T(8,128)(2,1)S(1)}, u32[]{:S(2)}, u32[]{:S(2)}) collective-permute-start(bf16[64,1024]{1,0:T(8,128)(2,1)S(1)} %constant_dynamic-slice_fusion.rest_0_.refs_0_), channel_id=1, source_target_pairs={{0,8},{4,12},{8,0},{12,4},{16,24},{20,28},{24,16},{28,20},{1,9},{5... | collective-permute-start | bytes 393224 | tf_op jit(solution)/shard_map/ppermute | solution.py:164
  6.8 8.9 %copy-start.1 = (s32[16]{0:T(128)S(1)}, s32[16]{0:T(128)}, u32[]{:S(2)}) copy-start(s32[16]{0:T(128)} %lens.1) | copy-start | bytes 196
  16.8 1.3 %collective-permute-start = (bf16[2,128,128]{2,1,0:T(8,128)(2,1)S(1)}, bf16[2,128,128]{2,1,0:T(8,128)(2,1)S(1)}, u32[]{:S(2)}, u32[]{:S(2)}) collective-permute-start(bf16[2,128,128]{2,1,0:T(8,128)(2,1)S(1)} %get-tuple-element.16), channel_id=1, source_target_pairs={{0,1},{1,0},{2,3},{3,2},{4,5},{5,4},{6,7},{7,6},{8,9},{9,8},{10,11... | collective-permute-start | bytes 196616 | tf_op jit(solution)/shard_map/ppermute | solution.py:161
  18.1 4.0 %collective-permute-start.4 = (bf16[128,128]{1,0:T(8,128)(2,1)S(1)}, bf16[128,128]{1,0:T(8,128)(2,1)S(1)}, u32[]{:S(2)}, u32[]{:S(2)}) collective-permute-start(bf16[128,128]{1,0:T(8,128)(2,1)S(1)} %get-tuple-element.18), channel_id=1, source_target_pairs={{0,2},{1,3},{2,0},{3,1},{4,6},{5,7},{6,4},{7,5},{8,10},{9,11},{10,... | collective-permute-start | bytes 98312 | tf_op jit(solution)/shard_map/ppermute | solution.py:161
  22.2 4.0 %collective-permute-start.5 = (bf16[16,1024]{1,0:T(8,128)(2,1)S(1)}, bf16[16,1024]{1,0:T(8,128)(2,1)S(1)}, u32[]{:S(2)}, u32[]{:S(2)}) collective-permute-start(bf16[16,1024]{1,0:T(8,128)(2,1)S(1)} %get-tuple-element.19.left), channel_id=1, source_target_pairs={{0,4},{4,0},{8,12},{12,8},{16,20},{20,16},{24,28},{28,24},{1,5},{5... | collective-permute-start | bytes 98312 | tf_op jit(solution)/shard_map/ppermute | solution.py:164
  26.5 3.8 %collective-permute-start.6 = (f32[16,256]{1,0:T(8,128)S(1)}, f32[16,256]{1,0:T(8,128)S(1)}, u32[]{:S(2)}, u32[]{:S(2)}) collective-permute-start(f32[16,256]{1,0:T(8,128)S(1)} %other_scores.1), channel_id=1, source_target_pairs={{0,4},{4,0},{8,12},{12,8},{16,20},{20,16},{24,28},{28,24},{1,5},{5... | collective-permute-start | bytes 49160 | tf_op jit(solution)/shard_map/ppermute | solution.py:164
  30.6 3.8 %collective-permute-start.7 = (f32[2,4,640]{2,1,0:T(4,128)S(1)}, f32[2,4,640]{2,1,0:T(4,128)S(1)}, u32[]{:S(2)}, u32[]{:S(2)}) collective-permute-start(f32[2,4,640]{2,1,0:T(4,128)S(1)} %get-tuple-element.22), channel_id=1, source_target_pairs={{0,2},{1,3},{2,0},{3,1},{4,6},{5,7},{6,4},{7,5},{8,10},{9,11},{10,... | collective-permute-start | bytes 61448 | tf_op jit(solution)/shard_map/ppermute | solution.py:161
  34.5 1.2 %collective-permute-start.8 = (f32[4,640]{1,0:T(4,128)S(1)}, f32[4,640]{1,0:T(4,128)S(1)}, u32[]{:S(2)}, u32[]{:S(2)}) collective-permute-start(f32[4,640]{1,0:T(4,128)S(1)} %get-tuple-element.24), channel_id=1, source_target_pairs={{0,1},{1,0},{2,3},{3,2},{4,5},{5,4},{6,7},{7,6},{8,9},{9,8},{10,11... | collective-permute-start | bytes 30728 | tf_op jit(solution)/shard_map/ppermute | solution.py:161

commit v6 on v5

--- a/solution.py
+++ b/solution.py
@@ -15,13 +15,20 @@
 BY_ROWS = (((1,), (1,)), ((), ()))
 
 
-def grads_kernel(dims, lens, xp_in, gp_in, send, keep, store):
-    cands, tokens, width, groups = dims
+def cut_kernel(queries, out, sem):
+    part = out.shape[1]
+    column = pl.multiple_of((lax.axis_index("grp") // 2) * part, part)
+    load = pltpu.make_async_copy(queries.at[:, pl.ds(column, part)], out, sem)
+    load.start()
+    load.wait()
+
+
+def grads_kernel(dims, lens, xp_in, gp_in, send, keep):
+    cands, tokens, width, slices = dims
     half = cands // 2
     rows = 4 * tokens
-    grp = lax.axis_index("grp")
-    lines = width // groups
-    position = lax.broadcasted_iota(jnp.int32, (tokens, width), 0) + grp * tokens
+    lines = width // slices
+    position = lax.broadcasted_iota(jnp.int32, (tokens, width), 0) + lax.axis_index("grp") * tokens
     row_blk = lax.broadcasted_iota(jnp.int32, (rows, rows), 0) // tokens
     col_blk = lax.broadcasted_iota(jnp.int32, (rows, 4 * width), 1) // width
     diagonal = row_blk == col_blk // 2 + 2 * (col_blk % 2)
@@ -38,15 +45,11 @@
         right = jnp.where(diagonal, wide, 0.0).astype(BF16)
         blocks = jnp.dot(left, right, preferred_element_type=F32)
         for t in range(2):
-            pair = 2 * i + t
-            for s in range(groups):
-                store[s, pair * lines : (pair + 1) * lines, :] = blocks[
-                    s * lines : (s + 1) * lines, t * 128 : (t + 1) * 128
-                ]
-    core = lax.rem(grp, 2)
-    for x in range(groups // 2):
-        send[x] = store[2 * x + 1 - core].astype(BF16)
-        keep[x] = store[2 * x + core]
+            here = slice((2 * i + t) * lines, (2 * i + t + 1) * lines)
+            for s in range(slices):
+                block = blocks[s * lines : (s + 1) * lines, t * 128 : (t + 1) * 128]
+                keep[s, here, :] = block
+                send[s, here, :] = block.astype(BF16)
 
 
 def fold_kernel(keep, came, *rest):
@@ -92,7 +95,7 @@
 
 
 def own_kernel(dims, left, squares, *refs):
-    far, groups = dims
+    far, slices = dims
     queries = refs[:far]
     other, send, keep, place, result = refs[far:]
     own = near_scores(left[...], queries, place)
@@ -101,35 +104,31 @@
     even = jnp.where(is_even, own, back)
     odd = jnp.where(is_even, back, own)
     half = own.shape[1]
-    owned = own.shape[0] // groups
-    for g in range(groups):
-        here = slice(g * owned, (g + 1) * owned)
-        result[g, :, :half] = even[here]
-        result[g, :, half : 2 * half] = odd[here]
-        result[g, :, 2 * half :] = squares[here, :]
+    owned = own.shape[0] // slices
+    for s in range(slices):
+        here = slice(s * owned, (s + 1) * owned)
+        result[s, :, :half] = even[here]
+        result[s, :, half : 2 * half] = odd[here]
+        result[s, :, 2 * half :] = squares[here, :]
     x = lax.axis_index("grp") // 2
-    for core in range(2):
-        send[core] = result[2 * (1 - x) + core]
-        keep[core] = result[2 * x + core]
-
-
-def pass_kernel(keep, came, send, kept):
-    core = lax.rem(lax.axis_index("grp"), 2)
-    send[...] = keep[1 - core] + came[1 - core]
-    kept[...] = keep[core] + came[core]
-
-
-def finish_kernel(dims, kept, came, out):
+    send[...] = result[1 - x]
+    keep[...] = result[x]
+
+
+def scale_kernel(dims, kept, came, first, second):
     pdim, nq = dims
     total = kept[...] + came[...]
-    width = out.shape[1]
+    width = first.shape[1]
     mean = jnp.sum(total[:, width:], axis=1, keepdims=True) / pdim
     scaled = total[:, :width] * lax.rsqrt(mean + EPS)
     columns = []
     for start in range(0, width // 2, nq):
         columns.append(scaled[:, start : start + nq])
         columns.append(scaled[:, width // 2 + start : width // 2 + start + nq])
-    out[...] = jnp.concatenate(columns, axis=1)
+    rows = jnp.concatenate(columns, axis=1)
+    owned = first.shape[0]
+    first[...] = rows[:owned]
+    second[...] = rows[owned:]
 
 
 def small(kernel, out_shape, operands, scratch_shapes=(), name=None, first=VMEM):
@@ -149,45 +148,54 @@
     _, cands, tokens, depth = acts.shape
     width = proj_in.shape[2]
     far = blks // 2
+    slices = groups // 2
     pdim = width * width
-    lines = width // groups
+    lines = width // slices
     nq = queries.shape[0]
     total_q = nq * blks
     owned = cands // groups
-    slice_width = pdim // groups
+    slice_width = pdim // slices
     shape = jax.ShapeDtypeStruct
 
-    def grp_swap(x, k):
-        return lax.ppermute(x, "grp", [(g, g ^ k) for g in range(groups)])
-
-    def blk_swap(x, k):
-        return lax.ppermute(x, "blk", [(b, b ^ k) for b in range(blks)])
-
-    cut = lax.dynamic_slice(queries, (0, lax.axis_index("grp") * slice_width), (nq, slice_width))
-    gathered = [cut] + [blk_swap(cut, 2 * k) for k in range(1, far)]
+    def lead_swap(x, blk_flip, grp_flip):
+        pairs = [
+            (b * groups + g, (b ^ blk_flip) * groups + (g ^ grp_flip))
+            for b in range(blks)
+            for g in range(1, groups, 2)
+        ]
+        return lax.ppermute(x, ("blk", "grp"), pairs)
+
+    cut = pl.pallas_call(
+        cut_kernel,
+        out_shape=shape((nq, slice_width), BF16),
+        in_specs=[pl.BlockSpec(memory_space=pl.ANY)],
+        out_specs=VMEM,
+        scratch_shapes=[pltpu.SemaphoreType.DMA],
+        compiler_params=pltpu.CompilerParams(vmem_limit_bytes=4 * 2**20),
+        cost_estimate=pl.CostEstimate(flops=0, bytes_accessed=64 * 2**20, transcendentals=0),
+        name="cut",
+    )(queries)
+    gathered = [cut] + [lead_swap(cut, 2 * k, 0) for k in range(1, far)]
 
     rows = cands * tokens
     piece = (cands // 2 * lines, 128)
     gp = jnp.dot(out_grads.reshape(rows, depth), proj_out[0], preferred_element_type=F32).astype(BF16)
     xp = jnp.dot(acts.reshape(rows, depth), proj_in[0], preferred_element_type=F32).astype(BF16)
     send, keep = small(
-        functools.partial(grads_kernel, (cands, tokens, width, groups)),
-        [shape((groups // 2,) + piece, BF16), shape((groups // 2,) + piece, F32)],
+        functools.partial(grads_kernel, (cands, tokens, width, slices)),
+        [shape((slices,) + piece, BF16), shape((slices,) + piece, F32)],
         (lengths, xp.T, gp.T),
-        [pltpu.VMEM((groups,) + piece, F32)],
         name="grads",
         first=SMEM,
     )
+    came = lax.ppermute(send, "grp", [(g, g + 1) for g in range(0, groups, 2)])
     send, kept = small(
-        fold_kernel,
-        [shape(piece, BF16), shape(piece, F32)],
-        (keep, grp_swap(send, 1), *gathered),
-        name="fold",
+        fold_kernel, [shape(piece, BF16), shape(piece, F32)], (keep, came, *gathered), name="fold"
     )
     own, squares = small(
         functools.partial(combine_kernel, (cands // 2, lines, width)),
         [shape((cands, slice_width), BF16), shape((cands, 128), F32)],
-        (kept, grp_swap(send, 2)),
+        (kept, lead_swap(send, 0, 2)),
         [pltpu.VMEM(piece, F32)],
         name="combine",
     )
@@ -195,25 +203,26 @@
     back = small(
         functools.partial(other_kernel, far),
         shape((cands, total_q // 2), F32),
-        (blk_swap(own, 1), *gathered),
+        (lead_swap(own, 1, 0), *gathered),
         [place],
         name="other_scores",
     )
-    line = (owned, total_q + 128)
+    line = (cands // slices, total_q + 128)
     send, keep = small(
-        functools.partial(own_kernel, (far, groups)),
-        [shape((groups // 2,) + line, F32)] * 2,
-        (own, squares, *gathered, blk_swap(back, 1)),
-        [place, pltpu.VMEM((groups,) + line, F32)],
+        functools.partial(own_kernel, (far, slices)),
+        [shape(line, F32)] * 2,
+        (own, squares, *gathered, lead_swap(back, 1, 0)),
+        [place, pltpu.VMEM((slices,) + line, F32)],
         name="own_scores",
     )
-    send, kept = small(pass_kernel, [shape(line, F32)] * 2, (keep, grp_swap(send, 2)), name="pass")
-    return small(
-        functools.partial(finish_kernel, (pdim, nq)),
-        shape((owned, total_q), F32),
-        (kept, grp_swap(send, 1)),
-        name="finish",
-    )
+    first, second = small(
+        functools.partial(scale_kernel, (pdim, nq)),
+        [shape((owned, total_q), F32)] * 2,
+        (keep, lead_swap(send, 0, 2)),
+        name="scale",
+    )
+    came = lax.ppermute(first, "grp", [(g + 1, g) for g in range(0, groups, 2)])
+    return jnp.where(lax.rem(lax.axis_index("grp"), 2) == 0, came, second)
 
 
 def solution(mesh):

time: 36.6 us -> 48.4 us (1.32)
  waiting for transfers between devices: 11.2 us -> 18.3 us
  starting transfers between devices: 12.6 us -> 16.9 us
  other arithmetic: 0 us -> 0.6 us
    ppermute x9, waiting for transfers between devices: 11.2 us -> 18.3 us  [the longest x1 17.3 us: on_device(): came = lax.ppermute(first, 'grp', [(g + 1, g) for g in range(0, groups, 2)])]
    ppermute x9, starting transfers between devices: 12.6 us -> 16.9 us  [the longest x1 10.5 us: on_device(): came = lax.ppermute(send, 'grp', [(g, g + 1) for g in range(0, groups, 2)])]
    select_n x0 -> x1, other arithmetic: none -> 0.6 us  [on_device(): return jnp.where(lax.rem(lax.axis_index('grp'), 2) == 0, came, second)]
    pallas_call x7 -> x6, Pallas kernels: 2.58 us -> 2.26 us  [small(): pl.pallas_call(kernel, out_shape=out_shape, in_specs=[first] + [VMEM] * (...]
    unnamed x8 -> x10, local copies, waits for them, and re-layouts: 1.05 us -> 1.12 us
  transfers between devices with their start and end apart: 9 -> 9, of which waited for: 6 -> 2; matrix products, arithmetic and copies ran while one was open for 24% -> 18% of each run, Pallas kernels for 3% -> 2%
where the time goes in v6:
time: 48.4 us; the launch traced here: 48.1 us
  waiting for transfers between devices  18.3 us (38%)
  starting transfers between devices  16.9 us (35%)
  matrix products  8.73 us (18%)
  Pallas kernels  2.29 us (5%)
  local copies, waits for them, and re-layouts  1.12 us (2%)
  other arithmetic  0.6 us (1%)
    ppermute x1, waiting for transfers between devices, on_device(): came = lax.ppermute(first, 'grp', [(g + 1, g) for g in range(0, groups, 2)])  17.3 us
    ppermute x1, starting transfers between devices, on_device(): came = lax.ppermute(send, 'grp', [(g, g + 1) for g in range(0, groups, 2)])  10.5 us
    dot_general x1, matrix products, on_device(): jnp.dot(acts.reshape(rows, depth), proj_in[0], preferred_element_type=F32)  6.07 us
    ppermute x7, starting transfers between devices, lead_swap(): return lax.ppermute(x, ('blk', 'grp'), pairs)  5.09 us
    dot_general x1, matrix products, on_device(): jnp.dot(out_grads.reshape(rows, depth), proj_out[0], preferred_element_ty...  2.66 us
    pallas_call x6, Pallas kernels, small(): pl.pallas_call(kernel, out_shape=out_shape, in_specs=[first] + [VMEM] * (...  2.26 us
    ppermute x1, starting transfers between devices, on_device(): came = lax.ppermute(first, 'grp', [(g + 1, g) for g in range(0, groups, 2)])  1.29 us
    unnamed x10, local copies, waits for them, and re-layouts  1.12 us
  transfers between devices with their start and end apart: 9, of which 2 were waited for; matrix products, arithmetic and copies ran while one was open for 18% of the time, Pallas kernels for 2%

profile of v6, /device:TPU:0, one launch (start us, length us, event | category | flops | bytes accessed | tf_op | source)
XLA Modules:
  0.0 48.1 jit_solution(5126361359448715992)
XLA Ops:
  0.0 0.0 copy-start
  0.0 1.1 %copy-done.1 = bf16[64,4096]{1,0:T(8,128)(2,1)S(1)} copy-done((bf16[64,4096]{1,0:T(8,128)(2,1)S(1)}, bf16[64,4096]{1,0:T(8,128)(2,1)}, u32[]{:S(2)}) %copy-start.1) | copy-done | bytes 524312
  1.1 0.8 %collective-permute-start.1 = (bf16[64,2048]{1,0:T(8,128)(2,1)S(1)}, bf16[64,2048]{1,0:T(8,128)(2,1)S(1)}, u32[]{:S(2)}, u32[]{:S(2)}) collective-permute-start(bf16[64,2048]{1,0:T(8,128)(2,1)S(1)} %cut.1.rest_0_.refs_0_), channel_id=1, source_target_pairs={{1,9},{3,11},{5,13},{7,15},{9,1},{11,3},{13,5},{15,7},{17,25},{19,... | collective-permute-start | bytes 786440 | tf_op jit(solution)/shard_map/ppermute | solution.py:166
  2.0 0.8 %collective-permute-start.2 = (bf16[64,2048]{1,0:T(8,128)(2,1)S(1)}, bf16[64,2048]{1,0:T(8,128)(2,1)S(1)}, u32[]{:S(2)}, u32[]{:S(2)}) collective-permute-start(bf16[64,2048]{1,0:T(8,128)(2,1)S(1)} %cut.1.rest_0_.refs_0_), channel_id=1, source_target_pairs={{1,17},{3,19},{5,21},{7,23},{9,25},{11,27},{13,29},{15,31},{17,1},... | collective-permute-start | bytes 786440 | tf_op jit(solution)/shard_map/ppermute | solution.py:166
  2.8 0.8 %collective-permute-start.3 = (bf16[64,2048]{1,0:T(8,128)(2,1)S(1)}, bf16[64,2048]{1,0:T(8,128)(2,1)S(1)}, u32[]{:S(2)}, u32[]{:S(2)}) collective-permute-start(bf16[64,2048]{1,0:T(8,128)(2,1)S(1)} %cut.1.rest_0_.refs_0_), channel_id=1, source_target_pairs={{1,25},{3,27},{5,29},{7,31},{9,17},{11,19},{13,21},{15,23},{17,9},... | collective-permute-start | bytes 786440 | tf_op jit(solution)/shard_map/ppermute | solution.py:166
  3.6 0.0 copy-done
  3.6 0.0 copy-start.2
  3.6 6.1 %convolution_convert_fusion.1.xp_in = bf16[64,1024]{1,0:T(8,128)(2,1)S(1)} fusion(bf16[1024,4096]{1,0:T(8,128)(2,1)} %bitcast.10, bf16[1,4096,64]{1,2,0:T(8,128)(2,1)S(1)} %copy-done), kind=kOutput, calls=%fused_computation.1 | convolution fusion | flops 536936448 | bytes 9043968 | tf_op jit(solution)/shard_map/dot_general | solution.py:183
  9.7 0.0 copy-done.3
  9.7 0.0 copy-done.4
  9.7 2.7 %convolution_convert_fusion.gp_in = bf16[64,1024]{1,0:T(8,128)(2,1)S(1)} fusion(bf16[1024,4096]{1,0:T(8,128)(2,1)S(1)} %bitcast.11, bf16[1,4096,64]{1,2,0:T(8,128)(2,1)S(1)} %copy-done.4), kind=kOutput, calls=%fused_computation | convolution fusion | flops 536936448 | bytes 9043968 | tf_op jit(solution)/shard_map/dot_general | solution.py:182
  12.4 1.0 %grads.1 = (bf16[2,256,128]{2,1,0:T(8,128)(2,1)S(1)}, f32[2,256,128]{2,1,0:T(8,128)S(1)}) custom-call(s32[16]{0:T(128)S(1)} %copy-done.2, bf16[64,1024]{1,0:T(8,128)(2,1)S(1)} %convolution_convert_fusion.1.xp_in, bf16[64,1024]{1,0:T(8,128)(2,1)S(1)} %convolution_convert_fusion.gp_in), custom_call_target="tpu_custom_call" | custom-call | tf_op jit(solution)/shard_map/grads/pallas_call | solution.py:136
  13.4 10.5 %collective-permute-start = (bf16[2,256,128]{2,1,0:T(8,128)(2,1)S(1)}, bf16[2,256,128]{2,1,0:T(8,128)(2,1)S(1)}, u32[]{:S(2)}, u32[]{:S(2)}) collective-permute-start(bf16[2,256,128]{2,1,0:T(8,128)(2,1)S(1)} %get-tuple-element.16), channel_id=1, source_target_pairs={{0,1},{2,3},{4,5},{6,7},{8,9},{10,11},{12,13},{14,15},{16,17},{18,... | collective-permute-start | bytes 393224 | tf_op jit(solution)/shard_map/ppermute | solution.py:191
  23.9 1.0 %collective-permute-done.came = bf16[2,256,128]{2,1,0:T(8,128)(2,1)S(1)} collective-permute-done((bf16[2,256,128]{2,1,0:T(8,128)(2,1)S(1)}, bf16[2,256,128]{2,1,0:T(8,128)(2,1)S(1)}, u32[]{:S(2)}, u32[]{:S(2)}) %collective-permute-start) | collective-permute-done | bytes 131104 | tf_op jit(solution)/shard_map/ppermute | solution.py:191
  24.8 0.0 collective-permute-done.1.rest_1_.refs_1_
  24.8 0.0 collective-permute-done.2.rest_2_.refs_2_
  24.8 0.0 collective-permute-done.3.rest_3_.refs_3_
  24.9 0.7 %collective-permute-start.4 = (bf16[256,128]{1,0:T(8,128)(2,1)S(1)}, bf16[256,128]{1,0:T(8,128)(2,1)S(1)}, u32[]{:S(2)}, u32[]{:S(2)}) collective-permute-start(bf16[256,128]{1,0:T(8,128)(2,1)S(1)} %get-tuple-element.18), channel_id=1, source_target_pairs={{1,3},{3,1},{5,7},{7,5},{9,11},{11,9},{13,15},{15,13},{17,19},{19,... | collective-permute-start | bytes 196616 | tf_op jit(solution)/shard_map/ppermute | solution.py:166
  25.6 0.0 collective-permute-done.4.came
  25.6 0.2 combine.1
  25.7 0.7 %collective-permute-start.5 = (bf16[16,2048]{1,0:T(8,128)(2,1)S(1)}, bf16[16,2048]{1,0:T(8,128)(2,1)S(1)}, u32[]{:S(2)}, u32[]{:S(2)}) collective-permute-start(bf16[16,2048]{1,0:T(8,128)(2,1)S(1)} %get-tuple-element.19.left), channel_id=1, source_target_pairs={{1,5},{3,7},{5,1},{7,3},{9,13},{11,15},{13,9},{15,11},{17,21},{19,... | collective-permute-start | bytes 196616 | tf_op jit(solution)/shard_map/ppermute | solution.py:166
  26.4 0.0 collective-permute-done.5.left
  26.4 0.5 other_scores.1
  26.9 0.7 %collective-permute-start.6 = (f32[16,256]{1,0:T(8,128)S(1)}, f32[16,256]{1,0:T(8,128)S(1)}, u32[]{:S(2)}, u32[]{:S(2)}) collective-permute-start(f32[16,256]{1,0:T(8,128)S(1)} %other_scores.1), channel_id=1, source_target_pairs={{1,5},{3,7},{5,1},{7,3},{9,13},{11,15},{13,9},{15,11},{17,21},{19,... | collective-permute-start | bytes 49160 | tf_op jit(solution)/shard_map/ppermute | solution.py:166
  27.5 0.0 collective-permute-done.6.refs_4_
  27.6 0.5 own_scores.1
  28.0 0.7 %collective-permute-start.7 = (f32[8,640]{1,0:T(8,128)S(1)}, f32[8,640]{1,0:T(8,128)S(1)}, u32[]{:S(2)}, u32[]{:S(2)}) collective-permute-start(f32[8,640]{1,0:T(8,128)S(1)} %get-tuple-element.22), channel_id=1, source_target_pairs={{1,3},{3,1},{5,7},{7,5},{9,11},{11,9},{13,15},{15,13},{17,19},{19,... | collective-permute-start | bytes 61448 | tf_op jit(solution)/shard_map/ppermute | solution.py:166
  28.7 0.0 collective-permute-done.7.came
  28.7 0.2 scale.1
  28.9 1.3 %collective-permute-start.8 = (f32[4,512]{1,0:T(4,128)S(1)}, f32[4,512]{1,0:T(4,128)S(1)}, u32[]{:S(2)}, u32[]{:S(2)}) collective-permute-start(f32[4,512]{1,0:T(4,128)S(1)} %get-tuple-element.23), channel_id=1, source_target_pairs={{1,0},{3,2},{5,4},{7,6},{9,8},{11,10},{13,12},{15,14},{17,16},{19,... | collective-permute-start | bytes 24584 | tf_op jit(solution)/shard_map/ppermute | solution.py:224
  30.2 17.3 %collective-permute-done.8 = f32[4,512]{1,0:T(4,128)S(1)} collective-permute-done((f32[4,512]{1,0:T(4,128)S(1)}, f32[4,512]{1,0:T(4,128)S(1)}, u32[]{:S(2)}, u32[]{:S(2)}) %collective-permute-start.8) | collective-permute-done | bytes 8224 | tf_op jit(solution)/shard_map/ppermute | solution.py:224
  47.5 0.6 %broadcast_select_fusion = f32[4,512]{1,0:T(4,128)} fusion(f32[4,512]{1,0:T(4,128)S(1)} %collective-permute-done.8, f32[4,512]{1,0:T(4,128)S(1)} %get-tuple-element.24, pred[]{:T(512)S(6)} %eq.3), kind=kLoop, calls=%fused_computation.4 | loop fusion | flops 2048 | bytes 24577 | tf_op jit(solution)/shard_map/jit(_where)/select_n | solution.py:225
  (6 shorter events, 0.1 us)
Async XLA Ops:
  0.0 3.6 %copy-start = (bf16[1,4096,64]{1,2,0:T(8,128)(2,1)S(1)}, bf16[1,4096,64]{1,2,0:T(8,128)(2,1)}, u32[]{:S(2)}) copy-start(bf16[1,4096,64]{1,2,0:T(8,128)(2,1)} %param.8) | copy-start | bytes 1572868
  0.0 1.1 %copy-start.1 = (bf16[64,4096]{1,0:T(8,128)(2,1)S(1)}, bf16[64,4096]{1,0:T(8,128)(2,1)}, u32[]{:S(2)}) copy-start(bf16[64,4096]{1,0:T(8,128)(2,1)} %queries.1) | copy-start | bytes 1572868
  1.1 8.6 %copy-start.3 = (bf16[1,16,64,4096]{3,2,1,0:T(8,128)(2,1)S(1)}, bf16[1,16,64,4096]{3,2,1,0:T(8,128)(2,1)}, u32[]{:S(2)}) copy-start(bf16[1,16,64,4096]{3,2,1,0:T(8,128)(2,1)} %param.7) | copy-start | bytes 25165828
  1.1 8.6 %copy-start.4 = (bf16[1,4096,64]{1,2,0:T(8,128)(2,1)S(1)}, bf16[1,4096,64]{1,2,0:T(8,128)(2,1)}, u32[]{:S(2)}) copy-start(bf16[1,4096,64]{1,2,0:T(8,128)(2,1)} %param.9) | copy-start | bytes 1572868
  1.1 23.7 %collective-permute-start.1 = (bf16[64,2048]{1,0:T(8,128)(2,1)S(1)}, bf16[64,2048]{1,0:T(8,128)(2,1)S(1)}, u32[]{:S(2)}, u32[]{:S(2)}) collective-permute-start(bf16[64,2048]{1,0:T(8,128)(2,1)S(1)} %cut.1.rest_0_.refs_0_), channel_id=1, source_target_pairs={{1,9},{3,11},{5,13},{7,15},{9,1},{11,3},{13,5},{15,7},{17,25},{19,... | collective-permute-start | bytes 786440 | tf_op jit(solution)/shard_map/ppermute | solution.py:166
  2.0 22.9 %collective-permute-start.2 = (bf16[64,2048]{1,0:T(8,128)(2,1)S(1)}, bf16[64,2048]{1,0:T(8,128)(2,1)S(1)}, u32[]{:S(2)}, u32[]{:S(2)}) collective-permute-start(bf16[64,2048]{1,0:T(8,128)(2,1)S(1)} %cut.1.rest_0_.refs_0_), channel_id=1, source_target_pairs={{1,17},{3,19},{5,21},{7,23},{9,25},{11,27},{13,29},{15,31},{17,1},... | collective-permute-start | bytes 786440 | tf_op jit(solution)/shard_map/ppermute | solution.py:166
  2.8 22.1 %collective-permute-start.3 = (bf16[64,2048]{1,0:T(8,128)(2,1)S(1)}, bf16[64,2048]{1,0:T(8,128)(2,1)S(1)}, u32[]{:S(2)}, u32[]{:S(2)}) collective-permute-start(bf16[64,2048]{1,0:T(8,128)(2,1)S(1)} %cut.1.rest_0_.refs_0_), channel_id=1, source_target_pairs={{1,25},{3,27},{5,29},{7,31},{9,17},{11,19},{13,21},{15,23},{17,9},... | collective-permute-start | bytes 786440 | tf_op jit(solution)/shard_map/ppermute | solution.py:166
  3.6 8.8 %copy-start.2 = (s32[16]{0:T(128)S(1)}, s32[16]{0:T(128)}, u32[]{:S(2)}) copy-start(s32[16]{0:T(128)} %lens.1) | copy-start | bytes 196
  13.4 11.5 %collective-permute-start = (bf16[2,256,128]{2,1,0:T(8,128)(2,1)S(1)}, bf16[2,256,128]{2,1,0:T(8,128)(2,1)S(1)}, u32[]{:S(2)}, u32[]{:S(2)}) collective-permute-start(bf16[2,256,128]{2,1,0:T(8,128)(2,1)S(1)} %get-tuple-element.16), channel_id=1, source_target_pairs={{0,1},{2,3},{4,5},{6,7},{8,9},{10,11},{12,13},{14,15},{16,17},{18,... | collective-permute-start | bytes 393224 | tf_op jit(solution)/shard_map/ppermute | solution.py:191
  24.9 0.7 %collective-permute-start.4 = (bf16[256,128]{1,0:T(8,128)(2,1)S(1)}, bf16[256,128]{1,0:T(8,128)(2,1)S(1)}, u32[]{:S(2)}, u32[]{:S(2)}) collective-permute-start(bf16[256,128]{1,0:T(8,128)(2,1)S(1)} %get-tuple-element.18), channel_id=1, source_target_pairs={{1,3},{3,1},{5,7},{7,5},{9,11},{11,9},{13,15},{15,13},{17,19},{19,... | collective-permute-start | bytes 196616 | tf_op jit(solution)/shard_map/ppermute | solution.py:166
  25.7 0.7 %collective-permute-start.5 = (bf16[16,2048]{1,0:T(8,128)(2,1)S(1)}, bf16[16,2048]{1,0:T(8,128)(2,1)S(1)}, u32[]{:S(2)}, u32[]{:S(2)}) collective-permute-start(bf16[16,2048]{1,0:T(8,128)(2,1)S(1)} %get-tuple-element.19.left), channel_id=1, source_target_pairs={{1,5},{3,7},{5,1},{7,3},{9,13},{11,15},{13,9},{15,11},{17,21},{19,... | collective-permute-start | bytes 196616 | tf_op jit(solution)/shard_map/ppermute | solution.py:166
  26.9 0.7 %collective-permute-start.6 = (f32[16,256]{1,0:T(8,128)S(1)}, f32[16,256]{1,0:T(8,128)S(1)}, u32[]{:S(2)}, u32[]{:S(2)}) collective-permute-start(f32[16,256]{1,0:T(8,128)S(1)} %other_scores.1), channel_id=1, source_target_pairs={{1,5},{3,7},{5,1},{7,3},{9,13},{11,15},{13,9},{15,11},{17,21},{19,... | collective-permute-start | bytes 49160 | tf_op jit(solution)/shard_map/ppermute | solution.py:166
  28.0 0.7 %collective-permute-start.7 = (f32[8,640]{1,0:T(8,128)S(1)}, f32[8,640]{1,0:T(8,128)S(1)}, u32[]{:S(2)}, u32[]{:S(2)}) collective-permute-start(f32[8,640]{1,0:T(8,128)S(1)} %get-tuple-element.22), channel_id=1, source_target_pairs={{1,3},{3,1},{5,7},{7,5},{9,11},{11,9},{13,15},{15,13},{17,19},{19,... | collective-permute-start | bytes 61448 | tf_op jit(solution)/shard_map/ppermute | solution.py:166
  28.9 18.6 %collective-permute-start.8 = (f32[4,512]{1,0:T(4,128)S(1)}, f32[4,512]{1,0:T(4,128)S(1)}, u32[]{:S(2)}, u32[]{:S(2)}) collective-permute-start(f32[4,512]{1,0:T(4,128)S(1)} %get-tuple-element.23), channel_id=1, source_target_pairs={{1,0},{3,2},{5,4},{7,6},{9,8},{11,10},{13,12},{15,14},{17,16},{19,... | collective-permute-start | bytes 24584 | tf_op jit(solution)/shard_map/ppermute | solution.py:224

commit v7 on v6

--- a/solution.py
+++ b/solution.py
@@ -8,10 +8,11 @@
 from jax.sharding import PartitionSpec as P
 
 EPS = 1e-06
+GRANT = 54784
 F32 = jnp.float32
 BF16 = jnp.bfloat16
 VMEM = pl.BlockSpec(memory_space=pltpu.VMEM)
-SMEM = pl.BlockSpec(memory_space=pltpu.SMEM)
+ANY = pl.BlockSpec(memory_space=pl.ANY)
 BY_ROWS = (((1,), (1,)), ((), ()))
 
 
@@ -23,33 +24,75 @@
     load.wait()
 
 
-def grads_kernel(dims, lens, xp_in, gp_in, send, keep):
+def grads_kernel(dims, lens_in, acts, grads, w_in, w_out, send, keep, *scratch):
     cands, tokens, width, slices = dims
+    act_buf, grad_buf, win_raw, wout_raw, win, wout, lens, sems, wsems = scratch
     half = cands // 2
+    chunks = half // 2
     rows = 4 * tokens
+    loads = []
+    for i in range(chunks):
+        for side, (source, buf) in enumerate(((grads, grad_buf), (acts, act_buf))):
+            loads.append(
+                [
+                    pltpu.make_async_copy(
+                        source.at[pl.ds((2 * i + h * half) * tokens, rows // 2)],
+                        buf.at[pl.ds(i * rows + h * (rows // 2), rows // 2)],
+                        sems.at[side, 2 * i + h],
+                    )
+                    for h in range(2)
+                ]
+            )
+
+    def start(n):
+        if n < len(loads):
+            for load in loads[n]:
+                load.start()
+
+    def wait(n):
+        for load in loads[n]:
+            load.wait()
+
+    load_lens = pltpu.make_async_copy(lens_in, lens, wsems.at[2])
+    load_wout = pltpu.make_async_copy(w_out, wout_raw, wsems.at[0])
+    load_win = pltpu.make_async_copy(w_in, win_raw, wsems.at[1])
+    load_wout.start()
+    load_win.start()
+    load_lens.start()
+    start(0)
+    start(1)
     lines = width // slices
     position = lax.broadcasted_iota(jnp.int32, (tokens, width), 0) + lax.axis_index("grp") * tokens
     row_blk = lax.broadcasted_iota(jnp.int32, (rows, rows), 0) // tokens
     col_blk = lax.broadcasted_iota(jnp.int32, (rows, 4 * width), 1) // width
     diagonal = row_blk == col_blk // 2 + 2 * (col_blk % 2)
-    for i in range(half // 2):
-        members = [2 * i, 2 * i + 1, 2 * i + half, 2 * i + 1 + half]
-        parts = [slice(cand * tokens, (cand + 2) * tokens) for cand in members[::2]]
-        left = jnp.concatenate([gp_in[:, part] for part in parts], axis=1)
-        xp = jnp.concatenate([xp_in[:, part].astype(F32).T for part in parts], axis=0)
-        used = [
-            jnp.where(position < lens[cand], xp[j * tokens : (j + 1) * tokens], 0.0)
-            for j, cand in enumerate(members)
-        ]
+    load_wout.wait()
+    wout[...] = wout_raw[...].T
+    load_win.wait()
+    win[...] = win_raw[...].T
+    load_lens.wait()
+    for i in range(chunks):
+        part = pl.ds(i * rows, rows)
+        wait(2 * i)
+        start(2 * i + 2)
+        gp = jnp.dot(grad_buf[part, :], wout[...], preferred_element_type=F32)
+        left = gp.T.astype(BF16)
+        wait(2 * i + 1)
+        start(2 * i + 3)
+        xp = jnp.dot(act_buf[part, :], win[...], preferred_element_type=F32)
+        used = []
+        for j in range(4):
+            cand = 2 * i + j % 2 + (j // 2) * half
+            used.append(jnp.where(position < lens[cand], xp[j * tokens : (j + 1) * tokens], 0.0))
         wide = jnp.concatenate([jnp.concatenate(used, axis=0)] * 4, axis=1)
         right = jnp.where(diagonal, wide, 0.0).astype(BF16)
-        blocks = jnp.dot(left, right, preferred_element_type=F32)
+        sums = jnp.dot(left, right, preferred_element_type=F32)
         for t in range(2):
-            here = slice((2 * i + t) * lines, (2 * i + t + 1) * lines)
+            there = slice((2 * i + t) * lines, (2 * i + t + 1) * lines)
             for s in range(slices):
-                block = blocks[s * lines : (s + 1) * lines, t * 128 : (t + 1) * 128]
-                keep[s, here, :] = block
-                send[s, here, :] = block.astype(BF16)
+                block = sums[s * lines : (s + 1) * lines, t * 128 : (t + 1) * 128]
+                keep[s, there, :] = block
+                send[s, there, :] = block.astype(BF16)
 
 
 def fold_kernel(keep, came, *rest):
@@ -131,12 +174,12 @@
     second[...] = rows[owned:]
 
 
-def small(kernel, out_shape, operands, scratch_shapes=(), name=None, first=VMEM):
+def small(kernel, out_shape, operands, scratch_shapes=(), name=None):
     one = not isinstance(out_shape, list)
     return pl.pallas_call(
         kernel,
         out_shape=out_shape,
-        in_specs=[first] + [VMEM] * (len(operands) - 1),
+        in_specs=[VMEM] * len(operands),
         out_specs=VMEM if one else [VMEM] * len(out_shape),
         scratch_shapes=list(scratch_shapes),
         compiler_params=pltpu.CompilerParams(vmem_limit_bytes=16 * 2**20),
@@ -159,36 +202,55 @@
 
     def lead_swap(x, blk_flip, grp_flip):
         pairs = [
-            (b * groups + g, (b ^ blk_flip) * groups + (g ^ grp_flip))
+            (b * groups + g, (b ^ blk_flip) * groups + (g ^ grp_flip) if g % 2 else b * groups + g)
             for b in range(blks)
-            for g in range(1, groups, 2)
+            for g in range(groups)
         ]
         return lax.ppermute(x, ("blk", "grp"), pairs)
 
     cut = pl.pallas_call(
         cut_kernel,
         out_shape=shape((nq, slice_width), BF16),
-        in_specs=[pl.BlockSpec(memory_space=pl.ANY)],
+        in_specs=[ANY],
         out_specs=VMEM,
         scratch_shapes=[pltpu.SemaphoreType.DMA],
         compiler_params=pltpu.CompilerParams(vmem_limit_bytes=4 * 2**20),
-        cost_estimate=pl.CostEstimate(flops=0, bytes_accessed=64 * 2**20, transcendentals=0),
+        cost_estimate=pl.CostEstimate(flops=0, bytes_accessed=2 * nq * slice_width * 2, transcendentals=0),
         name="cut",
     )(queries)
     gathered = [cut] + [lead_swap(cut, 2 * k, 0) for k in range(1, far)]
 
     rows = cands * tokens
     piece = (cands // 2 * lines, 128)
-    gp = jnp.dot(out_grads.reshape(rows, depth), proj_out[0], preferred_element_type=F32).astype(BF16)
-    xp = jnp.dot(acts.reshape(rows, depth), proj_in[0], preferred_element_type=F32).astype(BF16)
-    send, keep = small(
+    send, keep = pl.pallas_call(
         functools.partial(grads_kernel, (cands, tokens, width, slices)),
-        [shape((slices,) + piece, BF16), shape((slices,) + piece, F32)],
-        (lengths, xp.T, gp.T),
+        out_shape=[shape((slices,) + piece, BF16), shape((slices,) + piece, F32)],
+        in_specs=[ANY] * 5,
+        out_specs=[VMEM] * 2,
+        scratch_shapes=[
+            pltpu.VMEM((rows, depth), BF16),
+            pltpu.VMEM((rows, depth), BF16),
+            pltpu.VMEM((width, depth), BF16),
+            pltpu.VMEM((width, depth), BF16),
+            pltpu.VMEM((depth, width), BF16),
+            pltpu.VMEM((depth, width), BF16),
+            pltpu.SMEM((cands,), jnp.int32),
+            pltpu.SemaphoreType.DMA((2, cands // 2)),
+            pltpu.SemaphoreType.DMA((3,)),
+        ],
+        compiler_params=pltpu.CompilerParams(vmem_limit_bytes=GRANT * 2**10),
+        cost_estimate=pl.CostEstimate(
+            flops=16 * rows * depth * width, bytes_accessed=4 * rows * depth, transcendentals=0
+        ),
         name="grads",
-        first=SMEM,
-    )
-    came = lax.ppermute(send, "grp", [(g, g + 1) for g in range(0, groups, 2)])
+    )(
+        lengths,
+        acts.reshape(rows, depth),
+        out_grads.reshape(rows, depth),
+        proj_in[0].T,
+        proj_out[0].T,
+    )
+    came = lax.ppermute(send, "grp", [(g, g ^ 1) for g in range(groups)])
     send, kept = small(
         fold_kernel, [shape(piece, BF16), shape(piece, F32)], (keep, came, *gathered), name="fold"
     )
@@ -221,7 +283,7 @@
         (keep, lead_swap(send, 0, 2)),
         name="scale",
     )
-    came = lax.ppermute(first, "grp", [(g + 1, g) for g in range(0, groups, 2)])
+    came = lax.ppermute(first, "grp", [(g, g ^ 1) for g in range(groups)])
     return jnp.where(lax.rem(lax.axis_index("grp"), 2) == 0, came, second)
 
 

time: 48.4 us -> 45 us (0.930)
  waiting for transfers between devices: 18.3 us -> 1.83 us
  starting transfers between devices: 16.9 us -> 30 us
  matrix products: 8.73 us -> 0 us
  Pallas kernels: 2.29 us -> 10.4 us
  local copies, waits for them, and re-layouts: 1.12 us -> 1.69 us
    ppermute x2, waiting for transfers between devices: 18.3 us -> 1.81 us  [the longest x1 0.99 us: on_device(): came = lax.ppermute(send, 'grp', [(g, g ^ 1) for g in range(groups)])]
    ppermute x2, starting transfers between devices: 11.8 us -> 25.3 us  [the longest x1 16.7 us: on_device(): came = lax.ppermute(first, 'grp', [(g, g ^ 1) for g in range(groups)])]
    dot_general x2 -> x0, matrix products: 8.73 us -> none  [the longest x1 6.07 us: on_device(): jnp.dot(acts.reshape(rows, depth), proj_in[0], preferred_element_type=F32)]
    pallas_call x6, Pallas kernels: 2.26 us -> 10.4 us  [the longest x1 9.1 us: on_device(): pl.pallas_call(functools.partial(grads_kernel, (cands, tokens, width, sli...]
    unnamed x10 -> x4, local copies, waits for them, and re-layouts: 1.12 us -> 1.69 us
  transfers between devices with their start and end apart: 9 -> 9, of which waited for: 2 -> 2; matrix products, arithmetic and copies ran while one was open for 18% -> 0% of each run, Pallas kernels for 2% -> 20%
where the time goes in v7:
time: 45 us; the launch traced here: 44.7 us
  starting transfers between devices  30 us (67%)
  Pallas kernels  10.4 us (23%)
  waiting for transfers between devices  1.83 us (4%)
  local copies, waits for them, and re-layouts  1.69 us (4%)
  other arithmetic  0.6 us (1%)
    ppermute x1, starting transfers between devices, on_device(): came = lax.ppermute(first, 'grp', [(g, g ^ 1) for g in range(groups)])  16.7 us
    pallas_call x1, Pallas kernels, on_device(): pl.pallas_call(functools.partial(grads_kernel, (cands, tokens, width, sli...  9.1 us
    ppermute x1, starting transfers between devices, on_device(): came = lax.ppermute(send, 'grp', [(g, g ^ 1) for g in range(groups)])  8.66 us
    ppermute x7, starting transfers between devices, lead_swap(): return lax.ppermute(x, ('blk', 'grp'), pairs)  4.7 us
    unnamed x4, local copies, waits for them, and re-layouts  1.69 us
    pallas_call x5, Pallas kernels, small(): pl.pallas_call(kernel, out_shape=out_shape, in_specs=[VMEM] * len(operand...  1.27 us
    ppermute x1, waiting for transfers between devices, on_device(): came = lax.ppermute(send, 'grp', [(g, g ^ 1) for g in range(groups)])  0.99 us
  transfers between devices with their start and end apart: 9, of which 2 were waited for; matrix products, arithmetic and copies ran while one was open for 0% of the time, Pallas kernels for 20%

profile of v7, /device:TPU:0, one launch (start us, length us, event | category | flops | bytes accessed | tf_op | source)
XLA Modules:
  0.0 44.7 jit_solution(16834703269371767943)
XLA Ops:
  0.0 0.0 copy-start
  0.0 1.0 %copy-done = bf16[64,4096]{1,0:T(8,128)(2,1)S(1)} copy-done((bf16[64,4096]{1,0:T(8,128)(2,1)S(1)}, bf16[64,4096]{1,0:T(8,128)(2,1)}, u32[]{:S(2)}) %copy-start) | copy-done | bytes 524312
  1.1 0.7 %collective-permute-start.1 = (bf16[64,2048]{1,0:T(8,128)(2,1)S(1)}, bf16[64,2048]{1,0:T(8,128)(2,1)S(1)}, u32[]{:S(2)}, u32[]{:S(2)}) collective-permute-start(bf16[64,2048]{1,0:T(8,128)(2,1)S(1)} %cut.1.rest_0_.refs_0_), channel_id=1, source_target_pairs={{0,0},{1,9},{2,2},{3,11},{4,4},{5,13},{6,6},{7,15},{8,8},{9,1},{10... | collective-permute-start | bytes 786440 | tf_op jit(solution)/shard_map/ppermute | solution.py:209
  1.8 0.7 %collective-permute-start.2 = (bf16[64,2048]{1,0:T(8,128)(2,1)S(1)}, bf16[64,2048]{1,0:T(8,128)(2,1)S(1)}, u32[]{:S(2)}, u32[]{:S(2)}) collective-permute-start(bf16[64,2048]{1,0:T(8,128)(2,1)S(1)} %cut.1.rest_0_.refs_0_), channel_id=1, source_target_pairs={{0,0},{1,17},{2,2},{3,19},{4,4},{5,21},{6,6},{7,23},{8,8},{9,25},{... | collective-permute-start | bytes 786440 | tf_op jit(solution)/shard_map/ppermute | solution.py:209
  2.4 0.7 %collective-permute-start.3 = (bf16[64,2048]{1,0:T(8,128)(2,1)S(1)}, bf16[64,2048]{1,0:T(8,128)(2,1)S(1)}, u32[]{:S(2)}, u32[]{:S(2)}) collective-permute-start(bf16[64,2048]{1,0:T(8,128)(2,1)S(1)} %cut.1.rest_0_.refs_0_), channel_id=1, source_target_pairs={{0,0},{1,25},{2,2},{3,27},{4,4},{5,29},{6,6},{7,31},{8,8},{9,17},{... | collective-permute-start | bytes 786440 | tf_op jit(solution)/shard_map/ppermute | solution.py:209
  3.1 0.0 copy-start.1
  3.1 0.6 %copy-done.1 = s32[16]{0:T(128)S(1)} copy-done((s32[16]{0:T(128)S(1)}, s32[16]{0:T(128)}, u32[]{:S(2)}) %copy-start.1) | copy-done | bytes 88
  3.8 9.1 %grads.1 = (bf16[2,256,128]{2,1,0:T(8,128)(2,1)S(1)}, f32[2,256,128]{2,1,0:T(8,128)S(1)}) custom-call(s32[16]{0:T(128)S(1)} %copy-done.1, bf16[1024,4096]{1,0:T(8,128)(2,1)} %bitcast.8, bf16[1024,4096]{1,0:T(8,128)(2,1)} %bitcast.9, bf16[64,4096]{1,0:T(8,128)(2,1)} %bitcast.10, bf16[64,4096]{1,0:T(8,128)(2,1)} %bitcast.11), custom_call_target="tpu_custom_call" | custom-call | flops 4294967296 | bytes 16777216 | tf_op jit(solution)/shard_map/grads/pallas_call | solution.py:225
  12.9 8.7 %collective-permute-start = (bf16[2,256,128]{2,1,0:T(8,128)(2,1)S(1)}, bf16[2,256,128]{2,1,0:T(8,128)(2,1)S(1)}, u32[]{:S(2)}, u32[]{:S(2)}) collective-permute-start(bf16[2,256,128]{2,1,0:T(8,128)(2,1)S(1)} %get-tuple-element.16), channel_id=1, source_target_pairs={{0,1},{1,0},{2,3},{3,2},{4,5},{5,4},{6,7},{7,6},{8,9},{9,8},{10,11... | collective-permute-start | bytes 393224 | tf_op jit(solution)/shard_map/ppermute | solution.py:253
  21.6 1.0 %collective-permute-done.came = bf16[2,256,128]{2,1,0:T(8,128)(2,1)S(1)} collective-permute-done((bf16[2,256,128]{2,1,0:T(8,128)(2,1)S(1)}, bf16[2,256,128]{2,1,0:T(8,128)(2,1)S(1)}, u32[]{:S(2)}, u32[]{:S(2)}) %collective-permute-start) | collective-permute-done | bytes 131104 | tf_op jit(solution)/shard_map/ppermute | solution.py:253
  22.5 0.0 collective-permute-done.1.rest_1_.refs_1_
  22.6 0.0 collective-permute-done.2.rest_2_.refs_2_
  22.6 0.0 collective-permute-done.3.rest_3_.refs_3_
  22.6 0.7 %collective-permute-start.4 = (bf16[256,128]{1,0:T(8,128)(2,1)S(1)}, bf16[256,128]{1,0:T(8,128)(2,1)S(1)}, u32[]{:S(2)}, u32[]{:S(2)}) collective-permute-start(bf16[256,128]{1,0:T(8,128)(2,1)S(1)} %get-tuple-element.18), channel_id=1, source_target_pairs={{0,0},{1,3},{2,2},{3,1},{4,4},{5,7},{6,6},{7,5},{8,8},{9,11},{10,1... | collective-permute-start | bytes 196616 | tf_op jit(solution)/shard_map/ppermute | solution.py:209
  23.3 0.0 collective-permute-done.4.came
  23.3 0.2 combine.1
  23.5 0.7 %collective-permute-start.5 = (bf16[16,2048]{1,0:T(8,128)(2,1)S(1)}, bf16[16,2048]{1,0:T(8,128)(2,1)S(1)}, u32[]{:S(2)}, u32[]{:S(2)}) collective-permute-start(bf16[16,2048]{1,0:T(8,128)(2,1)S(1)} %get-tuple-element.19.left), channel_id=1, source_target_pairs={{0,0},{1,5},{2,2},{3,7},{4,4},{5,1},{6,6},{7,3},{8,8},{9,13},{10,1... | collective-permute-start | bytes 196616 | tf_op jit(solution)/shard_map/ppermute | solution.py:209
  24.1 0.0 collective-permute-done.5.left
  24.1 0.5 %other_scores.1 = f32[16,256]{1,0:T(8,128)S(1)} custom-call(bf16[16,2048]{1,0:T(8,128)(2,1)S(1)} %collective-permute-done.5.left, bf16[64,2048]{1,0:T(8,128)(2,1)S(1)} %cut.1.rest_0_.refs_0_, bf16[64,2048]{1,0:T(8,128)(2,1)S(1)} %collective-permute-done.1.rest_1_.refs_1_, bf16[64,2048]{1,0:T(8,128)(2,1)S(1)} %collective-permute-done.2.rest_2_.refs_2_, ...), custom_call_target="tpu_custom_call" | custom-call | tf_op jit(solution)/shard_map/other_scores/pallas_call | solution.py:179
  24.6 0.7 %collective-permute-start.6 = (f32[16,256]{1,0:T(8,128)S(1)}, f32[16,256]{1,0:T(8,128)S(1)}, u32[]{:S(2)}, u32[]{:S(2)}) collective-permute-start(f32[16,256]{1,0:T(8,128)S(1)} %other_scores.1), channel_id=1, source_target_pairs={{0,0},{1,5},{2,2},{3,7},{4,4},{5,1},{6,6},{7,3},{8,8},{9,13},{10,1... | collective-permute-start | bytes 49160 | tf_op jit(solution)/shard_map/ppermute | solution.py:209
  25.3 0.0 collective-permute-done.6.refs_4_
  25.3 0.5 %own_scores.1 = (f32[8,640]{1,0:T(8,128)S(1)}, f32[8,640]{1,0:T(8,128)S(1)}) custom-call(bf16[16,2048]{1,0:T(8,128)(2,1)S(1)} %get-tuple-element.19.left, f32[16,128]{1,0:T(8,128)S(1)} %get-tuple-element.20.squares, bf16[64,2048]{1,0:T(8,128)(2,1)S(1)} %cut.1.rest_0_.refs_0_, bf16[64,2048]{1,0:T(8,128)(2,1)S(1)} %collective-permute-done.1.rest_1_.refs_1_, ...), custom_call_target="tpu_custom_call" | custom-call | tf_op jit(solution)/shard_map/own_scores/pallas_call | solution.py:179
  25.7 0.7 %collective-permute-start.7 = (f32[8,640]{1,0:T(8,128)S(1)}, f32[8,640]{1,0:T(8,128)S(1)}, u32[]{:S(2)}, u32[]{:S(2)}) collective-permute-start(f32[8,640]{1,0:T(8,128)S(1)} %get-tuple-element.22), channel_id=1, source_target_pairs={{0,0},{1,3},{2,2},{3,1},{4,4},{5,7},{6,6},{7,5},{8,8},{9,11},{10,1... | collective-permute-start | bytes 61448 | tf_op jit(solution)/shard_map/ppermute | solution.py:209
  26.4 0.0 collective-permute-done.7.came
  26.4 0.2 scale.1
  26.6 16.7 %collective-permute-start.8 = (f32[4,512]{1,0:T(4,128)S(1)}, f32[4,512]{1,0:T(4,128)S(1)}, u32[]{:S(2)}, u32[]{:S(2)}) collective-permute-start(f32[4,512]{1,0:T(4,128)S(1)} %get-tuple-element.23), channel_id=1, source_target_pairs={{0,1},{1,0},{2,3},{3,2},{4,5},{5,4},{6,7},{7,6},{8,9},{9,8},{10,11... | collective-permute-start | bytes 24584 | tf_op jit(solution)/shard_map/ppermute | solution.py:286
  43.2 0.8 %collective-permute-done.8 = f32[4,512]{1,0:T(4,128)S(1)} collective-permute-done((f32[4,512]{1,0:T(4,128)S(1)}, f32[4,512]{1,0:T(4,128)S(1)}, u32[]{:S(2)}, u32[]{:S(2)}) %collective-permute-start.8) | collective-permute-done | bytes 8224 | tf_op jit(solution)/shard_map/ppermute | solution.py:286
  44.1 0.6 %broadcast_select_fusion = f32[4,512]{1,0:T(4,128)} fusion(f32[4,512]{1,0:T(4,128)S(1)} %collective-permute-done.8, f32[4,512]{1,0:T(4,128)S(1)} %get-tuple-element.24, pred[]{:T(512)S(6)} %eq.3), kind=kLoop, calls=%fused_computation | loop fusion | flops 2048 | bytes 24577 | tf_op jit(solution)/shard_map/jit(_where)/select_n | solution.py:287
  (2 shorter events, 0.1 us)
Async XLA Ops:
  0.0 1.0 %copy-start = (bf16[64,4096]{1,0:T(8,128)(2,1)S(1)}, bf16[64,4096]{1,0:T(8,128)(2,1)}, u32[]{:S(2)}) copy-start(bf16[64,4096]{1,0:T(8,128)(2,1)} %queries.1) | copy-start | bytes 1572868
  1.1 21.5 %collective-permute-start.1 = (bf16[64,2048]{1,0:T(8,128)(2,1)S(1)}, bf16[64,2048]{1,0:T(8,128)(2,1)S(1)}, u32[]{:S(2)}, u32[]{:S(2)}) collective-permute-start(bf16[64,2048]{1,0:T(8,128)(2,1)S(1)} %cut.1.rest_0_.refs_0_), channel_id=1, source_target_pairs={{0,0},{1,9},{2,2},{3,11},{4,4},{5,13},{6,6},{7,15},{8,8},{9,1},{10... | collective-permute-start | bytes 786440 | tf_op jit(solution)/shard_map/ppermute | solution.py:209
  1.8 20.8 %collective-permute-start.2 = (bf16[64,2048]{1,0:T(8,128)(2,1)S(1)}, bf16[64,2048]{1,0:T(8,128)(2,1)S(1)}, u32[]{:S(2)}, u32[]{:S(2)}) collective-permute-start(bf16[64,2048]{1,0:T(8,128)(2,1)S(1)} %cut.1.rest_0_.refs_0_), channel_id=1, source_target_pairs={{0,0},{1,17},{2,2},{3,19},{4,4},{5,21},{6,6},{7,23},{8,8},{9,25},{... | collective-permute-start | bytes 786440 | tf_op jit(solution)/shard_map/ppermute | solution.py:209
  2.4 20.1 %collective-permute-start.3 = (bf16[64,2048]{1,0:T(8,128)(2,1)S(1)}, bf16[64,2048]{1,0:T(8,128)(2,1)S(1)}, u32[]{:S(2)}, u32[]{:S(2)}) collective-permute-start(bf16[64,2048]{1,0:T(8,128)(2,1)S(1)} %cut.1.rest_0_.refs_0_), channel_id=1, source_target_pairs={{0,0},{1,25},{2,2},{3,27},{4,4},{5,29},{6,6},{7,31},{8,8},{9,17},{... | collective-permute-start | bytes 786440 | tf_op jit(solution)/shard_map/ppermute | solution.py:209
  3.1 0.7 %copy-start.1 = (s32[16]{0:T(128)S(1)}, s32[16]{0:T(128)}, u32[]{:S(2)}) copy-start(s32[16]{0:T(128)} %lens_in.1) | copy-start | bytes 196
  12.9 9.6 %collective-permute-start = (bf16[2,256,128]{2,1,0:T(8,128)(2,1)S(1)}, bf16[2,256,128]{2,1,0:T(8,128)(2,1)S(1)}, u32[]{:S(2)}, u32[]{:S(2)}) collective-permute-start(bf16[2,256,128]{2,1,0:T(8,128)(2,1)S(1)} %get-tuple-element.16), channel_id=1, source_target_pairs={{0,1},{1,0},{2,3},{3,2},{4,5},{5,4},{6,7},{7,6},{8,9},{9,8},{10,11... | collective-permute-start | bytes 393224 | tf_op jit(solution)/shard_map/ppermute | solution.py:253
  22.6 0.7 %collective-permute-start.4 = (bf16[256,128]{1,0:T(8,128)(2,1)S(1)}, bf16[256,128]{1,0:T(8,128)(2,1)S(1)}, u32[]{:S(2)}, u32[]{:S(2)}) collective-permute-start(bf16[256,128]{1,0:T(8,128)(2,1)S(1)} %get-tuple-element.18), channel_id=1, source_target_pairs={{0,0},{1,3},{2,2},{3,1},{4,4},{5,7},{6,6},{7,5},{8,8},{9,11},{10,1... | collective-permute-start | bytes 196616 | tf_op jit(solution)/shard_map/ppermute | solution.py:209
  23.5 0.7 %collective-permute-start.5 = (bf16[16,2048]{1,0:T(8,128)(2,1)S(1)}, bf16[16,2048]{1,0:T(8,128)(2,1)S(1)}, u32[]{:S(2)}, u32[]{:S(2)}) collective-permute-start(bf16[16,2048]{1,0:T(8,128)(2,1)S(1)} %get-tuple-element.19.left), channel_id=1, source_target_pairs={{0,0},{1,5},{2,2},{3,7},{4,4},{5,1},{6,6},{7,3},{8,8},{9,13},{10,1... | collective-permute-start | bytes 196616 | tf_op jit(solution)/shard_map/ppermute | solution.py:209
  24.6 0.7 %collective-permute-start.6 = (f32[16,256]{1,0:T(8,128)S(1)}, f32[16,256]{1,0:T(8,128)S(1)}, u32[]{:S(2)}, u32[]{:S(2)}) collective-permute-start(f32[16,256]{1,0:T(8,128)S(1)} %other_scores.1), channel_id=1, source_target_pairs={{0,0},{1,5},{2,2},{3,7},{4,4},{5,1},{6,6},{7,3},{8,8},{9,13},{10,1... | collective-permute-start | bytes 49160 | tf_op jit(solution)/shard_map/ppermute | solution.py:209
  25.7 0.7 %collective-permute-start.7 = (f32[8,640]{1,0:T(8,128)S(1)}, f32[8,640]{1,0:T(8,128)S(1)}, u32[]{:S(2)}, u32[]{:S(2)}) collective-permute-start(f32[8,640]{1,0:T(8,128)S(1)} %get-tuple-element.22), channel_id=1, source_target_pairs={{0,0},{1,3},{2,2},{3,1},{4,4},{5,7},{6,6},{7,5},{8,8},{9,11},{10,1... | collective-permute-start | bytes 61448 | tf_op jit(solution)/shard_map/ppermute | solution.py:209
  26.6 17.5 %collective-permute-start.8 = (f32[4,512]{1,0:T(4,128)S(1)}, f32[4,512]{1,0:T(4,128)S(1)}, u32[]{:S(2)}, u32[]{:S(2)}) collective-permute-start(f32[4,512]{1,0:T(4,128)S(1)} %get-tuple-element.23), channel_id=1, source_target_pairs={{0,1},{1,0},{2,3},{3,2},{4,5},{5,4},{6,7},{7,6},{8,9},{9,8},{10,11... | collective-permute-start | bytes 24584 | tf_op jit(solution)/shard_map/ppermute | solution.py:286

commit v8 on v5

--- a/solution.py
+++ b/solution.py
@@ -56,8 +56,9 @@
     kept[...] = keep[x] + came[x].astype(F32)
 
 
-def combine_kernel(dims, kept, came, out, squares, grads):
+def combine_kernel(dims, kept, came, *rest):
     half, lines, width = dims
+    out, squares, grads = rest[-3:]
     grads[...] = kept[...] + came[...].astype(F32)
     low = lax.broadcasted_iota(jnp.int32, (half, 128), 1) < width
     sums, columns = None, []
@@ -77,36 +78,35 @@
     out[...] = jnp.concatenate(columns, axis=1)
 
 
-def near_scores(left, queries, place):
-    far = len(queries)
-    z = lax.axis_index("blk") // 2
-    for k in range(far):
-        place[jnp.bitwise_xor(z, k)] = lax.dot_general(
-            left, queries[k][...], BY_ROWS, preferred_element_type=F32
+def join_kernel(count, *refs):
+    out = refs[-1]
+    nq = refs[-2].shape[0]
+    for n, ref in enumerate(refs[-1 - count : -1]):
+        out[n * nq : (n + 1) * nq, :] = ref[...]
+
+
+def scores_kernel(dims, left, squares, *refs):
+    blks, groups = dims
+    pieces = refs[: blks // 2 + 2]
+    far, send, keep, place, result = refs[blks // 2 + 2 :]
+    rows = left[...]
+    blk = lax.axis_index("blk")
+    nq = pieces[0].shape[0]
+    table = {0: pieces[0], 1: pieces[1], 2: pieces[2], 3: pieces[3]}
+    for k in range(2, blks // 2):
+        table[2 * k] = pieces[k + 2]
+        table[2 * k + 1] = far.at[pl.ds((k - 2) * nq, nq)]
+    for flip, piece in table.items():
+        place[jnp.bitwise_xor(blk, flip)] = lax.dot_general(
+            rows, piece[...], BY_ROWS, preferred_element_type=F32
         )
-    return jnp.concatenate([place[k] for k in range(far)], axis=1)
-
-
-def other_kernel(far, left, *refs):
-    refs[far][...] = near_scores(left[...], refs[:far], refs[far + 1])
-
-
-def own_kernel(dims, left, squares, *refs):
-    far, groups = dims
-    queries = refs[:far]
-    other, send, keep, place, result = refs[far:]
-    own = near_scores(left[...], queries, place)
-    is_even = lax.rem(lax.axis_index("blk"), 2) == 0
-    back = other[...]
-    even = jnp.where(is_even, own, back)
-    odd = jnp.where(is_even, back, own)
-    half = own.shape[1]
-    owned = own.shape[0] // groups
+    scores = jnp.concatenate([place[b] for b in range(blks)], axis=1)
+    width = blks * nq
+    owned = scores.shape[0] // groups
     for g in range(groups):
         here = slice(g * owned, (g + 1) * owned)
-        result[g, :, :half] = even[here]
-        result[g, :, half : 2 * half] = odd[here]
-        result[g, :, 2 * half :] = squares[here, :]
+        result[g, :, :width] = scores[here]
+        result[g, :, width:] = squares[here, :]
     x = lax.axis_index("grp") // 2
     for core in range(2):
         send[core] = result[2 * (1 - x) + core]
@@ -119,17 +119,11 @@
     kept[...] = keep[core] + came[core]
 
 
-def finish_kernel(dims, kept, came, out):
-    pdim, nq = dims
+def finish_kernel(pdim, kept, came, out):
     total = kept[...] + came[...]
     width = out.shape[1]
     mean = jnp.sum(total[:, width:], axis=1, keepdims=True) / pdim
-    scaled = total[:, :width] * lax.rsqrt(mean + EPS)
-    columns = []
-    for start in range(0, width // 2, nq):
-        columns.append(scaled[:, start : start + nq])
-        columns.append(scaled[:, width // 2 + start : width // 2 + start + nq])
-    out[...] = jnp.concatenate(columns, axis=1)
+    out[...] = total[:, :width] * lax.rsqrt(mean + EPS)
 
 
 def small(kernel, out_shape, operands, scratch_shapes=(), name=None, first=VMEM):
@@ -164,7 +158,8 @@
         return lax.ppermute(x, "blk", [(b, b ^ k) for b in range(blks)])
 
     cut = lax.dynamic_slice(queries, (0, lax.axis_index("grp") * slice_width), (nq, slice_width))
-    gathered = [cut] + [blk_swap(cut, 2 * k) for k in range(1, far)]
+    pieces = [cut, blk_swap(cut, 1), blk_swap(cut, 2), blk_swap(cut, 3)]
+    distant = [blk_swap(cut, 2 * k) for k in range(2, far)]
 
     rows = cands * tokens
     piece = (cands // 2 * lines, 128)
@@ -178,38 +173,37 @@
         name="grads",
         first=SMEM,
     )
+    joined = small(
+        functools.partial(join_kernel, far - 2),
+        shape(((far - 2) * nq, slice_width), BF16),
+        (*pieces[1:], keep, *distant),
+        name="join",
+    )
     send, kept = small(
         fold_kernel,
         [shape(piece, BF16), shape(piece, F32)],
-        (keep, grp_swap(send, 1), *gathered),
+        (keep, grp_swap(send, 1), joined),
         name="fold",
     )
+    passed = blk_swap(joined, 1)
     own, squares = small(
         functools.partial(combine_kernel, (cands // 2, lines, width)),
         [shape((cands, slice_width), BF16), shape((cands, 128), F32)],
-        (kept, grp_swap(send, 2)),
+        (kept, grp_swap(send, 2), passed),
         [pltpu.VMEM(piece, F32)],
         name="combine",
     )
-    place = pltpu.VMEM((far, cands, nq), F32)
-    back = small(
-        functools.partial(other_kernel, far),
-        shape((cands, total_q // 2), F32),
-        (blk_swap(own, 1), *gathered),
-        [place],
-        name="other_scores",
-    )
     line = (owned, total_q + 128)
     send, keep = small(
-        functools.partial(own_kernel, (far, groups)),
+        functools.partial(scores_kernel, (blks, groups)),
         [shape((groups // 2,) + line, F32)] * 2,
-        (own, squares, *gathered, blk_swap(back, 1)),
-        [place, pltpu.VMEM((groups,) + line, F32)],
-        name="own_scores",
+        (own, squares, *pieces, *distant, passed),
+        [pltpu.VMEM((blks, cands, nq), F32), pltpu.VMEM((groups,) + line, F32)],
+        name="scores",
     )
     send, kept = small(pass_kernel, [shape(line, F32)] * 2, (keep, grp_swap(send, 2)), name="pass")
     return small(
-        functools.partial(finish_kernel, (pdim, nq)),
+        functools.partial(finish_kernel, pdim),
         shape((owned, total_q), F32),
         (kept, grp_swap(send, 1)),
         name="finish",

time: 36.6 us -> 33.1 us (0.904)
  waiting for transfers between devices: 11.2 us -> 7.31 us
  starting transfers between devices: 12.6 us -> 13.3 us
    ppermute x5 -> x6, waiting for transfers between devices: 4.34 us -> 0.17 us  [blk_swap(): return lax.ppermute(x, 'blk', [(b, b ^ k) for b in range(blks)])]
    ppermute x5 -> x6, starting transfers between devices: 9.16 us -> 10.2 us  [blk_swap(): return lax.ppermute(x, 'blk', [(b, b ^ k) for b in range(blks)])]
  transfers between devices with their start and end apart: 9 -> 10, of which waited for: 6 -> 5; matrix products, arithmetic and copies ran while one was open for 24% -> 27% of each run, Pallas kernels for 3% -> 3%
where the time goes in v8:
time: 33.1 us; the launch traced here: 33 us
  starting transfers between devices  13.3 us (40%)
  matrix products  8.89 us (27%)
  waiting for transfers between devices  7.31 us (22%)
  Pallas kernels  2.34 us (7%)
  local copies, waits for them, and re-layouts  1.06 us (3%)
    ppermute x6, starting transfers between devices, blk_swap(): return lax.ppermute(x, 'blk', [(b, b ^ k) for b in range(blks)])  10.2 us
    ppermute x4, waiting for transfers between devices, grp_swap(): return lax.ppermute(x, 'grp', [(g, g ^ k) for g in range(groups)])  7.14 us
    dot_general x1, matrix products, on_device(): jnp.dot(acts.reshape(rows, depth), proj_in[0], preferred_element_type=F32)  6.23 us
    ppermute x4, starting transfers between devices, grp_swap(): return lax.ppermute(x, 'grp', [(g, g ^ k) for g in range(groups)])  3.12 us
    dot_general x1, matrix products, on_device(): jnp.dot(out_grads.reshape(rows, depth), proj_out[0], preferred_element_ty...  2.66 us
    pallas_call x7, Pallas kernels, small(): pl.pallas_call(kernel, out_shape=out_shape, in_specs=[first] + [VMEM] * (...  2.34 us
    unnamed x8, local copies, waits for them, and re-layouts  1.05 us
  transfers between devices with their start and end apart: 10, of which 5 were waited for; matrix products, arithmetic and copies ran while one was open for 27% of the time, Pallas kernels for 3%

profile of v8, /device:TPU:0, one launch (start us, length us, event | category | flops | bytes accessed | tf_op | source)
XLA Modules:
  0.0 33.0 jit_solution(17115574292189753574)
XLA Ops:
  0.0 0.0 copy-start
  0.0 0.0 copy-start.3
  0.0 1.0 %copy-done = bf16[64,4096]{1,0:T(8,128)(2,1)S(1)} copy-done((bf16[64,4096]{1,0:T(8,128)(2,1)S(1)}, bf16[64,4096]{1,0:T(8,128)(2,1)}, u32[]{:S(2)}) %copy-start) | copy-done | bytes 524312
  1.1 5.1 %collective-permute-start.5 = (bf16[64,1024]{1,0:T(8,128)(2,1)S(1)}, bf16[64,1024]{1,0:T(8,128)(2,1)S(1)}, u32[]{:S(2)}, u32[]{:S(2)}) collective-permute-start(bf16[64,1024]{1,0:T(8,128)(2,1)S(1)} %constant_dynamic-slice_fusion.refs_0_), channel_id=1, source_target_pairs={{0,24},{4,28},{8,16},{12,20},{16,8},{20,12},{24,0},{28,4},{1,25},{... | collective-permute-start | bytes 393224 | tf_op jit(solution)/shard_map/ppermute | solution.py:158
  6.2 0.0 collective-permute-start.4
  6.2 1.7 %collective-permute-start.3 = (bf16[64,1024]{1,0:T(8,128)(2,1)S(1)}, bf16[64,1024]{1,0:T(8,128)(2,1)S(1)}, u32[]{:S(2)}, u32[]{:S(2)}) collective-permute-start(bf16[64,1024]{1,0:T(8,128)(2,1)S(1)} %constant_dynamic-slice_fusion.refs_0_), channel_id=1, source_target_pairs={{0,12},{4,8},{8,4},{12,0},{16,28},{20,24},{24,20},{28,16},{1,13},{... | collective-permute-start | bytes 393224 | tf_op jit(solution)/shard_map/ppermute | solution.py:158
  7.9 1.2 %collective-permute-start.2 = (bf16[64,1024]{1,0:T(8,128)(2,1)S(1)}, bf16[64,1024]{1,0:T(8,128)(2,1)S(1)}, u32[]{:S(2)}, u32[]{:S(2)}) collective-permute-start(bf16[64,1024]{1,0:T(8,128)(2,1)S(1)} %constant_dynamic-slice_fusion.refs_0_), channel_id=1, source_target_pairs={{0,8},{4,12},{8,0},{12,4},{16,24},{20,28},{24,16},{28,20},{1,9},{5... | collective-permute-start | bytes 393224 | tf_op jit(solution)/shard_map/ppermute | solution.py:158
  9.2 0.5 %collective-permute-start.1 = (bf16[64,1024]{1,0:T(8,128)(2,1)S(1)}, bf16[64,1024]{1,0:T(8,128)(2,1)S(1)}, u32[]{:S(2)}, u32[]{:S(2)}) collective-permute-start(bf16[64,1024]{1,0:T(8,128)(2,1)S(1)} %constant_dynamic-slice_fusion.refs_0_), channel_id=1, source_target_pairs={{0,4},{4,0},{8,12},{12,8},{16,20},{20,16},{24,28},{28,24},{1,5},{5... | collective-permute-start | bytes 393224 | tf_op jit(solution)/shard_map/ppermute | solution.py:158
  9.7 6.2 %convolution_convert_fusion.1.xp_in = bf16[64,1024]{1,0:T(8,128)(2,1)S(1)} fusion(bf16[1024,4096]{1,0:T(8,128)(2,1)} %bitcast.10, bf16[1,4096,64]{1,2,0:T(8,128)(2,1)} %param.8), kind=kOutput, calls=%fused_computation.1 | convolution fusion | flops 536936448 | bytes 9043968 | tf_op jit(solution)/shard_map/dot_general | solution.py:167
  15.9 0.0 copy-done.3
  15.9 0.0 copy-done.2
  15.9 2.7 %convolution_convert_fusion.gp_in = bf16[64,1024]{1,0:T(8,128)(2,1)S(1)} fusion(bf16[1024,4096]{1,0:T(8,128)(2,1)S(1)} %bitcast.11, bf16[1,4096,64]{1,2,0:T(8,128)(2,1)S(1)} %copy-done.3), kind=kOutput, calls=%fused_computation | convolution fusion | flops 536936448 | bytes 9043968 | tf_op jit(solution)/shard_map/dot_general | solution.py:166
  18.6 0.0 copy-done.1
  18.6 1.0 %grads.1 = (bf16[2,128,128]{2,1,0:T(8,128)(2,1)S(1)}, f32[2,128,128]{2,1,0:T(8,128)S(1)}) custom-call(s32[16]{0:T(128)S(1)} %copy-done.1, bf16[64,1024]{1,0:T(8,128)(2,1)S(1)} %convolution_convert_fusion.1.xp_in, bf16[64,1024]{1,0:T(8,128)(2,1)S(1)} %convolution_convert_fusion.gp_in), custom_call_target="tpu_custom_call" | custom-call | tf_op jit(solution)/shard_map/grads/pallas_call | solution.py:131
  19.6 0.0 collective-permute-done.5.refs_5_
  19.6 0.0 collective-permute-done.4.refs_4_
  19.6 0.0 collective-permute-done.3.refs_2_.refs_3_
  19.7 0.0 collective-permute-done.2.refs_1_.refs_2_
  19.7 0.0 collective-permute-done.1.refs_0_.refs_1_
  19.7 1.6 %collective-permute-start.7 = (bf16[128,1024]{1,0:T(8,128)(2,1)S(1)}, bf16[128,1024]{1,0:T(8,128)(2,1)S(1)}, u32[]{:S(2)}, u32[]{:S(2)}) collective-permute-start(bf16[128,1024]{1,0:T(8,128)(2,1)S(1)} %join.1.rest_0_), channel_id=1, source_target_pairs={{0,4},{4,0},{8,12},{12,8},{16,20},{20,16},{24,28},{28,24},{1,5},{5... | collective-permute-start | bytes 786440 | tf_op jit(solution)/shard_map/ppermute | solution.py:158
  21.3 0.0 collective-permute-start
  21.3 1.3 %collective-permute-done.came = bf16[2,128,128]{2,1,0:T(8,128)(2,1)S(1)} collective-permute-done((bf16[2,128,128]{2,1,0:T(8,128)(2,1)S(1)}, bf16[2,128,128]{2,1,0:T(8,128)(2,1)S(1)}, u32[]{:S(2)}, u32[]{:S(2)}) %collective-permute-start) | collective-permute-done | bytes 65568 | tf_op jit(solution)/shard_map/ppermute | solution.py:155
  22.6 1.6 %collective-permute-start.6 = (bf16[128,128]{1,0:T(8,128)(2,1)S(1)}, bf16[128,128]{1,0:T(8,128)(2,1)S(1)}, u32[]{:S(2)}, u32[]{:S(2)}) collective-permute-start(bf16[128,128]{1,0:T(8,128)(2,1)S(1)} %get-tuple-element.18), channel_id=1, source_target_pairs={{0,2},{1,3},{2,0},{3,1},{4,6},{5,7},{6,4},{7,5},{8,10},{9,11},{10,... | collective-permute-start | bytes 98312 | tf_op jit(solution)/shard_map/ppermute | solution.py:155
  24.1 2.4 %collective-permute-done.6.came = bf16[128,128]{1,0:T(8,128)(2,1)S(1)} collective-permute-done((bf16[128,128]{1,0:T(8,128)(2,1)S(1)}, bf16[128,128]{1,0:T(8,128)(2,1)S(1)}, u32[]{:S(2)}, u32[]{:S(2)}) %collective-permute-start.6) | collective-permute-done | bytes 32800 | tf_op jit(solution)/shard_map/ppermute | solution.py:155
  26.5 0.2 collective-permute-done.7.rest_0_.refs_6_
  26.7 0.1 combine.1
  26.8 0.5 %scores.1 = (f32[2,4,640]{2,1,0:T(4,128)S(1)}, f32[2,4,640]{2,1,0:T(4,128)S(1)}) custom-call(bf16[16,1024]{1,0:T(8,128)(2,1)S(1)} %get-tuple-element.19.left, f32[16,128]{1,0:T(8,128)S(1)} %get-tuple-element.20.squares, bf16[64,1024]{1,0:T(8,128)(2,1)S(1)} %constant_dynamic-slice_fusion.refs_0_, bf16[64,1024]{1,0:T(8,128)(2,1)S(1)} %collective-permute-done.1.refs_0_.refs_1_, ...), custom_call_target="tpu_custom_call" | custom-call | tf_op jit(solution)/shard_map/scores/pallas_call | solution.py:131
  27.3 1.6 %collective-permute-start.8 = (f32[2,4,640]{2,1,0:T(4,128)S(1)}, f32[2,4,640]{2,1,0:T(4,128)S(1)}, u32[]{:S(2)}, u32[]{:S(2)}) collective-permute-start(f32[2,4,640]{2,1,0:T(4,128)S(1)} %get-tuple-element.22), channel_id=1, source_target_pairs={{0,2},{1,3},{2,0},{3,1},{4,6},{5,7},{6,4},{7,5},{8,10},{9,11},{10,... | collective-permute-start | bytes 61448 | tf_op jit(solution)/shard_map/ppermute | solution.py:155
  28.8 2.3 %collective-permute-done.8.came = f32[2,4,640]{2,1,0:T(4,128)S(1)} collective-permute-done((f32[2,4,640]{2,1,0:T(4,128)S(1)}, f32[2,4,640]{2,1,0:T(4,128)S(1)}, u32[]{:S(2)}, u32[]{:S(2)}) %collective-permute-start.8) | collective-permute-done | bytes 20512 | tf_op jit(solution)/shard_map/ppermute | solution.py:155
  31.1 0.0 collective-permute-start.9
  31.1 1.2 %collective-permute-done.9.came = f32[4,640]{1,0:T(4,128)S(1)} collective-permute-done((f32[4,640]{1,0:T(4,128)S(1)}, f32[4,640]{1,0:T(4,128)S(1)}, u32[]{:S(2)}, u32[]{:S(2)}) %collective-permute-start.9) | collective-permute-done | bytes 10272 | tf_op jit(solution)/shard_map/ppermute | solution.py:155
  32.3 0.7 %finish.1 = f32[4,512]{1,0:T(4,128)} custom-call(f32[4,640]{1,0:T(4,128)S(1)} %get-tuple-element.23.kept, f32[4,640]{1,0:T(4,128)S(1)} %collective-permute-done.9.came), custom_call_target="tpu_custom_call" | custom-call | tf_op jit(solution)/shard_map/finish/pallas_call | solution.py:131
  (6 shorter events, 0.1 us)
Async XLA Ops:
  0.0 1.0 %copy-start = (bf16[64,4096]{1,0:T(8,128)(2,1)S(1)}, bf16[64,4096]{1,0:T(8,128)(2,1)}, u32[]{:S(2)}) copy-start(bf16[64,4096]{1,0:T(8,128)(2,1)} %param.11) | copy-start | bytes 1572868
  0.0 15.9 %copy-start.3 = (bf16[1,4096,64]{1,2,0:T(8,128)(2,1)S(1)}, bf16[1,4096,64]{1,2,0:T(8,128)(2,1)}, u32[]{:S(2)}) copy-start(bf16[1,4096,64]{1,2,0:T(8,128)(2,1)} %param.9) | copy-start | bytes 1572868
  1.0 14.9 %copy-start.2 = (bf16[1,16,64,4096]{3,2,1,0:T(8,128)(2,1)S(1)}, bf16[1,16,64,4096]{3,2,1,0:T(8,128)(2,1)}, u32[]{:S(2)}) copy-start(bf16[1,16,64,4096]{3,2,1,0:T(8,128)(2,1)} %param.7) | copy-start | bytes 25165828
  1.1 18.6 %collective-permute-start.5 = (bf16[64,1024]{1,0:T(8,128)(2,1)S(1)}, bf16[64,1024]{1,0:T(8,128)(2,1)S(1)}, u32[]{:S(2)}, u32[]{:S(2)}) collective-permute-start(bf16[64,1024]{1,0:T(8,128)(2,1)S(1)} %constant_dynamic-slice_fusion.refs_0_), channel_id=1, source_target_pairs={{0,24},{4,28},{8,16},{12,20},{16,8},{20,12},{24,0},{28,4},{1,25},{... | collective-permute-start | bytes 393224 | tf_op jit(solution)/shard_map/ppermute | solution.py:158
  6.2 13.5 %collective-permute-start.4 = (bf16[64,1024]{1,0:T(8,128)(2,1)S(1)}, bf16[64,1024]{1,0:T(8,128)(2,1)S(1)}, u32[]{:S(2)}, u32[]{:S(2)}) collective-permute-start(bf16[64,1024]{1,0:T(8,128)(2,1)S(1)} %constant_dynamic-slice_fusion.refs_0_), channel_id=1, source_target_pairs={{0,16},{4,20},{8,24},{12,28},{16,0},{20,4},{24,8},{28,12},{1,17},{... | collective-permute-start | bytes 393224 | tf_op jit(solution)/shard_map/ppermute | solution.py:158
  6.2 13.5 %collective-permute-start.3 = (bf16[64,1024]{1,0:T(8,128)(2,1)S(1)}, bf16[64,1024]{1,0:T(8,128)(2,1)S(1)}, u32[]{:S(2)}, u32[]{:S(2)}) collective-permute-start(bf16[64,1024]{1,0:T(8,128)(2,1)S(1)} %constant_dynamic-slice_fusion.refs_0_), channel_id=1, source_target_pairs={{0,12},{4,8},{8,4},{12,0},{16,28},{20,24},{24,20},{28,16},{1,13},{... | collective-permute-start | bytes 393224 | tf_op jit(solution)/shard_map/ppermute | solution.py:158
  7.9 11.7 %collective-permute-start.2 = (bf16[64,1024]{1,0:T(8,128)(2,1)S(1)}, bf16[64,1024]{1,0:T(8,128)(2,1)S(1)}, u32[]{:S(2)}, u32[]{:S(2)}) collective-permute-start(bf16[64,1024]{1,0:T(8,128)(2,1)S(1)} %constant_dynamic-slice_fusion.refs_0_), channel_id=1, source_target_pairs={{0,8},{4,12},{8,0},{12,4},{16,24},{20,28},{24,16},{28,20},{1,9},{5... | collective-permute-start | bytes 393224 | tf_op jit(solution)/shard_map/ppermute | solution.py:158
  9.2 10.5 %collective-permute-start.1 = (bf16[64,1024]{1,0:T(8,128)(2,1)S(1)}, bf16[64,1024]{1,0:T(8,128)(2,1)S(1)}, u32[]{:S(2)}, u32[]{:S(2)}) collective-permute-start(bf16[64,1024]{1,0:T(8,128)(2,1)S(1)} %constant_dynamic-slice_fusion.refs_0_), channel_id=1, source_target_pairs={{0,4},{4,0},{8,12},{12,8},{16,20},{20,16},{24,28},{28,24},{1,5},{5... | collective-permute-start | bytes 393224 | tf_op jit(solution)/shard_map/ppermute | solution.py:158
  9.7 8.9 %copy-start.1 = (s32[16]{0:T(128)S(1)}, s32[16]{0:T(128)}, u32[]{:S(2)}) copy-start(s32[16]{0:T(128)} %lens.1) | copy-start | bytes 196
  19.7 7.0 %collective-permute-start.7 = (bf16[128,1024]{1,0:T(8,128)(2,1)S(1)}, bf16[128,1024]{1,0:T(8,128)(2,1)S(1)}, u32[]{:S(2)}, u32[]{:S(2)}) collective-permute-start(bf16[128,1024]{1,0:T(8,128)(2,1)S(1)} %join.1.rest_0_), channel_id=1, source_target_pairs={{0,4},{4,0},{8,12},{12,8},{16,20},{20,16},{24,28},{28,24},{1,5},{5... | collective-permute-start | bytes 786440 | tf_op jit(solution)/shard_map/ppermute | solution.py:158
  21.3 1.3 %collective-permute-start = (bf16[2,128,128]{2,1,0:T(8,128)(2,1)S(1)}, bf16[2,128,128]{2,1,0:T(8,128)(2,1)S(1)}, u32[]{:S(2)}, u32[]{:S(2)}) collective-permute-start(bf16[2,128,128]{2,1,0:T(8,128)(2,1)S(1)} %get-tuple-element.16), channel_id=1, source_target_pairs={{0,1},{1,0},{2,3},{3,2},{4,5},{5,4},{6,7},{7,6},{8,9},{9,8},{10,11... | collective-permute-start | bytes 196616 | tf_op jit(solution)/shard_map/ppermute | solution.py:155
  22.6 4.0 %collective-permute-start.6 = (bf16[128,128]{1,0:T(8,128)(2,1)S(1)}, bf16[128,128]{1,0:T(8,128)(2,1)S(1)}, u32[]{:S(2)}, u32[]{:S(2)}) collective-permute-start(bf16[128,128]{1,0:T(8,128)(2,1)S(1)} %get-tuple-element.18), channel_id=1, source_target_pairs={{0,2},{1,3},{2,0},{3,1},{4,6},{5,7},{6,4},{7,5},{8,10},{9,11},{10,... | collective-permute-start | bytes 98312 | tf_op jit(solution)/shard_map/ppermute | solution.py:155
  27.3 3.8 %collective-permute-start.8 = (f32[2,4,640]{2,1,0:T(4,128)S(1)}, f32[2,4,640]{2,1,0:T(4,128)S(1)}, u32[]{:S(2)}, u32[]{:S(2)}) collective-permute-start(f32[2,4,640]{2,1,0:T(4,128)S(1)} %get-tuple-element.22), channel_id=1, source_target_pairs={{0,2},{1,3},{2,0},{3,1},{4,6},{5,7},{6,4},{7,5},{8,10},{9,11},{10,... | collective-permute-start | bytes 61448 | tf_op jit(solution)/shard_map/ppermute | solution.py:155
  31.1 1.2 %collective-permute-start.9 = (f32[4,640]{1,0:T(4,128)S(1)}, f32[4,640]{1,0:T(4,128)S(1)}, u32[]{:S(2)}, u32[]{:S(2)}) collective-permute-start(f32[4,640]{1,0:T(4,128)S(1)} %get-tuple-element.24), channel_id=1, source_target_pairs={{0,1},{1,0},{2,3},{3,2},{4,5},{5,4},{6,7},{7,6},{8,9},{9,8},{10,11... | collective-permute-start | bytes 30728 | tf_op jit(solution)/shard_map/ppermute | solution.py:155

commit v9 on v8

--- a/solution.py
+++ b/solution.py
@@ -8,41 +8,91 @@
 from jax.sharding import PartitionSpec as P
 
 EPS = 1e-06
+GRANT = 54784
 F32 = jnp.float32
 BF16 = jnp.bfloat16
 VMEM = pl.BlockSpec(memory_space=pltpu.VMEM)
-SMEM = pl.BlockSpec(memory_space=pltpu.SMEM)
+ANY = pl.BlockSpec(memory_space=pl.ANY)
 BY_ROWS = (((1,), (1,)), ((), ()))
 
 
-def grads_kernel(dims, lens, xp_in, gp_in, send, keep, store):
+def grads_kernel(dims, lens_in, acts, grads, w_in, w_out, send, keep, *scratch):
     cands, tokens, width, groups = dims
+    act_buf, grad_buf, win_raw, wout_raw, win, wout, lens, store, sems, wsems = scratch
     half = cands // 2
+    chunks = half // 2
     rows = 4 * tokens
+    loads = []
+    for i in range(chunks):
+        for side, (source, buf) in enumerate(((grads, grad_buf), (acts, act_buf))):
+            loads.append(
+                [
+                    pltpu.make_async_copy(
+                        source.at[pl.ds((2 * i + h * half) * tokens, rows // 2)],
+                        buf.at[pl.ds(i * rows + h * (rows // 2), rows // 2)],
+                        sems.at[side, 2 * i + h],
+                    )
+                    for h in range(2)
+                ]
+            )
+
+    def start(n):
+        if n < len(loads):
+            for load in loads[n]:
+                load.start()
+
+    def wait(n):
+        for load in loads[n]:
+            load.wait()
+
+    load_lens = pltpu.make_async_copy(lens_in, lens, wsems.at[2])
+    load_wout = pltpu.make_async_copy(w_out, wout_raw, wsems.at[0])
+    load_win = pltpu.make_async_copy(w_in, win_raw, wsems.at[1])
+    load_wout.start()
+    start(0)
+    load_win.start()
+    load_lens.start()
     grp = lax.axis_index("grp")
     lines = width // groups
     position = lax.broadcasted_iota(jnp.int32, (tokens, width), 0) + grp * tokens
     row_blk = lax.broadcasted_iota(jnp.int32, (rows, rows), 0) // tokens
     col_blk = lax.broadcasted_iota(jnp.int32, (rows, 4 * width), 1) // width
     diagonal = row_blk == col_blk // 2 + 2 * (col_blk % 2)
-    for i in range(half // 2):
-        members = [2 * i, 2 * i + 1, 2 * i + half, 2 * i + 1 + half]
-        parts = [slice(cand * tokens, (cand + 2) * tokens) for cand in members[::2]]
-        left = jnp.concatenate([gp_in[:, part] for part in parts], axis=1)
-        xp = jnp.concatenate([xp_in[:, part].astype(F32).T for part in parts], axis=0)
-        used = [
-            jnp.where(position < lens[cand], xp[j * tokens : (j + 1) * tokens], 0.0)
-            for j, cand in enumerate(members)
-        ]
+
+    def add_up(i, left, xp):
+        used = []
+        for j in range(4):
+            cand = 2 * i + j % 2 + (j // 2) * half
+            used.append(jnp.where(position < lens[cand], xp[j * tokens : (j + 1) * tokens], 0.0))
         wide = jnp.concatenate([jnp.concatenate(used, axis=0)] * 4, axis=1)
         right = jnp.where(diagonal, wide, 0.0).astype(BF16)
-        blocks = jnp.dot(left, right, preferred_element_type=F32)
+        sums = jnp.dot(left, right, preferred_element_type=F32)
         for t in range(2):
-            pair = 2 * i + t
+            there = slice((2 * i + t) * lines, (2 * i + t + 1) * lines)
             for s in range(groups):
-                store[s, pair * lines : (pair + 1) * lines, :] = blocks[
-                    s * lines : (s + 1) * lines, t * 128 : (t + 1) * 128
-                ]
+                store[s, there, :] = sums[s * lines : (s + 1) * lines, t * 128 : (t + 1) * 128]
+
+    load_wout.wait()
+    start(1)
+    wout[...] = wout_raw[...].T
+    load_win.wait()
+    load_lens.wait()
+    pending = None
+    for i in range(chunks):
+        part = pl.ds(i * rows, rows)
+        wait(2 * i)
+        start(2 * i + 2)
+        gp = jnp.dot(grad_buf[part, :], wout[...], preferred_element_type=F32)
+        if i == 0:
+            win[...] = win_raw[...].T
+        else:
+            add_up(*pending)
+        left = gp.T.astype(BF16)
+        wait(2 * i + 1)
+        start(2 * i + 3)
+        xp = jnp.dot(act_buf[part, :], win[...], preferred_element_type=F32)
+        pending = (i, left, xp)
+    add_up(*pending)
     core = lax.rem(grp, 2)
     for x in range(groups // 2):
         send[x] = store[2 * x + 1 - core].astype(BF16)
@@ -126,12 +176,12 @@
     out[...] = total[:, :width] * lax.rsqrt(mean + EPS)
 
 
-def small(kernel, out_shape, operands, scratch_shapes=(), name=None, first=VMEM):
+def small(kernel, out_shape, operands, scratch_shapes=(), name=None):
     one = not isinstance(out_shape, list)
     return pl.pallas_call(
         kernel,
         out_shape=out_shape,
-        in_specs=[first] + [VMEM] * (len(operands) - 1),
+        in_specs=[VMEM] * len(operands),
         out_specs=VMEM if one else [VMEM] * len(out_shape),
         scratch_shapes=list(scratch_shapes),
         compiler_params=pltpu.CompilerParams(vmem_limit_bytes=16 * 2**20),
@@ -158,20 +208,40 @@
         return lax.ppermute(x, "blk", [(b, b ^ k) for b in range(blks)])
 
     cut = lax.dynamic_slice(queries, (0, lax.axis_index("grp") * slice_width), (nq, slice_width))
+    cut, lens = lax.optimization_barrier((cut, jnp.minimum(lengths, tokens * groups)))
     pieces = [cut, blk_swap(cut, 1), blk_swap(cut, 2), blk_swap(cut, 3)]
     distant = [blk_swap(cut, 2 * k) for k in range(2, far)]
 
     rows = cands * tokens
     piece = (cands // 2 * lines, 128)
-    gp = jnp.dot(out_grads.reshape(rows, depth), proj_out[0], preferred_element_type=F32).astype(BF16)
-    xp = jnp.dot(acts.reshape(rows, depth), proj_in[0], preferred_element_type=F32).astype(BF16)
-    send, keep = small(
+    send, keep = pl.pallas_call(
         functools.partial(grads_kernel, (cands, tokens, width, groups)),
-        [shape((groups // 2,) + piece, BF16), shape((groups // 2,) + piece, F32)],
-        (lengths, xp.T, gp.T),
-        [pltpu.VMEM((groups,) + piece, F32)],
+        out_shape=[shape((groups // 2,) + piece, BF16), shape((groups // 2,) + piece, F32)],
+        in_specs=[ANY] * 5,
+        out_specs=[VMEM] * 2,
+        scratch_shapes=[
+            pltpu.VMEM((rows, depth), BF16),
+            pltpu.VMEM((rows, depth), BF16),
+            pltpu.VMEM((width, depth), BF16),
+            pltpu.VMEM((width, depth), BF16),
+            pltpu.VMEM((depth, width), BF16),
+            pltpu.VMEM((depth, width), BF16),
+            pltpu.SMEM((cands,), jnp.int32),
+            pltpu.VMEM((groups,) + piece, F32),
+            pltpu.SemaphoreType.DMA((2, cands // 2)),
+            pltpu.SemaphoreType.DMA((3,)),
+        ],
+        compiler_params=pltpu.CompilerParams(vmem_limit_bytes=GRANT * 2**10),
+        cost_estimate=pl.CostEstimate(
+            flops=16 * rows * depth * width, bytes_accessed=4 * rows * depth, transcendentals=0
+        ),
         name="grads",
-        first=SMEM,
+    )(
+        lens,
+        acts.reshape(rows, depth),
+        out_grads.reshape(rows, depth),
+        proj_in[0].T,
+        proj_out[0].T,
     )
     joined = small(
         functools.partial(join_kernel, far - 2),

time: 33.1 us -> 32.5 us (0.982)
  matrix products: 8.89 us -> 0 us
  Pallas kernels: 2.34 us -> 10.2 us
  other arithmetic: 0 us -> 0.72 us
  local copies, waits for them, and re-layouts: 1.06 us -> 0.35 us
    dot_general x2 -> x0, matrix products: 8.89 us -> none  [the longest x1 6.23 us: on_device(): jnp.dot(acts.reshape(rows, depth), proj_in[0], preferred_element_type=F32)]
    pallas_call x7, Pallas kernels: 2.34 us -> 10.2 us  [the longest x1 8.95 us: on_device(): pl.pallas_call(functools.partial(grads_kernel, (cands, tokens, width, gro...]
    min x0 -> x1, other arithmetic: none -> 0.72 us  [on_device(): jnp.minimum(lengths, tokens * groups)]
    unnamed x8 -> x2, local copies, waits for them, and re-layouts: 1.05 us -> 0.34 us
  transfers between devices with their start and end apart: 10 -> 10, of which waited for: 5 -> 5; matrix products, arithmetic and copies ran while one was open for 27% -> 0% of each run, Pallas kernels for 3% -> 28%
where the time goes in v9:
time: 32.5 us; the launch traced here: 32.3 us
  starting transfers between devices  13.5 us (42%)
  Pallas kernels  10.2 us (31%)
  waiting for transfers between devices  7.47 us (23%)
  other arithmetic  0.72 us (2%)
  local copies, waits for them, and re-layouts  0.35 us (1%)
    ppermute x6, starting transfers between devices, blk_swap(): return lax.ppermute(x, 'blk', [(b, b ^ k) for b in range(blks)])  10.2 us
    pallas_call x1, Pallas kernels, on_device(): pl.pallas_call(functools.partial(grads_kernel, (cands, tokens, width, gro...  8.95 us
    ppermute x4, waiting for transfers between devices, grp_swap(): return lax.ppermute(x, 'grp', [(g, g ^ k) for g in range(groups)])  6.98 us
    ppermute x4, starting transfers between devices, grp_swap(): return lax.ppermute(x, 'grp', [(g, g ^ k) for g in range(groups)])  3.27 us
    pallas_call x6, Pallas kernels, small(): pl.pallas_call(kernel, out_shape=out_shape, in_specs=[VMEM] * len(operand...  1.3 us
    min x1, other arithmetic, on_device(): jnp.minimum(lengths, tokens * groups)  0.72 us
  transfers between devices with their start and end apart: 10, of which 5 were waited for; matrix products, arithmetic and copies ran while one was open for 0% of the time, Pallas kernels for 28%

profile of v9, /device:TPU:0, one launch (start us, length us, event | category | flops | bytes accessed | tf_op | source)
XLA Modules:
  0.0 32.3 jit_solution(11776238799277036051)
XLA Ops:
  0.0 0.0 copy-start
  0.0 0.7 %broadcast_minimum_fusion.lens_in = s32[16]{0:T(128)S(1)} fusion(s32[16]{0:T(128)} %param.10), kind=kLoop, calls=%fused_computation | loop fusion | flops 16 | bytes 128 | tf_op jit(solution)/shard_map/min | solution.py:211
  0.7 0.3 %copy-done = bf16[64,4096]{1,0:T(8,128)(2,1)S(1)} copy-done((bf16[64,4096]{1,0:T(8,128)(2,1)S(1)}, bf16[64,4096]{1,0:T(8,128)(2,1)}, u32[]{:S(2)}) %copy-start) | copy-done | bytes 524312
  1.1 5.1 %collective-permute-start.5 = (bf16[64,1024]{1,0:T(8,128)(2,1)S(1)}, bf16[64,1024]{1,0:T(8,128)(2,1)S(1)}, u32[]{:S(2)}, u32[]{:S(2)}) collective-permute-start(bf16[64,1024]{1,0:T(8,128)(2,1)S(1)} %constant_dynamic-slice_fusion.refs_0_), channel_id=1, source_target_pairs={{0,24},{4,28},{8,16},{12,20},{16,8},{20,12},{24,0},{28,4},{1,25},{... | collective-permute-start | bytes 393224 | tf_op jit(solution)/shard_map/ppermute | solution.py:208
  6.2 0.0 collective-permute-start.4
  6.2 1.7 %collective-permute-start.3 = (bf16[64,1024]{1,0:T(8,128)(2,1)S(1)}, bf16[64,1024]{1,0:T(8,128)(2,1)S(1)}, u32[]{:S(2)}, u32[]{:S(2)}) collective-permute-start(bf16[64,1024]{1,0:T(8,128)(2,1)S(1)} %constant_dynamic-slice_fusion.refs_0_), channel_id=1, source_target_pairs={{0,12},{4,8},{8,4},{12,0},{16,28},{20,24},{24,20},{28,16},{1,13},{... | collective-permute-start | bytes 393224 | tf_op jit(solution)/shard_map/ppermute | solution.py:208
  7.9 1.2 %collective-permute-start.2 = (bf16[64,1024]{1,0:T(8,128)(2,1)S(1)}, bf16[64,1024]{1,0:T(8,128)(2,1)S(1)}, u32[]{:S(2)}, u32[]{:S(2)}) collective-permute-start(bf16[64,1024]{1,0:T(8,128)(2,1)S(1)} %constant_dynamic-slice_fusion.refs_0_), channel_id=1, source_target_pairs={{0,8},{4,12},{8,0},{12,4},{16,24},{20,28},{24,16},{28,20},{1,9},{5... | collective-permute-start | bytes 393224 | tf_op jit(solution)/shard_map/ppermute | solution.py:208
  9.2 0.5 %collective-permute-start.1 = (bf16[64,1024]{1,0:T(8,128)(2,1)S(1)}, bf16[64,1024]{1,0:T(8,128)(2,1)S(1)}, u32[]{:S(2)}, u32[]{:S(2)}) collective-permute-start(bf16[64,1024]{1,0:T(8,128)(2,1)S(1)} %constant_dynamic-slice_fusion.refs_0_), channel_id=1, source_target_pairs={{0,4},{4,0},{8,12},{12,8},{16,20},{20,16},{24,28},{28,24},{1,5},{5... | collective-permute-start | bytes 393224 | tf_op jit(solution)/shard_map/ppermute | solution.py:208
  9.7 8.9 %grads.1 = (bf16[2,128,128]{2,1,0:T(8,128)(2,1)S(1)}, f32[2,128,128]{2,1,0:T(8,128)S(1)}) custom-call(s32[16]{0:T(128)S(1)} %broadcast_minimum_fusion.lens_in, bf16[1024,4096]{1,0:T(8,128)(2,1)} %bitcast.8, bf16[1024,4096]{1,0:T(8,128)(2,1)} %bitcast.9, bf16[64,4096]{1,0:T(8,128)(2,1)} %bitcast.10, bf16[64,4096]{1,0:T(8,128)(2,1)} %bitcast.11), custom_call_target="tpu_custom_call" | custom-call | flops 4294967296 | bytes 16777216 | tf_op jit(solution)/shard_map/grads/pallas_call | solution.py:217
  18.6 0.0 collective-permute-done.5.refs_5_
  18.6 0.0 collective-permute-done.4.refs_4_
  18.7 0.0 collective-permute-done.3.refs_2_.refs_3_
  18.7 0.0 collective-permute-done.2.refs_1_.refs_2_
  18.7 0.0 collective-permute-done.1.refs_0_.refs_1_
  18.7 1.6 %collective-permute-start.7 = (bf16[128,1024]{1,0:T(8,128)(2,1)S(1)}, bf16[128,1024]{1,0:T(8,128)(2,1)S(1)}, u32[]{:S(2)}, u32[]{:S(2)}) collective-permute-start(bf16[128,1024]{1,0:T(8,128)(2,1)S(1)} %join.1.rest_0_), channel_id=1, source_target_pairs={{0,4},{4,0},{8,12},{12,8},{16,20},{20,16},{24,28},{28,24},{1,5},{5... | collective-permute-start | bytes 786440 | tf_op jit(solution)/shard_map/ppermute | solution.py:208
  20.3 0.0 collective-permute-start
  20.3 1.3 %collective-permute-done.came = bf16[2,128,128]{2,1,0:T(8,128)(2,1)S(1)} collective-permute-done((bf16[2,128,128]{2,1,0:T(8,128)(2,1)S(1)}, bf16[2,128,128]{2,1,0:T(8,128)(2,1)S(1)}, u32[]{:S(2)}, u32[]{:S(2)}) %collective-permute-start) | collective-permute-done | bytes 65568 | tf_op jit(solution)/shard_map/ppermute | solution.py:205
  21.6 1.6 %collective-permute-start.6 = (bf16[128,128]{1,0:T(8,128)(2,1)S(1)}, bf16[128,128]{1,0:T(8,128)(2,1)S(1)}, u32[]{:S(2)}, u32[]{:S(2)}) collective-permute-start(bf16[128,128]{1,0:T(8,128)(2,1)S(1)} %get-tuple-element.22), channel_id=1, source_target_pairs={{0,2},{1,3},{2,0},{3,1},{4,6},{5,7},{6,4},{7,5},{8,10},{9,11},{10,... | collective-permute-start | bytes 98312 | tf_op jit(solution)/shard_map/ppermute | solution.py:205
  23.1 2.4 %collective-permute-done.6.came = bf16[128,128]{1,0:T(8,128)(2,1)S(1)} collective-permute-done((bf16[128,128]{1,0:T(8,128)(2,1)S(1)}, bf16[128,128]{1,0:T(8,128)(2,1)S(1)}, u32[]{:S(2)}, u32[]{:S(2)}) %collective-permute-start.6) | collective-permute-done | bytes 32800 | tf_op jit(solution)/shard_map/ppermute | solution.py:205
  25.6 0.5 %collective-permute-done.7.rest_0_.refs_6_ = bf16[128,1024]{1,0:T(8,128)(2,1)S(1)} collective-permute-done((bf16[128,1024]{1,0:T(8,128)(2,1)S(1)}, bf16[128,1024]{1,0:T(8,128)(2,1)S(1)}, u32[]{:S(2)}, u32[]{:S(2)}) %collective-permute-start.7) | collective-permute-done | bytes 262176 | tf_op jit(solution)/shard_map/ppermute | solution.py:208
  26.0 0.1 combine.1
  26.1 0.5 %scores.1 = (f32[2,4,640]{2,1,0:T(4,128)S(1)}, f32[2,4,640]{2,1,0:T(4,128)S(1)}) custom-call(bf16[16,1024]{1,0:T(8,128)(2,1)S(1)} %get-tuple-element.23.left, f32[16,128]{1,0:T(8,128)S(1)} %get-tuple-element.24.squares, bf16[64,1024]{1,0:T(8,128)(2,1)S(1)} %constant_dynamic-slice_fusion.refs_0_, bf16[64,1024]{1,0:T(8,128)(2,1)S(1)} %collective-permute-done.1.refs_0_.refs_1_, ...), custom_call_target="tpu_custom_call" | custom-call | tf_op jit(solution)/shard_map/scores/pallas_call | solution.py:181
  26.6 1.7 %collective-permute-start.8 = (f32[2,4,640]{2,1,0:T(4,128)S(1)}, f32[2,4,640]{2,1,0:T(4,128)S(1)}, u32[]{:S(2)}, u32[]{:S(2)}) collective-permute-start(f32[2,4,640]{2,1,0:T(4,128)S(1)} %get-tuple-element.26), channel_id=1, source_target_pairs={{0,2},{1,3},{2,0},{3,1},{4,6},{5,7},{6,4},{7,5},{8,10},{9,11},{10,... | collective-permute-start | bytes 61448 | tf_op jit(solution)/shard_map/ppermute | solution.py:205
  28.3 2.1 %collective-permute-done.8.came = f32[2,4,640]{2,1,0:T(4,128)S(1)} collective-permute-done((f32[2,4,640]{2,1,0:T(4,128)S(1)}, f32[2,4,640]{2,1,0:T(4,128)S(1)}, u32[]{:S(2)}, u32[]{:S(2)}) %collective-permute-start.8) | collective-permute-done | bytes 20512 | tf_op jit(solution)/shard_map/ppermute | solution.py:205
  30.5 0.0 collective-permute-start.9
  30.5 1.2 %collective-permute-done.9.came = f32[4,640]{1,0:T(4,128)S(1)} collective-permute-done((f32[4,640]{1,0:T(4,128)S(1)}, f32[4,640]{1,0:T(4,128)S(1)}, u32[]{:S(2)}, u32[]{:S(2)}) %collective-permute-start.9) | collective-permute-done | bytes 10272 | tf_op jit(solution)/shard_map/ppermute | solution.py:205
  31.6 0.7 %finish.1 = f32[4,512]{1,0:T(4,128)} custom-call(f32[4,640]{1,0:T(4,128)S(1)} %get-tuple-element.27.kept, f32[4,640]{1,0:T(4,128)S(1)} %collective-permute-done.9.came), custom_call_target="tpu_custom_call" | custom-call | tf_op jit(solution)/shard_map/finish/pallas_call | solution.py:181
  (4 shorter events, 0.1 us)
Async XLA Ops:
  0.0 1.1 %copy-start = (bf16[64,4096]{1,0:T(8,128)(2,1)S(1)}, bf16[64,4096]{1,0:T(8,128)(2,1)}, u32[]{:S(2)}) copy-start(bf16[64,4096]{1,0:T(8,128)(2,1)} %param.11) | copy-start | bytes 1572868
  1.1 17.6 %collective-permute-start.5 = (bf16[64,1024]{1,0:T(8,128)(2,1)S(1)}, bf16[64,1024]{1,0:T(8,128)(2,1)S(1)}, u32[]{:S(2)}, u32[]{:S(2)}) collective-permute-start(bf16[64,1024]{1,0:T(8,128)(2,1)S(1)} %constant_dynamic-slice_fusion.refs_0_), channel_id=1, source_target_pairs={{0,24},{4,28},{8,16},{12,20},{16,8},{20,12},{24,0},{28,4},{1,25},{... | collective-permute-start | bytes 393224 | tf_op jit(solution)/shard_map/ppermute | solution.py:208
  6.2 12.5 %collective-permute-start.4 = (bf16[64,1024]{1,0:T(8,128)(2,1)S(1)}, bf16[64,1024]{1,0:T(8,128)(2,1)S(1)}, u32[]{:S(2)}, u32[]{:S(2)}) collective-permute-start(bf16[64,1024]{1,0:T(8,128)(2,1)S(1)} %constant_dynamic-slice_fusion.refs_0_), channel_id=1, source_target_pairs={{0,16},{4,20},{8,24},{12,28},{16,0},{20,4},{24,8},{28,12},{1,17},{... | collective-permute-start | bytes 393224 | tf_op jit(solution)/shard_map/ppermute | solution.py:208
  6.2 12.5 %collective-permute-start.3 = (bf16[64,1024]{1,0:T(8,128)(2,1)S(1)}, bf16[64,1024]{1,0:T(8,128)(2,1)S(1)}, u32[]{:S(2)}, u32[]{:S(2)}) collective-permute-start(bf16[64,1024]{1,0:T(8,128)(2,1)S(1)} %constant_dynamic-slice_fusion.refs_0_), channel_id=1, source_target_pairs={{0,12},{4,8},{8,4},{12,0},{16,28},{20,24},{24,20},{28,16},{1,13},{... | collective-permute-start | bytes 393224 | tf_op jit(solution)/shard_map/ppermute | solution.py:208
  7.9 10.7 %collective-permute-start.2 = (bf16[64,1024]{1,0:T(8,128)(2,1)S(1)}, bf16[64,1024]{1,0:T(8,128)(2,1)S(1)}, u32[]{:S(2)}, u32[]{:S(2)}) collective-permute-start(bf16[64,1024]{1,0:T(8,128)(2,1)S(1)} %constant_dynamic-slice_fusion.refs_0_), channel_id=1, source_target_pairs={{0,8},{4,12},{8,0},{12,4},{16,24},{20,28},{24,16},{28,20},{1,9},{5... | collective-permute-start | bytes 393224 | tf_op jit(solution)/shard_map/ppermute | solution.py:208
  9.2 9.5 %collective-permute-start.1 = (bf16[64,1024]{1,0:T(8,128)(2,1)S(1)}, bf16[64,1024]{1,0:T(8,128)(2,1)S(1)}, u32[]{:S(2)}, u32[]{:S(2)}) collective-permute-start(bf16[64,1024]{1,0:T(8,128)(2,1)S(1)} %constant_dynamic-slice_fusion.refs_0_), channel_id=1, source_target_pairs={{0,4},{4,0},{8,12},{12,8},{16,20},{20,16},{24,28},{28,24},{1,5},{5... | collective-permute-start | bytes 393224 | tf_op jit(solution)/shard_map/ppermute | solution.py:208
  18.7 7.3 %collective-permute-start.7 = (bf16[128,1024]{1,0:T(8,128)(2,1)S(1)}, bf16[128,1024]{1,0:T(8,128)(2,1)S(1)}, u32[]{:S(2)}, u32[]{:S(2)}) collective-permute-start(bf16[128,1024]{1,0:T(8,128)(2,1)S(1)} %join.1.rest_0_), channel_id=1, source_target_pairs={{0,4},{4,0},{8,12},{12,8},{16,20},{20,16},{24,28},{28,24},{1,5},{5... | collective-permute-start | bytes 786440 | tf_op jit(solution)/shard_map/ppermute | solution.py:208
  20.3 1.3 %collective-permute-start = (bf16[2,128,128]{2,1,0:T(8,128)(2,1)S(1)}, bf16[2,128,128]{2,1,0:T(8,128)(2,1)S(1)}, u32[]{:S(2)}, u32[]{:S(2)}) collective-permute-start(bf16[2,128,128]{2,1,0:T(8,128)(2,1)S(1)} %get-tuple-element.19), channel_id=1, source_target_pairs={{0,1},{1,0},{2,3},{3,2},{4,5},{5,4},{6,7},{7,6},{8,9},{9,8},{10,11... | collective-permute-start | bytes 196616 | tf_op jit(solution)/shard_map/ppermute | solution.py:205
  21.6 4.0 %collective-permute-start.6 = (bf16[128,128]{1,0:T(8,128)(2,1)S(1)}, bf16[128,128]{1,0:T(8,128)(2,1)S(1)}, u32[]{:S(2)}, u32[]{:S(2)}) collective-permute-start(bf16[128,128]{1,0:T(8,128)(2,1)S(1)} %get-tuple-element.22), channel_id=1, source_target_pairs={{0,2},{1,3},{2,0},{3,1},{4,6},{5,7},{6,4},{7,5},{8,10},{9,11},{10,... | collective-permute-start | bytes 98312 | tf_op jit(solution)/shard_map/ppermute | solution.py:205
  26.6 3.8 %collective-permute-start.8 = (f32[2,4,640]{2,1,0:T(4,128)S(1)}, f32[2,4,640]{2,1,0:T(4,128)S(1)}, u32[]{:S(2)}, u32[]{:S(2)}) collective-permute-start(f32[2,4,640]{2,1,0:T(4,128)S(1)} %get-tuple-element.26), channel_id=1, source_target_pairs={{0,2},{1,3},{2,0},{3,1},{4,6},{5,7},{6,4},{7,5},{8,10},{9,11},{10,... | collective-permute-start | bytes 61448 | tf_op jit(solution)/shard_map/ppermute | solution.py:205
  30.5 1.2 %collective-permute-start.9 = (f32[4,640]{1,0:T(4,128)S(1)}, f32[4,640]{1,0:T(4,128)S(1)}, u32[]{:S(2)}, u32[]{:S(2)}) collective-permute-start(f32[4,640]{1,0:T(4,128)S(1)} %get-tuple-element.28), channel_id=1, source_target_pairs={{0,1},{1,0},{2,3},{3,2},{4,5},{5,4},{6,7},{7,6},{8,9},{9,8},{10,11... | collective-permute-start | bytes 30728 | tf_op jit(solution)/shard_map/ppermute | solution.py:205

commit v10 on v9

--- a/solution.py
+++ b/solution.py
@@ -49,9 +49,10 @@
     load_wout = pltpu.make_async_copy(w_out, wout_raw, wsems.at[0])
     load_win = pltpu.make_async_copy(w_in, win_raw, wsems.at[1])
     load_wout.start()
-    start(0)
     load_win.start()
     load_lens.start()
+    for n in range(3):
+        start(n)
     grp = lax.axis_index("grp")
     lines = width // groups
     position = lax.broadcasted_iota(jnp.int32, (tokens, width), 0) + grp * tokens
@@ -73,7 +74,6 @@
                 store[s, there, :] = sums[s * lines : (s + 1) * lines, t * 128 : (t + 1) * 128]
 
     load_wout.wait()
-    start(1)
     wout[...] = wout_raw[...].T
     load_win.wait()
     load_lens.wait()
@@ -81,16 +81,24 @@
     for i in range(chunks):
         part = pl.ds(i * rows, rows)
         wait(2 * i)
-        start(2 * i + 2)
+        start(2 * i + 3)
         gp = jnp.dot(grad_buf[part, :], wout[...], preferred_element_type=F32)
         if i == 0:
             win[...] = win_raw[...].T
         else:
             add_up(*pending)
         left = gp.T.astype(BF16)
-        wait(2 * i + 1)
-        start(2 * i + 3)
-        xp = jnp.dot(act_buf[part, :], win[...], preferred_element_type=F32)
+        if i < chunks - 1:
+            wait(2 * i + 1)
+            start(2 * i + 4)
+            xp = jnp.dot(act_buf[part, :], win[...], preferred_element_type=F32)
+        else:
+            pieces = []
+            for h, load in enumerate(loads[2 * i + 1]):
+                load.wait()
+                piece = pl.ds(i * rows + h * (rows // 2), rows // 2)
+                pieces.append(jnp.dot(act_buf[piece, :], win[...], preferred_element_type=F32))
+            xp = jnp.concatenate(pieces, axis=0)
         pending = (i, left, xp)
     add_up(*pending)
     core = lax.rem(grp, 2)
@@ -135,20 +143,24 @@
         out[n * nq : (n + 1) * nq, :] = ref[...]
 
 
-def scores_kernel(dims, left, squares, *refs):
+def near_kernel(dims, left, *refs):
+    blk = lax.axis_index("blk")
+    place = refs[-1]
+    for flip, piece in zip(dims, refs[:-1]):
+        place[jnp.bitwise_xor(blk, flip)] = lax.dot_general(
+            left[...], piece[...], BY_ROWS, preferred_element_type=F32
+        )
+
+
+def scores_kernel(dims, left, squares, near, passed, send, keep, place, result):
     blks, groups = dims
-    pieces = refs[: blks // 2 + 2]
-    far, send, keep, place, result = refs[blks // 2 + 2 :]
     rows = left[...]
     blk = lax.axis_index("blk")
-    nq = pieces[0].shape[0]
-    table = {0: pieces[0], 1: pieces[1], 2: pieces[2], 3: pieces[3]}
-    for k in range(2, blks // 2):
-        table[2 * k] = pieces[k + 2]
-        table[2 * k + 1] = far.at[pl.ds((k - 2) * nq, nq)]
-    for flip, piece in table.items():
-        place[jnp.bitwise_xor(blk, flip)] = lax.dot_general(
-            rows, piece[...], BY_ROWS, preferred_element_type=F32
+    nq = near.shape[2]
+    place[...] = near[...]
+    for n in range(blks // 2 - 2):
+        place[jnp.bitwise_xor(blk, 2 * n + 5)] = lax.dot_general(
+            rows, passed[n * nq : (n + 1) * nq, :], BY_ROWS, preferred_element_type=F32
         )
     scores = jnp.concatenate([place[b] for b in range(blks)], axis=1)
     width = blks * nq
@@ -259,15 +271,21 @@
     own, squares = small(
         functools.partial(combine_kernel, (cands // 2, lines, width)),
         [shape((cands, slice_width), BF16), shape((cands, 128), F32)],
-        (kept, grp_swap(send, 2), passed),
+        (kept, grp_swap(send, 2)),
         [pltpu.VMEM(piece, F32)],
         name="combine",
+    )
+    near = small(
+        functools.partial(near_kernel, [0, 1, 2, 3] + [2 * k for k in range(2, far)]),
+        shape((blks, cands, nq), F32),
+        (own, *pieces, *distant),
+        name="near",
     )
     line = (owned, total_q + 128)
     send, keep = small(
         functools.partial(scores_kernel, (blks, groups)),
         [shape((groups // 2,) + line, F32)] * 2,
-        (own, squares, *pieces, *distant, passed),
+        (own, squares, near, passed),
         [pltpu.VMEM((blks, cands, nq), F32), pltpu.VMEM((groups,) + line, F32)],
         name="scores",
     )

time: 32.5 us -> 32.2 us (level)
    pallas_call x6 -> x7, Pallas kernels: 1.3 us -> 1.4 us  [small(): pl.pallas_call(kernel, out_shape=out_shape, in_specs=[VMEM] * len(operand...]
  transfers between devices with their start and end apart: 10 -> 10, of which waited for: 5 -> 5; matrix products, arithmetic and copies ran while one was open for 0% -> 0% of each run, Pallas kernels for 28% -> 29%
where the time goes in v10:
time: 32.2 us; the launch traced here: 32 us
  starting transfers between devices  13.5 us (42%)
  Pallas kernels  10.2 us (32%)
  waiting for transfers between devices  7.18 us (22%)
  other arithmetic  0.72 us (2%)
  local copies, waits for them, and re-layouts  0.35 us (1%)
    ppermute x6, starting transfers between devices, blk_swap(): return lax.ppermute(x, 'blk', [(b, b ^ k) for b in range(blks)])  10.2 us
    pallas_call x1, Pallas kernels, on_device(): pl.pallas_call(functools.partial(grads_kernel, (cands, tokens, width, gro...  8.83 us
    ppermute x4, waiting for transfers between devices, grp_swap(): return lax.ppermute(x, 'grp', [(g, g ^ k) for g in range(groups)])  6.98 us
    ppermute x4, starting transfers between devices, grp_swap(): return lax.ppermute(x, 'grp', [(g, g ^ k) for g in range(groups)])  3.27 us
    pallas_call x7, Pallas kernels, small(): pl.pallas_call(kernel, out_shape=out_shape, in_specs=[VMEM] * len(operand...  1.4 us
    min x1, other arithmetic, on_device(): jnp.minimum(lengths, tokens * groups)  0.72 us
  transfers between devices with their start and end apart: 10, of which 5 were waited for; matrix products, arithmetic and copies ran while one was open for 0% of the time, Pallas kernels for 29%

profile of v10, /device:TPU:0, one launch (start us, length us, event | category | flops | bytes accessed | tf_op | source)
XLA Modules:
  0.0 32.0 jit_solution(1710341831207621955)
XLA Ops:
  0.0 0.0 copy-start
  0.0 0.7 %broadcast_minimum_fusion.lens_in = s32[16]{0:T(128)S(1)} fusion(s32[16]{0:T(128)} %param.10), kind=kLoop, calls=%fused_computation | loop fusion | flops 16 | bytes 128 | tf_op jit(solution)/shard_map/min | solution.py:223
  0.7 0.3 %copy-done = bf16[64,4096]{1,0:T(8,128)(2,1)S(1)} copy-done((bf16[64,4096]{1,0:T(8,128)(2,1)S(1)}, bf16[64,4096]{1,0:T(8,128)(2,1)}, u32[]{:S(2)}) %copy-start) | copy-done | bytes 524312
  1.1 5.1 %collective-permute-start.5 = (bf16[64,1024]{1,0:T(8,128)(2,1)S(1)}, bf16[64,1024]{1,0:T(8,128)(2,1)S(1)}, u32[]{:S(2)}, u32[]{:S(2)}) collective-permute-start(bf16[64,1024]{1,0:T(8,128)(2,1)S(1)} %constant_dynamic-slice_fusion.refs_0_), channel_id=1, source_target_pairs={{0,24},{4,28},{8,16},{12,20},{16,8},{20,12},{24,0},{28,4},{1,25},{... | collective-permute-start | bytes 393224 | tf_op jit(solution)/shard_map/ppermute | solution.py:220
  6.2 0.0 collective-permute-start.4
  6.2 1.7 %collective-permute-start.3 = (bf16[64,1024]{1,0:T(8,128)(2,1)S(1)}, bf16[64,1024]{1,0:T(8,128)(2,1)S(1)}, u32[]{:S(2)}, u32[]{:S(2)}) collective-permute-start(bf16[64,1024]{1,0:T(8,128)(2,1)S(1)} %constant_dynamic-slice_fusion.refs_0_), channel_id=1, source_target_pairs={{0,12},{4,8},{8,4},{12,0},{16,28},{20,24},{24,20},{28,16},{1,13},{... | collective-permute-start | bytes 393224 | tf_op jit(solution)/shard_map/ppermute | solution.py:220
  7.9 1.2 %collective-permute-start.2 = (bf16[64,1024]{1,0:T(8,128)(2,1)S(1)}, bf16[64,1024]{1,0:T(8,128)(2,1)S(1)}, u32[]{:S(2)}, u32[]{:S(2)}) collective-permute-start(bf16[64,1024]{1,0:T(8,128)(2,1)S(1)} %constant_dynamic-slice_fusion.refs_0_), channel_id=1, source_target_pairs={{0,8},{4,12},{8,0},{12,4},{16,24},{20,28},{24,16},{28,20},{1,9},{5... | collective-permute-start | bytes 393224 | tf_op jit(solution)/shard_map/ppermute | solution.py:220
  9.2 0.5 %collective-permute-start.1 = (bf16[64,1024]{1,0:T(8,128)(2,1)S(1)}, bf16[64,1024]{1,0:T(8,128)(2,1)S(1)}, u32[]{:S(2)}, u32[]{:S(2)}) collective-permute-start(bf16[64,1024]{1,0:T(8,128)(2,1)S(1)} %constant_dynamic-slice_fusion.refs_0_), channel_id=1, source_target_pairs={{0,4},{4,0},{8,12},{12,8},{16,20},{20,16},{24,28},{28,24},{1,5},{5... | collective-permute-start | bytes 393224 | tf_op jit(solution)/shard_map/ppermute | solution.py:220
  9.7 8.8 %grads.1 = (bf16[2,128,128]{2,1,0:T(8,128)(2,1)S(1)}, f32[2,128,128]{2,1,0:T(8,128)S(1)}) custom-call(s32[16]{0:T(128)S(1)} %broadcast_minimum_fusion.lens_in, bf16[1024,4096]{1,0:T(8,128)(2,1)} %bitcast.8, bf16[1024,4096]{1,0:T(8,128)(2,1)} %bitcast.9, bf16[64,4096]{1,0:T(8,128)(2,1)} %bitcast.10, bf16[64,4096]{1,0:T(8,128)(2,1)} %bitcast.11), custom_call_target="tpu_custom_call" | custom-call | flops 4294967296 | bytes 16777216 | tf_op jit(solution)/shard_map/grads/pallas_call | solution.py:229
  18.5 0.0 collective-permute-done.5.refs_5_
  18.5 0.0 collective-permute-done.4.refs_4_
  18.5 0.0 collective-permute-done.3.refs_2_.refs_3_
  18.5 0.0 collective-permute-done.2.refs_1_.refs_2_
  18.6 0.0 collective-permute-done.1.refs_0_.refs_1_
  18.6 1.6 %collective-permute-start.7 = (bf16[128,1024]{1,0:T(8,128)(2,1)S(1)}, bf16[128,1024]{1,0:T(8,128)(2,1)S(1)}, u32[]{:S(2)}, u32[]{:S(2)}) collective-permute-start(bf16[128,1024]{1,0:T(8,128)(2,1)S(1)} %join.1.rest_0_), channel_id=1, source_target_pairs={{0,4},{4,0},{8,12},{12,8},{16,20},{20,16},{24,28},{28,24},{1,5},{5... | collective-permute-start | bytes 786440 | tf_op jit(solution)/shard_map/ppermute | solution.py:220
  20.2 0.0 collective-permute-start
  20.2 1.3 %collective-permute-done.came = bf16[2,128,128]{2,1,0:T(8,128)(2,1)S(1)} collective-permute-done((bf16[2,128,128]{2,1,0:T(8,128)(2,1)S(1)}, bf16[2,128,128]{2,1,0:T(8,128)(2,1)S(1)}, u32[]{:S(2)}, u32[]{:S(2)}) %collective-permute-start) | collective-permute-done | bytes 65568 | tf_op jit(solution)/shard_map/ppermute | solution.py:217
  21.5 1.6 %collective-permute-start.6 = (bf16[128,128]{1,0:T(8,128)(2,1)S(1)}, bf16[128,128]{1,0:T(8,128)(2,1)S(1)}, u32[]{:S(2)}, u32[]{:S(2)}) collective-permute-start(bf16[128,128]{1,0:T(8,128)(2,1)S(1)} %get-tuple-element.22), channel_id=1, source_target_pairs={{0,2},{1,3},{2,0},{3,1},{4,6},{5,7},{6,4},{7,5},{8,10},{9,11},{10,... | collective-permute-start | bytes 98312 | tf_op jit(solution)/shard_map/ppermute | solution.py:217
  23.0 2.4 %collective-permute-done.6.came = bf16[128,128]{1,0:T(8,128)(2,1)S(1)} collective-permute-done((bf16[128,128]{1,0:T(8,128)(2,1)S(1)}, bf16[128,128]{1,0:T(8,128)(2,1)S(1)}, u32[]{:S(2)}, u32[]{:S(2)}) %collective-permute-start.6) | collective-permute-done | bytes 32800 | tf_op jit(solution)/shard_map/ppermute | solution.py:217
  25.4 0.1 combine.1
  25.5 0.3 near.1
  25.8 0.2 collective-permute-done.7.passed
  26.0 0.3 scores.1
  26.3 1.7 %collective-permute-start.8 = (f32[2,4,640]{2,1,0:T(4,128)S(1)}, f32[2,4,640]{2,1,0:T(4,128)S(1)}, u32[]{:S(2)}, u32[]{:S(2)}) collective-permute-start(f32[2,4,640]{2,1,0:T(4,128)S(1)} %get-tuple-element.26), channel_id=1, source_target_pairs={{0,2},{1,3},{2,0},{3,1},{4,6},{5,7},{6,4},{7,5},{8,10},{9,11},{10,... | collective-permute-start | bytes 61448 | tf_op jit(solution)/shard_map/ppermute | solution.py:217
  28.0 2.1 %collective-permute-done.8.came = f32[2,4,640]{2,1,0:T(4,128)S(1)} collective-permute-done((f32[2,4,640]{2,1,0:T(4,128)S(1)}, f32[2,4,640]{2,1,0:T(4,128)S(1)}, u32[]{:S(2)}, u32[]{:S(2)}) %collective-permute-start.8) | collective-permute-done | bytes 20512 | tf_op jit(solution)/shard_map/ppermute | solution.py:217
  30.2 0.0 collective-permute-start.9
  30.2 1.2 %collective-permute-done.9.came = f32[4,640]{1,0:T(4,128)S(1)} collective-permute-done((f32[4,640]{1,0:T(4,128)S(1)}, f32[4,640]{1,0:T(4,128)S(1)}, u32[]{:S(2)}, u32[]{:S(2)}) %collective-permute-start.9) | collective-permute-done | bytes 10272 | tf_op jit(solution)/shard_map/ppermute | solution.py:217
  31.3 0.7 %finish.1 = f32[4,512]{1,0:T(4,128)} custom-call(f32[4,640]{1,0:T(4,128)S(1)} %get-tuple-element.27.kept, f32[4,640]{1,0:T(4,128)S(1)} %collective-permute-done.9.came), custom_call_target="tpu_custom_call" | custom-call | tf_op jit(solution)/shard_map/finish/pallas_call | solution.py:193
  (4 shorter events, 0.1 us)
Async XLA Ops:
  0.0 1.1 %copy-start = (bf16[64,4096]{1,0:T(8,128)(2,1)S(1)}, bf16[64,4096]{1,0:T(8,128)(2,1)}, u32[]{:S(2)}) copy-start(bf16[64,4096]{1,0:T(8,128)(2,1)} %param.11) | copy-start | bytes 1572868
  1.1 17.4 %collective-permute-start.5 = (bf16[64,1024]{1,0:T(8,128)(2,1)S(1)}, bf16[64,1024]{1,0:T(8,128)(2,1)S(1)}, u32[]{:S(2)}, u32[]{:S(2)}) collective-permute-start(bf16[64,1024]{1,0:T(8,128)(2,1)S(1)} %constant_dynamic-slice_fusion.refs_0_), channel_id=1, source_target_pairs={{0,24},{4,28},{8,16},{12,20},{16,8},{20,12},{24,0},{28,4},{1,25},{... | collective-permute-start | bytes 393224 | tf_op jit(solution)/shard_map/ppermute | solution.py:220
  6.2 12.3 %collective-permute-start.4 = (bf16[64,1024]{1,0:T(8,128)(2,1)S(1)}, bf16[64,1024]{1,0:T(8,128)(2,1)S(1)}, u32[]{:S(2)}, u32[]{:S(2)}) collective-permute-start(bf16[64,1024]{1,0:T(8,128)(2,1)S(1)} %constant_dynamic-slice_fusion.refs_0_), channel_id=1, source_target_pairs={{0,16},{4,20},{8,24},{12,28},{16,0},{20,4},{24,8},{28,12},{1,17},{... | collective-permute-start | bytes 393224 | tf_op jit(solution)/shard_map/ppermute | solution.py:220
  6.2 12.3 %collective-permute-start.3 = (bf16[64,1024]{1,0:T(8,128)(2,1)S(1)}, bf16[64,1024]{1,0:T(8,128)(2,1)S(1)}, u32[]{:S(2)}, u32[]{:S(2)}) collective-permute-start(bf16[64,1024]{1,0:T(8,128)(2,1)S(1)} %constant_dynamic-slice_fusion.refs_0_), channel_id=1, source_target_pairs={{0,12},{4,8},{8,4},{12,0},{16,28},{20,24},{24,20},{28,16},{1,13},{... | collective-permute-start | bytes 393224 | tf_op jit(solution)/shard_map/ppermute | solution.py:220
  7.9 10.6 %collective-permute-start.2 = (bf16[64,1024]{1,0:T(8,128)(2,1)S(1)}, bf16[64,1024]{1,0:T(8,128)(2,1)S(1)}, u32[]{:S(2)}, u32[]{:S(2)}) collective-permute-start(bf16[64,1024]{1,0:T(8,128)(2,1)S(1)} %constant_dynamic-slice_fusion.refs_0_), channel_id=1, source_target_pairs={{0,8},{4,12},{8,0},{12,4},{16,24},{20,28},{24,16},{28,20},{1,9},{5... | collective-permute-start | bytes 393224 | tf_op jit(solution)/shard_map/ppermute | solution.py:220
  9.2 9.4 %collective-permute-start.1 = (bf16[64,1024]{1,0:T(8,128)(2,1)S(1)}, bf16[64,1024]{1,0:T(8,128)(2,1)S(1)}, u32[]{:S(2)}, u32[]{:S(2)}) collective-permute-start(bf16[64,1024]{1,0:T(8,128)(2,1)S(1)} %constant_dynamic-slice_fusion.refs_0_), channel_id=1, source_target_pairs={{0,4},{4,0},{8,12},{12,8},{16,20},{20,16},{24,28},{28,24},{1,5},{5... | collective-permute-start | bytes 393224 | tf_op jit(solution)/shard_map/ppermute | solution.py:220
  18.6 7.4 %collective-permute-start.7 = (bf16[128,1024]{1,0:T(8,128)(2,1)S(1)}, bf16[128,1024]{1,0:T(8,128)(2,1)S(1)}, u32[]{:S(2)}, u32[]{:S(2)}) collective-permute-start(bf16[128,1024]{1,0:T(8,128)(2,1)S(1)} %join.1.rest_0_), channel_id=1, source_target_pairs={{0,4},{4,0},{8,12},{12,8},{16,20},{20,16},{24,28},{28,24},{1,5},{5... | collective-permute-start | bytes 786440 | tf_op jit(solution)/shard_map/ppermute | solution.py:220
  20.2 1.3 %collective-permute-start = (bf16[2,128,128]{2,1,0:T(8,128)(2,1)S(1)}, bf16[2,128,128]{2,1,0:T(8,128)(2,1)S(1)}, u32[]{:S(2)}, u32[]{:S(2)}) collective-permute-start(bf16[2,128,128]{2,1,0:T(8,128)(2,1)S(1)} %get-tuple-element.19), channel_id=1, source_target_pairs={{0,1},{1,0},{2,3},{3,2},{4,5},{5,4},{6,7},{7,6},{8,9},{9,8},{10,11... | collective-permute-start | bytes 196616 | tf_op jit(solution)/shard_map/ppermute | solution.py:217
  21.5 4.0 %collective-permute-start.6 = (bf16[128,128]{1,0:T(8,128)(2,1)S(1)}, bf16[128,128]{1,0:T(8,128)(2,1)S(1)}, u32[]{:S(2)}, u32[]{:S(2)}) collective-permute-start(bf16[128,128]{1,0:T(8,128)(2,1)S(1)} %get-tuple-element.22), channel_id=1, source_target_pairs={{0,2},{1,3},{2,0},{3,1},{4,6},{5,7},{6,4},{7,5},{8,10},{9,11},{10,... | collective-permute-start | bytes 98312 | tf_op jit(solution)/shard_map/ppermute | solution.py:217
  26.3 3.8 %collective-permute-start.8 = (f32[2,4,640]{2,1,0:T(4,128)S(1)}, f32[2,4,640]{2,1,0:T(4,128)S(1)}, u32[]{:S(2)}, u32[]{:S(2)}) collective-permute-start(f32[2,4,640]{2,1,0:T(4,128)S(1)} %get-tuple-element.26), channel_id=1, source_target_pairs={{0,2},{1,3},{2,0},{3,1},{4,6},{5,7},{6,4},{7,5},{8,10},{9,11},{10,... | collective-permute-start | bytes 61448 | tf_op jit(solution)/shard_map/ppermute | solution.py:217
  30.2 1.2 %collective-permute-start.9 = (f32[4,640]{1,0:T(4,128)S(1)}, f32[4,640]{1,0:T(4,128)S(1)}, u32[]{:S(2)}, u32[]{:S(2)}) collective-permute-start(f32[4,640]{1,0:T(4,128)S(1)} %get-tuple-element.28), channel_id=1, source_target_pairs={{0,1},{1,0},{2,3},{3,2},{4,5},{5,4},{6,7},{7,6},{8,9},{9,8},{10,11... | collective-permute-start | bytes 30728 | tf_op jit(solution)/shard_map/ppermute | solution.py:217

commit v11 on v10

--- a/solution.py
+++ b/solution.py
@@ -19,20 +19,17 @@
 def grads_kernel(dims, lens_in, acts, grads, w_in, w_out, send, keep, *scratch):
     cands, tokens, width, groups = dims
     act_buf, grad_buf, win_raw, wout_raw, win, wout, lens, store, sems, wsems = scratch
-    half = cands // 2
-    chunks = half // 2
+    chunks = cands // 4
     rows = 4 * tokens
     loads = []
     for i in range(chunks):
         for side, (source, buf) in enumerate(((grads, grad_buf), (acts, act_buf))):
+            cuts = 2 if side == 1 and i == chunks - 1 else 1
             loads.append(
                 [
-                    pltpu.make_async_copy(
-                        source.at[pl.ds((2 * i + h * half) * tokens, rows // 2)],
-                        buf.at[pl.ds(i * rows + h * (rows // 2), rows // 2)],
-                        sems.at[side, 2 * i + h],
-                    )
-                    for h in range(2)
+                    pltpu.make_async_copy(source.at[part], buf.at[part], sems.at[side, i + h])
+                    for h in range(cuts)
+                    for part in [pl.ds(i * rows + h * (rows // 2), rows // cuts)]
                 ]
             )
 
@@ -51,7 +48,7 @@
     load_wout.start()
     load_win.start()
     load_lens.start()
-    for n in range(3):
+    for n in range(2):
         start(n)
     grp = lax.axis_index("grp")
     lines = width // groups
@@ -63,8 +60,7 @@
     def add_up(i, left, xp):
         used = []
         for j in range(4):
-            cand = 2 * i + j % 2 + (j // 2) * half
-            used.append(jnp.where(position < lens[cand], xp[j * tokens : (j + 1) * tokens], 0.0))
+            used.append(jnp.where(position < lens[4 * i + j], xp[j * tokens : (j + 1) * tokens], 0.0))
         wide = jnp.concatenate([jnp.concatenate(used, axis=0)] * 4, axis=1)
         right = jnp.where(diagonal, wide, 0.0).astype(BF16)
         sums = jnp.dot(left, right, preferred_element_type=F32)
@@ -81,7 +77,7 @@
     for i in range(chunks):
         part = pl.ds(i * rows, rows)
         wait(2 * i)
-        start(2 * i + 3)
+        start(2 * i + 2)
         gp = jnp.dot(grad_buf[part, :], wout[...], preferred_element_type=F32)
         if i == 0:
             win[...] = win_raw[...].T
@@ -90,7 +86,7 @@
         left = gp.T.astype(BF16)
         if i < chunks - 1:
             wait(2 * i + 1)
-            start(2 * i + 4)
+            start(2 * i + 3)
             xp = jnp.dot(act_buf[part, :], win[...], preferred_element_type=F32)
         else:
             pieces = []
@@ -152,23 +148,29 @@
         )
 
 
-def scores_kernel(dims, left, squares, near, passed, send, keep, place, result):
+def scores_kernel(dims, left, squares, near, late, passed, send, keep, place, result):
     blks, groups = dims
     rows = left[...]
     blk = lax.axis_index("blk")
     nq = near.shape[2]
     place[...] = near[...]
+    place[jnp.bitwise_xor(blk, 2)] = lax.dot_general(
+        rows, late[...], BY_ROWS, preferred_element_type=F32
+    )
     for n in range(blks // 2 - 2):
         place[jnp.bitwise_xor(blk, 2 * n + 5)] = lax.dot_general(
             rows, passed[n * nq : (n + 1) * nq, :], BY_ROWS, preferred_element_type=F32
         )
     scores = jnp.concatenate([place[b] for b in range(blks)], axis=1)
     width = blks * nq
-    owned = scores.shape[0] // groups
+    half = scores.shape[0] // 2
+    owned = half // groups
     for g in range(groups):
-        here = slice(g * owned, (g + 1) * owned)
-        result[g, :, :width] = scores[here]
-        result[g, :, width:] = squares[here, :]
+        for h in range(2):
+            here = slice(h * half + g * owned, h * half + (g + 1) * owned)
+            there = slice(h * owned, (h + 1) * owned)
+            result[g, there, :width] = scores[here]
+            result[g, there, width:] = squares[here, :]
     x = lax.axis_index("grp") // 2
     for core in range(2):
         send[core] = result[2 * (1 - x) + core]
@@ -221,7 +223,7 @@
 
     cut = lax.dynamic_slice(queries, (0, lax.axis_index("grp") * slice_width), (nq, slice_width))
     cut, lens = lax.optimization_barrier((cut, jnp.minimum(lengths, tokens * groups)))
-    pieces = [cut, blk_swap(cut, 1), blk_swap(cut, 2), blk_swap(cut, 3)]
+    pieces = [cut, blk_swap(cut, 1), blk_swap(cut, 3)]
     distant = [blk_swap(cut, 2 * k) for k in range(2, far)]
 
     rows = cands * tokens
@@ -240,7 +242,7 @@
             pltpu.VMEM((depth, width), BF16),
             pltpu.SMEM((cands,), jnp.int32),
             pltpu.VMEM((groups,) + piece, F32),
-            pltpu.SemaphoreType.DMA((2, cands // 2)),
+            pltpu.SemaphoreType.DMA((2, cands // 4 + 1)),
             pltpu.SemaphoreType.DMA((3,)),
         ],
         compiler_params=pltpu.CompilerParams(vmem_limit_bytes=GRANT * 2**10),
@@ -261,6 +263,8 @@
         (*pieces[1:], keep, *distant),
         name="join",
     )
+    late, joined = lax.optimization_barrier((cut, joined))
+    late = blk_swap(late, 2)
     send, kept = small(
         fold_kernel,
         [shape(piece, BF16), shape(piece, F32)],
@@ -276,7 +280,7 @@
         name="combine",
     )
     near = small(
-        functools.partial(near_kernel, [0, 1, 2, 3] + [2 * k for k in range(2, far)]),
+        functools.partial(near_kernel, [0, 1, 3] + [2 * k for k in range(2, far)]),
         shape((blks, cands, nq), F32),
         (own, *pieces, *distant),
         name="near",
@@ -285,7 +289,7 @@
     send, keep = small(
         functools.partial(scores_kernel, (blks, groups)),
         [shape((groups // 2,) + line, F32)] * 2,
-        (own, squares, near, passed),
+        (own, squares, near, late, passed),
         [pltpu.VMEM((blks, cands, nq), F32), pltpu.VMEM((groups,) + line, F32)],
         name="scores",
     )

time: 32.2 us -> 32.3 us (level)
  transfers between devices with their start and end apart: 10 -> 10, of which waited for: 5 -> 4; matrix products, arithmetic and copies ran while one was open for 0% -> 0% of each run, Pallas kernels for 29% -> 30%
where the time goes in v11:
time: 32.3 us; the launch traced here: 32.1 us
  starting transfers between devices  13.3 us (41%)
  Pallas kernels  10.5 us (33%)
  waiting for transfers between devices  7.16 us (22%)
  other arithmetic  0.72 us (2%)
  local copies, waits for them, and re-layouts  0.35 us (1%)
    ppermute x6, starting transfers between devices, blk_swap(): return lax.ppermute(x, 'blk', [(b, b ^ k) for b in range(blks)])  10.2 us
    pallas_call x1, Pallas kernels, on_device(): pl.pallas_call(functools.partial(grads_kernel, (cands, tokens, width, gro...  9.09 us
    ppermute x4, waiting for transfers between devices, grp_swap(): return lax.ppermute(x, 'grp', [(g, g ^ k) for g in range(groups)])  7.14 us
    ppermute x4, starting transfers between devices, grp_swap(): return lax.ppermute(x, 'grp', [(g, g ^ k) for g in range(groups)])  3.11 us
    pallas_call x7, Pallas kernels, small(): pl.pallas_call(kernel, out_shape=out_shape, in_specs=[VMEM] * len(operand...  1.43 us
    min x1, other arithmetic, on_device(): jnp.minimum(lengths, tokens * groups)  0.72 us
  transfers between devices with their start and end apart: 10, of which 4 were waited for; matrix products, arithmetic and copies ran while one was open for 0% of the time, Pallas kernels for 30%

profile of v11, /device:TPU:0, one launch (start us, length us, event | category | flops | bytes accessed | tf_op | source)
XLA Modules:
  0.0 32.1 jit_solution(1873224230384792172)
XLA Ops:
  0.0 0.0 copy-start
  0.0 0.7 %broadcast_minimum_fusion.lens_in = s32[16]{0:T(128)S(1)} fusion(s32[16]{0:T(128)} %param.10), kind=kLoop, calls=%fused_computation | loop fusion | flops 16 | bytes 128 | tf_op jit(solution)/shard_map/min | solution.py:225
  0.7 0.3 %copy-done = bf16[64,4096]{1,0:T(8,128)(2,1)S(1)} copy-done((bf16[64,4096]{1,0:T(8,128)(2,1)S(1)}, bf16[64,4096]{1,0:T(8,128)(2,1)}, u32[]{:S(2)}) %copy-start) | copy-done | bytes 524312
  1.1 5.1 %collective-permute-start.4 = (bf16[64,1024]{1,0:T(8,128)(2,1)S(1)}, bf16[64,1024]{1,0:T(8,128)(2,1)S(1)}, u32[]{:S(2)}, u32[]{:S(2)}) collective-permute-start(bf16[64,1024]{1,0:T(8,128)(2,1)S(1)} %constant_dynamic-slice_fusion.refs_0_), channel_id=1, source_target_pairs={{0,24},{4,28},{8,16},{12,20},{16,8},{20,12},{24,0},{28,4},{1,25},{... | collective-permute-start | bytes 393224 | tf_op jit(solution)/shard_map/ppermute | solution.py:222
  6.2 0.0 collective-permute-start.3
  6.2 1.7 %collective-permute-start.2 = (bf16[64,1024]{1,0:T(8,128)(2,1)S(1)}, bf16[64,1024]{1,0:T(8,128)(2,1)S(1)}, u32[]{:S(2)}, u32[]{:S(2)}) collective-permute-start(bf16[64,1024]{1,0:T(8,128)(2,1)S(1)} %constant_dynamic-slice_fusion.refs_0_), channel_id=1, source_target_pairs={{0,12},{4,8},{8,4},{12,0},{16,28},{20,24},{24,20},{28,16},{1,13},{... | collective-permute-start | bytes 393224 | tf_op jit(solution)/shard_map/ppermute | solution.py:222
  7.9 0.4 %collective-permute-start.1 = (bf16[64,1024]{1,0:T(8,128)(2,1)S(1)}, bf16[64,1024]{1,0:T(8,128)(2,1)S(1)}, u32[]{:S(2)}, u32[]{:S(2)}) collective-permute-start(bf16[64,1024]{1,0:T(8,128)(2,1)S(1)} %constant_dynamic-slice_fusion.refs_0_), channel_id=1, source_target_pairs={{0,4},{4,0},{8,12},{12,8},{16,20},{20,16},{24,28},{28,24},{1,5},{5... | collective-permute-start | bytes 393224 | tf_op jit(solution)/shard_map/ppermute | solution.py:222
  8.3 9.1 %grads.1 = (bf16[2,128,128]{2,1,0:T(8,128)(2,1)S(1)}, f32[2,128,128]{2,1,0:T(8,128)S(1)}) custom-call(s32[16]{0:T(128)S(1)} %broadcast_minimum_fusion.lens_in, bf16[1024,4096]{1,0:T(8,128)(2,1)} %bitcast.8, bf16[1024,4096]{1,0:T(8,128)(2,1)} %bitcast.9, bf16[64,4096]{1,0:T(8,128)(2,1)} %bitcast.10, bf16[64,4096]{1,0:T(8,128)(2,1)} %bitcast.11), custom_call_target="tpu_custom_call" | custom-call | flops 4294967296 | bytes 16777216 | tf_op jit(solution)/shard_map/grads/pallas_call | solution.py:231
  17.4 0.0 collective-permute-done.4.refs_4_
  17.4 0.0 collective-permute-done.3.refs_3_
  17.4 0.0 collective-permute-done.2.refs_1_.refs_2_
  17.4 0.0 collective-permute-done.1.refs_0_.refs_1_
  17.5 1.7 %collective-permute-start.7 = (bf16[128,1024]{1,0:T(8,128)(2,1)S(1)}, bf16[128,1024]{1,0:T(8,128)(2,1)S(1)}, u32[]{:S(2)}, u32[]{:S(2)}) collective-permute-start(bf16[128,1024]{1,0:T(8,128)(2,1)S(1)} %join.1.rest_0_), channel_id=1, source_target_pairs={{0,4},{4,0},{8,12},{12,8},{16,20},{20,16},{24,28},{28,24},{1,5},{5... | collective-permute-start | bytes 786440 | tf_op jit(solution)/shard_map/ppermute | solution.py:222
  19.2 1.2 %collective-permute-start.6 = (bf16[64,1024]{1,0:T(8,128)(2,1)S(1)}, bf16[64,1024]{1,0:T(8,128)(2,1)S(1)}, u32[]{:S(2)}, u32[]{:S(2)}) collective-permute-start(bf16[64,1024]{1,0:T(8,128)(2,1)S(1)} %constant_dynamic-slice_fusion.refs_0_), channel_id=1, source_target_pairs={{0,8},{4,12},{8,0},{12,4},{16,24},{20,28},{24,16},{28,20},{1,9},{5... | collective-permute-start | bytes 393224 | tf_op jit(solution)/shard_map/ppermute | solution.py:222
  20.4 0.0 collective-permute-start
  20.4 1.3 %collective-permute-done.came = bf16[2,128,128]{2,1,0:T(8,128)(2,1)S(1)} collective-permute-done((bf16[2,128,128]{2,1,0:T(8,128)(2,1)S(1)}, bf16[2,128,128]{2,1,0:T(8,128)(2,1)S(1)}, u32[]{:S(2)}, u32[]{:S(2)}) %collective-permute-start) | collective-permute-done | bytes 65568 | tf_op jit(solution)/shard_map/ppermute | solution.py:219
  21.7 1.6 %collective-permute-start.5 = (bf16[128,128]{1,0:T(8,128)(2,1)S(1)}, bf16[128,128]{1,0:T(8,128)(2,1)S(1)}, u32[]{:S(2)}, u32[]{:S(2)}) collective-permute-start(bf16[128,128]{1,0:T(8,128)(2,1)S(1)} %get-tuple-element.25), channel_id=1, source_target_pairs={{0,2},{1,3},{2,0},{3,1},{4,6},{5,7},{6,4},{7,5},{8,10},{9,11},{10,... | collective-permute-start | bytes 98312 | tf_op jit(solution)/shard_map/ppermute | solution.py:219
  23.3 2.4 %collective-permute-done.5.came = bf16[128,128]{1,0:T(8,128)(2,1)S(1)} collective-permute-done((bf16[128,128]{1,0:T(8,128)(2,1)S(1)}, bf16[128,128]{1,0:T(8,128)(2,1)S(1)}, u32[]{:S(2)}, u32[]{:S(2)}) %collective-permute-start.5) | collective-permute-done | bytes 32800 | tf_op jit(solution)/shard_map/ppermute | solution.py:219
  25.7 0.1 combine.1
  25.8 0.3 near.1
  26.1 0.0 collective-permute-done.6.late
  26.1 0.0 collective-permute-done.7.passed
  26.1 0.3 %scores.1 = (f32[2,4,640]{2,1,0:T(4,128)S(1)}, f32[2,4,640]{2,1,0:T(4,128)S(1)}) custom-call(bf16[16,1024]{1,0:T(8,128)(2,1)S(1)} %get-tuple-element.26.left, f32[16,128]{1,0:T(8,128)S(1)} %get-tuple-element.27.squares, f32[8,16,64]{2,1,0:T(8,128)S(1)} %near.1, bf16[64,1024]{1,0:T(8,128)(2,1)S(1)} %collective-permute-done.6.late, ...), custom_call_target="tpu_custom_call" | custom-call | tf_op jit(solution)/shard_map/scores/pallas_call | solution.py:195
  26.4 1.6 %collective-permute-start.8 = (f32[2,4,640]{2,1,0:T(4,128)S(1)}, f32[2,4,640]{2,1,0:T(4,128)S(1)}, u32[]{:S(2)}, u32[]{:S(2)}) collective-permute-start(f32[2,4,640]{2,1,0:T(4,128)S(1)} %get-tuple-element.30), channel_id=1, source_target_pairs={{0,2},{1,3},{2,0},{3,1},{4,6},{5,7},{6,4},{7,5},{8,10},{9,11},{10,... | collective-permute-start | bytes 61448 | tf_op jit(solution)/shard_map/ppermute | solution.py:219
  28.0 2.3 %collective-permute-done.8.came = f32[2,4,640]{2,1,0:T(4,128)S(1)} collective-permute-done((f32[2,4,640]{2,1,0:T(4,128)S(1)}, f32[2,4,640]{2,1,0:T(4,128)S(1)}, u32[]{:S(2)}, u32[]{:S(2)}) %collective-permute-start.8) | collective-permute-done | bytes 20512 | tf_op jit(solution)/shard_map/ppermute | solution.py:219
  30.3 0.0 collective-permute-start.9
  30.3 1.2 %collective-permute-done.9.came = f32[4,640]{1,0:T(4,128)S(1)} collective-permute-done((f32[4,640]{1,0:T(4,128)S(1)}, f32[4,640]{1,0:T(4,128)S(1)}, u32[]{:S(2)}, u32[]{:S(2)}) %collective-permute-start.9) | collective-permute-done | bytes 10272 | tf_op jit(solution)/shard_map/ppermute | solution.py:219
  31.4 0.7 %finish.1 = f32[4,512]{1,0:T(4,128)} custom-call(f32[4,640]{1,0:T(4,128)S(1)} %get-tuple-element.31.kept, f32[4,640]{1,0:T(4,128)S(1)} %collective-permute-done.9.came), custom_call_target="tpu_custom_call" | custom-call | tf_op jit(solution)/shard_map/finish/pallas_call | solution.py:195
  (4 shorter events, 0.1 us)
Async XLA Ops:
  0.0 1.1 %copy-start = (bf16[64,4096]{1,0:T(8,128)(2,1)S(1)}, bf16[64,4096]{1,0:T(8,128)(2,1)}, u32[]{:S(2)}) copy-start(bf16[64,4096]{1,0:T(8,128)(2,1)} %param.11) | copy-start | bytes 1572868
  1.1 16.3 %collective-permute-start.4 = (bf16[64,1024]{1,0:T(8,128)(2,1)S(1)}, bf16[64,1024]{1,0:T(8,128)(2,1)S(1)}, u32[]{:S(2)}, u32[]{:S(2)}) collective-permute-start(bf16[64,1024]{1,0:T(8,128)(2,1)S(1)} %constant_dynamic-slice_fusion.refs_0_), channel_id=1, source_target_pairs={{0,24},{4,28},{8,16},{12,20},{16,8},{20,12},{24,0},{28,4},{1,25},{... | collective-permute-start | bytes 393224 | tf_op jit(solution)/shard_map/ppermute | solution.py:222
  6.2 11.2 %collective-permute-start.3 = (bf16[64,1024]{1,0:T(8,128)(2,1)S(1)}, bf16[64,1024]{1,0:T(8,128)(2,1)S(1)}, u32[]{:S(2)}, u32[]{:S(2)}) collective-permute-start(bf16[64,1024]{1,0:T(8,128)(2,1)S(1)} %constant_dynamic-slice_fusion.refs_0_), channel_id=1, source_target_pairs={{0,16},{4,20},{8,24},{12,28},{16,0},{20,4},{24,8},{28,12},{1,17},{... | collective-permute-start | bytes 393224 | tf_op jit(solution)/shard_map/ppermute | solution.py:222
  6.2 11.2 %collective-permute-start.2 = (bf16[64,1024]{1,0:T(8,128)(2,1)S(1)}, bf16[64,1024]{1,0:T(8,128)(2,1)S(1)}, u32[]{:S(2)}, u32[]{:S(2)}) collective-permute-start(bf16[64,1024]{1,0:T(8,128)(2,1)S(1)} %constant_dynamic-slice_fusion.refs_0_), channel_id=1, source_target_pairs={{0,12},{4,8},{8,4},{12,0},{16,28},{20,24},{24,20},{28,16},{1,13},{... | collective-permute-start | bytes 393224 | tf_op jit(solution)/shard_map/ppermute | solution.py:222
  7.9 9.5 %collective-permute-start.1 = (bf16[64,1024]{1,0:T(8,128)(2,1)S(1)}, bf16[64,1024]{1,0:T(8,128)(2,1)S(1)}, u32[]{:S(2)}, u32[]{:S(2)}) collective-permute-start(bf16[64,1024]{1,0:T(8,128)(2,1)S(1)} %constant_dynamic-slice_fusion.refs_0_), channel_id=1, source_target_pairs={{0,4},{4,0},{8,12},{12,8},{16,20},{20,16},{24,28},{28,24},{1,5},{5... | collective-permute-start | bytes 393224 | tf_op jit(solution)/shard_map/ppermute | solution.py:222
  17.5 8.6 %collective-permute-start.7 = (bf16[128,1024]{1,0:T(8,128)(2,1)S(1)}, bf16[128,1024]{1,0:T(8,128)(2,1)S(1)}, u32[]{:S(2)}, u32[]{:S(2)}) collective-permute-start(bf16[128,1024]{1,0:T(8,128)(2,1)S(1)} %join.1.rest_0_), channel_id=1, source_target_pairs={{0,4},{4,0},{8,12},{12,8},{16,20},{20,16},{24,28},{28,24},{1,5},{5... | collective-permute-start | bytes 786440 | tf_op jit(solution)/shard_map/ppermute | solution.py:222
  19.2 6.9 %collective-permute-start.6 = (bf16[64,1024]{1,0:T(8,128)(2,1)S(1)}, bf16[64,1024]{1,0:T(8,128)(2,1)S(1)}, u32[]{:S(2)}, u32[]{:S(2)}) collective-permute-start(bf16[64,1024]{1,0:T(8,128)(2,1)S(1)} %constant_dynamic-slice_fusion.refs_0_), channel_id=1, source_target_pairs={{0,8},{4,12},{8,0},{12,4},{16,24},{20,28},{24,16},{28,20},{1,9},{5... | collective-permute-start | bytes 393224 | tf_op jit(solution)/shard_map/ppermute | solution.py:222
  20.4 1.3 %collective-permute-start = (bf16[2,128,128]{2,1,0:T(8,128)(2,1)S(1)}, bf16[2,128,128]{2,1,0:T(8,128)(2,1)S(1)}, u32[]{:S(2)}, u32[]{:S(2)}) collective-permute-start(bf16[2,128,128]{2,1,0:T(8,128)(2,1)S(1)} %get-tuple-element.21), channel_id=1, source_target_pairs={{0,1},{1,0},{2,3},{3,2},{4,5},{5,4},{6,7},{7,6},{8,9},{9,8},{10,11... | collective-permute-start | bytes 196616 | tf_op jit(solution)/shard_map/ppermute | solution.py:219
  21.7 4.0 %collective-permute-start.5 = (bf16[128,128]{1,0:T(8,128)(2,1)S(1)}, bf16[128,128]{1,0:T(8,128)(2,1)S(1)}, u32[]{:S(2)}, u32[]{:S(2)}) collective-permute-start(bf16[128,128]{1,0:T(8,128)(2,1)S(1)} %get-tuple-element.25), channel_id=1, source_target_pairs={{0,2},{1,3},{2,0},{3,1},{4,6},{5,7},{6,4},{7,5},{8,10},{9,11},{10,... | collective-permute-start | bytes 98312 | tf_op jit(solution)/shard_map/ppermute | solution.py:219
  26.4 3.8 %collective-permute-start.8 = (f32[2,4,640]{2,1,0:T(4,128)S(1)}, f32[2,4,640]{2,1,0:T(4,128)S(1)}, u32[]{:S(2)}, u32[]{:S(2)}) collective-permute-start(f32[2,4,640]{2,1,0:T(4,128)S(1)} %get-tuple-element.30), channel_id=1, source_target_pairs={{0,2},{1,3},{2,0},{3,1},{4,6},{5,7},{6,4},{7,5},{8,10},{9,11},{10,... | collective-permute-start | bytes 61448 | tf_op jit(solution)/shard_map/ppermute | solution.py:219
  30.3 1.2 %collective-permute-start.9 = (f32[4,640]{1,0:T(4,128)S(1)}, f32[4,640]{1,0:T(4,128)S(1)}, u32[]{:S(2)}, u32[]{:S(2)}) collective-permute-start(f32[4,640]{1,0:T(4,128)S(1)} %get-tuple-element.32), channel_id=1, source_target_pairs={{0,1},{1,0},{2,3},{3,2},{4,5},{5,4},{6,7},{7,6},{8,9},{9,8},{10,11... | collective-permute-start | bytes 30728 | tf_op jit(solution)/shard_map/ppermute | solution.py:219

commit v12 on v11

--- a/solution.py
+++ b/solution.py
@@ -24,12 +24,11 @@
     loads = []
     for i in range(chunks):
         for side, (source, buf) in enumerate(((grads, grad_buf), (acts, act_buf))):
-            cuts = 2 if side == 1 and i == chunks - 1 else 1
+            parts = [pl.ds((2 * i + h) * (rows // 2), rows // 2) for h in range(2)]
             loads.append(
                 [
-                    pltpu.make_async_copy(source.at[part], buf.at[part], sems.at[side, i + h])
-                    for h in range(cuts)
-                    for part in [pl.ds(i * rows + h * (rows // 2), rows // cuts)]
+                    pltpu.make_async_copy(source.at[part], buf.at[part], sems.at[side, 2 * i + h])
+                    for h, part in enumerate(parts)
                 ]
             )
 
@@ -48,7 +47,7 @@
     load_wout.start()
     load_win.start()
     load_lens.start()
-    for n in range(2):
+    for n in range(3):
         start(n)
     grp = lax.axis_index("grp")
     lines = width // groups
@@ -77,7 +76,7 @@
     for i in range(chunks):
         part = pl.ds(i * rows, rows)
         wait(2 * i)
-        start(2 * i + 2)
+        start(2 * i + 3)
         gp = jnp.dot(grad_buf[part, :], wout[...], preferred_element_type=F32)
         if i == 0:
             win[...] = win_raw[...].T
@@ -86,7 +85,7 @@
         left = gp.T.astype(BF16)
         if i < chunks - 1:
             wait(2 * i + 1)
-            start(2 * i + 3)
+            start(2 * i + 4)
             xp = jnp.dot(act_buf[part, :], win[...], preferred_element_type=F32)
         else:
             pieces = []
@@ -99,15 +98,15 @@
     add_up(*pending)
     core = lax.rem(grp, 2)
     for x in range(groups // 2):
-        send[x] = store[2 * x + 1 - core].astype(BF16)
+        send[x] = store[2 * x + 1 - core]
         keep[x] = store[2 * x + core]
 
 
 def fold_kernel(keep, came, *rest):
     send, kept = rest[-2:]
     x = lax.axis_index("grp") // 2
-    send[...] = (keep[1 - x] + came[1 - x].astype(F32)).astype(BF16)
-    kept[...] = keep[x] + came[x].astype(F32)
+    send[...] = (keep[1 - x] + came[1 - x]).astype(BF16)
+    kept[...] = keep[x] + came[x]
 
 
 def combine_kernel(dims, kept, came, *rest):
@@ -230,7 +229,7 @@
     piece = (cands // 2 * lines, 128)
     send, keep = pl.pallas_call(
         functools.partial(grads_kernel, (cands, tokens, width, groups)),
-        out_shape=[shape((groups // 2,) + piece, BF16), shape((groups // 2,) + piece, F32)],
+        out_shape=[shape((groups // 2,) + piece, F32)] * 2,
         in_specs=[ANY] * 5,
         out_specs=[VMEM] * 2,
         scratch_shapes=[
@@ -242,7 +241,7 @@
             pltpu.VMEM((depth, width), BF16),
             pltpu.SMEM((cands,), jnp.int32),
             pltpu.VMEM((groups,) + piece, F32),
-            pltpu.SemaphoreType.DMA((2, cands // 4 + 1)),
+            pltpu.SemaphoreType.DMA((2, cands // 2)),
             pltpu.SemaphoreType.DMA((3,)),
         ],
         compiler_params=pltpu.CompilerParams(vmem_limit_bytes=GRANT * 2**10),

time: 32.3 us -> 31 us (0.960)
  waiting for transfers between devices: 7.16 us -> 6.31 us
    ppermute x4, waiting for transfers between devices: 7.14 us -> 5.98 us  [grp_swap(): return lax.ppermute(x, 'grp', [(g, g ^ k) for g in range(groups)])]
  transfers between devices with their start and end apart: 10 -> 10, of which waited for: 4 -> 6; matrix products, arithmetic and copies ran while one was open for 0% -> 0% of each run, Pallas kernels for 30% -> 30%
where the time goes in v12:
time: 31 us; the launch traced here: 30.9 us
  starting transfers between devices  13.2 us (43%)
  Pallas kernels  10.2 us (33%)
  waiting for transfers between devices  6.31 us (20%)
  other arithmetic  0.72 us (2%)
  local copies, waits for them, and re-layouts  0.35 us (1%)
    ppermute x6, starting transfers between devices, blk_swap(): return lax.ppermute(x, 'blk', [(b, b ^ k) for b in range(blks)])  10.1 us
    pallas_call x1, Pallas kernels, on_device(): pl.pallas_call(functools.partial(grads_kernel, (cands, tokens, width, gro...  8.82 us
    ppermute x4, waiting for transfers between devices, grp_swap(): return lax.ppermute(x, 'grp', [(g, g ^ k) for g in range(groups)])  5.98 us
    ppermute x4, starting transfers between devices, grp_swap(): return lax.ppermute(x, 'grp', [(g, g ^ k) for g in range(groups)])  3.12 us
    pallas_call x7, Pallas kernels, small(): pl.pallas_call(kernel, out_shape=out_shape, in_specs=[VMEM] * len(operand...  1.4 us
    min x1, other arithmetic, on_device(): jnp.minimum(lengths, tokens * groups)  0.72 us
  transfers between devices with their start and end apart: 10, of which 6 were waited for; matrix products, arithmetic and copies ran while one was open for 0% of the time, Pallas kernels for 30%

profile of v12, /device:TPU:0, one launch (start us, length us, event | category | flops | bytes accessed | tf_op | source)
XLA Modules:
  0.0 30.9 jit_solution(15586240617454592514)
XLA Ops:
  0.0 0.0 copy-start
  0.0 0.7 %broadcast_minimum_fusion.lens_in = s32[16]{0:T(128)S(1)} fusion(s32[16]{0:T(128)} %param.10), kind=kLoop, calls=%fused_computation | loop fusion | flops 16 | bytes 128 | tf_op jit(solution)/shard_map/min | solution.py:224
  0.7 0.3 %copy-done = bf16[64,4096]{1,0:T(8,128)(2,1)S(1)} copy-done((bf16[64,4096]{1,0:T(8,128)(2,1)S(1)}, bf16[64,4096]{1,0:T(8,128)(2,1)}, u32[]{:S(2)}) %copy-start) | copy-done | bytes 524312
  1.1 5.1 %collective-permute-start.4 = (bf16[64,1024]{1,0:T(8,128)(2,1)S(1)}, bf16[64,1024]{1,0:T(8,128)(2,1)S(1)}, u32[]{:S(2)}, u32[]{:S(2)}) collective-permute-start(bf16[64,1024]{1,0:T(8,128)(2,1)S(1)} %constant_dynamic-slice_fusion.refs_0_), channel_id=1, source_target_pairs={{0,24},{4,28},{8,16},{12,20},{16,8},{20,12},{24,0},{28,4},{1,25},{... | collective-permute-start | bytes 393224 | tf_op jit(solution)/shard_map/ppermute | solution.py:221
  6.2 0.0 collective-permute-start.3
  6.2 1.7 %collective-permute-start.2 = (bf16[64,1024]{1,0:T(8,128)(2,1)S(1)}, bf16[64,1024]{1,0:T(8,128)(2,1)S(1)}, u32[]{:S(2)}, u32[]{:S(2)}) collective-permute-start(bf16[64,1024]{1,0:T(8,128)(2,1)S(1)} %constant_dynamic-slice_fusion.refs_0_), channel_id=1, source_target_pairs={{0,12},{4,8},{8,4},{12,0},{16,28},{20,24},{24,20},{28,16},{1,13},{... | collective-permute-start | bytes 393224 | tf_op jit(solution)/shard_map/ppermute | solution.py:221
  7.9 0.4 %collective-permute-start.1 = (bf16[64,1024]{1,0:T(8,128)(2,1)S(1)}, bf16[64,1024]{1,0:T(8,128)(2,1)S(1)}, u32[]{:S(2)}, u32[]{:S(2)}) collective-permute-start(bf16[64,1024]{1,0:T(8,128)(2,1)S(1)} %constant_dynamic-slice_fusion.refs_0_), channel_id=1, source_target_pairs={{0,4},{4,0},{8,12},{12,8},{16,20},{20,16},{24,28},{28,24},{1,5},{5... | collective-permute-start | bytes 393224 | tf_op jit(solution)/shard_map/ppermute | solution.py:221
  8.3 8.8 %grads.1 = (f32[2,128,128]{2,1,0:T(8,128)S(1)}, f32[2,128,128]{2,1,0:T(8,128)S(1)}) custom-call(s32[16]{0:T(128)S(1)} %broadcast_minimum_fusion.lens_in, bf16[1024,4096]{1,0:T(8,128)(2,1)} %bitcast.8, bf16[1024,4096]{1,0:T(8,128)(2,1)} %bitcast.9, bf16[64,4096]{1,0:T(8,128)(2,1)} %bitcast.10, bf16[64,4096]{1,0:T(8,128)(2,1)} %bitcast.11), custom_call_target="tpu_custom_call" | custom-call | flops 4294967296 | bytes 16777216 | tf_op jit(solution)/shard_map/grads/pallas_call | solution.py:230
  17.1 0.0 collective-permute-done.4.refs_4_
  17.1 0.1 collective-permute-done.3.refs_3_
  17.3 0.0 collective-permute-done.2.refs_1_.refs_2_
  17.3 0.0 collective-permute-done.1.refs_0_.refs_1_
  17.3 1.6 %collective-permute-start.7 = (bf16[128,1024]{1,0:T(8,128)(2,1)S(1)}, bf16[128,1024]{1,0:T(8,128)(2,1)S(1)}, u32[]{:S(2)}, u32[]{:S(2)}) collective-permute-start(bf16[128,1024]{1,0:T(8,128)(2,1)S(1)} %join.1.rest_0_), channel_id=1, source_target_pairs={{0,4},{4,0},{8,12},{12,8},{16,20},{20,16},{24,28},{28,24},{1,5},{5... | collective-permute-start | bytes 786440 | tf_op jit(solution)/shard_map/ppermute | solution.py:221
  18.9 0.0 collective-permute-start
  18.9 1.2 %collective-permute-start.6 = (bf16[64,1024]{1,0:T(8,128)(2,1)S(1)}, bf16[64,1024]{1,0:T(8,128)(2,1)S(1)}, u32[]{:S(2)}, u32[]{:S(2)}) collective-permute-start(bf16[64,1024]{1,0:T(8,128)(2,1)S(1)} %constant_dynamic-slice_fusion.refs_0_), channel_id=1, source_target_pairs={{0,8},{4,12},{8,0},{12,4},{16,24},{20,28},{24,16},{28,20},{1,9},{5... | collective-permute-start | bytes 393224 | tf_op jit(solution)/shard_map/ppermute | solution.py:221
  20.2 0.1 collective-permute-done.came
  20.3 1.6 %collective-permute-start.5 = (bf16[128,128]{1,0:T(8,128)(2,1)S(1)}, bf16[128,128]{1,0:T(8,128)(2,1)S(1)}, u32[]{:S(2)}, u32[]{:S(2)}) collective-permute-start(bf16[128,128]{1,0:T(8,128)(2,1)S(1)} %get-tuple-element.25), channel_id=1, source_target_pairs={{0,2},{1,3},{2,0},{3,1},{4,6},{5,7},{6,4},{7,5},{8,10},{9,11},{10,... | collective-permute-start | bytes 98312 | tf_op jit(solution)/shard_map/ppermute | solution.py:218
  21.9 2.4 %collective-permute-done.5.came = bf16[128,128]{1,0:T(8,128)(2,1)S(1)} collective-permute-done((bf16[128,128]{1,0:T(8,128)(2,1)S(1)}, bf16[128,128]{1,0:T(8,128)(2,1)S(1)}, u32[]{:S(2)}, u32[]{:S(2)}) %collective-permute-start.5) | collective-permute-done | bytes 32800 | tf_op jit(solution)/shard_map/ppermute | solution.py:218
  24.3 0.1 combine.1
  24.4 0.3 near.1
  24.6 0.2 collective-permute-done.6.late
  24.8 0.0 collective-permute-done.7.passed
  24.8 0.3 scores.1
  25.2 1.6 %collective-permute-start.8 = (f32[2,4,640]{2,1,0:T(4,128)S(1)}, f32[2,4,640]{2,1,0:T(4,128)S(1)}, u32[]{:S(2)}, u32[]{:S(2)}) collective-permute-start(f32[2,4,640]{2,1,0:T(4,128)S(1)} %get-tuple-element.30), channel_id=1, source_target_pairs={{0,2},{1,3},{2,0},{3,1},{4,6},{5,7},{6,4},{7,5},{8,10},{9,11},{10,... | collective-permute-start | bytes 61448 | tf_op jit(solution)/shard_map/ppermute | solution.py:218
  26.7 2.3 %collective-permute-done.8.came = f32[2,4,640]{2,1,0:T(4,128)S(1)} collective-permute-done((f32[2,4,640]{2,1,0:T(4,128)S(1)}, f32[2,4,640]{2,1,0:T(4,128)S(1)}, u32[]{:S(2)}, u32[]{:S(2)}) %collective-permute-start.8) | collective-permute-done | bytes 20512 | tf_op jit(solution)/shard_map/ppermute | solution.py:218
  29.0 0.0 collective-permute-start.9
  29.0 1.2 %collective-permute-done.9.came = f32[4,640]{1,0:T(4,128)S(1)} collective-permute-done((f32[4,640]{1,0:T(4,128)S(1)}, f32[4,640]{1,0:T(4,128)S(1)}, u32[]{:S(2)}, u32[]{:S(2)}) %collective-permute-start.9) | collective-permute-done | bytes 10272 | tf_op jit(solution)/shard_map/ppermute | solution.py:218
  30.2 0.7 %finish.1 = f32[4,512]{1,0:T(4,128)} custom-call(f32[4,640]{1,0:T(4,128)S(1)} %get-tuple-element.31.kept, f32[4,640]{1,0:T(4,128)S(1)} %collective-permute-done.9.came), custom_call_target="tpu_custom_call" | custom-call | tf_op jit(solution)/shard_map/finish/pallas_call | solution.py:194
  (4 shorter events, 0.0 us)
Async XLA Ops:
  0.0 1.1 %copy-start = (bf16[64,4096]{1,0:T(8,128)(2,1)S(1)}, bf16[64,4096]{1,0:T(8,128)(2,1)}, u32[]{:S(2)}) copy-start(bf16[64,4096]{1,0:T(8,128)(2,1)} %param.11) | copy-start | bytes 1572868
  1.1 16.1 %collective-permute-start.4 = (bf16[64,1024]{1,0:T(8,128)(2,1)S(1)}, bf16[64,1024]{1,0:T(8,128)(2,1)S(1)}, u32[]{:S(2)}, u32[]{:S(2)}) collective-permute-start(bf16[64,1024]{1,0:T(8,128)(2,1)S(1)} %constant_dynamic-slice_fusion.refs_0_), channel_id=1, source_target_pairs={{0,24},{4,28},{8,16},{12,20},{16,8},{20,12},{24,0},{28,4},{1,25},{... | collective-permute-start | bytes 393224 | tf_op jit(solution)/shard_map/ppermute | solution.py:221
  6.2 11.1 %collective-permute-start.3 = (bf16[64,1024]{1,0:T(8,128)(2,1)S(1)}, bf16[64,1024]{1,0:T(8,128)(2,1)S(1)}, u32[]{:S(2)}, u32[]{:S(2)}) collective-permute-start(bf16[64,1024]{1,0:T(8,128)(2,1)S(1)} %constant_dynamic-slice_fusion.refs_0_), channel_id=1, source_target_pairs={{0,16},{4,20},{8,24},{12,28},{16,0},{20,4},{24,8},{28,12},{1,17},{... | collective-permute-start | bytes 393224 | tf_op jit(solution)/shard_map/ppermute | solution.py:221
  6.2 11.1 %collective-permute-start.2 = (bf16[64,1024]{1,0:T(8,128)(2,1)S(1)}, bf16[64,1024]{1,0:T(8,128)(2,1)S(1)}, u32[]{:S(2)}, u32[]{:S(2)}) collective-permute-start(bf16[64,1024]{1,0:T(8,128)(2,1)S(1)} %constant_dynamic-slice_fusion.refs_0_), channel_id=1, source_target_pairs={{0,12},{4,8},{8,4},{12,0},{16,28},{20,24},{24,20},{28,16},{1,13},{... | collective-permute-start | bytes 393224 | tf_op jit(solution)/shard_map/ppermute | solution.py:221
  7.9 9.3 %collective-permute-start.1 = (bf16[64,1024]{1,0:T(8,128)(2,1)S(1)}, bf16[64,1024]{1,0:T(8,128)(2,1)S(1)}, u32[]{:S(2)}, u32[]{:S(2)}) collective-permute-start(bf16[64,1024]{1,0:T(8,128)(2,1)S(1)} %constant_dynamic-slice_fusion.refs_0_), channel_id=1, source_target_pairs={{0,4},{4,0},{8,12},{12,8},{16,20},{20,16},{24,28},{28,24},{1,5},{5... | collective-permute-start | bytes 393224 | tf_op jit(solution)/shard_map/ppermute | solution.py:221
  17.3 7.6 %collective-permute-start.7 = (bf16[128,1024]{1,0:T(8,128)(2,1)S(1)}, bf16[128,1024]{1,0:T(8,128)(2,1)S(1)}, u32[]{:S(2)}, u32[]{:S(2)}) collective-permute-start(bf16[128,1024]{1,0:T(8,128)(2,1)S(1)} %join.1.rest_0_), channel_id=1, source_target_pairs={{0,4},{4,0},{8,12},{12,8},{16,20},{20,16},{24,28},{28,24},{1,5},{5... | collective-permute-start | bytes 786440 | tf_op jit(solution)/shard_map/ppermute | solution.py:221
  18.9 1.3 %collective-permute-start = (f32[2,128,128]{2,1,0:T(8,128)S(1)}, f32[2,128,128]{2,1,0:T(8,128)S(1)}, u32[]{:S(2)}, u32[]{:S(2)}) collective-permute-start(f32[2,128,128]{2,1,0:T(8,128)S(1)} %get-tuple-element.21), channel_id=1, source_target_pairs={{0,1},{1,0},{2,3},{3,2},{4,5},{5,4},{6,7},{7,6},{8,9},{9,8},{10,11... | collective-permute-start | bytes 393224 | tf_op jit(solution)/shard_map/ppermute | solution.py:218
  18.9 5.9 %collective-permute-start.6 = (bf16[64,1024]{1,0:T(8,128)(2,1)S(1)}, bf16[64,1024]{1,0:T(8,128)(2,1)S(1)}, u32[]{:S(2)}, u32[]{:S(2)}) collective-permute-start(bf16[64,1024]{1,0:T(8,128)(2,1)S(1)} %constant_dynamic-slice_fusion.refs_0_), channel_id=1, source_target_pairs={{0,8},{4,12},{8,0},{12,4},{16,24},{20,28},{24,16},{28,20},{1,9},{5... | collective-permute-start | bytes 393224 | tf_op jit(solution)/shard_map/ppermute | solution.py:221
  20.3 4.0 %collective-permute-start.5 = (bf16[128,128]{1,0:T(8,128)(2,1)S(1)}, bf16[128,128]{1,0:T(8,128)(2,1)S(1)}, u32[]{:S(2)}, u32[]{:S(2)}) collective-permute-start(bf16[128,128]{1,0:T(8,128)(2,1)S(1)} %get-tuple-element.25), channel_id=1, source_target_pairs={{0,2},{1,3},{2,0},{3,1},{4,6},{5,7},{6,4},{7,5},{8,10},{9,11},{10,... | collective-permute-start | bytes 98312 | tf_op jit(solution)/shard_map/ppermute | solution.py:218
  25.2 3.8 %collective-permute-start.8 = (f32[2,4,640]{2,1,0:T(4,128)S(1)}, f32[2,4,640]{2,1,0:T(4,128)S(1)}, u32[]{:S(2)}, u32[]{:S(2)}) collective-permute-start(f32[2,4,640]{2,1,0:T(4,128)S(1)} %get-tuple-element.30), channel_id=1, source_target_pairs={{0,2},{1,3},{2,0},{3,1},{4,6},{5,7},{6,4},{7,5},{8,10},{9,11},{10,... | collective-permute-start | bytes 61448 | tf_op jit(solution)/shard_map/ppermute | solution.py:218
  29.0 1.2 %collective-permute-start.9 = (f32[4,640]{1,0:T(4,128)S(1)}, f32[4,640]{1,0:T(4,128)S(1)}, u32[]{:S(2)}, u32[]{:S(2)}) collective-permute-start(f32[4,640]{1,0:T(4,128)S(1)} %get-tuple-element.32), channel_id=1, source_target_pairs={{0,1},{1,0},{2,3},{3,2},{4,5},{5,4},{6,7},{7,6},{8,9},{9,8},{10,11... | collective-permute-start | bytes 30728 | tf_op jit(solution)/shard_map/ppermute | solution.py:218

commit v13 on v12

--- a/solution.py
+++ b/solution.py
@@ -147,8 +147,10 @@
         )
 
 
-def scores_kernel(dims, left, squares, near, late, passed, send, keep, place, result):
+def scores_kernel(dims, left, squares, near, late, passed, *rest):
     blks, groups = dims
+    outs = rest[:groups]
+    place, result = rest[groups:]
     rows = left[...]
     blk = lax.axis_index("blk")
     nq = near.shape[2]
@@ -170,20 +172,16 @@
             there = slice(h * owned, (h + 1) * owned)
             result[g, there, :width] = scores[here]
             result[g, there, width:] = squares[here, :]
-    x = lax.axis_index("grp") // 2
-    for core in range(2):
-        send[core] = result[2 * (1 - x) + core]
-        keep[core] = result[2 * x + core]
-
-
-def pass_kernel(keep, came, send, kept):
-    core = lax.rem(lax.axis_index("grp"), 2)
-    send[...] = keep[1 - core] + came[1 - core]
-    kept[...] = keep[core] + came[core]
-
-
-def finish_kernel(pdim, kept, came, out):
-    total = kept[...] + came[...]
+    grp = lax.axis_index("grp")
+    for k in range(groups):
+        outs[k][...] = result[jnp.bitwise_xor(grp, k)]
+
+
+def finish_kernel(pdim, *refs):
+    out = refs[-1]
+    total = refs[0][...]
+    for ref in refs[1:-1]:
+        total = total + ref[...]
     width = out.shape[1]
     mean = jnp.sum(total[:, width:], axis=1, keepdims=True) / pdim
     out[...] = total[:, :width] * lax.rsqrt(mean + EPS)
@@ -285,18 +283,17 @@
         name="near",
     )
     line = (owned, total_q + 128)
-    send, keep = small(
+    sums = small(
         functools.partial(scores_kernel, (blks, groups)),
-        [shape((groups // 2,) + line, F32)] * 2,
+        [shape(line, F32)] * groups,
         (own, squares, near, late, passed),
         [pltpu.VMEM((blks, cands, nq), F32), pltpu.VMEM((groups,) + line, F32)],
         name="scores",
     )
-    send, kept = small(pass_kernel, [shape(line, F32)] * 2, (keep, grp_swap(send, 2)), name="pass")
     return small(
         functools.partial(finish_kernel, pdim),
         shape((owned, total_q), F32),
-        (kept, grp_swap(send, 1)),
+        (sums[0], *[grp_swap(sums[k], k) for k in range(1, groups)]),
         name="finish",
     )
 

time: 31 us -> 30.7 us (level)
  waiting for transfers between devices: 6.31 us -> 5.64 us
  starting transfers between devices: 13.2 us -> 13.6 us
    ppermute x4 -> x5, waiting for transfers between devices: 5.98 us -> 5.32 us  [grp_swap(): return lax.ppermute(x, 'grp', [(g, g ^ k) for g in range(groups)])]
    ppermute x4 -> x5, starting transfers between devices: 3.12 us -> 3.49 us  [grp_swap(): return lax.ppermute(x, 'grp', [(g, g ^ k) for g in range(groups)])]
    pallas_call x7 -> x6, Pallas kernels: 1.4 us -> 1.4 us  [small(): pl.pallas_call(kernel, out_shape=out_shape, in_specs=[VMEM] * len(operand...]
  transfers between devices with their start and end apart: 10 -> 11, of which waited for: 6 -> 6; matrix products, arithmetic and copies ran while one was open for 0% -> 0% of each run, Pallas kernels for 30% -> 30%
where the time goes in v13:
time: 30.7 us; the launch traced here: 30.6 us
  starting transfers between devices  13.6 us (44%)
  Pallas kernels  10.2 us (33%)
  waiting for transfers between devices  5.64 us (18%)
  other arithmetic  0.72 us (2%)
  local copies, waits for them, and re-layouts  0.35 us (1%)
    ppermute x6, starting transfers between devices, blk_swap(): return lax.ppermute(x, 'blk', [(b, b ^ k) for b in range(blks)])  10.1 us
    pallas_call x1, Pallas kernels, on_device(): pl.pallas_call(functools.partial(grads_kernel, (cands, tokens, width, gro...  8.82 us
    ppermute x5, waiting for transfers between devices, grp_swap(): return lax.ppermute(x, 'grp', [(g, g ^ k) for g in range(groups)])  5.32 us
    ppermute x5, starting transfers between devices, grp_swap(): return lax.ppermute(x, 'grp', [(g, g ^ k) for g in range(groups)])  3.49 us
    pallas_call x6, Pallas kernels, small(): pl.pallas_call(kernel, out_shape=out_shape, in_specs=[VMEM] * len(operand...  1.4 us
    min x1, other arithmetic, on_device(): jnp.minimum(lengths, tokens * groups)  0.72 us
  transfers between devices with their start and end apart: 11, of which 6 were waited for; matrix products, arithmetic and copies ran while one was open for 0% of the time, Pallas kernels for 30%

profile of v13, /device:TPU:0, one launch (start us, length us, event | category | flops | bytes accessed | tf_op | source)
XLA Modules:
  0.0 30.6 jit_solution(143062998100924955)
XLA Ops:
  0.0 0.0 copy-start
  0.0 0.7 %broadcast_minimum_fusion.lens_in = s32[16]{0:T(128)S(1)} fusion(s32[16]{0:T(128)} %param.10), kind=kLoop, calls=%fused_computation | loop fusion | flops 16 | bytes 128 | tf_op jit(solution)/shard_map/min | solution.py:222
  0.7 0.3 %copy-done = bf16[64,4096]{1,0:T(8,128)(2,1)S(1)} copy-done((bf16[64,4096]{1,0:T(8,128)(2,1)S(1)}, bf16[64,4096]{1,0:T(8,128)(2,1)}, u32[]{:S(2)}) %copy-start) | copy-done | bytes 524312
  1.1 5.1 %collective-permute-start.4 = (bf16[64,1024]{1,0:T(8,128)(2,1)S(1)}, bf16[64,1024]{1,0:T(8,128)(2,1)S(1)}, u32[]{:S(2)}, u32[]{:S(2)}) collective-permute-start(bf16[64,1024]{1,0:T(8,128)(2,1)S(1)} %constant_dynamic-slice_fusion.refs_0_), channel_id=1, source_target_pairs={{0,24},{4,28},{8,16},{12,20},{16,8},{20,12},{24,0},{28,4},{1,25},{... | collective-permute-start | bytes 393224 | tf_op jit(solution)/shard_map/ppermute | solution.py:219
  6.2 0.0 collective-permute-start.3
  6.2 1.7 %collective-permute-start.2 = (bf16[64,1024]{1,0:T(8,128)(2,1)S(1)}, bf16[64,1024]{1,0:T(8,128)(2,1)S(1)}, u32[]{:S(2)}, u32[]{:S(2)}) collective-permute-start(bf16[64,1024]{1,0:T(8,128)(2,1)S(1)} %constant_dynamic-slice_fusion.refs_0_), channel_id=1, source_target_pairs={{0,12},{4,8},{8,4},{12,0},{16,28},{20,24},{24,20},{28,16},{1,13},{... | collective-permute-start | bytes 393224 | tf_op jit(solution)/shard_map/ppermute | solution.py:219
  7.9 0.4 %collective-permute-start.1 = (bf16[64,1024]{1,0:T(8,128)(2,1)S(1)}, bf16[64,1024]{1,0:T(8,128)(2,1)S(1)}, u32[]{:S(2)}, u32[]{:S(2)}) collective-permute-start(bf16[64,1024]{1,0:T(8,128)(2,1)S(1)} %constant_dynamic-slice_fusion.refs_0_), channel_id=1, source_target_pairs={{0,4},{4,0},{8,12},{12,8},{16,20},{20,16},{24,28},{28,24},{1,5},{5... | collective-permute-start | bytes 393224 | tf_op jit(solution)/shard_map/ppermute | solution.py:219
  8.3 8.8 %grads.1 = (f32[2,128,128]{2,1,0:T(8,128)S(1)}, f32[2,128,128]{2,1,0:T(8,128)S(1)}) custom-call(s32[16]{0:T(128)S(1)} %broadcast_minimum_fusion.lens_in, bf16[1024,4096]{1,0:T(8,128)(2,1)} %bitcast.8, bf16[1024,4096]{1,0:T(8,128)(2,1)} %bitcast.9, bf16[64,4096]{1,0:T(8,128)(2,1)} %bitcast.10, bf16[64,4096]{1,0:T(8,128)(2,1)} %bitcast.11), custom_call_target="tpu_custom_call" | custom-call | flops 4294967296 | bytes 16777216 | tf_op jit(solution)/shard_map/grads/pallas_call | solution.py:228
  17.1 0.0 collective-permute-done.4.refs_4_
  17.1 0.1 collective-permute-done.3.refs_3_
  17.3 0.0 collective-permute-done.2.refs_1_.refs_2_
  17.3 0.0 collective-permute-done.1.refs_0_.refs_1_
  17.3 1.6 %collective-permute-start.7 = (bf16[128,1024]{1,0:T(8,128)(2,1)S(1)}, bf16[128,1024]{1,0:T(8,128)(2,1)S(1)}, u32[]{:S(2)}, u32[]{:S(2)}) collective-permute-start(bf16[128,1024]{1,0:T(8,128)(2,1)S(1)} %join.1.rest_0_), channel_id=1, source_target_pairs={{0,4},{4,0},{8,12},{12,8},{16,20},{20,16},{24,28},{28,24},{1,5},{5... | collective-permute-start | bytes 786440 | tf_op jit(solution)/shard_map/ppermute | solution.py:219
  18.9 0.0 collective-permute-start
  18.9 1.2 %collective-permute-start.6 = (bf16[64,1024]{1,0:T(8,128)(2,1)S(1)}, bf16[64,1024]{1,0:T(8,128)(2,1)S(1)}, u32[]{:S(2)}, u32[]{:S(2)}) collective-permute-start(bf16[64,1024]{1,0:T(8,128)(2,1)S(1)} %constant_dynamic-slice_fusion.refs_0_), channel_id=1, source_target_pairs={{0,8},{4,12},{8,0},{12,4},{16,24},{20,28},{24,16},{28,20},{1,9},{5... | collective-permute-start | bytes 393224 | tf_op jit(solution)/shard_map/ppermute | solution.py:219
  20.2 0.1 collective-permute-done.came
  20.3 1.6 %collective-permute-start.5 = (bf16[128,128]{1,0:T(8,128)(2,1)S(1)}, bf16[128,128]{1,0:T(8,128)(2,1)S(1)}, u32[]{:S(2)}, u32[]{:S(2)}) collective-permute-start(bf16[128,128]{1,0:T(8,128)(2,1)S(1)} %get-tuple-element.25), channel_id=1, source_target_pairs={{0,2},{1,3},{2,0},{3,1},{4,6},{5,7},{6,4},{7,5},{8,10},{9,11},{10,... | collective-permute-start | bytes 98312 | tf_op jit(solution)/shard_map/ppermute | solution.py:216
  21.9 2.4 %collective-permute-done.5.came = bf16[128,128]{1,0:T(8,128)(2,1)S(1)} collective-permute-done((bf16[128,128]{1,0:T(8,128)(2,1)S(1)}, bf16[128,128]{1,0:T(8,128)(2,1)S(1)}, u32[]{:S(2)}, u32[]{:S(2)}) %collective-permute-start.5) | collective-permute-done | bytes 32800 | tf_op jit(solution)/shard_map/ppermute | solution.py:216
  24.3 0.1 combine.1
  24.4 0.3 near.1
  24.7 0.2 collective-permute-done.6.late
  24.8 0.0 collective-permute-done.7.passed
  24.8 0.3 %scores.1 = (f32[4,640]{1,0:T(4,128)S(1)}, f32[4,640]{1,0:T(4,128)S(1)}, f32[4,640]{1,0:T(4,128)S(1)}, f32[4,640]{1,0:T(4,128)S(1)}) custom-call(bf16[16,1024]{1,0:T(8,128)(2,1)S(1)} %get-tuple-element.26.left, f32[16,128]{1,0:T(8,128)S(1)} %get-tuple-element.27.squares, f32[8,16,64]{2,1,0:T(8,128)S(1)} %near.1, ...), custom_call_target="tpu_custom_call" | custom-call | tf_op jit(solution)/shard_map/scores/pallas_call | solution.py:192
  25.2 0.1 collective-permute-start.8
  25.2 1.6 %collective-permute-start.9 = (f32[4,640]{1,0:T(4,128)S(1)}, f32[4,640]{1,0:T(4,128)S(1)}, u32[]{:S(2)}, u32[]{:S(2)}) collective-permute-start(f32[4,640]{1,0:T(4,128)S(1)} %get-tuple-element.31), channel_id=1, source_target_pairs={{0,2},{1,3},{2,0},{3,1},{4,6},{5,7},{6,4},{7,5},{8,10},{9,11},{10,... | collective-permute-start | bytes 30728 | tf_op jit(solution)/shard_map/ppermute | solution.py:216
  26.8 0.3 collective-permute-start.10
  27.1 0.0 collective-permute-done.8.refs_1_
  27.1 1.9 %collective-permute-done.9.refs_2_ = f32[4,640]{1,0:T(4,128)S(1)} collective-permute-done((f32[4,640]{1,0:T(4,128)S(1)}, f32[4,640]{1,0:T(4,128)S(1)}, u32[]{:S(2)}, u32[]{:S(2)}) %collective-permute-start.9) | collective-permute-done | bytes 10272 | tf_op jit(solution)/shard_map/ppermute | solution.py:216
  29.0 0.9 %collective-permute-done.10.refs_3_ = f32[4,640]{1,0:T(4,128)S(1)} collective-permute-done((f32[4,640]{1,0:T(4,128)S(1)}, f32[4,640]{1,0:T(4,128)S(1)}, u32[]{:S(2)}, u32[]{:S(2)}) %collective-permute-start.10) | collective-permute-done | bytes 10272 | tf_op jit(solution)/shard_map/ppermute | solution.py:216
  29.9 0.7 %finish.1 = f32[4,512]{1,0:T(4,128)} custom-call(f32[4,640]{1,0:T(4,128)S(1)} %get-tuple-element.29.refs_0_, f32[4,640]{1,0:T(4,128)S(1)} %collective-permute-done.8.refs_1_, f32[4,640]{1,0:T(4,128)S(1)} %collective-permute-done.9.refs_2_, f32[4,640]{1,0:T(4,128)S(1)} %collective-permute-done.10.refs_3_), custom_call_target="tpu_custom_call" | custom-call | tf_op jit(solution)/shard_map/finish/pallas_call | solution.py:192
  (3 shorter events, 0.0 us)
Async XLA Ops:
  0.0 1.1 %copy-start = (bf16[64,4096]{1,0:T(8,128)(2,1)S(1)}, bf16[64,4096]{1,0:T(8,128)(2,1)}, u32[]{:S(2)}) copy-start(bf16[64,4096]{1,0:T(8,128)(2,1)} %param.11) | copy-start | bytes 1572868
  1.1 16.1 %collective-permute-start.4 = (bf16[64,1024]{1,0:T(8,128)(2,1)S(1)}, bf16[64,1024]{1,0:T(8,128)(2,1)S(1)}, u32[]{:S(2)}, u32[]{:S(2)}) collective-permute-start(bf16[64,1024]{1,0:T(8,128)(2,1)S(1)} %constant_dynamic-slice_fusion.refs_0_), channel_id=1, source_target_pairs={{0,24},{4,28},{8,16},{12,20},{16,8},{20,12},{24,0},{28,4},{1,25},{... | collective-permute-start | bytes 393224 | tf_op jit(solution)/shard_map/ppermute | solution.py:219
  6.2 11.1 %collective-permute-start.3 = (bf16[64,1024]{1,0:T(8,128)(2,1)S(1)}, bf16[64,1024]{1,0:T(8,128)(2,1)S(1)}, u32[]{:S(2)}, u32[]{:S(2)}) collective-permute-start(bf16[64,1024]{1,0:T(8,128)(2,1)S(1)} %constant_dynamic-slice_fusion.refs_0_), channel_id=1, source_target_pairs={{0,16},{4,20},{8,24},{12,28},{16,0},{20,4},{24,8},{28,12},{1,17},{... | collective-permute-start | bytes 393224 | tf_op jit(solution)/shard_map/ppermute | solution.py:219
  6.2 11.1 %collective-permute-start.2 = (bf16[64,1024]{1,0:T(8,128)(2,1)S(1)}, bf16[64,1024]{1,0:T(8,128)(2,1)S(1)}, u32[]{:S(2)}, u32[]{:S(2)}) collective-permute-start(bf16[64,1024]{1,0:T(8,128)(2,1)S(1)} %constant_dynamic-slice_fusion.refs_0_), channel_id=1, source_target_pairs={{0,12},{4,8},{8,4},{12,0},{16,28},{20,24},{24,20},{28,16},{1,13},{... | collective-permute-start | bytes 393224 | tf_op jit(solution)/shard_map/ppermute | solution.py:219
  7.9 9.3 %collective-permute-start.1 = (bf16[64,1024]{1,0:T(8,128)(2,1)S(1)}, bf16[64,1024]{1,0:T(8,128)(2,1)S(1)}, u32[]{:S(2)}, u32[]{:S(2)}) collective-permute-start(bf16[64,1024]{1,0:T(8,128)(2,1)S(1)} %constant_dynamic-slice_fusion.refs_0_), channel_id=1, source_target_pairs={{0,4},{4,0},{8,12},{12,8},{16,20},{20,16},{24,28},{28,24},{1,5},{5... | collective-permute-start | bytes 393224 | tf_op jit(solution)/shard_map/ppermute | solution.py:219
  17.3 7.6 %collective-permute-start.7 = (bf16[128,1024]{1,0:T(8,128)(2,1)S(1)}, bf16[128,1024]{1,0:T(8,128)(2,1)S(1)}, u32[]{:S(2)}, u32[]{:S(2)}) collective-permute-start(bf16[128,1024]{1,0:T(8,128)(2,1)S(1)} %join.1.rest_0_), channel_id=1, source_target_pairs={{0,4},{4,0},{8,12},{12,8},{16,20},{20,16},{24,28},{28,24},{1,5},{5... | collective-permute-start | bytes 786440 | tf_op jit(solution)/shard_map/ppermute | solution.py:219
  18.9 1.3 %collective-permute-start = (f32[2,128,128]{2,1,0:T(8,128)S(1)}, f32[2,128,128]{2,1,0:T(8,128)S(1)}, u32[]{:S(2)}, u32[]{:S(2)}) collective-permute-start(f32[2,128,128]{2,1,0:T(8,128)S(1)} %get-tuple-element.21), channel_id=1, source_target_pairs={{0,1},{1,0},{2,3},{3,2},{4,5},{5,4},{6,7},{7,6},{8,9},{9,8},{10,11... | collective-permute-start | bytes 393224 | tf_op jit(solution)/shard_map/ppermute | solution.py:216
  18.9 5.9 %collective-permute-start.6 = (bf16[64,1024]{1,0:T(8,128)(2,1)S(1)}, bf16[64,1024]{1,0:T(8,128)(2,1)S(1)}, u32[]{:S(2)}, u32[]{:S(2)}) collective-permute-start(bf16[64,1024]{1,0:T(8,128)(2,1)S(1)} %constant_dynamic-slice_fusion.refs_0_), channel_id=1, source_target_pairs={{0,8},{4,12},{8,0},{12,4},{16,24},{20,28},{24,16},{28,20},{1,9},{5... | collective-permute-start | bytes 393224 | tf_op jit(solution)/shard_map/ppermute | solution.py:219
  20.3 4.0 %collective-permute-start.5 = (bf16[128,128]{1,0:T(8,128)(2,1)S(1)}, bf16[128,128]{1,0:T(8,128)(2,1)S(1)}, u32[]{:S(2)}, u32[]{:S(2)}) collective-permute-start(bf16[128,128]{1,0:T(8,128)(2,1)S(1)} %get-tuple-element.25), channel_id=1, source_target_pairs={{0,2},{1,3},{2,0},{3,1},{4,6},{5,7},{6,4},{7,5},{8,10},{9,11},{10,... | collective-permute-start | bytes 98312 | tf_op jit(solution)/shard_map/ppermute | solution.py:216
  25.2 1.9 %collective-permute-start.8 = (f32[4,640]{1,0:T(4,128)S(1)}, f32[4,640]{1,0:T(4,128)S(1)}, u32[]{:S(2)}, u32[]{:S(2)}) collective-permute-start(f32[4,640]{1,0:T(4,128)S(1)} %get-tuple-element.30), channel_id=1, source_target_pairs={{0,1},{1,0},{2,3},{3,2},{4,5},{5,4},{6,7},{7,6},{8,9},{9,8},{10,11... | collective-permute-start | bytes 30728 | tf_op jit(solution)/shard_map/ppermute | solution.py:216
  25.2 3.7 %collective-permute-start.9 = (f32[4,640]{1,0:T(4,128)S(1)}, f32[4,640]{1,0:T(4,128)S(1)}, u32[]{:S(2)}, u32[]{:S(2)}) collective-permute-start(f32[4,640]{1,0:T(4,128)S(1)} %get-tuple-element.31), channel_id=1, source_target_pairs={{0,2},{1,3},{2,0},{3,1},{4,6},{5,7},{6,4},{7,5},{8,10},{9,11},{10,... | collective-permute-start | bytes 30728 | tf_op jit(solution)/shard_map/ppermute | solution.py:216
  26.8 3.1 %collective-permute-start.10 = (f32[4,640]{1,0:T(4,128)S(1)}, f32[4,640]{1,0:T(4,128)S(1)}, u32[]{:S(2)}, u32[]{:S(2)}) collective-permute-start(f32[4,640]{1,0:T(4,128)S(1)} %get-tuple-element.32), channel_id=1, source_target_pairs={{0,3},{1,2},{2,1},{3,0},{4,7},{5,6},{6,5},{7,4},{8,11},{9,10},{10,... | collective-permute-start | bytes 30728 | tf_op jit(solution)/shard_map/ppermute | solution.py:216

commit v14 on v13

--- a/solution.py
+++ b/solution.py
@@ -22,8 +22,8 @@
     chunks = cands // 4
     rows = 4 * tokens
     loads = []
-    for i in range(chunks):
-        for side, (source, buf) in enumerate(((grads, grad_buf), (acts, act_buf))):
+    for side, (source, buf) in enumerate(((grads, grad_buf), (acts, act_buf))):
+        for i in range(chunks):
             parts = [pl.ds((2 * i + h) * (rows // 2), rows // 2) for h in range(2)]
             loads.append(
                 [
@@ -72,29 +72,32 @@
     wout[...] = wout_raw[...].T
     load_win.wait()
     load_lens.wait()
-    pending = None
+    lefts = []
     for i in range(chunks):
+        wait(i)
+        start(i + 3)
         part = pl.ds(i * rows, rows)
-        wait(2 * i)
-        start(2 * i + 3)
         gp = jnp.dot(grad_buf[part, :], wout[...], preferred_element_type=F32)
         if i == 0:
             win[...] = win_raw[...].T
-        else:
-            add_up(*pending)
-        left = gp.T.astype(BF16)
+        lefts.append(gp.T.astype(BF16))
+    pending = None
+    for i in range(chunks):
         if i < chunks - 1:
-            wait(2 * i + 1)
-            start(2 * i + 4)
+            wait(chunks + i)
+            start(chunks + i + 3)
+            part = pl.ds(i * rows, rows)
             xp = jnp.dot(act_buf[part, :], win[...], preferred_element_type=F32)
         else:
             pieces = []
-            for h, load in enumerate(loads[2 * i + 1]):
+            for h, load in enumerate(loads[chunks + i]):
                 load.wait()
                 piece = pl.ds(i * rows + h * (rows // 2), rows // 2)
                 pieces.append(jnp.dot(act_buf[piece, :], win[...], preferred_element_type=F32))
             xp = jnp.concatenate(pieces, axis=0)
-        pending = (i, left, xp)
+        if pending is not None:
+            add_up(*pending)
+        pending = (i, lefts[i], xp)
     add_up(*pending)
     core = lax.rem(grp, 2)
     for x in range(groups // 2):
@@ -147,6 +150,10 @@
         )
 
 
+def late_kernel(left, queries, out):
+    out[...] = lax.dot_general(left[...], queries[...], BY_ROWS, preferred_element_type=F32)
+
+
 def scores_kernel(dims, left, squares, near, late, passed, *rest):
     blks, groups = dims
     outs = rest[:groups]
@@ -155,13 +162,10 @@
     blk = lax.axis_index("blk")
     nq = near.shape[2]
     place[...] = near[...]
-    place[jnp.bitwise_xor(blk, 2)] = lax.dot_general(
-        rows, late[...], BY_ROWS, preferred_element_type=F32
-    )
+    place[jnp.bitwise_xor(blk, 2)] = late[...]
+    handed = lax.dot_general(rows, passed[...], BY_ROWS, preferred_element_type=F32)
     for n in range(blks // 2 - 2):
-        place[jnp.bitwise_xor(blk, 2 * n + 5)] = lax.dot_general(
-            rows, passed[n * nq : (n + 1) * nq, :], BY_ROWS, preferred_element_type=F32
-        )
+        place[jnp.bitwise_xor(blk, 2 * n + 5)] = handed[:, n * nq : (n + 1) * nq]
     scores = jnp.concatenate([place[b] for b in range(blks)], axis=1)
     width = blks * nq
     half = scores.shape[0] // 2
@@ -282,6 +286,7 @@
         (own, *pieces, *distant),
         name="near",
     )
+    late = small(late_kernel, shape((cands, nq), F32), (own, late), name="late")
     line = (owned, total_q + 128)
     sums = small(
         functools.partial(scores_kernel, (blks, groups)),

time: 30.7 us -> 31 us (level)
    pallas_call x6 -> x7, Pallas kernels: 1.4 us -> 1.59 us  [small(): pl.pallas_call(kernel, out_shape=out_shape, in_specs=[VMEM] * len(operand...]
where the time goes in v14:
time: 31 us; the launch traced here: 30.8 us
  starting transfers between devices  13.6 us (44%)
  Pallas kernels  10.4 us (34%)
  waiting for transfers between devices  5.61 us (18%)
  other arithmetic  0.72 us (2%)
  local copies, waits for them, and re-layouts  0.35 us (1%)
    ppermute x6, starting transfers between devices, blk_swap(): return lax.ppermute(x, 'blk', [(b, b ^ k) for b in range(blks)])  10.1 us
    pallas_call x1, Pallas kernels, on_device(): pl.pallas_call(functools.partial(grads_kernel, (cands, tokens, width, gro...  8.85 us
    ppermute x5, waiting for transfers between devices, grp_swap(): return lax.ppermute(x, 'grp', [(g, g ^ k) for g in range(groups)])  5.32 us
    ppermute x5, starting transfers between devices, grp_swap(): return lax.ppermute(x, 'grp', [(g, g ^ k) for g in range(groups)])  3.49 us
    pallas_call x7, Pallas kernels, small(): pl.pallas_call(kernel, out_shape=out_shape, in_specs=[VMEM] * len(operand...  1.59 us
    min x1, other arithmetic, on_device(): jnp.minimum(lengths, tokens * groups)  0.72 us
  transfers between devices with their start and end apart: 11, of which 6 were waited for; matrix products, arithmetic and copies ran while one was open for 0% of the time, Pallas kernels for 30%

profile of v14, /device:TPU:0, one launch (start us, length us, event | category | flops | bytes accessed | tf_op | source)
XLA Modules:
  0.0 30.8 jit_solution(5983708800498567521)
XLA Ops:
  0.0 0.0 copy-start
  0.0 0.7 %broadcast_minimum_fusion.lens_in = s32[16]{0:T(128)S(1)} fusion(s32[16]{0:T(128)} %param.10), kind=kLoop, calls=%fused_computation | loop fusion | flops 16 | bytes 128 | tf_op jit(solution)/shard_map/min | solution.py:226
  0.7 0.3 %copy-done = bf16[64,4096]{1,0:T(8,128)(2,1)S(1)} copy-done((bf16[64,4096]{1,0:T(8,128)(2,1)S(1)}, bf16[64,4096]{1,0:T(8,128)(2,1)}, u32[]{:S(2)}) %copy-start) | copy-done | bytes 524312
  1.1 5.1 %collective-permute-start.4 = (bf16[64,1024]{1,0:T(8,128)(2,1)S(1)}, bf16[64,1024]{1,0:T(8,128)(2,1)S(1)}, u32[]{:S(2)}, u32[]{:S(2)}) collective-permute-start(bf16[64,1024]{1,0:T(8,128)(2,1)S(1)} %constant_dynamic-slice_fusion.refs_0_), channel_id=1, source_target_pairs={{0,24},{4,28},{8,16},{12,20},{16,8},{20,12},{24,0},{28,4},{1,25},{... | collective-permute-start | bytes 393224 | tf_op jit(solution)/shard_map/ppermute | solution.py:223
  6.2 0.0 collective-permute-start.3
  6.2 1.7 %collective-permute-start.2 = (bf16[64,1024]{1,0:T(8,128)(2,1)S(1)}, bf16[64,1024]{1,0:T(8,128)(2,1)S(1)}, u32[]{:S(2)}, u32[]{:S(2)}) collective-permute-start(bf16[64,1024]{1,0:T(8,128)(2,1)S(1)} %constant_dynamic-slice_fusion.refs_0_), channel_id=1, source_target_pairs={{0,12},{4,8},{8,4},{12,0},{16,28},{20,24},{24,20},{28,16},{1,13},{... | collective-permute-start | bytes 393224 | tf_op jit(solution)/shard_map/ppermute | solution.py:223
  7.9 0.4 %collective-permute-start.1 = (bf16[64,1024]{1,0:T(8,128)(2,1)S(1)}, bf16[64,1024]{1,0:T(8,128)(2,1)S(1)}, u32[]{:S(2)}, u32[]{:S(2)}) collective-permute-start(bf16[64,1024]{1,0:T(8,128)(2,1)S(1)} %constant_dynamic-slice_fusion.refs_0_), channel_id=1, source_target_pairs={{0,4},{4,0},{8,12},{12,8},{16,20},{20,16},{24,28},{28,24},{1,5},{5... | collective-permute-start | bytes 393224 | tf_op jit(solution)/shard_map/ppermute | solution.py:223
  8.3 8.9 %grads.1 = (f32[2,128,128]{2,1,0:T(8,128)S(1)}, f32[2,128,128]{2,1,0:T(8,128)S(1)}) custom-call(s32[16]{0:T(128)S(1)} %broadcast_minimum_fusion.lens_in, bf16[1024,4096]{1,0:T(8,128)(2,1)} %bitcast.8, bf16[1024,4096]{1,0:T(8,128)(2,1)} %bitcast.9, bf16[64,4096]{1,0:T(8,128)(2,1)} %bitcast.10, bf16[64,4096]{1,0:T(8,128)(2,1)} %bitcast.11), custom_call_target="tpu_custom_call" | custom-call | flops 4294967296 | bytes 16777216 | tf_op jit(solution)/shard_map/grads/pallas_call | solution.py:232
  17.2 0.0 collective-permute-done.4.refs_4_
  17.2 0.1 collective-permute-done.3.refs_3_
  17.3 0.0 collective-permute-done.2.refs_1_.refs_2_
  17.3 0.0 collective-permute-done.1.refs_0_.refs_1_
  17.3 1.7 %collective-permute-start.7 = (bf16[128,1024]{1,0:T(8,128)(2,1)S(1)}, bf16[128,1024]{1,0:T(8,128)(2,1)S(1)}, u32[]{:S(2)}, u32[]{:S(2)}) collective-permute-start(bf16[128,1024]{1,0:T(8,128)(2,1)S(1)} %join.1.rest_0_), channel_id=1, source_target_pairs={{0,4},{4,0},{8,12},{12,8},{16,20},{20,16},{24,28},{28,24},{1,5},{5... | collective-permute-start | bytes 786440 | tf_op jit(solution)/shard_map/ppermute | solution.py:223
  19.0 0.0 collective-permute-start
  19.0 1.2 %collective-permute-start.6 = (bf16[64,1024]{1,0:T(8,128)(2,1)S(1)}, bf16[64,1024]{1,0:T(8,128)(2,1)S(1)}, u32[]{:S(2)}, u32[]{:S(2)}) collective-permute-start(bf16[64,1024]{1,0:T(8,128)(2,1)S(1)} %constant_dynamic-slice_fusion.refs_0_), channel_id=1, source_target_pairs={{0,8},{4,12},{8,0},{12,4},{16,24},{20,28},{24,16},{28,20},{1,9},{5... | collective-permute-start | bytes 393224 | tf_op jit(solution)/shard_map/ppermute | solution.py:223
  20.2 0.1 collective-permute-done.came
  20.3 1.6 %collective-permute-start.5 = (bf16[128,128]{1,0:T(8,128)(2,1)S(1)}, bf16[128,128]{1,0:T(8,128)(2,1)S(1)}, u32[]{:S(2)}, u32[]{:S(2)}) collective-permute-start(bf16[128,128]{1,0:T(8,128)(2,1)S(1)} %get-tuple-element.25), channel_id=1, source_target_pairs={{0,2},{1,3},{2,0},{3,1},{4,6},{5,7},{6,4},{7,5},{8,10},{9,11},{10,... | collective-permute-start | bytes 98312 | tf_op jit(solution)/shard_map/ppermute | solution.py:220
  21.9 2.4 %collective-permute-done.5.came = bf16[128,128]{1,0:T(8,128)(2,1)S(1)} collective-permute-done((bf16[128,128]{1,0:T(8,128)(2,1)S(1)}, bf16[128,128]{1,0:T(8,128)(2,1)S(1)}, u32[]{:S(2)}, u32[]{:S(2)}) %collective-permute-start.5) | collective-permute-done | bytes 32800 | tf_op jit(solution)/shard_map/ppermute | solution.py:220
  24.3 0.1 combine.1
  24.4 0.3 near.1
  24.7 0.2 collective-permute-done.6.queries
  24.9 0.1 late.1
  25.0 0.0 collective-permute-done.7.passed
  25.0 0.4 %scores.1 = (f32[4,640]{1,0:T(4,128)S(1)}, f32[4,640]{1,0:T(4,128)S(1)}, f32[4,640]{1,0:T(4,128)S(1)}, f32[4,640]{1,0:T(4,128)S(1)}) custom-call(bf16[16,1024]{1,0:T(8,128)(2,1)S(1)} %get-tuple-element.26.left, f32[16,128]{1,0:T(8,128)S(1)} %get-tuple-element.27.squares, f32[8,16,64]{2,1,0:T(8,128)S(1)} %near.1, f32[16,64]{1,0:T(8,128)S(1)} %late.1, ...), custom_call_target="tpu_custom_call" | custom-call | tf_op jit(solution)/shard_map/scores/pallas_call | solution.py:196
  25.4 0.1 collective-permute-start.8
  25.5 1.6 %collective-permute-start.9 = (f32[4,640]{1,0:T(4,128)S(1)}, f32[4,640]{1,0:T(4,128)S(1)}, u32[]{:S(2)}, u32[]{:S(2)}) collective-permute-start(f32[4,640]{1,0:T(4,128)S(1)} %get-tuple-element.31), channel_id=1, source_target_pairs={{0,2},{1,3},{2,0},{3,1},{4,6},{5,7},{6,4},{7,5},{8,10},{9,11},{10,... | collective-permute-start | bytes 30728 | tf_op jit(solution)/shard_map/ppermute | solution.py:220
  27.0 0.3 collective-permute-start.10
  27.3 0.0 collective-permute-done.8.refs_1_
  27.3 1.9 %collective-permute-done.9.refs_2_ = f32[4,640]{1,0:T(4,128)S(1)} collective-permute-done((f32[4,640]{1,0:T(4,128)S(1)}, f32[4,640]{1,0:T(4,128)S(1)}, u32[]{:S(2)}, u32[]{:S(2)}) %collective-permute-start.9) | collective-permute-done | bytes 10272 | tf_op jit(solution)/shard_map/ppermute | solution.py:220
  29.2 0.9 %collective-permute-done.10.refs_3_ = f32[4,640]{1,0:T(4,128)S(1)} collective-permute-done((f32[4,640]{1,0:T(4,128)S(1)}, f32[4,640]{1,0:T(4,128)S(1)}, u32[]{:S(2)}, u32[]{:S(2)}) %collective-permute-start.10) | collective-permute-done | bytes 10272 | tf_op jit(solution)/shard_map/ppermute | solution.py:220
  30.1 0.7 %finish.1 = f32[4,512]{1,0:T(4,128)} custom-call(f32[4,640]{1,0:T(4,128)S(1)} %get-tuple-element.29.refs_0_, f32[4,640]{1,0:T(4,128)S(1)} %collective-permute-done.8.refs_1_, f32[4,640]{1,0:T(4,128)S(1)} %collective-permute-done.9.refs_2_, f32[4,640]{1,0:T(4,128)S(1)} %collective-permute-done.10.refs_3_), custom_call_target="tpu_custom_call" | custom-call | tf_op jit(solution)/shard_map/finish/pallas_call | solution.py:196
  (3 shorter events, 0.0 us)
Async XLA Ops:
  0.0 1.1 %copy-start = (bf16[64,4096]{1,0:T(8,128)(2,1)S(1)}, bf16[64,4096]{1,0:T(8,128)(2,1)}, u32[]{:S(2)}) copy-start(bf16[64,4096]{1,0:T(8,128)(2,1)} %param.11) | copy-start | bytes 1572868
  1.1 16.1 %collective-permute-start.4 = (bf16[64,1024]{1,0:T(8,128)(2,1)S(1)}, bf16[64,1024]{1,0:T(8,128)(2,1)S(1)}, u32[]{:S(2)}, u32[]{:S(2)}) collective-permute-start(bf16[64,1024]{1,0:T(8,128)(2,1)S(1)} %constant_dynamic-slice_fusion.refs_0_), channel_id=1, source_target_pairs={{0,24},{4,28},{8,16},{12,20},{16,8},{20,12},{24,0},{28,4},{1,25},{... | collective-permute-start | bytes 393224 | tf_op jit(solution)/shard_map/ppermute | solution.py:223
  6.2 11.1 %collective-permute-start.3 = (bf16[64,1024]{1,0:T(8,128)(2,1)S(1)}, bf16[64,1024]{1,0:T(8,128)(2,1)S(1)}, u32[]{:S(2)}, u32[]{:S(2)}) collective-permute-start(bf16[64,1024]{1,0:T(8,128)(2,1)S(1)} %constant_dynamic-slice_fusion.refs_0_), channel_id=1, source_target_pairs={{0,16},{4,20},{8,24},{12,28},{16,0},{20,4},{24,8},{28,12},{1,17},{... | collective-permute-start | bytes 393224 | tf_op jit(solution)/shard_map/ppermute | solution.py:223
  6.2 11.1 %collective-permute-start.2 = (bf16[64,1024]{1,0:T(8,128)(2,1)S(1)}, bf16[64,1024]{1,0:T(8,128)(2,1)S(1)}, u32[]{:S(2)}, u32[]{:S(2)}) collective-permute-start(bf16[64,1024]{1,0:T(8,128)(2,1)S(1)} %constant_dynamic-slice_fusion.refs_0_), channel_id=1, source_target_pairs={{0,12},{4,8},{8,4},{12,0},{16,28},{20,24},{24,20},{28,16},{1,13},{... | collective-permute-start | bytes 393224 | tf_op jit(solution)/shard_map/ppermute | solution.py:223
  7.9 9.3 %collective-permute-start.1 = (bf16[64,1024]{1,0:T(8,128)(2,1)S(1)}, bf16[64,1024]{1,0:T(8,128)(2,1)S(1)}, u32[]{:S(2)}, u32[]{:S(2)}) collective-permute-start(bf16[64,1024]{1,0:T(8,128)(2,1)S(1)} %constant_dynamic-slice_fusion.refs_0_), channel_id=1, source_target_pairs={{0,4},{4,0},{8,12},{12,8},{16,20},{20,16},{24,28},{28,24},{1,5},{5... | collective-permute-start | bytes 393224 | tf_op jit(solution)/shard_map/ppermute | solution.py:223
  17.3 7.7 %collective-permute-start.7 = (bf16[128,1024]{1,0:T(8,128)(2,1)S(1)}, bf16[128,1024]{1,0:T(8,128)(2,1)S(1)}, u32[]{:S(2)}, u32[]{:S(2)}) collective-permute-start(bf16[128,1024]{1,0:T(8,128)(2,1)S(1)} %join.1.rest_0_), channel_id=1, source_target_pairs={{0,4},{4,0},{8,12},{12,8},{16,20},{20,16},{24,28},{28,24},{1,5},{5... | collective-permute-start | bytes 786440 | tf_op jit(solution)/shard_map/ppermute | solution.py:223
  19.0 1.3 %collective-permute-start = (f32[2,128,128]{2,1,0:T(8,128)S(1)}, f32[2,128,128]{2,1,0:T(8,128)S(1)}, u32[]{:S(2)}, u32[]{:S(2)}) collective-permute-start(f32[2,128,128]{2,1,0:T(8,128)S(1)} %get-tuple-element.21), channel_id=1, source_target_pairs={{0,1},{1,0},{2,3},{3,2},{4,5},{5,4},{6,7},{7,6},{8,9},{9,8},{10,11... | collective-permute-start | bytes 393224 | tf_op jit(solution)/shard_map/ppermute | solution.py:220
  19.0 5.9 %collective-permute-start.6 = (bf16[64,1024]{1,0:T(8,128)(2,1)S(1)}, bf16[64,1024]{1,0:T(8,128)(2,1)S(1)}, u32[]{:S(2)}, u32[]{:S(2)}) collective-permute-start(bf16[64,1024]{1,0:T(8,128)(2,1)S(1)} %constant_dynamic-slice_fusion.refs_0_), channel_id=1, source_target_pairs={{0,8},{4,12},{8,0},{12,4},{16,24},{20,28},{24,16},{28,20},{1,9},{5... | collective-permute-start | bytes 393224 | tf_op jit(solution)/shard_map/ppermute | solution.py:223
  20.3 4.0 %collective-permute-start.5 = (bf16[128,128]{1,0:T(8,128)(2,1)S(1)}, bf16[128,128]{1,0:T(8,128)(2,1)S(1)}, u32[]{:S(2)}, u32[]{:S(2)}) collective-permute-start(bf16[128,128]{1,0:T(8,128)(2,1)S(1)} %get-tuple-element.25), channel_id=1, source_target_pairs={{0,2},{1,3},{2,0},{3,1},{4,6},{5,7},{6,4},{7,5},{8,10},{9,11},{10,... | collective-permute-start | bytes 98312 | tf_op jit(solution)/shard_map/ppermute | solution.py:220
  25.4 1.9 %collective-permute-start.8 = (f32[4,640]{1,0:T(4,128)S(1)}, f32[4,640]{1,0:T(4,128)S(1)}, u32[]{:S(2)}, u32[]{:S(2)}) collective-permute-start(f32[4,640]{1,0:T(4,128)S(1)} %get-tuple-element.30), channel_id=1, source_target_pairs={{0,1},{1,0},{2,3},{3,2},{4,5},{5,4},{6,7},{7,6},{8,9},{9,8},{10,11... | collective-permute-start | bytes 30728 | tf_op jit(solution)/shard_map/ppermute | solution.py:220
  25.5 3.7 %collective-permute-start.9 = (f32[4,640]{1,0:T(4,128)S(1)}, f32[4,640]{1,0:T(4,128)S(1)}, u32[]{:S(2)}, u32[]{:S(2)}) collective-permute-start(f32[4,640]{1,0:T(4,128)S(1)} %get-tuple-element.31), channel_id=1, source_target_pairs={{0,2},{1,3},{2,0},{3,1},{4,6},{5,7},{6,4},{7,5},{8,10},{9,11},{10,... | collective-permute-start | bytes 30728 | tf_op jit(solution)/shard_map/ppermute | solution.py:220
  27.0 3.1 %collective-permute-start.10 = (f32[4,640]{1,0:T(4,128)S(1)}, f32[4,640]{1,0:T(4,128)S(1)}, u32[]{:S(2)}, u32[]{:S(2)}) collective-permute-start(f32[4,640]{1,0:T(4,128)S(1)} %get-tuple-element.32), channel_id=1, source_target_pairs={{0,3},{1,2},{2,1},{3,0},{4,7},{5,6},{6,5},{7,4},{8,11},{9,10},{10,... | collective-permute-start | bytes 30728 | tf_op jit(solution)/shard_map/ppermute | solution.py:220

commit v15 on v13

--- a/solution.py
+++ b/solution.py
@@ -293,7 +293,7 @@
     return small(
         functools.partial(finish_kernel, pdim),
         shape((owned, total_q), F32),
-        (sums[0], *[grp_swap(sums[k], k) for k in range(1, groups)]),
+        (sums[0], *[grp_swap(sums[k], k) for k in range(groups - 1, 0, -1)]),
         name="finish",
     )
 

time: 30.7 us -> 30.6 us (level)
  no operation moved by 1% of the time
where the time goes in v15:
time: 30.6 us; the launch traced here: 30.4 us
  starting transfers between devices  13.6 us (44%)
  Pallas kernels  10.2 us (33%)
  waiting for transfers between devices  5.48 us (18%)
  other arithmetic  0.72 us (2%)
  local copies, waits for them, and re-layouts  0.35 us (1%)
    ppermute x6, starting transfers between devices, blk_swap(): return lax.ppermute(x, 'blk', [(b, b ^ k) for b in range(blks)])  10.1 us
    pallas_call x1, Pallas kernels, on_device(): pl.pallas_call(functools.partial(grads_kernel, (cands, tokens, width, gro...  8.82 us
    ppermute x5, waiting for transfers between devices, grp_swap(): return lax.ppermute(x, 'grp', [(g, g ^ k) for g in range(groups)])  5.16 us
    ppermute x5, starting transfers between devices, grp_swap(): return lax.ppermute(x, 'grp', [(g, g ^ k) for g in range(groups)])  3.49 us
    pallas_call x6, Pallas kernels, small(): pl.pallas_call(kernel, out_shape=out_shape, in_specs=[VMEM] * len(operand...  1.4 us
    min x1, other arithmetic, on_device(): jnp.minimum(lengths, tokens * groups)  0.72 us
  transfers between devices with their start and end apart: 11, of which 6 were waited for; matrix products, arithmetic and copies ran while one was open for 0% of the time, Pallas kernels for 30%

profile of v15, /device:TPU:0, one launch (start us, length us, event | category | flops | bytes accessed | tf_op | source)
XLA Modules:
  0.0 30.4 jit_solution(5425224175878520281)
XLA Ops:
  0.0 0.0 copy-start
  0.0 0.7 %broadcast_minimum_fusion.lens_in = s32[16]{0:T(128)S(1)} fusion(s32[16]{0:T(128)} %param.10), kind=kLoop, calls=%fused_computation | loop fusion | flops 16 | bytes 128 | tf_op jit(solution)/shard_map/min | solution.py:222
  0.7 0.3 %copy-done = bf16[64,4096]{1,0:T(8,128)(2,1)S(1)} copy-done((bf16[64,4096]{1,0:T(8,128)(2,1)S(1)}, bf16[64,4096]{1,0:T(8,128)(2,1)}, u32[]{:S(2)}) %copy-start) | copy-done | bytes 524312
  1.1 5.1 %collective-permute-start.4 = (bf16[64,1024]{1,0:T(8,128)(2,1)S(1)}, bf16[64,1024]{1,0:T(8,128)(2,1)S(1)}, u32[]{:S(2)}, u32[]{:S(2)}) collective-permute-start(bf16[64,1024]{1,0:T(8,128)(2,1)S(1)} %constant_dynamic-slice_fusion.refs_0_), channel_id=1, source_target_pairs={{0,24},{4,28},{8,16},{12,20},{16,8},{20,12},{24,0},{28,4},{1,25},{... | collective-permute-start | bytes 393224 | tf_op jit(solution)/shard_map/ppermute | solution.py:219
  6.2 0.0 collective-permute-start.3
  6.2 1.7 %collective-permute-start.2 = (bf16[64,1024]{1,0:T(8,128)(2,1)S(1)}, bf16[64,1024]{1,0:T(8,128)(2,1)S(1)}, u32[]{:S(2)}, u32[]{:S(2)}) collective-permute-start(bf16[64,1024]{1,0:T(8,128)(2,1)S(1)} %constant_dynamic-slice_fusion.refs_0_), channel_id=1, source_target_pairs={{0,12},{4,8},{8,4},{12,0},{16,28},{20,24},{24,20},{28,16},{1,13},{... | collective-permute-start | bytes 393224 | tf_op jit(solution)/shard_map/ppermute | solution.py:219
  7.9 0.4 %collective-permute-start.1 = (bf16[64,1024]{1,0:T(8,128)(2,1)S(1)}, bf16[64,1024]{1,0:T(8,128)(2,1)S(1)}, u32[]{:S(2)}, u32[]{:S(2)}) collective-permute-start(bf16[64,1024]{1,0:T(8,128)(2,1)S(1)} %constant_dynamic-slice_fusion.refs_0_), channel_id=1, source_target_pairs={{0,4},{4,0},{8,12},{12,8},{16,20},{20,16},{24,28},{28,24},{1,5},{5... | collective-permute-start | bytes 393224 | tf_op jit(solution)/shard_map/ppermute | solution.py:219
  8.3 8.8 %grads.1 = (f32[2,128,128]{2,1,0:T(8,128)S(1)}, f32[2,128,128]{2,1,0:T(8,128)S(1)}) custom-call(s32[16]{0:T(128)S(1)} %broadcast_minimum_fusion.lens_in, bf16[1024,4096]{1,0:T(8,128)(2,1)} %bitcast.8, bf16[1024,4096]{1,0:T(8,128)(2,1)} %bitcast.9, bf16[64,4096]{1,0:T(8,128)(2,1)} %bitcast.10, bf16[64,4096]{1,0:T(8,128)(2,1)} %bitcast.11), custom_call_target="tpu_custom_call" | custom-call | flops 4294967296 | bytes 16777216 | tf_op jit(solution)/shard_map/grads/pallas_call | solution.py:228
  17.1 0.0 collective-permute-done.4.refs_4_
  17.1 0.1 collective-permute-done.3.refs_3_
  17.3 0.0 collective-permute-done.2.refs_1_.refs_2_
  17.3 0.0 collective-permute-done.1.refs_0_.refs_1_
  17.3 1.6 %collective-permute-start.7 = (bf16[128,1024]{1,0:T(8,128)(2,1)S(1)}, bf16[128,1024]{1,0:T(8,128)(2,1)S(1)}, u32[]{:S(2)}, u32[]{:S(2)}) collective-permute-start(bf16[128,1024]{1,0:T(8,128)(2,1)S(1)} %join.1.rest_0_), channel_id=1, source_target_pairs={{0,4},{4,0},{8,12},{12,8},{16,20},{20,16},{24,28},{28,24},{1,5},{5... | collective-permute-start | bytes 786440 | tf_op jit(solution)/shard_map/ppermute | solution.py:219
  18.9 0.0 collective-permute-start
  18.9 1.2 %collective-permute-start.6 = (bf16[64,1024]{1,0:T(8,128)(2,1)S(1)}, bf16[64,1024]{1,0:T(8,128)(2,1)S(1)}, u32[]{:S(2)}, u32[]{:S(2)}) collective-permute-start(bf16[64,1024]{1,0:T(8,128)(2,1)S(1)} %constant_dynamic-slice_fusion.refs_0_), channel_id=1, source_target_pairs={{0,8},{4,12},{8,0},{12,4},{16,24},{20,28},{24,16},{28,20},{1,9},{5... | collective-permute-start | bytes 393224 | tf_op jit(solution)/shard_map/ppermute | solution.py:219
  20.2 0.1 collective-permute-done.came
  20.3 1.6 %collective-permute-start.5 = (bf16[128,128]{1,0:T(8,128)(2,1)S(1)}, bf16[128,128]{1,0:T(8,128)(2,1)S(1)}, u32[]{:S(2)}, u32[]{:S(2)}) collective-permute-start(bf16[128,128]{1,0:T(8,128)(2,1)S(1)} %get-tuple-element.25), channel_id=1, source_target_pairs={{0,2},{1,3},{2,0},{3,1},{4,6},{5,7},{6,4},{7,5},{8,10},{9,11},{10,... | collective-permute-start | bytes 98312 | tf_op jit(solution)/shard_map/ppermute | solution.py:216
  21.9 2.4 %collective-permute-done.5.came = bf16[128,128]{1,0:T(8,128)(2,1)S(1)} collective-permute-done((bf16[128,128]{1,0:T(8,128)(2,1)S(1)}, bf16[128,128]{1,0:T(8,128)(2,1)S(1)}, u32[]{:S(2)}, u32[]{:S(2)}) %collective-permute-start.5) | collective-permute-done | bytes 32800 | tf_op jit(solution)/shard_map/ppermute | solution.py:216
  24.3 0.1 combine.1
  24.4 0.3 near.1
  24.7 0.2 collective-permute-done.6.late
  24.8 0.0 collective-permute-done.7.passed
  24.8 0.3 %scores.1 = (f32[4,640]{1,0:T(4,128)S(1)}, f32[4,640]{1,0:T(4,128)S(1)}, f32[4,640]{1,0:T(4,128)S(1)}, f32[4,640]{1,0:T(4,128)S(1)}) custom-call(bf16[16,1024]{1,0:T(8,128)(2,1)S(1)} %get-tuple-element.26.left, f32[16,128]{1,0:T(8,128)S(1)} %get-tuple-element.27.squares, f32[8,16,64]{2,1,0:T(8,128)S(1)} %near.1, ...), custom_call_target="tpu_custom_call" | custom-call | tf_op jit(solution)/shard_map/scores/pallas_call | solution.py:192
  25.2 0.9 %collective-permute-start.8 = (f32[4,640]{1,0:T(4,128)S(1)}, f32[4,640]{1,0:T(4,128)S(1)}, u32[]{:S(2)}, u32[]{:S(2)}) collective-permute-start(f32[4,640]{1,0:T(4,128)S(1)} %get-tuple-element.30), channel_id=1, source_target_pairs={{0,3},{1,2},{2,1},{3,0},{4,7},{5,6},{6,5},{7,4},{8,11},{9,10},{10,... | collective-permute-start | bytes 30728 | tf_op jit(solution)/shard_map/ppermute | solution.py:216
  26.0 0.7 %collective-permute-start.9 = (f32[4,640]{1,0:T(4,128)S(1)}, f32[4,640]{1,0:T(4,128)S(1)}, u32[]{:S(2)}, u32[]{:S(2)}) collective-permute-start(f32[4,640]{1,0:T(4,128)S(1)} %get-tuple-element.31), channel_id=1, source_target_pairs={{0,2},{1,3},{2,0},{3,1},{4,6},{5,7},{6,4},{7,5},{8,10},{9,11},{10,... | collective-permute-start | bytes 30728 | tf_op jit(solution)/shard_map/ppermute | solution.py:216
  26.8 0.3 collective-permute-start.10
  27.1 1.3 %collective-permute-done.8.refs_1_ = f32[4,640]{1,0:T(4,128)S(1)} collective-permute-done((f32[4,640]{1,0:T(4,128)S(1)}, f32[4,640]{1,0:T(4,128)S(1)}, u32[]{:S(2)}, u32[]{:S(2)}) %collective-permute-start.8) | collective-permute-done | bytes 10272 | tf_op jit(solution)/shard_map/ppermute | solution.py:216
  28.4 1.3 %collective-permute-done.9.refs_2_ = f32[4,640]{1,0:T(4,128)S(1)} collective-permute-done((f32[4,640]{1,0:T(4,128)S(1)}, f32[4,640]{1,0:T(4,128)S(1)}, u32[]{:S(2)}, u32[]{:S(2)}) %collective-permute-start.9) | collective-permute-done | bytes 10272 | tf_op jit(solution)/shard_map/ppermute | solution.py:216
  29.7 0.0 collective-permute-done.10.refs_3_
  29.7 0.7 %finish.1 = f32[4,512]{1,0:T(4,128)} custom-call(f32[4,640]{1,0:T(4,128)S(1)} %get-tuple-element.29.refs_0_, f32[4,640]{1,0:T(4,128)S(1)} %collective-permute-done.8.refs_1_, f32[4,640]{1,0:T(4,128)S(1)} %collective-permute-done.9.refs_2_, f32[4,640]{1,0:T(4,128)S(1)} %collective-permute-done.10.refs_3_), custom_call_target="tpu_custom_call" | custom-call | tf_op jit(solution)/shard_map/finish/pallas_call | solution.py:192
  (3 shorter events, 0.0 us)
Async XLA Ops:
  0.0 1.1 %copy-start = (bf16[64,4096]{1,0:T(8,128)(2,1)S(1)}, bf16[64,4096]{1,0:T(8,128)(2,1)}, u32[]{:S(2)}) copy-start(bf16[64,4096]{1,0:T(8,128)(2,1)} %param.11) | copy-start | bytes 1572868
  1.1 16.1 %collective-permute-start.4 = (bf16[64,1024]{1,0:T(8,128)(2,1)S(1)}, bf16[64,1024]{1,0:T(8,128)(2,1)S(1)}, u32[]{:S(2)}, u32[]{:S(2)}) collective-permute-start(bf16[64,1024]{1,0:T(8,128)(2,1)S(1)} %constant_dynamic-slice_fusion.refs_0_), channel_id=1, source_target_pairs={{0,24},{4,28},{8,16},{12,20},{16,8},{20,12},{24,0},{28,4},{1,25},{... | collective-permute-start | bytes 393224 | tf_op jit(solution)/shard_map/ppermute | solution.py:219
  6.2 11.1 %collective-permute-start.3 = (bf16[64,1024]{1,0:T(8,128)(2,1)S(1)}, bf16[64,1024]{1,0:T(8,128)(2,1)S(1)}, u32[]{:S(2)}, u32[]{:S(2)}) collective-permute-start(bf16[64,1024]{1,0:T(8,128)(2,1)S(1)} %constant_dynamic-slice_fusion.refs_0_), channel_id=1, source_target_pairs={{0,16},{4,20},{8,24},{12,28},{16,0},{20,4},{24,8},{28,12},{1,17},{... | collective-permute-start | bytes 393224 | tf_op jit(solution)/shard_map/ppermute | solution.py:219
  6.2 11.1 %collective-permute-start.2 = (bf16[64,1024]{1,0:T(8,128)(2,1)S(1)}, bf16[64,1024]{1,0:T(8,128)(2,1)S(1)}, u32[]{:S(2)}, u32[]{:S(2)}) collective-permute-start(bf16[64,1024]{1,0:T(8,128)(2,1)S(1)} %constant_dynamic-slice_fusion.refs_0_), channel_id=1, source_target_pairs={{0,12},{4,8},{8,4},{12,0},{16,28},{20,24},{24,20},{28,16},{1,13},{... | collective-permute-start | bytes 393224 | tf_op jit(solution)/shard_map/ppermute | solution.py:219
  7.9 9.3 %collective-permute-start.1 = (bf16[64,1024]{1,0:T(8,128)(2,1)S(1)}, bf16[64,1024]{1,0:T(8,128)(2,1)S(1)}, u32[]{:S(2)}, u32[]{:S(2)}) collective-permute-start(bf16[64,1024]{1,0:T(8,128)(2,1)S(1)} %constant_dynamic-slice_fusion.refs_0_), channel_id=1, source_target_pairs={{0,4},{4,0},{8,12},{12,8},{16,20},{20,16},{24,28},{28,24},{1,5},{5... | collective-permute-start | bytes 393224 | tf_op jit(solution)/shard_map/ppermute | solution.py:219
  17.3 7.6 %collective-permute-start.7 = (bf16[128,1024]{1,0:T(8,128)(2,1)S(1)}, bf16[128,1024]{1,0:T(8,128)(2,1)S(1)}, u32[]{:S(2)}, u32[]{:S(2)}) collective-permute-start(bf16[128,1024]{1,0:T(8,128)(2,1)S(1)} %join.1.rest_0_), channel_id=1, source_target_pairs={{0,4},{4,0},{8,12},{12,8},{16,20},{20,16},{24,28},{28,24},{1,5},{5... | collective-permute-start | bytes 786440 | tf_op jit(solution)/shard_map/ppermute | solution.py:219
  18.9 1.3 %collective-permute-start = (f32[2,128,128]{2,1,0:T(8,128)S(1)}, f32[2,128,128]{2,1,0:T(8,128)S(1)}, u32[]{:S(2)}, u32[]{:S(2)}) collective-permute-start(f32[2,128,128]{2,1,0:T(8,128)S(1)} %get-tuple-element.21), channel_id=1, source_target_pairs={{0,1},{1,0},{2,3},{3,2},{4,5},{5,4},{6,7},{7,6},{8,9},{9,8},{10,11... | collective-permute-start | bytes 393224 | tf_op jit(solution)/shard_map/ppermute | solution.py:216
  18.9 5.9 %collective-permute-start.6 = (bf16[64,1024]{1,0:T(8,128)(2,1)S(1)}, bf16[64,1024]{1,0:T(8,128)(2,1)S(1)}, u32[]{:S(2)}, u32[]{:S(2)}) collective-permute-start(bf16[64,1024]{1,0:T(8,128)(2,1)S(1)} %constant_dynamic-slice_fusion.refs_0_), channel_id=1, source_target_pairs={{0,8},{4,12},{8,0},{12,4},{16,24},{20,28},{24,16},{28,20},{1,9},{5... | collective-permute-start | bytes 393224 | tf_op jit(solution)/shard_map/ppermute | solution.py:219
  20.3 4.0 %collective-permute-start.5 = (bf16[128,128]{1,0:T(8,128)(2,1)S(1)}, bf16[128,128]{1,0:T(8,128)(2,1)S(1)}, u32[]{:S(2)}, u32[]{:S(2)}) collective-permute-start(bf16[128,128]{1,0:T(8,128)(2,1)S(1)} %get-tuple-element.25), channel_id=1, source_target_pairs={{0,2},{1,3},{2,0},{3,1},{4,6},{5,7},{6,4},{7,5},{8,10},{9,11},{10,... | collective-permute-start | bytes 98312 | tf_op jit(solution)/shard_map/ppermute | solution.py:216
  25.2 3.2 %collective-permute-start.8 = (f32[4,640]{1,0:T(4,128)S(1)}, f32[4,640]{1,0:T(4,128)S(1)}, u32[]{:S(2)}, u32[]{:S(2)}) collective-permute-start(f32[4,640]{1,0:T(4,128)S(1)} %get-tuple-element.30), channel_id=1, source_target_pairs={{0,3},{1,2},{2,1},{3,0},{4,7},{5,6},{6,5},{7,4},{8,11},{9,10},{10,... | collective-permute-start | bytes 30728 | tf_op jit(solution)/shard_map/ppermute | solution.py:216
  26.0 3.7 %collective-permute-start.9 = (f32[4,640]{1,0:T(4,128)S(1)}, f32[4,640]{1,0:T(4,128)S(1)}, u32[]{:S(2)}, u32[]{:S(2)}) collective-permute-start(f32[4,640]{1,0:T(4,128)S(1)} %get-tuple-element.31), channel_id=1, source_target_pairs={{0,2},{1,3},{2,0},{3,1},{4,6},{5,7},{6,4},{7,5},{8,10},{9,11},{10,... | collective-permute-start | bytes 30728 | tf_op jit(solution)/shard_map/ppermute | solution.py:216
  26.8 2.9 %collective-permute-start.10 = (f32[4,640]{1,0:T(4,128)S(1)}, f32[4,640]{1,0:T(4,128)S(1)}, u32[]{:S(2)}, u32[]{:S(2)}) collective-permute-start(f32[4,640]{1,0:T(4,128)S(1)} %get-tuple-element.32), channel_id=1, source_target_pairs={{0,1},{1,0},{2,3},{3,2},{4,5},{5,4},{6,7},{7,6},{8,9},{9,8},{10,11... | collective-permute-start | bytes 30728 | tf_op jit(solution)/shard_map/ppermute | solution.py:216

commit v16 on v15

--- a/solution.py
+++ b/solution.py
@@ -177,16 +177,6 @@
         outs[k][...] = result[jnp.bitwise_xor(grp, k)]
 
 
-def finish_kernel(pdim, *refs):
-    out = refs[-1]
-    total = refs[0][...]
-    for ref in refs[1:-1]:
-        total = total + ref[...]
-    width = out.shape[1]
-    mean = jnp.sum(total[:, width:], axis=1, keepdims=True) / pdim
-    out[...] = total[:, :width] * lax.rsqrt(mean + EPS)
-
-
 def small(kernel, out_shape, operands, scratch_shapes=(), name=None):
     one = not isinstance(out_shape, list)
     return pl.pallas_call(
@@ -290,12 +280,11 @@
         [pltpu.VMEM((blks, cands, nq), F32), pltpu.VMEM((groups,) + line, F32)],
         name="scores",
     )
-    return small(
-        functools.partial(finish_kernel, pdim),
-        shape((owned, total_q), F32),
-        (sums[0], *[grp_swap(sums[k], k) for k in range(groups - 1, 0, -1)]),
-        name="finish",
-    )
+    total = sums[0]
+    for k in range(groups - 1, 0, -1):
+        total = total + grp_swap(sums[k], k)
+    mean = jnp.sum(total[:, total_q:], axis=1, keepdims=True) / pdim
+    return total[:, :total_q] * lax.rsqrt(mean + EPS)
 
 
 def solution(mesh):

time: 30.6 us -> 30.7 us (level)
  other arithmetic: 0.72 us -> 1.52 us
  Pallas kernels: 10.2 us -> 9.54 us
    pallas_call x6 -> x5, Pallas kernels: 1.4 us -> 0.72 us  [small(): pl.pallas_call(kernel, out_shape=out_shape, in_specs=[VMEM] * len(operand...]
    mul x0 -> x1, other arithmetic: none -> 0.68 us  [on_device(): return total[:, :total_q] * lax.rsqrt(mean + EPS)]
where the time goes in v16:
time: 30.7 us; the launch traced here: 30.5 us
  starting transfers between devices  13.6 us (44%)
  Pallas kernels  9.54 us (31%)
  waiting for transfers between devices  5.48 us (18%)
  other arithmetic  1.52 us (5%)
  local copies, waits for them, and re-layouts  0.35 us (1%)
    ppermute x6, starting transfers between devices, blk_swap(): return lax.ppermute(x, 'blk', [(b, b ^ k) for b in range(blks)])  10.1 us
    pallas_call x1, Pallas kernels, on_device(): pl.pallas_call(functools.partial(grads_kernel, (cands, tokens, width, gro...  8.82 us
    ppermute x5, waiting for transfers between devices, grp_swap(): return lax.ppermute(x, 'grp', [(g, g ^ k) for g in range(groups)])  5.16 us
    ppermute x5, starting transfers between devices, grp_swap(): return lax.ppermute(x, 'grp', [(g, g ^ k) for g in range(groups)])  3.49 us
    pallas_call x5, Pallas kernels, small(): pl.pallas_call(kernel, out_shape=out_shape, in_specs=[VMEM] * len(operand...  0.72 us
    min x1, other arithmetic, on_device(): jnp.minimum(lengths, tokens * groups)  0.72 us
    mul x1, other arithmetic, on_device(): return total[:, :total_q] * lax.rsqrt(mean + EPS)  0.68 us
  transfers between devices with their start and end apart: 11, of which 6 were waited for; matrix products, arithmetic and copies ran while one was open for 0% of the time, Pallas kernels for 30%

profile of v16, /device:TPU:0, one launch (start us, length us, event | category | flops | bytes accessed | tf_op | source)
XLA Modules:
  0.0 30.5 jit_solution(15515120702818678905)
XLA Ops:
  0.0 0.0 copy-start
  0.0 0.7 %broadcast_minimum_fusion.lens_in = s32[16]{0:T(128)S(1)} fusion(s32[16]{0:T(128)} %param.10), kind=kLoop, calls=%fused_computation.4 | loop fusion | flops 16 | bytes 128 | tf_op jit(solution)/shard_map/min | solution.py:212
  0.7 0.3 %copy-done = bf16[64,4096]{1,0:T(8,128)(2,1)S(1)} copy-done((bf16[64,4096]{1,0:T(8,128)(2,1)S(1)}, bf16[64,4096]{1,0:T(8,128)(2,1)}, u32[]{:S(2)}) %copy-start) | copy-done | bytes 524312
  1.1 5.1 %collective-permute-start.4 = (bf16[64,1024]{1,0:T(8,128)(2,1)S(1)}, bf16[64,1024]{1,0:T(8,128)(2,1)S(1)}, u32[]{:S(2)}, u32[]{:S(2)}) collective-permute-start(bf16[64,1024]{1,0:T(8,128)(2,1)S(1)} %constant_dynamic-slice_fusion.refs_0_), channel_id=1, source_target_pairs={{0,24},{4,28},{8,16},{12,20},{16,8},{20,12},{24,0},{28,4},{1,25},{... | collective-permute-start | bytes 393224 | tf_op jit(solution)/shard_map/ppermute | solution.py:209
  6.2 0.0 collective-permute-start.3
  6.2 1.7 %collective-permute-start.2 = (bf16[64,1024]{1,0:T(8,128)(2,1)S(1)}, bf16[64,1024]{1,0:T(8,128)(2,1)S(1)}, u32[]{:S(2)}, u32[]{:S(2)}) collective-permute-start(bf16[64,1024]{1,0:T(8,128)(2,1)S(1)} %constant_dynamic-slice_fusion.refs_0_), channel_id=1, source_target_pairs={{0,12},{4,8},{8,4},{12,0},{16,28},{20,24},{24,20},{28,16},{1,13},{... | collective-permute-start | bytes 393224 | tf_op jit(solution)/shard_map/ppermute | solution.py:209
  7.9 0.4 %collective-permute-start.1 = (bf16[64,1024]{1,0:T(8,128)(2,1)S(1)}, bf16[64,1024]{1,0:T(8,128)(2,1)S(1)}, u32[]{:S(2)}, u32[]{:S(2)}) collective-permute-start(bf16[64,1024]{1,0:T(8,128)(2,1)S(1)} %constant_dynamic-slice_fusion.refs_0_), channel_id=1, source_target_pairs={{0,4},{4,0},{8,12},{12,8},{16,20},{20,16},{24,28},{28,24},{1,5},{5... | collective-permute-start | bytes 393224 | tf_op jit(solution)/shard_map/ppermute | solution.py:209
  8.3 8.8 %grads.1 = (f32[2,128,128]{2,1,0:T(8,128)S(1)}, f32[2,128,128]{2,1,0:T(8,128)S(1)}) custom-call(s32[16]{0:T(128)S(1)} %broadcast_minimum_fusion.lens_in, bf16[1024,4096]{1,0:T(8,128)(2,1)} %bitcast.8, bf16[1024,4096]{1,0:T(8,128)(2,1)} %bitcast.9, bf16[64,4096]{1,0:T(8,128)(2,1)} %bitcast.10, bf16[64,4096]{1,0:T(8,128)(2,1)} %bitcast.11), custom_call_target="tpu_custom_call" | custom-call | flops 4294967296 | bytes 16777216 | tf_op jit(solution)/shard_map/grads/pallas_call | solution.py:218
  17.1 0.0 collective-permute-done.4.refs_4_
  17.1 0.1 collective-permute-done.3.refs_3_
  17.3 0.0 collective-permute-done.2.refs_1_.refs_2_
  17.3 0.0 collective-permute-done.1.refs_0_.refs_1_
  17.3 1.6 %collective-permute-start.7 = (bf16[128,1024]{1,0:T(8,128)(2,1)S(1)}, bf16[128,1024]{1,0:T(8,128)(2,1)S(1)}, u32[]{:S(2)}, u32[]{:S(2)}) collective-permute-start(bf16[128,1024]{1,0:T(8,128)(2,1)S(1)} %join.1.rest_0_), channel_id=1, source_target_pairs={{0,4},{4,0},{8,12},{12,8},{16,20},{20,16},{24,28},{28,24},{1,5},{5... | collective-permute-start | bytes 786440 | tf_op jit(solution)/shard_map/ppermute | solution.py:209
  18.9 0.0 collective-permute-start
  18.9 1.2 %collective-permute-start.6 = (bf16[64,1024]{1,0:T(8,128)(2,1)S(1)}, bf16[64,1024]{1,0:T(8,128)(2,1)S(1)}, u32[]{:S(2)}, u32[]{:S(2)}) collective-permute-start(bf16[64,1024]{1,0:T(8,128)(2,1)S(1)} %constant_dynamic-slice_fusion.refs_0_), channel_id=1, source_target_pairs={{0,8},{4,12},{8,0},{12,4},{16,24},{20,28},{24,16},{28,20},{1,9},{5... | collective-permute-start | bytes 393224 | tf_op jit(solution)/shard_map/ppermute | solution.py:209
  20.2 0.1 collective-permute-done.came
  20.3 1.6 %collective-permute-start.5 = (bf16[128,128]{1,0:T(8,128)(2,1)S(1)}, bf16[128,128]{1,0:T(8,128)(2,1)S(1)}, u32[]{:S(2)}, u32[]{:S(2)}) collective-permute-start(bf16[128,128]{1,0:T(8,128)(2,1)S(1)} %get-tuple-element.25), channel_id=1, source_target_pairs={{0,2},{1,3},{2,0},{3,1},{4,6},{5,7},{6,4},{7,5},{8,10},{9,11},{10,... | collective-permute-start | bytes 98312 | tf_op jit(solution)/shard_map/ppermute | solution.py:206
  21.9 2.4 %collective-permute-done.5.came = bf16[128,128]{1,0:T(8,128)(2,1)S(1)} collective-permute-done((bf16[128,128]{1,0:T(8,128)(2,1)S(1)}, bf16[128,128]{1,0:T(8,128)(2,1)S(1)}, u32[]{:S(2)}, u32[]{:S(2)}) %collective-permute-start.5) | collective-permute-done | bytes 32800 | tf_op jit(solution)/shard_map/ppermute | solution.py:206
  24.3 0.1 combine.1
  24.4 0.3 near.1
  24.7 0.2 collective-permute-done.6.late
  24.8 0.0 collective-permute-done.7.passed
  24.8 0.3 %scores.1 = (f32[4,640]{1,0:T(4,128)S(1)}, f32[4,640]{1,0:T(4,128)S(1)}, f32[4,640]{1,0:T(4,128)S(1)}, f32[4,640]{1,0:T(4,128)S(1)}) custom-call(bf16[16,1024]{1,0:T(8,128)(2,1)S(1)} %get-tuple-element.26.left, f32[16,128]{1,0:T(8,128)S(1)} %get-tuple-element.27.squares, f32[8,16,64]{2,1,0:T(8,128)S(1)} %near.1, ...), custom_call_target="tpu_custom_call" | custom-call | tf_op jit(solution)/shard_map/scores/pallas_call | solution.py:182
  25.2 0.9 %collective-permute-start.8 = (f32[4,640]{1,0:T(4,128)S(1)}, f32[4,640]{1,0:T(4,128)S(1)}, u32[]{:S(2)}, u32[]{:S(2)}) collective-permute-start(f32[4,640]{1,0:T(4,128)S(1)} %get-tuple-element.30), channel_id=1, source_target_pairs={{0,3},{1,2},{2,1},{3,0},{4,7},{5,6},{6,5},{7,4},{8,11},{9,10},{10,... | collective-permute-start | bytes 30728 | tf_op jit(solution)/shard_map/ppermute | solution.py:206
  26.0 0.7 %collective-permute-start.9 = (f32[4,640]{1,0:T(4,128)S(1)}, f32[4,640]{1,0:T(4,128)S(1)}, u32[]{:S(2)}, u32[]{:S(2)}) collective-permute-start(f32[4,640]{1,0:T(4,128)S(1)} %get-tuple-element.31), channel_id=1, source_target_pairs={{0,2},{1,3},{2,0},{3,1},{4,6},{5,7},{6,4},{7,5},{8,10},{9,11},{10,... | collective-permute-start | bytes 30728 | tf_op jit(solution)/shard_map/ppermute | solution.py:206
  26.8 0.3 collective-permute-start.10
  27.1 1.3 %collective-permute-done.8 = f32[4,640]{1,0:T(4,128)S(1)} collective-permute-done((f32[4,640]{1,0:T(4,128)S(1)}, f32[4,640]{1,0:T(4,128)S(1)}, u32[]{:S(2)}, u32[]{:S(2)}) %collective-permute-start.8) | collective-permute-done | bytes 10272 | tf_op jit(solution)/shard_map/ppermute | solution.py:206
  28.4 1.3 %collective-permute-done.9 = f32[4,640]{1,0:T(4,128)S(1)} collective-permute-done((f32[4,640]{1,0:T(4,128)S(1)}, f32[4,640]{1,0:T(4,128)S(1)}, u32[]{:S(2)}, u32[]{:S(2)}) %collective-permute-start.9) | collective-permute-done | bytes 10272 | tf_op jit(solution)/shard_map/ppermute | solution.py:206
  29.7 0.0 collective-permute-done.10
  29.7 0.1 slice_reduce_fusion
  29.9 0.7 %slice_multiply_fusion = f32[4,512]{1,0:T(4,128)} fusion(f32[4,640]{1,0:T(4,128)S(1)} %add_add_fusion, f32[4]{0:T(128)S(1)} %add_rsqrt_fusion), kind=kLoop, calls=%fused_computation.1 | loop fusion | flops 2048 | bytes 16400 | tf_op jit(solution)/shard_map/mul | solution.py:287
  (5 shorter events, 0.1 us)
Async XLA Ops:
  0.0 1.1 %copy-start = (bf16[64,4096]{1,0:T(8,128)(2,1)S(1)}, bf16[64,4096]{1,0:T(8,128)(2,1)}, u32[]{:S(2)}) copy-start(bf16[64,4096]{1,0:T(8,128)(2,1)} %param.11) | copy-start | bytes 1572868
  1.1 16.1 %collective-permute-start.4 = (bf16[64,1024]{1,0:T(8,128)(2,1)S(1)}, bf16[64,1024]{1,0:T(8,128)(2,1)S(1)}, u32[]{:S(2)}, u32[]{:S(2)}) collective-permute-start(bf16[64,1024]{1,0:T(8,128)(2,1)S(1)} %constant_dynamic-slice_fusion.refs_0_), channel_id=1, source_target_pairs={{0,24},{4,28},{8,16},{12,20},{16,8},{20,12},{24,0},{28,4},{1,25},{... | collective-permute-start | bytes 393224 | tf_op jit(solution)/shard_map/ppermute | solution.py:209
  6.2 11.1 %collective-permute-start.3 = (bf16[64,1024]{1,0:T(8,128)(2,1)S(1)}, bf16[64,1024]{1,0:T(8,128)(2,1)S(1)}, u32[]{:S(2)}, u32[]{:S(2)}) collective-permute-start(bf16[64,1024]{1,0:T(8,128)(2,1)S(1)} %constant_dynamic-slice_fusion.refs_0_), channel_id=1, source_target_pairs={{0,16},{4,20},{8,24},{12,28},{16,0},{20,4},{24,8},{28,12},{1,17},{... | collective-permute-start | bytes 393224 | tf_op jit(solution)/shard_map/ppermute | solution.py:209
  6.2 11.1 %collective-permute-start.2 = (bf16[64,1024]{1,0:T(8,128)(2,1)S(1)}, bf16[64,1024]{1,0:T(8,128)(2,1)S(1)}, u32[]{:S(2)}, u32[]{:S(2)}) collective-permute-start(bf16[64,1024]{1,0:T(8,128)(2,1)S(1)} %constant_dynamic-slice_fusion.refs_0_), channel_id=1, source_target_pairs={{0,12},{4,8},{8,4},{12,0},{16,28},{20,24},{24,20},{28,16},{1,13},{... | collective-permute-start | bytes 393224 | tf_op jit(solution)/shard_map/ppermute | solution.py:209
  7.9 9.3 %collective-permute-start.1 = (bf16[64,1024]{1,0:T(8,128)(2,1)S(1)}, bf16[64,1024]{1,0:T(8,128)(2,1)S(1)}, u32[]{:S(2)}, u32[]{:S(2)}) collective-permute-start(bf16[64,1024]{1,0:T(8,128)(2,1)S(1)} %constant_dynamic-slice_fusion.refs_0_), channel_id=1, source_target_pairs={{0,4},{4,0},{8,12},{12,8},{16,20},{20,16},{24,28},{28,24},{1,5},{5... | collective-permute-start | bytes 393224 | tf_op jit(solution)/shard_map/ppermute | solution.py:209
  17.3 7.6 %collective-permute-start.7 = (bf16[128,1024]{1,0:T(8,128)(2,1)S(1)}, bf16[128,1024]{1,0:T(8,128)(2,1)S(1)}, u32[]{:S(2)}, u32[]{:S(2)}) collective-permute-start(bf16[128,1024]{1,0:T(8,128)(2,1)S(1)} %join.1.rest_0_), channel_id=1, source_target_pairs={{0,4},{4,0},{8,12},{12,8},{16,20},{20,16},{24,28},{28,24},{1,5},{5... | collective-permute-start | bytes 786440 | tf_op jit(solution)/shard_map/ppermute | solution.py:209
  18.9 1.3 %collective-permute-start = (f32[2,128,128]{2,1,0:T(8,128)S(1)}, f32[2,128,128]{2,1,0:T(8,128)S(1)}, u32[]{:S(2)}, u32[]{:S(2)}) collective-permute-start(f32[2,128,128]{2,1,0:T(8,128)S(1)} %get-tuple-element.21), channel_id=1, source_target_pairs={{0,1},{1,0},{2,3},{3,2},{4,5},{5,4},{6,7},{7,6},{8,9},{9,8},{10,11... | collective-permute-start | bytes 393224 | tf_op jit(solution)/shard_map/ppermute | solution.py:206
  18.9 5.9 %collective-permute-start.6 = (bf16[64,1024]{1,0:T(8,128)(2,1)S(1)}, bf16[64,1024]{1,0:T(8,128)(2,1)S(1)}, u32[]{:S(2)}, u32[]{:S(2)}) collective-permute-start(bf16[64,1024]{1,0:T(8,128)(2,1)S(1)} %constant_dynamic-slice_fusion.refs_0_), channel_id=1, source_target_pairs={{0,8},{4,12},{8,0},{12,4},{16,24},{20,28},{24,16},{28,20},{1,9},{5... | collective-permute-start | bytes 393224 | tf_op jit(solution)/shard_map/ppermute | solution.py:209
  20.3 4.0 %collective-permute-start.5 = (bf16[128,128]{1,0:T(8,128)(2,1)S(1)}, bf16[128,128]{1,0:T(8,128)(2,1)S(1)}, u32[]{:S(2)}, u32[]{:S(2)}) collective-permute-start(bf16[128,128]{1,0:T(8,128)(2,1)S(1)} %get-tuple-element.25), channel_id=1, source_target_pairs={{0,2},{1,3},{2,0},{3,1},{4,6},{5,7},{6,4},{7,5},{8,10},{9,11},{10,... | collective-permute-start | bytes 98312 | tf_op jit(solution)/shard_map/ppermute | solution.py:206
  25.2 3.2 %collective-permute-start.8 = (f32[4,640]{1,0:T(4,128)S(1)}, f32[4,640]{1,0:T(4,128)S(1)}, u32[]{:S(2)}, u32[]{:S(2)}) collective-permute-start(f32[4,640]{1,0:T(4,128)S(1)} %get-tuple-element.30), channel_id=1, source_target_pairs={{0,3},{1,2},{2,1},{3,0},{4,7},{5,6},{6,5},{7,4},{8,11},{9,10},{10,... | collective-permute-start | bytes 30728 | tf_op jit(solution)/shard_map/ppermute | solution.py:206
  26.0 3.7 %collective-permute-start.9 = (f32[4,640]{1,0:T(4,128)S(1)}, f32[4,640]{1,0:T(4,128)S(1)}, u32[]{:S(2)}, u32[]{:S(2)}) collective-permute-start(f32[4,640]{1,0:T(4,128)S(1)} %get-tuple-element.31), channel_id=1, source_target_pairs={{0,2},{1,3},{2,0},{3,1},{4,6},{5,7},{6,4},{7,5},{8,10},{9,11},{10,... | collective-permute-start | bytes 30728 | tf_op jit(solution)/shard_map/ppermute | solution.py:206
  26.8 2.9 %collective-permute-start.10 = (f32[4,640]{1,0:T(4,128)S(1)}, f32[4,640]{1,0:T(4,128)S(1)}, u32[]{:S(2)}, u32[]{:S(2)}) collective-permute-start(f32[4,640]{1,0:T(4,128)S(1)} %get-tuple-element.32), channel_id=1, source_target_pairs={{0,1},{1,0},{2,3},{3,2},{4,5},{5,4},{6,7},{7,6},{8,9},{9,8},{10,11... | collective-permute-start | bytes 30728 | tf_op jit(solution)/shard_map/ppermute | solution.py:206

commit v17 on v15

--- a/solution.py
+++ b/solution.py
@@ -159,7 +159,7 @@
         rows, late[...], BY_ROWS, preferred_element_type=F32
     )
     for n in range(blks // 2 - 2):
-        place[jnp.bitwise_xor(blk, 2 * n + 5)] = lax.dot_general(
+        place[jnp.bitwise_xor(blk, blks - 1 - 2 * n)] = lax.dot_general(
             rows, passed[n * nq : (n + 1) * nq, :], BY_ROWS, preferred_element_type=F32
         )
     scores = jnp.concatenate([place[b] for b in range(blks)], axis=1)
@@ -257,7 +257,7 @@
     joined = small(
         functools.partial(join_kernel, far - 2),
         shape(((far - 2) * nq, slice_width), BF16),
-        (*pieces[1:], keep, *distant),
+        (*pieces[1:], keep, *distant[::-1]),
         name="join",
     )
     late, joined = lax.optimization_barrier((cut, joined))

time: 30.6 us -> 30.5 us (level)
  waiting for transfers between devices: 5.48 us -> 4.99 us
  starting transfers between devices: 13.6 us -> 14 us
    ppermute x6, starting transfers between devices: 10.1 us -> 10.5 us  [blk_swap(): return lax.ppermute(x, 'blk', [(b, b ^ k) for b in range(blks)])]
    ppermute x6, waiting for transfers between devices: 0.32 us -> 0.02 us  [blk_swap(): return lax.ppermute(x, 'blk', [(b, b ^ k) for b in range(blks)])]
  transfers between devices with their start and end apart: 11 -> 11, of which waited for: 6 -> 3; matrix products, arithmetic and copies ran while one was open for 0% -> 0% of each run, Pallas kernels for 30% -> 30%
where the time goes in v17:
time: 30.5 us; the launch traced here: 30.4 us
  starting transfers between devices  14 us (46%)
  Pallas kernels  10.3 us (34%)
  waiting for transfers between devices  4.99 us (16%)
  other arithmetic  0.72 us (2%)
  local copies, waits for them, and re-layouts  0.35 us (1%)
    ppermute x6, starting transfers between devices, blk_swap(): return lax.ppermute(x, 'blk', [(b, b ^ k) for b in range(blks)])  10.5 us
    pallas_call x1, Pallas kernels, on_device(): pl.pallas_call(functools.partial(grads_kernel, (cands, tokens, width, gro...  8.82 us
    ppermute x5, waiting for transfers between devices, grp_swap(): return lax.ppermute(x, 'grp', [(g, g ^ k) for g in range(groups)])  4.97 us
    ppermute x5, starting transfers between devices, grp_swap(): return lax.ppermute(x, 'grp', [(g, g ^ k) for g in range(groups)])  3.49 us
    pallas_call x6, Pallas kernels, small(): pl.pallas_call(kernel, out_shape=out_shape, in_specs=[VMEM] * len(operand...  1.43 us
    min x1, other arithmetic, on_device(): jnp.minimum(lengths, tokens * groups)  0.72 us
  transfers between devices with their start and end apart: 11, of which 3 were waited for; matrix products, arithmetic and copies ran while one was open for 0% of the time, Pallas kernels for 30%

profile of v17, /device:TPU:0, one launch (start us, length us, event | category | flops | bytes accessed | tf_op | source)
XLA Modules:
  0.0 30.4 jit_solution(14576067424226734181)
XLA Ops:
  0.0 0.0 copy-start
  0.0 0.7 %broadcast_minimum_fusion.lens_in = s32[16]{0:T(128)S(1)} fusion(s32[16]{0:T(128)} %param.10), kind=kLoop, calls=%fused_computation | loop fusion | flops 16 | bytes 128 | tf_op jit(solution)/shard_map/min | solution.py:222
  0.7 0.3 %copy-done = bf16[64,4096]{1,0:T(8,128)(2,1)S(1)} copy-done((bf16[64,4096]{1,0:T(8,128)(2,1)S(1)}, bf16[64,4096]{1,0:T(8,128)(2,1)}, u32[]{:S(2)}) %copy-start) | copy-done | bytes 524312
  1.1 4.1 %collective-permute-start.4 = (bf16[64,1024]{1,0:T(8,128)(2,1)S(1)}, bf16[64,1024]{1,0:T(8,128)(2,1)S(1)}, u32[]{:S(2)}, u32[]{:S(2)}) collective-permute-start(bf16[64,1024]{1,0:T(8,128)(2,1)S(1)} %constant_dynamic-slice_fusion.refs_0_), channel_id=1, source_target_pairs={{0,16},{4,20},{8,24},{12,28},{16,0},{20,4},{24,8},{28,12},{1,17},{... | collective-permute-start | bytes 393224 | tf_op jit(solution)/shard_map/ppermute | solution.py:219
  5.2 1.3 %collective-permute-start.3 = (bf16[64,1024]{1,0:T(8,128)(2,1)S(1)}, bf16[64,1024]{1,0:T(8,128)(2,1)S(1)}, u32[]{:S(2)}, u32[]{:S(2)}) collective-permute-start(bf16[64,1024]{1,0:T(8,128)(2,1)S(1)} %constant_dynamic-slice_fusion.refs_0_), channel_id=1, source_target_pairs={{0,24},{4,28},{8,16},{12,20},{16,8},{20,12},{24,0},{28,4},{1,25},{... | collective-permute-start | bytes 393224 | tf_op jit(solution)/shard_map/ppermute | solution.py:219
  6.5 1.2 %collective-permute-start.2 = (bf16[64,1024]{1,0:T(8,128)(2,1)S(1)}, bf16[64,1024]{1,0:T(8,128)(2,1)S(1)}, u32[]{:S(2)}, u32[]{:S(2)}) collective-permute-start(bf16[64,1024]{1,0:T(8,128)(2,1)S(1)} %constant_dynamic-slice_fusion.refs_0_), channel_id=1, source_target_pairs={{0,12},{4,8},{8,4},{12,0},{16,28},{20,24},{24,20},{28,16},{1,13},{... | collective-permute-start | bytes 393224 | tf_op jit(solution)/shard_map/ppermute | solution.py:219
  7.7 0.5 %collective-permute-start.1 = (bf16[64,1024]{1,0:T(8,128)(2,1)S(1)}, bf16[64,1024]{1,0:T(8,128)(2,1)S(1)}, u32[]{:S(2)}, u32[]{:S(2)}) collective-permute-start(bf16[64,1024]{1,0:T(8,128)(2,1)S(1)} %constant_dynamic-slice_fusion.refs_0_), channel_id=1, source_target_pairs={{0,4},{4,0},{8,12},{12,8},{16,20},{20,16},{24,28},{28,24},{1,5},{5... | collective-permute-start | bytes 393224 | tf_op jit(solution)/shard_map/ppermute | solution.py:219
  8.2 8.8 %grads.1 = (f32[2,128,128]{2,1,0:T(8,128)S(1)}, f32[2,128,128]{2,1,0:T(8,128)S(1)}) custom-call(s32[16]{0:T(128)S(1)} %broadcast_minimum_fusion.lens_in, bf16[1024,4096]{1,0:T(8,128)(2,1)} %bitcast.8, bf16[1024,4096]{1,0:T(8,128)(2,1)} %bitcast.9, bf16[64,4096]{1,0:T(8,128)(2,1)} %bitcast.10, bf16[64,4096]{1,0:T(8,128)(2,1)} %bitcast.11), custom_call_target="tpu_custom_call" | custom-call | flops 4294967296 | bytes 16777216 | tf_op jit(solution)/shard_map/grads/pallas_call | solution.py:228
  17.0 0.0 collective-permute-done.4.refs_4_.refs_3_
  17.1 0.0 collective-permute-done.3.refs_3_.refs_4_
  17.1 0.0 collective-permute-done.2.refs_1_.refs_2_
  17.1 0.0 collective-permute-done.1.refs_0_.refs_1_
  17.1 1.6 %collective-permute-start.7 = (bf16[128,1024]{1,0:T(8,128)(2,1)S(1)}, bf16[128,1024]{1,0:T(8,128)(2,1)S(1)}, u32[]{:S(2)}, u32[]{:S(2)}) collective-permute-start(bf16[128,1024]{1,0:T(8,128)(2,1)S(1)} %join.1.rest_0_), channel_id=1, source_target_pairs={{0,4},{4,0},{8,12},{12,8},{16,20},{20,16},{24,28},{28,24},{1,5},{5... | collective-permute-start | bytes 786440 | tf_op jit(solution)/shard_map/ppermute | solution.py:219
  18.7 0.0 collective-permute-start
  18.7 1.8 %collective-permute-start.6 = (bf16[64,1024]{1,0:T(8,128)(2,1)S(1)}, bf16[64,1024]{1,0:T(8,128)(2,1)S(1)}, u32[]{:S(2)}, u32[]{:S(2)}) collective-permute-start(bf16[64,1024]{1,0:T(8,128)(2,1)S(1)} %constant_dynamic-slice_fusion.refs_0_), channel_id=1, source_target_pairs={{0,8},{4,12},{8,0},{12,4},{16,24},{20,28},{24,16},{28,20},{1,9},{5... | collective-permute-start | bytes 393224 | tf_op jit(solution)/shard_map/ppermute | solution.py:219
  20.5 0.0 collective-permute-done.came
  20.5 1.6 %collective-permute-start.5 = (bf16[128,128]{1,0:T(8,128)(2,1)S(1)}, bf16[128,128]{1,0:T(8,128)(2,1)S(1)}, u32[]{:S(2)}, u32[]{:S(2)}) collective-permute-start(bf16[128,128]{1,0:T(8,128)(2,1)S(1)} %get-tuple-element.25), channel_id=1, source_target_pairs={{0,2},{1,3},{2,0},{3,1},{4,6},{5,7},{6,4},{7,5},{8,10},{9,11},{10,... | collective-permute-start | bytes 98312 | tf_op jit(solution)/shard_map/ppermute | solution.py:216
  22.1 2.4 %collective-permute-done.5.came = bf16[128,128]{1,0:T(8,128)(2,1)S(1)} collective-permute-done((bf16[128,128]{1,0:T(8,128)(2,1)S(1)}, bf16[128,128]{1,0:T(8,128)(2,1)S(1)}, u32[]{:S(2)}, u32[]{:S(2)}) %collective-permute-start.5) | collective-permute-done | bytes 32800 | tf_op jit(solution)/shard_map/ppermute | solution.py:216
  24.5 0.1 combine.1
  24.6 0.3 near.1
  24.9 0.0 collective-permute-done.6.late
  24.9 0.0 collective-permute-done.7.passed
  24.9 0.3 %scores.1 = (f32[4,640]{1,0:T(4,128)S(1)}, f32[4,640]{1,0:T(4,128)S(1)}, f32[4,640]{1,0:T(4,128)S(1)}, f32[4,640]{1,0:T(4,128)S(1)}) custom-call(bf16[16,1024]{1,0:T(8,128)(2,1)S(1)} %get-tuple-element.26.left, f32[16,128]{1,0:T(8,128)S(1)} %get-tuple-element.27.squares, f32[8,16,64]{2,1,0:T(8,128)S(1)} %near.1, ...), custom_call_target="tpu_custom_call" | custom-call | tf_op jit(solution)/shard_map/scores/pallas_call | solution.py:192
  25.2 0.7 %collective-permute-start.8 = (f32[4,640]{1,0:T(4,128)S(1)}, f32[4,640]{1,0:T(4,128)S(1)}, u32[]{:S(2)}, u32[]{:S(2)}) collective-permute-start(f32[4,640]{1,0:T(4,128)S(1)} %get-tuple-element.30), channel_id=1, source_target_pairs={{0,3},{1,2},{2,1},{3,0},{4,7},{5,6},{6,5},{7,4},{8,11},{9,10},{10,... | collective-permute-start | bytes 30728 | tf_op jit(solution)/shard_map/ppermute | solution.py:216
  25.9 0.9 %collective-permute-start.9 = (f32[4,640]{1,0:T(4,128)S(1)}, f32[4,640]{1,0:T(4,128)S(1)}, u32[]{:S(2)}, u32[]{:S(2)}) collective-permute-start(f32[4,640]{1,0:T(4,128)S(1)} %get-tuple-element.31), channel_id=1, source_target_pairs={{0,2},{1,3},{2,0},{3,1},{4,6},{5,7},{6,4},{7,5},{8,10},{9,11},{10,... | collective-permute-start | bytes 30728 | tf_op jit(solution)/shard_map/ppermute | solution.py:216
  26.9 0.3 collective-permute-start.10
  27.2 1.3 %collective-permute-done.8.refs_1_ = f32[4,640]{1,0:T(4,128)S(1)} collective-permute-done((f32[4,640]{1,0:T(4,128)S(1)}, f32[4,640]{1,0:T(4,128)S(1)}, u32[]{:S(2)}, u32[]{:S(2)}) %collective-permute-start.8) | collective-permute-done | bytes 10272 | tf_op jit(solution)/shard_map/ppermute | solution.py:216
  28.5 1.3 %collective-permute-done.9.refs_2_ = f32[4,640]{1,0:T(4,128)S(1)} collective-permute-done((f32[4,640]{1,0:T(4,128)S(1)}, f32[4,640]{1,0:T(4,128)S(1)}, u32[]{:S(2)}, u32[]{:S(2)}) %collective-permute-start.9) | collective-permute-done | bytes 10272 | tf_op jit(solution)/shard_map/ppermute | solution.py:216
  29.7 0.0 collective-permute-done.10.refs_3_
  29.7 0.7 %finish.1 = f32[4,512]{1,0:T(4,128)} custom-call(f32[4,640]{1,0:T(4,128)S(1)} %get-tuple-element.29.refs_0_, f32[4,640]{1,0:T(4,128)S(1)} %collective-permute-done.8.refs_1_, f32[4,640]{1,0:T(4,128)S(1)} %collective-permute-done.9.refs_2_, f32[4,640]{1,0:T(4,128)S(1)} %collective-permute-done.10.refs_3_), custom_call_target="tpu_custom_call" | custom-call | tf_op jit(solution)/shard_map/finish/pallas_call | solution.py:192
  (3 shorter events, 0.0 us)
Async XLA Ops:
  0.0 1.1 %copy-start = (bf16[64,4096]{1,0:T(8,128)(2,1)S(1)}, bf16[64,4096]{1,0:T(8,128)(2,1)}, u32[]{:S(2)}) copy-start(bf16[64,4096]{1,0:T(8,128)(2,1)} %param.11) | copy-start | bytes 1572868
  1.1 16.0 %collective-permute-start.4 = (bf16[64,1024]{1,0:T(8,128)(2,1)S(1)}, bf16[64,1024]{1,0:T(8,128)(2,1)S(1)}, u32[]{:S(2)}, u32[]{:S(2)}) collective-permute-start(bf16[64,1024]{1,0:T(8,128)(2,1)S(1)} %constant_dynamic-slice_fusion.refs_0_), channel_id=1, source_target_pairs={{0,16},{4,20},{8,24},{12,28},{16,0},{20,4},{24,8},{28,12},{1,17},{... | collective-permute-start | bytes 393224 | tf_op jit(solution)/shard_map/ppermute | solution.py:219
  5.2 11.9 %collective-permute-start.3 = (bf16[64,1024]{1,0:T(8,128)(2,1)S(1)}, bf16[64,1024]{1,0:T(8,128)(2,1)S(1)}, u32[]{:S(2)}, u32[]{:S(2)}) collective-permute-start(bf16[64,1024]{1,0:T(8,128)(2,1)S(1)} %constant_dynamic-slice_fusion.refs_0_), channel_id=1, source_target_pairs={{0,24},{4,28},{8,16},{12,20},{16,8},{20,12},{24,0},{28,4},{1,25},{... | collective-permute-start | bytes 393224 | tf_op jit(solution)/shard_map/ppermute | solution.py:219
  6.5 10.6 %collective-permute-start.2 = (bf16[64,1024]{1,0:T(8,128)(2,1)S(1)}, bf16[64,1024]{1,0:T(8,128)(2,1)S(1)}, u32[]{:S(2)}, u32[]{:S(2)}) collective-permute-start(bf16[64,1024]{1,0:T(8,128)(2,1)S(1)} %constant_dynamic-slice_fusion.refs_0_), channel_id=1, source_target_pairs={{0,12},{4,8},{8,4},{12,0},{16,28},{20,24},{24,20},{28,16},{1,13},{... | collective-permute-start | bytes 393224 | tf_op jit(solution)/shard_map/ppermute | solution.py:219
  7.7 9.4 %collective-permute-start.1 = (bf16[64,1024]{1,0:T(8,128)(2,1)S(1)}, bf16[64,1024]{1,0:T(8,128)(2,1)S(1)}, u32[]{:S(2)}, u32[]{:S(2)}) collective-permute-start(bf16[64,1024]{1,0:T(8,128)(2,1)S(1)} %constant_dynamic-slice_fusion.refs_0_), channel_id=1, source_target_pairs={{0,4},{4,0},{8,12},{12,8},{16,20},{20,16},{24,28},{28,24},{1,5},{5... | collective-permute-start | bytes 393224 | tf_op jit(solution)/shard_map/ppermute | solution.py:219
  17.1 7.8 %collective-permute-start.7 = (bf16[128,1024]{1,0:T(8,128)(2,1)S(1)}, bf16[128,1024]{1,0:T(8,128)(2,1)S(1)}, u32[]{:S(2)}, u32[]{:S(2)}) collective-permute-start(bf16[128,1024]{1,0:T(8,128)(2,1)S(1)} %join.1.rest_0_), channel_id=1, source_target_pairs={{0,4},{4,0},{8,12},{12,8},{16,20},{20,16},{24,28},{28,24},{1,5},{5... | collective-permute-start | bytes 786440 | tf_op jit(solution)/shard_map/ppermute | solution.py:219
  18.7 1.8 %collective-permute-start = (f32[2,128,128]{2,1,0:T(8,128)S(1)}, f32[2,128,128]{2,1,0:T(8,128)S(1)}, u32[]{:S(2)}, u32[]{:S(2)}) collective-permute-start(f32[2,128,128]{2,1,0:T(8,128)S(1)} %get-tuple-element.21), channel_id=1, source_target_pairs={{0,1},{1,0},{2,3},{3,2},{4,5},{5,4},{6,7},{7,6},{8,9},{9,8},{10,11... | collective-permute-start | bytes 393224 | tf_op jit(solution)/shard_map/ppermute | solution.py:216
  18.7 6.2 %collective-permute-start.6 = (bf16[64,1024]{1,0:T(8,128)(2,1)S(1)}, bf16[64,1024]{1,0:T(8,128)(2,1)S(1)}, u32[]{:S(2)}, u32[]{:S(2)}) collective-permute-start(bf16[64,1024]{1,0:T(8,128)(2,1)S(1)} %constant_dynamic-slice_fusion.refs_0_), channel_id=1, source_target_pairs={{0,8},{4,12},{8,0},{12,4},{16,24},{20,28},{24,16},{28,20},{1,9},{5... | collective-permute-start | bytes 393224 | tf_op jit(solution)/shard_map/ppermute | solution.py:219
  20.5 4.0 %collective-permute-start.5 = (bf16[128,128]{1,0:T(8,128)(2,1)S(1)}, bf16[128,128]{1,0:T(8,128)(2,1)S(1)}, u32[]{:S(2)}, u32[]{:S(2)}) collective-permute-start(bf16[128,128]{1,0:T(8,128)(2,1)S(1)} %get-tuple-element.25), channel_id=1, source_target_pairs={{0,2},{1,3},{2,0},{3,1},{4,6},{5,7},{6,4},{7,5},{8,10},{9,11},{10,... | collective-permute-start | bytes 98312 | tf_op jit(solution)/shard_map/ppermute | solution.py:216
  25.2 3.2 %collective-permute-start.8 = (f32[4,640]{1,0:T(4,128)S(1)}, f32[4,640]{1,0:T(4,128)S(1)}, u32[]{:S(2)}, u32[]{:S(2)}) collective-permute-start(f32[4,640]{1,0:T(4,128)S(1)} %get-tuple-element.30), channel_id=1, source_target_pairs={{0,3},{1,2},{2,1},{3,0},{4,7},{5,6},{6,5},{7,4},{8,11},{9,10},{10,... | collective-permute-start | bytes 30728 | tf_op jit(solution)/shard_map/ppermute | solution.py:216
  25.9 3.8 %collective-permute-start.9 = (f32[4,640]{1,0:T(4,128)S(1)}, f32[4,640]{1,0:T(4,128)S(1)}, u32[]{:S(2)}, u32[]{:S(2)}) collective-permute-start(f32[4,640]{1,0:T(4,128)S(1)} %get-tuple-element.31), channel_id=1, source_target_pairs={{0,2},{1,3},{2,0},{3,1},{4,6},{5,7},{6,4},{7,5},{8,10},{9,11},{10,... | collective-permute-start | bytes 30728 | tf_op jit(solution)/shard_map/ppermute | solution.py:216
  26.9 2.8 %collective-permute-start.10 = (f32[4,640]{1,0:T(4,128)S(1)}, f32[4,640]{1,0:T(4,128)S(1)}, u32[]{:S(2)}, u32[]{:S(2)}) collective-permute-start(f32[4,640]{1,0:T(4,128)S(1)} %get-tuple-element.32), channel_id=1, source_target_pairs={{0,1},{1,0},{2,3},{3,2},{4,5},{5,4},{6,7},{7,6},{8,9},{9,8},{10,11... | collective-permute-start | bytes 30728 | tf_op jit(solution)/shard_map/ppermute | solution.py:216
